TPU v7x, 32 devices: a whole 2x2x4 slice. The times are simulated.
32 devices in a mesh: slab: 8 (over z, x), depth: 4 (over y, core).
Axes of the slice: x: 2, y: 2, z: 4, core: 2. Of those that a mesh axis runs over, the one named last changes fastest.
Arguments:
- nutrient: float32 [64, 128, 512], P('slab', 'depth'), may hold values from 0.5 to 2
- species: bfloat16 [32768, 128], P(('slab', 'depth')), may hold values from -6 to 6
- agent_cell: int32 [32768], P(('slab', 'depth')), may hold values from 0 to 131071
- death_flag: int32 [32768], P(('slab', 'depth')), may hold values 0 or 1
- divide_flag: int32 [32768], P(('slab', 'depth')), may hold values 0 or 1
- slab_move: int32 [32768], P(('slab', 'depth')), may hold values from 0 to 2, as said below
- depth_route: int32 [32768, 1], P(('slab', 'depth')), may hold values from 0 to 3; in each aligned block of 1024 rows (0 to 1023, 1024 to 2047, ...) at most 512 rows name the same one
- net_weight: bfloat16 [128, 128], replicated, may hold values from -0.5 to 0.5
- sensing: float32 [128], replicated, may hold values from -1 to 1
- uptake_weight: bfloat16 [128], replicated, may hold values from -0.5 to 0.5
Outputs:
- nutrient_next: float32 [64, 128, 512], P('slab', 'depth')
- species_after_step: bfloat16 [73728, 128], P(('slab', 'depth'))
Inputs may be any that keep to these rules, and one draw needn't show every extreme that they name: `slab_move`: within each device's 1024 rows at most 128 carry 1 and at most 128 carry 2; some device has exactly 128 carrying 1 and some device exactly 128 carrying 2. `depth_route`: within each device's 1024 rows no depth index is named more than 512 times; one is named exactly 512 times in some device.
All inputs are finite; a program needn't handle non-finite values. No bound on the sum of `death_flag` or of `divide_flag` on one device may be relied on, other than what follows from the above.
Results may differ from a plain program's by a relative error of at most 0.0045.
Values may be sent and summed in bfloat16 or wider, within the bound.
No kernel may reach another device: no remote copies, remote signals or barrier semaphores. Data moves between devices by JAX's collectives and lax.ppermute only.
A program may use at most 128 MiB of HBM per device.

v0:
```python
import jax
import jax.numpy as jnp
from jax import lax
from jax.sharding import PartitionSpec as P

COARSE = 4
MIG = 128


SCREENING = 0.05
DAMPING = 2.0 / 3.0


def extended(block, sides, width, periodic):
    for axis, dim in sides:
        count = lax.axis_size(axis)
        forward = [(i, i + 1) for i in range(count - 1)]
        if periodic:
            forward.append((count - 1, 0))
        backward = [(target, source) for source, target in forward]
        low = lax.ppermute(
            lax.slice_in_dim(block, block.shape[dim] - width, None, axis=dim), axis, forward
        )
        high = lax.ppermute(lax.slice_in_dim(block, 0, width, axis=dim), axis, backward)
        block = jnp.concatenate([low, block, high], axis=dim)
    return block


def passed_along(array, axis, by):
    count = lax.axis_size(axis)
    return lax.ppermute(array, axis, [(i, (i + by) % count) for i in range(count)])


def neighbours(grid_field):
    first_padded = extended(grid_field.astype(jnp.bfloat16), (("slab", 0),), 1, True).astype(
        grid_field.dtype
    )
    neighbour_total = first_padded[2:] + first_padded[:-2]
    second_padded = extended(grid_field.astype(jnp.bfloat16), (("depth", 1),), 1, False).astype(
        grid_field.dtype
    )
    neighbour_total = neighbour_total + second_padded[:, 2:] + second_padded[:, :-2]
    third_padded = jnp.pad(grid_field, ((0, 0), (0, 0), (1, 1)))
    return neighbour_total + third_padded[:, :, 2:] + third_padded[:, :, :-2]


def relax_step(grid_field, target, centre):
    image_field = centre * grid_field - neighbours(grid_field)
    return grid_field + DAMPING * (target - image_field) / centre


def padded_relax(padded_field, padded_target, centre):
    inner = padded_field[1:-1, 1:-1]
    neighbour_total = padded_field[2:, 1:-1] + padded_field[:-2, 1:-1]
    neighbour_total = neighbour_total + padded_field[1:-1, 2:] + padded_field[1:-1, :-2]
    third_padded = jnp.pad(inner, ((0, 0), (0, 0), (1, 1)))
    neighbour_total = neighbour_total + third_padded[:, :, 2:] + third_padded[:, :, :-2]
    image_field = centre * inner - neighbour_total
    return inner + DAMPING * (padded_target - image_field) / centre


def smooth_phase(grid_field, target, centre):
    depths = lax.axis_size("depth")
    depth_place = lax.axis_index("depth")
    second_cells = grid_field.shape[1]
    row_index = jnp.arange(second_cells + 2, dtype=jnp.int32)
    keep_rows = jnp.logical_and(
        jnp.logical_or(row_index >= 1, depth_place > 0),
        jnp.logical_or(row_index <= second_cells, depth_place < depths - 1),
    )
    keep_rows = keep_rows.astype(jnp.float32)[None, :, None]
    stacked = jnp.stack([grid_field, target])
    slab_padded = extended(stacked.astype(jnp.bfloat16), (("slab", 1),), 2, True).astype(
        stacked.dtype
    )
    full_padded = extended(slab_padded.astype(jnp.bfloat16), (("depth", 2),), 2, False).astype(
        slab_padded.dtype
    )
    field_padded = full_padded[0]
    target_padded = full_padded[1]
    first_pass = padded_relax(field_padded, target_padded[1:-1, 1:-1], centre) * keep_rows
    grid_field = padded_relax(first_pass, target_padded[2:-2, 2:-2], centre)
    return grid_field


def network_update(row_block, sensed_level, keep_mask, net_weight, sensing):
    activation = jnp.dot(row_block, net_weight, preferred_element_type=jnp.float32)
    activation = activation + sensed_level.astype(jnp.float32)[..., None] * sensing
    return (
        keep_mask[..., None] * (0.5 * row_block.astype(jnp.float32) + jnp.tanh(activation))
    ).astype(jnp.bfloat16)


def local(
    nutrient,
    species,
    agent_cell,
    death_flag,
    divide_flag,
    slab_move,
    depth_route,
    net_weight,
    sensing,
    uptake_weight,
):
    depths = lax.axis_size("depth")
    rows_here = species.shape[0]
    capacity = 2 * rows_here // depths
    width = species.shape[1]
    flat_field = nutrient.reshape(-1)
    sample = flat_field[agent_cell]
    alive_mask = (1 - death_flag).astype(jnp.float32)
    uptake_score = jnp.dot(species, uptake_weight, preferred_element_type=jnp.float32)
    uptake = (
        alive_mask
        * (1.0 + divide_flag.astype(jnp.float32))
        * jax.nn.softplus(uptake_score)
        * sample
        / (0.5 + sample)
    )
    source = jnp.zeros_like(flat_field).at[agent_cell].add(uptake).reshape(nutrient.shape)
    sensed = sample.astype(jnp.bfloat16)
    stay_mask = slab_move == 0
    target_device = depth_route[:, 0]
    dest_hits = (target_device[:, None] == jnp.arange(depths, dtype=jnp.int32)[None, :]).astype(
        jnp.int32
    )
    earlier = jnp.cumsum(dest_hits, axis=0) - dest_hits
    destination_slot = jnp.sum(earlier * dest_hits, axis=1)
    outgoing = []
    updated = network_update(species, sensed, alive_mask, net_weight, sensing)
    remaining_agents = jnp.where(stay_mask[:, None], updated, jnp.zeros_like(updated))
    packed = (
        jnp.zeros((depths, capacity, width), jnp.bfloat16)
        .at[target_device, destination_slot]
        .set(remaining_agents)
    )
    arrived = lax.all_to_all(packed, "depth", split_axis=0, concat_axis=0, tiled=True)
    for move_code in (1, 2):
        chosen = (slab_move == move_code).astype(jnp.int32)
        rank_order = jnp.cumsum(chosen) - chosen
        outgoing.append(
            jnp.zeros((MIG, width), jnp.bfloat16)
            .at[jnp.where(chosen == 1, rank_order, MIG)]
            .set(updated, mode="drop")
        )
    arrivals = []
    for shift_by, buffer in ((1, outgoing[0]), (-1, outgoing[1])):
        arrivals.append(passed_along(buffer, "slab", shift_by))
    species_after_step = jnp.concatenate(
        [arrived.reshape(depths * capacity, width), arrivals[0], arrivals[1]], axis=0
    )
    centre = 6.0 + SCREENING
    target = SCREENING * nutrient - source
    grid_field = smooth_phase(nutrient, target, centre)
    residual = target - (centre * grid_field - neighbours(grid_field))
    first_cells, second_cells, third_cells = residual.shape
    coarse_target = 4.0 * residual.reshape(
        first_cells // 2, 2, second_cells // 2, 2, third_cells // 2, 2
    ).mean(axis=(1, 3, 5))
    coarse_centre = 6.0 + 4.0 * SCREENING
    coarse = jnp.zeros_like(coarse_target)
    for sweep_step in range(COARSE):
        coarse = relax_step(coarse, coarse_target, coarse_centre)
    grid_field = grid_field + jnp.repeat(jnp.repeat(jnp.repeat(coarse, 2, 0), 2, 1), 2, 2)
    grid_field = smooth_phase(grid_field, target, centre)
    return (grid_field, species_after_step)


def solution(mesh):
    in_specs = (
        P("slab", "depth", None),
        P(("slab", "depth"), None),
        P(("slab", "depth")),
        P(("slab", "depth")),
        P(("slab", "depth")),
        P(("slab", "depth")),
        P(("slab", "depth"), None),
        P(),
        P(),
        P(),
    )
    out_specs = (P("slab", "depth", None), P(("slab", "depth"), None))
    return jax.shard_map(local, mesh=mesh, in_specs=in_specs, out_specs=out_specs, check_vma=False)
```

profile of v0, /device:TPU:0, one launch (start us, length us, event | category | flops | bytes accessed | tf_op | source)
XLA Modules:
  0.0 177.3 jit_solution(1650585459823876579)
XLA Ops:
  0.7 2.4 %collective-permute-start.10 = (bf16[4,1,256]{2,1,0:T(2,128)(2,1)S(1)}, bf16[4,1,256]{2,1,0:T(2,128)(2,1)S(1)}, u32[]{:S(2)}, u32[]{:S(2)}) collective-permute-start(bf16[4,1,256]{2,1,0:T(2,128)(2,1)S(1)} %broadcast.149), channel_id=1, source_target_pairs={{0,1},{1,2},{2,3},{4,5},{5,6},{6,7},{8,9},{9,10},{10,11},{12,13},{... | collective-permute-start | bytes 6152 | tf_op jit(solution)/shard_map/ppermute | solution.py:21
  3.0 1.3 collective-permute-start.11
  4.3 0.7 broadcast_clamp_fusion
  5.0 1.2 copy.21
  6.2 6.2 %gather_fusion = f32[1024]{0:T(1024)S(1)} fusion(f32[131072]{0:T(1024)S(1)} %bitcast.59, s32[1024]{0:T(1024)S(1)} %get-tuple-element.52), kind=kCustom, calls=%fused_computation | custom fusion | bytes 12288 | tf_op jit(solution)/shard_map/gather | solution.py:111
  12.7 6.1 %scatter_custom_fusion = f32[131072]{0:T(1024)S(1)} fusion(s32[1024]{0:T(1024)S(1)} %get-tuple-element.53, f32[1024]{0:T(1024)S(1)} %get-tuple-element.51, f32[]{:T(128)} %constant.29.clone.1), kind=kCustom, calls=%fused_computation.100 | custom fusion | flops 1024 | bytes 524292 | tf_op jit(solution)/shard_map/scatter-add | solution.py:121
  19.0 2.4 %collective-permute-start = (bf16[2,2,32,512]{3,2,1,0:T(8,128)(2,1)S(1)}, bf16[2,2,32,512]{3,2,1,0:T(8,128)(2,1)S(1)}, u32[]{:S(2)}, u32[]{:S(2)}) collective-permute-start(bf16[2,2,32,512]{3,2,1,0:T(8,128)(2,1)S(1)} %get-tuple-element.26), channel_id=1, source_target_pairs={{0,4},{4,8},{8,12},{12,16},{16,20},{20,24},{24,28},{28,0},{1,5},{5... | collective-permute-start | bytes 393224 | tf_op jit(solution)/shard_map/ppermute | solution.py:21
  21.4 3.1 %collective-permute-start.1 = (bf16[2,2,32,512]{3,2,1,0:T(8,128)(2,1)S(1)}, bf16[2,2,32,512]{3,2,1,0:T(8,128)(2,1)S(1)}, u32[]{:S(2)}, u32[]{:S(2)}) collective-permute-start(bf16[2,2,32,512]{3,2,1,0:T(8,128)(2,1)S(1)} %get-tuple-element.27), channel_id=1, source_target_pairs={{4,0},{8,4},{12,8},{16,12},{20,16},{24,20},{28,24},{0,28},{5,1},{9... | collective-permute-start | bytes 393224 | tf_op jit(solution)/shard_map/ppermute | solution.py:24
  24.6 1.1 reduce-window.24
  26.9 4.5 %scatter_custom_fusion.3 = bf16[2048,128]{1,0:T(8,128)(2,1)} fusion(s32[1024]{0:T(1024)S(1)} %broadcast_select_fusion, bf16[]{:T(256)} %constant.78.clone.1, bf16[1024,128]{1,0:T(8,128)(2,1)S(1)} %fusion.3, pred[1024]{0:T(1024)(128)(4,1)S(1)} %get-tuple-element.47), kind=kCustom, calls=%fused_computation.97 | custom fusion | flops 131072 | bytes 788480
  31.4 5.4 %all-to-all-start = ((bf16[4,512,128]{2,1,0:T(8,128)(2,1)}), bf16[4,512,128]{2,1,0:T(8,128)(2,1)}, u32[]{:S(2)}, u32[]{:S(2)}) async-start(bf16[4,512,128]{2,1,0:T(8,128)(2,1)} %bitcast.15), calls=%async_computation | async-start | bytes 1048576 | tf_op jit(solution)/shard_map/all_to_all | solution.py:138
  37.9 3.7 %scatter_custom_fusion.1 = bf16[128,128]{1,0:T(8,128)(2,1)} fusion(s32[1024]{0:T(1024)S(1)} %compare_select_fusion.3, bf16[1024,128]{1,0:T(8,128)(2,1)S(1)} %fusion.3, bf16[]{:T(256)} %constant.78.clone.1), kind=kCustom, calls=%fused_computation.169 | custom fusion | bytes 32770 | tf_op jit(solution)/shard_map/scatter | solution.py:145
  41.6 4.7 %collective-permute-start.9 = (bf16[1,16,256]{2,1,0:T(8,128)(2,1)S(1)}, bf16[1,16,256]{2,1,0:T(8,128)(2,1)S(1)}, u32[]{:S(2)}, u32[]{:S(2)}) collective-permute-start(bf16[1,16,256]{2,1,0:T(8,128)(2,1)S(1)} %broadcast.147), channel_id=1, source_target_pairs={{4,0},{8,4},{12,8},{16,12},{20,16},{24,20},{28,24},{0,28},{5,1},{9... | collective-permute-start | bytes 24584 | tf_op jit(solution)/shard_map/ppermute | solution.py:24
  46.6 2.2 %collective-permute-start.2 = (bf16[2,12,2,512]{3,2,1,0:T(2,128)(2,1)S(1)}, bf16[2,12,2,512]{3,2,1,0:T(2,128)(2,1)S(1)}, u32[]{:S(2)}, u32[]{:S(2)}) collective-permute-start(bf16[2,12,2,512]{3,2,1,0:T(2,128)(2,1)S(1)} %get-tuple-element.22), channel_id=1, source_target_pairs={{0,1},{1,2},{2,3},{4,5},{5,6},{6,7},{8,9},{9,10},{10,11},{12,13},{... | collective-permute-start | bytes 147464 | tf_op jit(solution)/shard_map/ppermute | solution.py:21
  48.8 1.3 collective-permute-start.3
  50.2 4.0 %collective-permute-done.3 = bf16[2,12,2,512]{3,2,1,0:T(2,128)(2,1)S(1)} collective-permute-done((bf16[2,12,2,512]{3,2,1,0:T(2,128)(2,1)S(1)}, bf16[2,12,2,512]{3,2,1,0:T(2,128)(2,1)S(1)}, u32[]{:S(2)}, u32[]{:S(2)}) %collective-permute-start.3) | collective-permute-done | bytes 49184 | tf_op jit(solution)/shard_map/ppermute | solution.py:24
  54.8 0.8 fusion.20
  55.6 0.6 fusion.101
  56.2 4.7 %collective-permute-start.6 = (bf16[8,1,512]{2,1,0:T(2,128)(2,1)S(1)}, bf16[8,1,512]{2,1,0:T(2,128)(2,1)S(1)}, u32[]{:S(2)}, u32[]{:S(2)}) collective-permute-start(bf16[8,1,512]{2,1,0:T(2,128)(2,1)S(1)} %get-tuple-element.32), channel_id=1, source_target_pairs={{0,1},{1,2},{2,3},{4,5},{5,6},{6,7},{8,9},{9,10},{10,11},{12,13},{... | collective-permute-start | bytes 24584 | tf_op jit(solution)/shard_map/ppermute | solution.py:21
  60.9 1.3 collective-permute-start.7
  62.3 4.9 %collective-permute-start.5 = (bf16[1,32,512]{2,1,0:T(8,128)(2,1)S(1)}, bf16[1,32,512]{2,1,0:T(8,128)(2,1)S(1)}, u32[]{:S(2)}, u32[]{:S(2)}) collective-permute-start(bf16[1,32,512]{2,1,0:T(8,128)(2,1)S(1)} %get-tuple-element.31), channel_id=1, source_target_pairs={{4,0},{8,4},{12,8},{16,12},{20,16},{24,20},{28,24},{0,28},{5,1},{9... | collective-permute-start | bytes 98312 | tf_op jit(solution)/shard_map/ppermute | solution.py:24
  67.4 1.5 collective-permute-done.4
  69.5 34.8 %reshape.101 = f32[4,2,16,2,256,2]{5,4,3,2,1,0:T(8,128)} reshape(f32[8,32,512]{2,1,0:T(8,128)S(1)} %fusion.41) | data formatting | bytes 1048576 | tf_op jit(solution)/shard_map/reshape | solution.py:158
  104.3 12.2 %reduce_sum.20 = f32[4,16,256]{2,1,0:T(8,128)S(1)} reduce(f32[4,2,16,2,256,2]{5,4,3,2,1,0:T(8,128)} %reshape.101, f32[]{:T(128)} %constant.29.clone.1), dimensions={1,3,5}, to_apply=%region_1.2 | reduce | flops 114688 | bytes 589828 | tf_op jit(solution)/shard_map/reduce_sum | solution.py:160
  116.8 5.2 %collective-permute-start.13 = (bf16[1,16,256]{2,1,0:T(8,128)(2,1)S(1)}, bf16[1,16,256]{2,1,0:T(8,128)(2,1)S(1)}, u32[]{:S(2)}, u32[]{:S(2)}) collective-permute-start(bf16[1,16,256]{2,1,0:T(8,128)(2,1)S(1)} %get-tuple-element.43), channel_id=1, source_target_pairs={{4,0},{8,4},{12,8},{16,12},{20,16},{24,20},{28,24},{0,28},{5,1},{9... | collective-permute-start | bytes 24584 | tf_op jit(solution)/shard_map/ppermute | solution.py:24
  122.0 1.7 collective-permute-start.14
  123.7 1.3 collective-permute-start.15
  125.0 3.6 %collective-permute-done.15 = bf16[4,1,256]{2,1,0:T(2,128)(2,1)S(1)} collective-permute-done((bf16[4,1,256]{2,1,0:T(2,128)(2,1)S(1)}, bf16[4,1,256]{2,1,0:T(2,128)(2,1)S(1)}, u32[]{:S(2)}, u32[]{:S(2)}) %collective-permute-start.15) | collective-permute-done | bytes 2080 | tf_op jit(solution)/shard_map/ppermute | solution.py:24
  128.8 4.3 %collective-permute-start.18 = (bf16[4,1,256]{2,1,0:T(2,128)(2,1)S(1)}, bf16[4,1,256]{2,1,0:T(2,128)(2,1)S(1)}, u32[]{:S(2)}, u32[]{:S(2)}) collective-permute-start(bf16[4,1,256]{2,1,0:T(2,128)(2,1)S(1)} %get-tuple-element.40), channel_id=1, source_target_pairs={{0,1},{1,2},{2,3},{4,5},{5,6},{6,7},{8,9},{9,10},{10,11},{12,13},{... | collective-permute-start | bytes 6152 | tf_op jit(solution)/shard_map/ppermute | solution.py:21
  133.1 1.3 collective-permute-start.19
  134.5 4.7 %collective-permute-start.17 = (bf16[1,16,256]{2,1,0:T(8,128)(2,1)S(1)}, bf16[1,16,256]{2,1,0:T(8,128)(2,1)S(1)}, u32[]{:S(2)}, u32[]{:S(2)}) collective-permute-start(bf16[1,16,256]{2,1,0:T(8,128)(2,1)S(1)} %get-tuple-element.39), channel_id=1, source_target_pairs={{4,0},{8,4},{12,8},{16,12},{20,16},{24,20},{28,24},{0,28},{5,1},{9... | collective-permute-start | bytes 24584 | tf_op jit(solution)/shard_map/ppermute | solution.py:24
  139.2 1.6 collective-permute-done.16
  141.0 2.0 %collective-permute-start.22 = (bf16[4,1,256]{2,1,0:T(2,128)(2,1)S(1)}, bf16[4,1,256]{2,1,0:T(2,128)(2,1)S(1)}, u32[]{:S(2)}, u32[]{:S(2)}) collective-permute-start(bf16[4,1,256]{2,1,0:T(2,128)(2,1)S(1)} %get-tuple-element.36), channel_id=1, source_target_pairs={{0,1},{1,2},{2,3},{4,5},{5,6},{6,7},{8,9},{9,10},{10,11},{12,13},{... | collective-permute-start | bytes 6152 | tf_op jit(solution)/shard_map/ppermute | solution.py:21
  143.0 1.3 collective-permute-start.23
  144.4 4.7 %collective-permute-start.21 = (bf16[1,16,256]{2,1,0:T(8,128)(2,1)S(1)}, bf16[1,16,256]{2,1,0:T(8,128)(2,1)S(1)}, u32[]{:S(2)}, u32[]{:S(2)}) collective-permute-start(bf16[1,16,256]{2,1,0:T(8,128)(2,1)S(1)} %get-tuple-element.35), channel_id=1, source_target_pairs={{4,0},{8,4},{12,8},{16,12},{20,16},{24,20},{28,24},{0,28},{5,1},{9... | collective-permute-start | bytes 24584 | tf_op jit(solution)/shard_map/ppermute | solution.py:24
  149.1 1.6 collective-permute-done.20
  151.1 1.4 copy.19
  152.4 1.4 broadcast_in_dim.54
  153.8 0.7 copy.20
  154.7 4.8 %collective-permute-start.25 = (bf16[2,2,32,512]{3,2,1,0:T(8,128)(2,1)S(1)}, bf16[2,2,32,512]{3,2,1,0:T(8,128)(2,1)S(1)}, u32[]{:S(2)}, u32[]{:S(2)}) collective-permute-start(bf16[2,2,32,512]{3,2,1,0:T(8,128)(2,1)S(1)} %get-tuple-element.25), channel_id=1, source_target_pairs={{4,0},{8,4},{12,8},{16,12},{20,16},{24,20},{28,24},{0,28},{5,1},{9... | collective-permute-start | bytes 393224 | tf_op jit(solution)/shard_map/ppermute | solution.py:24
  159.5 3.5 %scatter_custom_fusion.2 = bf16[128,128]{1,0:T(8,128)(2,1)S(1)} fusion(s32[1024]{0:T(1024)S(1)} %compare_select_fusion.2, bf16[1024,128]{1,0:T(8,128)(2,1)} %copy-done.2, bf16[]{:T(256)} %constant.78.clone.1), kind=kCustom, calls=%fused_computation.167 | custom fusion | bytes 33280 | tf_op jit(solution)/shard_map/scatter | solution.py:145
  163.0 2.0 %collective-permute-start.29 = (bf16[128,128]{1,0:T(8,128)(2,1)S(1)}, bf16[128,128]{1,0:T(8,128)(2,1)S(1)}, u32[]{:S(2)}, u32[]{:S(2)}) collective-permute-start(bf16[128,128]{1,0:T(8,128)(2,1)S(1)} %scatter_custom_fusion.2), channel_id=1, source_target_pairs={{0,28},{4,0},{8,4},{12,8},{16,12},{20,16},{24,20},{28,24},{1,29},{... | collective-permute-start | bytes 98312 | tf_op jit(solution)/shard_map/ppermute | solution.py:31
  165.2 2.9 %collective-permute-start.26 = (bf16[2,12,2,512]{3,2,1,0:T(2,128)(2,1)S(1)}, bf16[2,12,2,512]{3,2,1,0:T(2,128)(2,1)S(1)}, u32[]{:S(2)}, u32[]{:S(2)}) collective-permute-start(bf16[2,12,2,512]{3,2,1,0:T(2,128)(2,1)S(1)} %get-tuple-element.20), channel_id=1, source_target_pairs={{0,1},{1,2},{2,3},{4,5},{5,6},{6,7},{8,9},{9,10},{10,11},{12,13},{... | collective-permute-start | bytes 147464 | tf_op jit(solution)/shard_map/ppermute | solution.py:21
  168.2 1.3 collective-permute-start.27
  169.5 1.9 %pad_maximum_fusion.4 = bf16[2304,128]{1,0:T(8,128)(2,1)} fusion(bf16[128,128]{1,0:T(8,128)(2,1)S(1)} %collective-permute-done.29, bf16[128,128]{1,0:T(8,128)(2,1)} %collective-permute-done.28, bf16[2048,128]{1,0:T(8,128)(2,1)} %bitcast.16), kind=kLoop, calls=%fused_computation.62 | loop fusion | flops 1769472 | bytes 1179648 | tf_op jit(solution)/shard_map/concatenate | solution.py:150
  171.4 3.1 %collective-permute-done.27 = bf16[2,12,2,512]{3,2,1,0:T(2,128)(2,1)S(1)} collective-permute-done((bf16[2,12,2,512]{3,2,1,0:T(2,128)(2,1)S(1)}, bf16[2,12,2,512]{3,2,1,0:T(2,128)(2,1)S(1)}, u32[]{:S(2)}, u32[]{:S(2)}) %collective-permute-start.27) | collective-permute-done | bytes 49184 | tf_op jit(solution)/shard_map/ppermute | solution.py:24
  175.2 0.8 fusion.27
  176.0 1.3 fusion.47
  (130 shorter events, 6.5 us)
Async XLA Ops:
  0.6 25.8 %copy-start = (bf16[128,128]{1,0:T(8,128)(2,1)S(1)}, bf16[128,128]{1,0:T(8,128)(2,1)}, u32[]{:S(2)}) copy-start(bf16[128,128]{1,0:T(8,128)(2,1)} %param.17) | copy-start | bytes 98308
  0.7 41.0 %collective-permute-start.10 = (bf16[4,1,256]{2,1,0:T(2,128)(2,1)S(1)}, bf16[4,1,256]{2,1,0:T(2,128)(2,1)S(1)}, u32[]{:S(2)}, u32[]{:S(2)}) collective-permute-start(bf16[4,1,256]{2,1,0:T(2,128)(2,1)S(1)} %broadcast.149), channel_id=1, source_target_pairs={{0,1},{1,2},{2,3},{4,5},{5,6},{6,7},{8,9},{9,10},{10,11},{12,13},{... | collective-permute-start | bytes 6152 | tf_op jit(solution)/shard_map/ppermute | solution.py:21
  3.0 43.3 %collective-permute-start.11 = (bf16[4,1,256]{2,1,0:T(2,128)(2,1)S(1)}, bf16[4,1,256]{2,1,0:T(2,128)(2,1)S(1)}, u32[]{:S(2)}, u32[]{:S(2)}) collective-permute-start(bf16[4,1,256]{2,1,0:T(2,128)(2,1)S(1)} %broadcast.149), channel_id=1, source_target_pairs={{1,0},{2,1},{3,2},{5,4},{6,5},{7,6},{9,8},{10,9},{11,10},{13,12},{... | collective-permute-start | bytes 6152 | tf_op jit(solution)/shard_map/ppermute | solution.py:24
  6.2 6.2 %copy-start.3 = (bf16[1024,128]{1,0:T(8,128)(2,1)S(1)}, bf16[1024,128]{1,0:T(8,128)(2,1)}, u32[]{:S(2)}) copy-start(bf16[1024,128]{1,0:T(8,128)(2,1)} %param.11) | copy-start | bytes 786436
  6.2 6.2 %copy-start.8 = (bf16[128]{0:T(256)(128)(2,1)S(1)}, bf16[128]{0:T(256)(128)(2,1)}, u32[]{:S(2)}) copy-start(bf16[128]{0:T(256)(128)(2,1)} %param.19) | copy-start | bytes 772
  6.2 6.4 %copy-start.5 = (s32[1024]{0:T(1024)S(1)}, s32[1024]{0:T(1024)}, u32[]{:S(2)}) copy-start(s32[1024]{0:T(1024)} %param.13) | copy-start | bytes 12292
  6.2 6.4 %copy-start.6 = (s32[1024]{0:T(1024)S(1)}, s32[1024]{0:T(1024)}, u32[]{:S(2)}) copy-start(s32[1024]{0:T(1024)} %param.14) | copy-start | bytes 12292
  12.4 6.4 %copy-start.1 = (f32[8,32,512]{2,1,0:T(8,128)S(1)}, f32[8,32,512]{2,1,0:T(8,128)}, u32[]{:S(2)}) copy-start(f32[8,32,512]{2,1,0:T(8,128)} %param.10) | copy-start | bytes 1572868
  12.6 11.9 %copy-start.4 = (s32[1024,1]{0,1:T(1,128)S(1)}, s32[1024,1]{0,1:T(1,128)}, u32[]{:S(2)}) copy-start(s32[1024,1]{0,1:T(1,128)} %param.16) | copy-start | bytes 12292
  12.7 13.6 %copy-start.10 = (s32[2]{0:T(128)S(1)}, s32[2]{0:T(128)}, u32[]{:S(2)}) copy-start(s32[2]{0:T(128)} %constant.104) | copy-start | bytes 28
  12.7 13.7 %copy-start.9 = (s32[2]{0:T(128)S(1)}, s32[2]{0:T(128)}, u32[]{:S(2)}) copy-start(s32[2]{0:T(128)} %constant.107) | copy-start | bytes 28
  12.7 13.7 %copy-start.7 = (s32[1024]{0:T(1024)S(1)}, s32[1024]{0:T(1024)}, u32[]{:S(2)}) copy-start(s32[1024]{0:T(1024)} %param.15) | copy-start | bytes 12292
  12.7 13.8 %copy-start.11 = (f32[128]{0:T(128)S(1)}, f32[128]{0:T(128)}, u32[]{:S(2)}) copy-start(f32[128]{0:T(128)} %param.18) | copy-start | bytes 1540
  19.0 27.3 %collective-permute-start = (bf16[2,2,32,512]{3,2,1,0:T(8,128)(2,1)S(1)}, bf16[2,2,32,512]{3,2,1,0:T(8,128)(2,1)S(1)}, u32[]{:S(2)}, u32[]{:S(2)}) collective-permute-start(bf16[2,2,32,512]{3,2,1,0:T(8,128)(2,1)S(1)} %get-tuple-element.26), channel_id=1, source_target_pairs={{0,4},{4,8},{8,12},{12,16},{16,20},{20,24},{24,28},{28,0},{1,5},{5... | collective-permute-start | bytes 393224 | tf_op jit(solution)/shard_map/ppermute | solution.py:21
  21.4 25.0 %collective-permute-start.1 = (bf16[2,2,32,512]{3,2,1,0:T(8,128)(2,1)S(1)}, bf16[2,2,32,512]{3,2,1,0:T(8,128)(2,1)S(1)}, u32[]{:S(2)}, u32[]{:S(2)}) collective-permute-start(bf16[2,2,32,512]{3,2,1,0:T(8,128)(2,1)S(1)} %get-tuple-element.27), channel_id=1, source_target_pairs={{4,0},{8,4},{12,8},{16,12},{20,16},{24,20},{28,24},{0,28},{5,1},{9... | collective-permute-start | bytes 393224 | tf_op jit(solution)/shard_map/ppermute | solution.py:24
  24.5 25.6 %collective-permute-start.8 = (bf16[1,16,256]{2,1,0:T(8,128)(2,1)S(1)}, bf16[1,16,256]{2,1,0:T(8,128)(2,1)S(1)}, u32[]{:S(2)}, u32[]{:S(2)}) collective-permute-start(bf16[1,16,256]{2,1,0:T(8,128)(2,1)S(1)} %broadcast.147), channel_id=1, source_target_pairs={{0,4},{4,8},{8,12},{12,16},{16,20},{20,24},{24,28},{28,0},{1,5},{5... | collective-permute-start | bytes 24584 | tf_op jit(solution)/shard_map/ppermute | solution.py:21
  26.8 19.5 %copy-start.2 = (bf16[1024,128]{1,0:T(8,128)(2,1)}, bf16[1024,128]{1,0:T(8,128)(2,1)S(1)}, u32[]{:S(2)}) copy-start(bf16[1024,128]{1,0:T(8,128)(2,1)S(1)} %fusion.3) | copy-start | bytes 786436
  31.4 138.1 %all-to-all-start = ((bf16[4,512,128]{2,1,0:T(8,128)(2,1)}), bf16[4,512,128]{2,1,0:T(8,128)(2,1)}, u32[]{:S(2)}, u32[]{:S(2)}) async-start(bf16[4,512,128]{2,1,0:T(8,128)(2,1)} %bitcast.15), calls=%async_computation | async-start | bytes 1048576 | tf_op jit(solution)/shard_map/all_to_all | solution.py:138
  41.6 8.5 %collective-permute-start.9 = (bf16[1,16,256]{2,1,0:T(8,128)(2,1)S(1)}, bf16[1,16,256]{2,1,0:T(8,128)(2,1)S(1)}, u32[]{:S(2)}, u32[]{:S(2)}) collective-permute-start(bf16[1,16,256]{2,1,0:T(8,128)(2,1)S(1)} %broadcast.147), channel_id=1, source_target_pairs={{4,0},{8,4},{12,8},{16,12},{20,16},{24,20},{28,24},{0,28},{5,1},{9... | collective-permute-start | bytes 24584 | tf_op jit(solution)/shard_map/ppermute | solution.py:24
  46.3 123.1 %collective-permute-start.28 = (bf16[128,128]{1,0:T(8,128)(2,1)}, bf16[128,128]{1,0:T(8,128)(2,1)}, u32[]{:S(2)}, u32[]{:S(2)}) collective-permute-start(bf16[128,128]{1,0:T(8,128)(2,1)} %scatter_custom_fusion.1), channel_id=1, source_target_pairs={{0,4},{4,8},{8,12},{12,16},{16,20},{20,24},{24,28},{28,0},{1,5},{5... | collective-permute-start | bytes 98312 | tf_op jit(solution)/shard_map/ppermute | solution.py:31
  46.6 3.6 %collective-permute-start.2 = (bf16[2,12,2,512]{3,2,1,0:T(2,128)(2,1)S(1)}, bf16[2,12,2,512]{3,2,1,0:T(2,128)(2,1)S(1)}, u32[]{:S(2)}, u32[]{:S(2)}) collective-permute-start(bf16[2,12,2,512]{3,2,1,0:T(2,128)(2,1)S(1)} %get-tuple-element.22), channel_id=1, source_target_pairs={{0,1},{1,2},{2,3},{4,5},{5,6},{6,7},{8,9},{9,10},{10,11},{12,13},{... | collective-permute-start | bytes 147464 | tf_op jit(solution)/shard_map/ppermute | solution.py:21
  48.8 5.3 %collective-permute-start.3 = (bf16[2,12,2,512]{3,2,1,0:T(2,128)(2,1)S(1)}, bf16[2,12,2,512]{3,2,1,0:T(2,128)(2,1)S(1)}, u32[]{:S(2)}, u32[]{:S(2)}) collective-permute-start(bf16[2,12,2,512]{3,2,1,0:T(2,128)(2,1)S(1)} %get-tuple-element.23), channel_id=1, source_target_pairs={{1,0},{2,1},{3,2},{5,4},{6,5},{7,6},{9,8},{10,9},{11,10},{13,12},{... | collective-permute-start | bytes 147464 | tf_op jit(solution)/shard_map/ppermute | solution.py:24
  56.2 11.0 %collective-permute-start.6 = (bf16[8,1,512]{2,1,0:T(2,128)(2,1)S(1)}, bf16[8,1,512]{2,1,0:T(2,128)(2,1)S(1)}, u32[]{:S(2)}, u32[]{:S(2)}) collective-permute-start(bf16[8,1,512]{2,1,0:T(2,128)(2,1)S(1)} %get-tuple-element.32), channel_id=1, source_target_pairs={{0,1},{1,2},{2,3},{4,5},{5,6},{6,7},{8,9},{9,10},{10,11},{12,13},{... | collective-permute-start | bytes 24584 | tf_op jit(solution)/shard_map/ppermute | solution.py:21
  60.9 6.3 %collective-permute-start.7 = (bf16[8,1,512]{2,1,0:T(2,128)(2,1)S(1)}, bf16[8,1,512]{2,1,0:T(2,128)(2,1)S(1)}, u32[]{:S(2)}, u32[]{:S(2)}) collective-permute-start(bf16[8,1,512]{2,1,0:T(2,128)(2,1)S(1)} %get-tuple-element.33), channel_id=1, source_target_pairs={{1,0},{2,1},{3,2},{5,4},{6,5},{7,6},{9,8},{10,9},{11,10},{13,12},{... | collective-permute-start | bytes 24584 | tf_op jit(solution)/shard_map/ppermute | solution.py:24
  62.2 6.7 %collective-permute-start.4 = (bf16[1,32,512]{2,1,0:T(8,128)(2,1)S(1)}, bf16[1,32,512]{2,1,0:T(8,128)(2,1)S(1)}, u32[]{:S(2)}, u32[]{:S(2)}) collective-permute-start(bf16[1,32,512]{2,1,0:T(8,128)(2,1)S(1)} %get-tuple-element.30), channel_id=1, source_target_pairs={{0,4},{4,8},{8,12},{12,16},{16,20},{20,24},{24,28},{28,0},{1,5},{5... | collective-permute-start | bytes 98312 | tf_op jit(solution)/shard_map/ppermute | solution.py:21
  62.3 6.6 %collective-permute-start.5 = (bf16[1,32,512]{2,1,0:T(8,128)(2,1)S(1)}, bf16[1,32,512]{2,1,0:T(8,128)(2,1)S(1)}, u32[]{:S(2)}, u32[]{:S(2)}) collective-permute-start(bf16[1,32,512]{2,1,0:T(8,128)(2,1)S(1)} %get-tuple-element.31), channel_id=1, source_target_pairs={{4,0},{8,4},{12,8},{16,12},{20,16},{24,20},{28,24},{0,28},{5,1},{9... | collective-permute-start | bytes 98312 | tf_op jit(solution)/shard_map/ppermute | solution.py:24
  116.7 11.9 %collective-permute-start.12 = (bf16[1,16,256]{2,1,0:T(8,128)(2,1)S(1)}, bf16[1,16,256]{2,1,0:T(8,128)(2,1)S(1)}, u32[]{:S(2)}, u32[]{:S(2)}) collective-permute-start(bf16[1,16,256]{2,1,0:T(8,128)(2,1)S(1)} %get-tuple-element.42), channel_id=1, source_target_pairs={{0,4},{4,8},{8,12},{12,16},{16,20},{20,24},{24,28},{28,0},{1,5},{5... | collective-permute-start | bytes 24584 | tf_op jit(solution)/shard_map/ppermute | solution.py:21
  116.8 11.9 %collective-permute-start.13 = (bf16[1,16,256]{2,1,0:T(8,128)(2,1)S(1)}, bf16[1,16,256]{2,1,0:T(8,128)(2,1)S(1)}, u32[]{:S(2)}, u32[]{:S(2)}) collective-permute-start(bf16[1,16,256]{2,1,0:T(8,128)(2,1)S(1)} %get-tuple-element.43), channel_id=1, source_target_pairs={{4,0},{8,4},{12,8},{16,12},{20,16},{24,20},{28,24},{0,28},{5,1},{9... | collective-permute-start | bytes 24584 | tf_op jit(solution)/shard_map/ppermute | solution.py:24
  122.0 3.1 %collective-permute-start.14 = (bf16[4,1,256]{2,1,0:T(2,128)(2,1)S(1)}, bf16[4,1,256]{2,1,0:T(2,128)(2,1)S(1)}, u32[]{:S(2)}, u32[]{:S(2)}) collective-permute-start(bf16[4,1,256]{2,1,0:T(2,128)(2,1)S(1)} %get-tuple-element.44), channel_id=1, source_target_pairs={{0,1},{1,2},{2,3},{4,5},{5,6},{6,7},{8,9},{9,10},{10,11},{12,13},{... | collective-permute-start | bytes 6152 | tf_op jit(solution)/shard_map/ppermute | solution.py:21
  123.7 4.9 %collective-permute-start.15 = (bf16[4,1,256]{2,1,0:T(2,128)(2,1)S(1)}, bf16[4,1,256]{2,1,0:T(2,128)(2,1)S(1)}, u32[]{:S(2)}, u32[]{:S(2)}) collective-permute-start(bf16[4,1,256]{2,1,0:T(2,128)(2,1)S(1)} %get-tuple-element.45), channel_id=1, source_target_pairs={{1,0},{2,1},{3,2},{5,4},{6,5},{7,6},{9,8},{10,9},{11,10},{13,12},{... | collective-permute-start | bytes 6152 | tf_op jit(solution)/shard_map/ppermute | solution.py:24
  128.8 10.4 %collective-permute-start.18 = (bf16[4,1,256]{2,1,0:T(2,128)(2,1)S(1)}, bf16[4,1,256]{2,1,0:T(2,128)(2,1)S(1)}, u32[]{:S(2)}, u32[]{:S(2)}) collective-permute-start(bf16[4,1,256]{2,1,0:T(2,128)(2,1)S(1)} %get-tuple-element.40), channel_id=1, source_target_pairs={{0,1},{1,2},{2,3},{4,5},{5,6},{6,7},{8,9},{9,10},{10,11},{12,13},{... | collective-permute-start | bytes 6152 | tf_op jit(solution)/shard_map/ppermute | solution.py:21
  133.1 6.1 %collective-permute-start.19 = (bf16[4,1,256]{2,1,0:T(2,128)(2,1)S(1)}, bf16[4,1,256]{2,1,0:T(2,128)(2,1)S(1)}, u32[]{:S(2)}, u32[]{:S(2)}) collective-permute-start(bf16[4,1,256]{2,1,0:T(2,128)(2,1)S(1)} %get-tuple-element.41), channel_id=1, source_target_pairs={{1,0},{2,1},{3,2},{5,4},{6,5},{7,6},{9,8},{10,9},{11,10},{13,12},{... | collective-permute-start | bytes 6152 | tf_op jit(solution)/shard_map/ppermute | solution.py:24
  134.4 6.4 %collective-permute-start.16 = (bf16[1,16,256]{2,1,0:T(8,128)(2,1)S(1)}, bf16[1,16,256]{2,1,0:T(8,128)(2,1)S(1)}, u32[]{:S(2)}, u32[]{:S(2)}) collective-permute-start(bf16[1,16,256]{2,1,0:T(8,128)(2,1)S(1)} %get-tuple-element.38), channel_id=1, source_target_pairs={{0,4},{4,8},{8,12},{12,16},{16,20},{20,24},{24,28},{28,0},{1,5},{5... | collective-permute-start | bytes 24584 | tf_op jit(solution)/shard_map/ppermute | solution.py:21
  134.5 6.3 %collective-permute-start.17 = (bf16[1,16,256]{2,1,0:T(8,128)(2,1)S(1)}, bf16[1,16,256]{2,1,0:T(8,128)(2,1)S(1)}, u32[]{:S(2)}, u32[]{:S(2)}) collective-permute-start(bf16[1,16,256]{2,1,0:T(8,128)(2,1)S(1)} %get-tuple-element.39), channel_id=1, source_target_pairs={{4,0},{8,4},{12,8},{16,12},{20,16},{24,20},{28,24},{0,28},{5,1},{9... | collective-permute-start | bytes 24584 | tf_op jit(solution)/shard_map/ppermute | solution.py:24
  141.0 8.1 %collective-permute-start.22 = (bf16[4,1,256]{2,1,0:T(2,128)(2,1)S(1)}, bf16[4,1,256]{2,1,0:T(2,128)(2,1)S(1)}, u32[]{:S(2)}, u32[]{:S(2)}) collective-permute-start(bf16[4,1,256]{2,1,0:T(2,128)(2,1)S(1)} %get-tuple-element.36), channel_id=1, source_target_pairs={{0,1},{1,2},{2,3},{4,5},{5,6},{6,7},{8,9},{9,10},{10,11},{12,13},{... | collective-permute-start | bytes 6152 | tf_op jit(solution)/shard_map/ppermute | solution.py:21
  143.0 6.1 %collective-permute-start.23 = (bf16[4,1,256]{2,1,0:T(2,128)(2,1)S(1)}, bf16[4,1,256]{2,1,0:T(2,128)(2,1)S(1)}, u32[]{:S(2)}, u32[]{:S(2)}) collective-permute-start(bf16[4,1,256]{2,1,0:T(2,128)(2,1)S(1)} %get-tuple-element.37), channel_id=1, source_target_pairs={{1,0},{2,1},{3,2},{5,4},{6,5},{7,6},{9,8},{10,9},{11,10},{13,12},{... | collective-permute-start | bytes 6152 | tf_op jit(solution)/shard_map/ppermute | solution.py:24
  144.3 6.4 %collective-permute-start.20 = (bf16[1,16,256]{2,1,0:T(8,128)(2,1)S(1)}, bf16[1,16,256]{2,1,0:T(8,128)(2,1)S(1)}, u32[]{:S(2)}, u32[]{:S(2)}) collective-permute-start(bf16[1,16,256]{2,1,0:T(8,128)(2,1)S(1)} %get-tuple-element.34), channel_id=1, source_target_pairs={{0,4},{4,8},{8,12},{12,16},{16,20},{20,24},{24,28},{28,0},{1,5},{5... | collective-permute-start | bytes 24584 | tf_op jit(solution)/shard_map/ppermute | solution.py:21
  144.4 6.3 %collective-permute-start.21 = (bf16[1,16,256]{2,1,0:T(8,128)(2,1)S(1)}, bf16[1,16,256]{2,1,0:T(8,128)(2,1)S(1)}, u32[]{:S(2)}, u32[]{:S(2)}) collective-permute-start(bf16[1,16,256]{2,1,0:T(8,128)(2,1)S(1)} %get-tuple-element.35), channel_id=1, source_target_pairs={{4,0},{8,4},{12,8},{16,12},{20,16},{24,20},{28,24},{0,28},{5,1},{9... | collective-permute-start | bytes 24584 | tf_op jit(solution)/shard_map/ppermute | solution.py:24
  154.6 10.4 %collective-permute-start.24 = (bf16[2,2,32,512]{3,2,1,0:T(8,128)(2,1)S(1)}, bf16[2,2,32,512]{3,2,1,0:T(8,128)(2,1)S(1)}, u32[]{:S(2)}, u32[]{:S(2)}) collective-permute-start(bf16[2,2,32,512]{3,2,1,0:T(8,128)(2,1)S(1)} %get-tuple-element.24), channel_id=1, source_target_pairs={{0,4},{4,8},{8,12},{12,16},{16,20},{20,24},{24,28},{28,0},{1,5},{5... | collective-permute-start | bytes 393224 | tf_op jit(solution)/shard_map/ppermute | solution.py:21
  154.7 10.4 %collective-permute-start.25 = (bf16[2,2,32,512]{3,2,1,0:T(8,128)(2,1)S(1)}, bf16[2,2,32,512]{3,2,1,0:T(8,128)(2,1)S(1)}, u32[]{:S(2)}, u32[]{:S(2)}) collective-permute-start(bf16[2,2,32,512]{3,2,1,0:T(8,128)(2,1)S(1)} %get-tuple-element.25), channel_id=1, source_target_pairs={{4,0},{8,4},{12,8},{16,12},{20,16},{24,20},{28,24},{0,28},{5,1},{9... | collective-permute-start | bytes 393224 | tf_op jit(solution)/shard_map/ppermute | solution.py:24
  163.0 6.5 %collective-permute-start.29 = (bf16[128,128]{1,0:T(8,128)(2,1)S(1)}, bf16[128,128]{1,0:T(8,128)(2,1)S(1)}, u32[]{:S(2)}, u32[]{:S(2)}) collective-permute-start(bf16[128,128]{1,0:T(8,128)(2,1)S(1)} %scatter_custom_fusion.2), channel_id=1, source_target_pairs={{0,28},{4,0},{8,4},{12,8},{16,12},{20,16},{24,20},{28,24},{1,29},{... | collective-permute-start | bytes 98312 | tf_op jit(solution)/shard_map/ppermute | solution.py:31
  165.2 6.2 %collective-permute-start.26 = (bf16[2,12,2,512]{3,2,1,0:T(2,128)(2,1)S(1)}, bf16[2,12,2,512]{3,2,1,0:T(2,128)(2,1)S(1)}, u32[]{:S(2)}, u32[]{:S(2)}) collective-permute-start(bf16[2,12,2,512]{3,2,1,0:T(2,128)(2,1)S(1)} %get-tuple-element.20), channel_id=1, source_target_pairs={{0,1},{1,2},{2,3},{4,5},{5,6},{6,7},{8,9},{9,10},{10,11},{12,13},{... | collective-permute-start | bytes 147464 | tf_op jit(solution)/shard_map/ppermute | solution.py:21
  168.2 6.4 %collective-permute-start.27 = (bf16[2,12,2,512]{3,2,1,0:T(2,128)(2,1)S(1)}, bf16[2,12,2,512]{3,2,1,0:T(2,128)(2,1)S(1)}, u32[]{:S(2)}, u32[]{:S(2)}) collective-permute-start(bf16[2,12,2,512]{3,2,1,0:T(2,128)(2,1)S(1)} %get-tuple-element.21), channel_id=1, source_target_pairs={{1,0},{2,1},{3,2},{5,4},{6,5},{7,6},{9,8},{10,9},{11,10},{13,12},{... | collective-permute-start | bytes 147464 | tf_op jit(solution)/shard_map/ppermute | solution.py:24
where the time goes:
time: 180 us; the launch traced here: 177 us
  starting transfers between devices  71.5 us (40%)
  local copies, waits for them, and re-layouts  54.6 us (30%)
  other arithmetic  33.8 us (19%)
  waiting for transfers between devices  15.4 us (9%)
    ppermute x14, starting transfers between devices, extended(): lax.ppermute(lax.slice_in_dim(block, 0, width, axis=dim), axis, backward)  41.2 us
    reshape x1, local copies, waits for them, and re-layouts, local(): residual.reshape(first_cells // 2, 2, second_cells // 2, 2, third_cells /...  34.8 us
    ppermute x14, starting transfers between devices, extended(): lax.ppermute(lax.slice_in_dim(block, block.shape[dim] - width, None, axis...  22.8 us
    reduce_sum x1, other arithmetic, local(): coarse_target = 4.0 * residual.reshape(first_cells // 2, 2, second_cells...  12.2 us
    ppermute x14, waiting for transfers between devices, extended(): lax.ppermute(lax.slice_in_dim(block, 0, width, axis=dim), axis, backward)  10.7 us
    scatter x2, local copies, waits for them, and re-layouts, local(): outgoing.append(jnp.zeros((MIG, width), jnp.bfloat16).at[jnp.where(chosen...  7.17 us
    gather x1, local copies, waits for them, and re-layouts, local(): sample = flat_field[agent_cell]  6.15 us
    scatter-add x1, other arithmetic, local(): jnp.zeros_like(flat_field).at[agent_cell].add(uptake)  6.06 us
  transfers between devices with their start and end apart: 31, of which 6 were waited for; matrix products, arithmetic and copies ran while one was open for 49% of the time, Pallas kernels for 0%

commit v1 on v0

v1 whole, which is shorter than its diff:
```python
import functools

import jax
import jax.numpy as jnp
from jax import lax
from jax.experimental import pallas as pl
from jax.experimental.pallas import tpu as pltpu
from jax.sharding import PartitionSpec as P

MIG = 128
SCREENING = 0.05
DAMPING = 2.0 / 3.0
CENTRE = 6.0 + SCREENING
COARSE_CENTRE = 6.0 + 4.0 * SCREENING
HALO = 4
F32, BF16 = jnp.float32, jnp.bfloat16
VMEM_SPEC = pl.BlockSpec(memory_space=pltpu.VMEM)
ANY_SPEC = pl.BlockSpec(memory_space=pl.ANY)
SMEM_SPEC = pl.BlockSpec(memory_space=pltpu.SMEM)
PARAMS = pltpu.CompilerParams(vmem_limit_bytes=40 * 1024 * 1024)


def dot(a, b, ca, cb):
    return lax.dot_general(a, b, (((ca,), (cb,)), ((), ())), preferred_element_type=F32)


def halves(x):
    high = x.astype(BF16)
    return high, (x - high.astype(F32)).astype(BF16)


def iota(shape, dim):
    return lax.broadcasted_iota(jnp.int32, shape, dim)


def cyclic(x, axis, by):
    count = lax.axis_size(axis)
    return lax.ppermute(x, axis, [(i, (i + by) % count) for i in range(count)])


def uptake_kernel(
    u_ref, cell_ref, death_ref, divide_ref, species_ref, weight_ref,
    t_ref, sensed_ref, low_ref, high_ref, front_ref, back_ref,
):
    nx, ny, nz = u_ref.shape
    agents = species_ref.shape[0]
    rows = nx * ny
    u = u_ref[...].reshape(rows, nz)
    cell = cell_ref[...].reshape(1, agents)
    cell_row = cell // nz
    cell_z = cell - cell_row * nz
    one_z = (iota((nz, agents), 0) == cell_z).astype(F32).astype(BF16)
    in_row = iota((rows, agents), 0) == cell_row
    high, low = halves(u)
    picked = dot(high, one_z, 1, 0) + dot(low, one_z, 1, 0)
    sample = jnp.sum(jnp.where(in_row, picked, 0.0), axis=0, keepdims=True)
    sensed_ref[...] = jnp.broadcast_to(sample, (8, agents)).astype(BF16).astype(F32)
    weight = jnp.broadcast_to(weight_ref[...].reshape(1, -1), (8, species_ref.shape[1]))
    score = dot(weight, species_ref[...], 1, 1)[0:1]
    softplus = jnp.maximum(score, 0.0) + jnp.log1p(jnp.exp(-jnp.abs(score)))
    alive = (1 - death_ref[...].reshape(1, agents)).astype(F32)
    divide = divide_ref[...].reshape(1, agents).astype(F32)
    uptake = alive * (1.0 + divide) * softplus * sample / (0.5 + sample)
    up_high = uptake.astype(BF16).astype(F32)
    a_high = jnp.where(in_row, up_high, 0.0).astype(BF16)
    a_low = jnp.where(in_row, uptake - up_high, 0.0).astype(BF16)
    source = dot(a_high, one_z, 1, 1) + dot(a_low, one_z, 1, 1)
    t_ref[...] = (SCREENING * u - source).reshape(nx, ny, nz)
    for pair in range(nx // 2):
        for ref, start in ((low_ref, 0), (high_ref, ny - HALO)):
            parts = []
            for plane in (2 * pair, 2 * pair + 1):
                parts.append(u_ref[plane, start : start + HALO])
                parts.append(t_ref[plane, start : start + HALO])
            ref[pair] = jnp.concatenate(parts, axis=0).astype(BF16)
    half = ny // 16
    for ref, u_start, t_start in ((front_ref, nx - HALO, nx - HALO + 1), (back_ref, 0, 0)):
        at = 0
        for field, start, count in ((u_ref, u_start, HALO), (t_ref, t_start, HALO - 1)):
            for plane in range(start, start + count):
                ref[at : at + half] = field[plane].astype(BF16).reshape(half, 16, nz)
                at += half


def network_kernel(
    me_ref, species_ref, sensed_ref, death_ref, move_ref, route_ref, net_ref, sensing_ref, *outs
):
    agents, width = species_ref.shape
    depths = len(outs) - 2
    capacity = outs[0].shape[0]
    species = species_ref[...]
    sensing = sensing_ref[...].reshape(1, width)
    first = sensing.astype(BF16)
    rest = sensing - first.astype(F32)
    second = rest.astype(BF16)
    third = (rest - second.astype(F32)).astype(BF16)
    line = iota((8, width), 0)
    terms = jnp.where(
        line == 0, first.astype(F32),
        jnp.where(line == 1, second.astype(F32), jnp.where(line == 2, third.astype(F32), 0.0)),
    ).astype(BF16)
    activation = dot(species, net_ref[...], 1, 0) + dot(sensed_ref[...].astype(BF16), terms, 0, 0)
    updated = (0.5 * species.astype(F32) + jnp.tanh(activation)).astype(BF16)
    lanes = 128
    lines = -(-(depths + 2) // 8) * 8
    line = iota((lines, lanes), 0)
    square = iota((lanes, 2 * lanes), 0)
    column = iota((lanes, 2 * lanes), 1)
    counter = jnp.where(jnp.logical_or(column >= lanes, square < column), 1.0, 0.0).astype(BF16)
    blocks = agents // lanes
    route = route_ref[...].reshape(1, agents)
    move = move_ref[...].reshape(1, agents)
    death = death_ref[...].reshape(1, agents)
    hits = []
    for block in range(blocks):
        cut = slice(block * lanes, (block + 1) * lanes)
        wanted = jnp.where(line < depths, route[:, cut], jnp.where(line < depths + 2, move[:, cut] + (depths - 1), -1))
        hits.append((wanted == line).astype(F32))
    counts = dot(jnp.concatenate(hits, axis=0).astype(BF16), counter, 1, 0)
    me = me_ref[0]
    running = jnp.zeros((lines, lanes), F32)
    keys = []
    for block in range(blocks):
        cut = slice(block * lanes, (block + 1) * lanes)
        own = slice(block * lines, (block + 1) * lines)
        before = (counts[own, :lanes] + running) * hits[block]
        running = running + counts[own, lanes:]
        slot = jnp.sum(jnp.where(line < depths, before, 0.0), axis=0, keepdims=True).astype(jnp.int32)
        rank = jnp.sum(jnp.where(line < depths, 0.0, before), axis=0, keepdims=True).astype(jnp.int32)
        hop = route[:, cut] - me
        hop = jnp.where(hop < 0, hop + depths, hop)
        key = jnp.where(
            move[:, cut] == 0, hop * capacity + slot, depths * capacity + (move[:, cut] - 1) * MIG + rank
        )
        keys.append(jnp.where(death[:, cut] == 0, key, -1))
    key = jnp.concatenate(keys, axis=1)
    start = 0
    for out in outs:
        size = out.shape[0]
        chosen = (iota((size, agents), 0) == key - start).astype(F32).astype(BF16)
        out[...] = dot(chosen, updated, 1, 0).astype(BF16)
        start += size


def third_sum(x):
    width = 128
    tiles = x.shape[1] // width
    lane = iota((x.shape[0], width), 1)
    parts = [x[:, i * width : (i + 1) * width] for i in range(tiles)]
    ups = [pltpu.roll(part, 1, 1) for part in parts]
    downs = [pltpu.roll(part, width - 1, 1) for part in parts]
    sums = []
    for i in range(tiles):
        before = ups[i - 1] if i else 0.0
        after = downs[i + 1] if i < tiles - 1 else 0.0
        sums.append(jnp.where(lane == 0, before, ups[i]) + jnp.where(lane == width - 1, after, downs[i]))
    return jnp.concatenate(sums, axis=1)


def neighbour_total(before, plane, after):
    rows = plane.shape[0]
    second = pltpu.roll(plane, 1, 0) + pltpu.roll(plane, rows - 1, 0)
    return before + after + second + third_sum(plane)


def relaxed(before, plane, after, target, centre):
    return (1.0 - DAMPING) * plane + (DAMPING / centre) * (
        target + neighbour_total(before, plane, after)
    )


def edge_mask(me, depths, halo):
    row = iota((2 * halo, 1), 0)
    return jnp.where(
        row < halo, (me < depths - 1).astype(F32), (me > 0).astype(F32)
    )


def masked(plane, own, mask):
    return jnp.concatenate([plane[:own], plane[own:] * mask], axis=0)


def smooth_kernel(
    depths, me_ref, u_ref, t_ref, above_ref, below_ref, before_ref, after_ref,
    u2_ref, text_ref, coarse_ref, coarse_all_ref, coarse_low_ref, coarse_high_ref,
    u0, u1, paired,
):
    nx, ny, nz = u_ref.shape
    ext = ny + 2 * HALO
    mask = edge_mask(me_ref[0], depths, HALO)

    def halo_rows(upper, lower, plane):
        at = 8 * (plane % 2)
        high = upper[at : at + 8]
        low = lower[at : at + 8]
        return (
            jnp.concatenate([high[:HALO], low[:HALO]], axis=0) * mask,
            jnp.concatenate([high[HALO:], low[HALO:]], axis=0),
        )

    half = ny // 16
    own_size = (2 * HALO - 1) * half
    pairs = HALO // 2
    for plane in range(nx):
        u0[HALO + plane, :ny] = u_ref[plane]
        text_ref[HALO - 1 + plane, :ny] = t_ref[plane]
        pair = plane // 2
        uh, th = halo_rows(above_ref[pair].astype(F32), below_ref[pair].astype(F32), plane)
        u0[HALO + plane, ny:] = uh
        text_ref[HALO - 1 + plane, ny:] = th
    for ref, u_at, t_at, shift in ((before_ref, 0, 0, 1), (after_ref, HALO + nx, HALO - 1 + nx, 0)):
        for k in range(HALO):
            u0[u_at + k, :ny] = ref[k * half : (k + 1) * half].astype(F32).reshape(ny, nz)
            pair = k // 2
            uh, th = halo_rows(
                ref[own_size + pair].astype(F32), ref[own_size + pairs + pair].astype(F32), k
            )
            u0[u_at + k, ny:] = uh
            j = k - shift
            if 0 <= j < HALO - 1:
                at = (HALO + j) * half
                text_ref[t_at + j, :ny] = ref[at : at + half].astype(F32).reshape(ny, nz)
                text_ref[t_at + j, ny:] = th

    def first(p, carry):
        v = relaxed(u0[p], u0[p + 1], u0[p + 2], text_ref[p], CENTRE)
        u1[p] = masked(v, ny, mask)
        return carry

    lax.fori_loop(0, nx + 2 * HALO - 2, first, 0)

    def second(p, carry):
        v = relaxed(u1[p], u1[p + 1], u1[p + 2], text_ref[p + 1], CENTRE)
        u2_ref[p] = masked(v, ny, mask)
        return carry

    lax.fori_loop(0, nx + 2 * HALO - 4, second, 0)

    def residual(p):
        v = u2_ref[p + 2]
        total = neighbour_total(u2_ref[p + 1], v, u2_ref[p + 3])
        return (text_ref[p + 3] - CENTRE * v + total)[:ny]

    def rest(q, carry):
        both = residual(2 * q) + residual(2 * q + 1)
        for i in range(nz // 128):
            paired[q, i] = both[:, i * 128 : (i + 1) * 128]
        return carry

    lax.fori_loop(0, nx // 2, rest, 0)
    cx, cy, cz = coarse_ref.shape
    flat = jnp.concatenate(
        [
            jnp.concatenate(
                [
                    paired[q, i, pl.ds(0, cy, 2), :] + paired[q, i, pl.ds(1, cy, 2), :]
                    for i in range(nz // 128)
                ],
                axis=1,
            )
            for q in range(cx)
        ],
        axis=0,
    )
    fold = ((iota((nz, cz), 0) >> 1) == iota((nz, cz), 1)).astype(F32).astype(BF16)
    high, low = halves(flat)
    coarse = 0.5 * (dot(high, fold, 1, 0) + dot(low, fold, 1, 0))
    coarse_ref[...] = coarse.reshape(cx, cy, cz)
    coarse_all_ref[...] = coarse.astype(BF16).reshape(cx, cy, cz)
    for ref, start in ((coarse_low_ref, 0), (coarse_high_ref, cy - HALO)):
        ref[0] = jnp.concatenate(
            [coarse_ref[q, start : start + HALO] for q in range(cx)], axis=0
        ).astype(BF16)


def correct_kernel(
    depths, me_ref, ct_ref, above_ref, below_ref, before_ref, after_ref, u2_ref, text_ref, *rest
):
    packed = rest[: depths + 2]
    out_ref, agents_ref, ca, cb, u3, u4, sem = rest[depths + 2 :]
    nx, ny, nz = out_ref.shape
    cx, cy, cz = ct_ref.shape
    me = me_ref[0]
    capacity = packed[0].shape[0]
    copies = []
    for k in range(depths):
        origin = me - k
        origin = jnp.where(origin < 0, origin + depths, origin)
        place = pl.ds(pl.multiple_of(origin * capacity, capacity), capacity)
        copies.append(pltpu.make_async_copy(packed[k], agents_ref.at[place], sem.at[k]))
    for k in range(2):
        place = pl.ds(depths * capacity + k * MIG, MIG)
        copies.append(pltpu.make_async_copy(packed[depths + k], agents_ref.at[place], sem.at[depths + k]))
    for copy in copies:
        copy.start()
    mask = edge_mask(me, depths, HALO)
    total_planes = cx + 2 * HALO
    planes = []
    for p in range(total_planes):
        if p < HALO:
            ref, k = before_ref, p + cx - HALO
        elif p < HALO + cx:
            ref, k = None, p - HALO
        else:
            ref, k = after_ref, p - HALO - cx
        rows = slice(HALO * k, HALO * (k + 1))
        if ref is None:
            own = ct_ref[k]
            high = above_ref[0].astype(F32)[rows]
            low = below_ref[0].astype(F32)[rows]
        else:
            own = ref[k].astype(F32)
            high = ref[cx].astype(F32)[rows]
            low = ref[cx + 1].astype(F32)[rows]
        planes.append(jnp.concatenate([own, jnp.concatenate([high, low], axis=0) * mask], axis=0))
    values = [(DAMPING / COARSE_CENTRE) * plane for plane in planes]
    for sweep in range(1, HALO):
        values = [
            masked(
                relaxed(values[i - 1], values[i], values[i + 1], planes[i + sweep - 1], COARSE_CENTRE),
                cy,
                mask,
            )
            for i in range(1, len(values) - 1)
        ]
    wide = cy + 4
    flat = jnp.concatenate(
        [jnp.concatenate([v[: cy + 2], v[cy + 2 * HALO - 2 :]], axis=0) for v in values], axis=0
    )
    spread = (iota((cz, nz), 0) == (iota((cz, nz), 1) >> 1)).astype(F32).astype(BF16)
    high, low = halves(flat)
    cb[...] = dot(high, spread, 1, 0) + dot(low, spread, 1, 0)
    for q in range(len(values)):
        for i in range(nz // 128):
            part = cb[q * wide : (q + 1) * wide, i * 128 : (i + 1) * 128]
            ca[q, i, pl.ds(0, wide, 2), :] = part
            ca[q, i, pl.ds(1, wide, 2), :] = part

    def add(p, carry):
        q = p // 2
        correction = jnp.concatenate([ca[q, i] for i in range(nz // 128)], axis=1)
        u3[p] = u2_ref[p] + correction
        return carry

    lax.fori_loop(0, nx + 4, add, 0)

    def first(p, carry):
        v = relaxed(u3[p], u3[p + 1], u3[p + 2], text_ref[p + 2], CENTRE)
        u4[p] = masked(v, ny, mask)
        return carry

    lax.fori_loop(0, nx + 2, first, 0)

    def second(p, carry):
        v = relaxed(u4[p], u4[p + 1], u4[p + 2], text_ref[p + 3], CENTRE)
        out_ref[p] = v[:ny]
        return carry

    lax.fori_loop(0, nx, second, 0)
    for copy in copies:
        copy.wait()


def local(
    nutrient, species, agent_cell, death_flag, divide_flag, slab_move, depth_route, net_weight, sensing, uptake_weight
):
    depths = lax.axis_size("depth")
    nx, ny, nz = nutrient.shape
    agents, width = species.shape
    capacity = 2 * agents // depths
    me = lax.axis_index("depth").astype(jnp.int32).reshape(1)
    shape = jax.ShapeDtypeStruct
    cells, death, divide = (x.reshape(1, agents) for x in (agent_cell, death_flag, divide_flag))
    move, route = slab_move.reshape(1, agents), depth_route.reshape(1, agents)
    slab_size = (2 * HALO - 1) * ny // 16
    target, sensed, low, high, front, back = pl.pallas_call(
        uptake_kernel,
        out_shape=(
            shape((nx, ny, nz), F32),
            shape((8, agents), F32),
            shape((nx // 2, 16, nz), BF16),
            shape((nx // 2, 16, nz), BF16),
            shape((slab_size, 16, nz), BF16),
            shape((slab_size, 16, nz), BF16),
        ),
        in_specs=[VMEM_SPEC] * 6,
        out_specs=[VMEM_SPEC] * 6,
        compiler_params=PARAMS,
        name="uptake",
    )(nutrient, cells, death, divide, species, uptake_weight.reshape(1, width))
    above = cyclic(low, "depth", -1)
    below = cyclic(high, "depth", 1)
    sent = pl.pallas_call(
        network_kernel,
        out_shape=tuple(shape((capacity, width), BF16) for _ in range(depths))
        + tuple(shape((MIG, width), BF16) for _ in range(2)),
        in_specs=[SMEM_SPEC] + [VMEM_SPEC] * 7,
        out_specs=[VMEM_SPEC] * (depths + 2),
        compiler_params=PARAMS,
        cost_estimate=pl.CostEstimate(flops=2 * 2304 * agents * width, bytes_accessed=1 << 20, transcendentals=agents * width),
        name="network",
    )(me, species, sensed, death, move, route, net_weight, sensing.reshape(1, width))
    pairs = HALO // 2
    all_pairs = nx // 2
    front = jnp.concatenate([front, above[all_pairs - pairs :], below[all_pairs - pairs :]], axis=0)
    back = jnp.concatenate([back, above[:pairs], below[:pairs]], axis=0)
    before = cyclic(front, "slab", 1)
    after = cyclic(back, "slab", -1)
    arrived = [sent[0]] + [cyclic(sent[k], "depth", k) for k in range(1, depths)]
    arrived += [cyclic(sent[depths], "slab", 1), cyclic(sent[depths + 1], "slab", -1)]
    cx, cy, cz = nx // 2, ny // 2, nz // 2
    ext = ny + 2 * HALO
    u2, text, ct, ct_all, ct_low, ct_high = pl.pallas_call(
        functools.partial(smooth_kernel, depths),
        out_shape=(
            shape((nx + 4, ext, nz), F32),
            shape((nx + 2 * HALO - 2, ext, nz), F32),
            shape((cx, cy, cz), F32),
            shape((cx, cy, cz), BF16),
            shape((1, cx * HALO, cz), BF16),
            shape((1, cx * HALO, cz), BF16),
        ),
        in_specs=[SMEM_SPEC] + [VMEM_SPEC] * 6,
        out_specs=[VMEM_SPEC] * 6,
        scratch_shapes=[
            pltpu.VMEM((nx + 2 * HALO, ext, nz), F32),
            pltpu.VMEM((nx + 2 * HALO - 2, ext, nz), F32),
            pltpu.VMEM((cx, nz // 128, ny, 128), F32),
        ],
        compiler_params=PARAMS,
        name="smooth",
    )(me, nutrient, target, above, below, before, after)
    ct_above = cyclic(ct_low, "depth", -1)
    ct_below = cyclic(ct_high, "depth", 1)
    message = jnp.concatenate([ct_all, ct_above, ct_below], axis=0)
    ct_before = cyclic(message, "slab", 1)
    ct_after = cyclic(message, "slab", -1)
    return pl.pallas_call(
        functools.partial(correct_kernel, depths),
        out_shape=(
            shape((nx, ny, nz), F32),
            shape((depths * capacity + 2 * MIG, width), BF16),
        ),
        in_specs=[SMEM_SPEC] + [VMEM_SPEC] * 7 + [ANY_SPEC] * (depths + 2),
        out_specs=[VMEM_SPEC, ANY_SPEC],
        scratch_shapes=[
            pltpu.VMEM((cx + 2, nz // 128, ext, 128), F32),
            pltpu.VMEM(((cx + 2) * (cy + 4), nz), F32),
            pltpu.VMEM((nx + 4, ext, nz), F32),
            pltpu.VMEM((nx + 2, ext, nz), F32),
            pltpu.SemaphoreType.DMA((depths + 2,)),
        ],
        compiler_params=PARAMS,
        name="correct",
    )(me, ct, ct_above, ct_below, ct_before, ct_after, u2, text, *arrived)


def solution(mesh):
    rows = P(("slab", "depth"))
    in_specs = (
        P("slab", "depth", None),
        P(("slab", "depth"), None),
        rows,
        rows,
        rows,
        rows,
        P(("slab", "depth"), None),
        P(),
        P(),
        P(),
    )
    out_specs = (P("slab", "depth", None), P(("slab", "depth"), None))
    return jax.shard_map(local, mesh=mesh, in_specs=in_specs, out_specs=out_specs, check_vma=False)
```

time: 180 us -> 54.3 us (0.30); the launches traced: 177 us -> 54 us
  starting transfers between devices: 71.5 us -> 20.8 us
  local copies, waits for them, and re-layouts: 54.6 us -> 4.76 us
  other arithmetic: 33.8 us -> 0.08 us
  Pallas kernels: 0 us -> 11.3 us
    ppermute x30 -> x13, starting transfers between devices: 66 us -> 20.8 us  [cyclic(): return lax.ppermute(x, axis, [(i, (i + by) % count) for i in range(count)])]
    reshape x5 -> x0, local copies, waits for them, and re-layouts: 37.1 us -> none  [the longest x1 34.8 us: local(): residual.reshape(first_cells // 2, 2, second_cells // 2, 2, third_cells /...]
    reduce_sum x2 -> x0, other arithmetic: 12.3 us -> none  [the longest x1 12.2 us: local(): coarse_target = 4.0 * residual.reshape(first_cells // 2, 2, second_cells...]
    pallas_call x0 -> x4, Pallas kernels: none -> 11.3 us  [the longest x1 4.02 us: local(): pl.pallas_call(functools.partial(smooth_kernel, depths), out_shape=(shape...]
    scatter x2 -> x0, local copies, waits for them, and re-layouts: 7.17 us -> none  [local(): outgoing.append(jnp.zeros((MIG, width), jnp.bfloat16).at[jnp.where(chosen...]
    gather x1 -> x0, local copies, waits for them, and re-layouts: 6.15 us -> none  [local(): sample = flat_field[agent_cell]]
    scatter-add x1 -> x0, other arithmetic: 6.06 us -> none  [local(): jnp.zeros_like(flat_field).at[agent_cell].add(uptake)]
    all_to_all x1 -> x0, starting transfers between devices: 5.45 us -> none  [local(): lax.all_to_all(packed, 'depth', split_axis=0, concat_axis=0, tiled=True)]
  transfers between devices with their start and end apart: 31 -> 13, of which waited for: 6 -> 9; matrix products, arithmetic and copies ran while one was open for 49% -> 0% of each run, Pallas kernels for 0% -> 11%
where the time goes in v1:
time: 54.3 us; the launch traced here: 54 us
  starting transfers between devices  20.8 us (38%)
  waiting for transfers between devices  16.3 us (30%)
  Pallas kernels  11.3 us (21%)
  local copies, waits for them, and re-layouts  4.76 us (9%)
  between operations  0.78 us (1%)
    ppermute x13, starting transfers between devices, cyclic(): return lax.ppermute(x, axis, [(i, (i + by) % count) for i in range(count)])  20.8 us
    ppermute x13, waiting for transfers between devices, cyclic(): return lax.ppermute(x, axis, [(i, (i + by) % count) for i in range(count)])  16.3 us
    unnamed x28, local copies, waits for them, and re-layouts  4.74 us
    pallas_call x1, Pallas kernels, local(): pl.pallas_call(functools.partial(smooth_kernel, depths), out_shape=(shape...  4.02 us
    pallas_call x1, Pallas kernels, local(): pl.pallas_call(functools.partial(correct_kernel, depths), out_shape=(shap...  3.84 us
    pallas_call x1, Pallas kernels, local(): pl.pallas_call(network_kernel, out_shape=tuple((shape((capacity, width),...  1.8 us
    pallas_call x1, Pallas kernels, local(): pl.pallas_call(uptake_kernel, out_shape=(shape((nx, ny, nz), F32), shape(...  1.6 us
  transfers between devices with their start and end apart: 13, of which 9 were waited for; matrix products, arithmetic and copies ran while one was open for 0% of the time, Pallas kernels for 11%

profile of v1, /device:TPU:0, one launch (start us, length us, event | category | flops | bytes accessed | tf_op | source)
XLA Modules:
  0.0 54.0 jit_solution(4921250810745307770)
XLA Ops:
  0.6 0.0 copy-start.7
  0.6 0.0 copy-start.12
  0.7 0.0 copy-start
  0.7 1.0 %copy-done = f32[8,32,512]{2,1,0:T(8,128)S(1)} copy-done((f32[8,32,512]{2,1,0:T(8,128)S(1)}, f32[8,32,512]{2,1,0:T(8,128)}, u32[]{:S(2)}) %copy-start) | copy-done | bytes 524312
  1.7 0.0 copy-start.2
  1.7 0.9 %copy-done.2 = bf16[1024,128]{1,0:T(8,128)(2,1)S(1)} copy-done((bf16[1024,128]{1,0:T(8,128)(2,1)S(1)}, bf16[1024,128]{1,0:T(8,128)(2,1)}, u32[]{:S(2)}) %copy-start.2) | copy-done | bytes 262168
  2.7 0.7 %copy-done.4 = s32[1024]{0:T(1024)S(1)} copy-done((s32[1024]{0:T(1024)S(1)}, s32[1024]{0:T(1024)}, u32[]{:S(2)}) %copy-start.4) | copy-done | bytes 4120
  3.3 0.7 %copy-done.5 = s32[1024]{0:T(1024)S(1)} copy-done((s32[1024]{0:T(1024)S(1)}, s32[1024]{0:T(1024)}, u32[]{:S(2)}) %copy-start.5) | copy-done | bytes 4120
  4.0 0.7 %copy-done.6 = s32[1024]{0:T(1024)S(1)} copy-done((s32[1024]{0:T(1024)S(1)}, s32[1024]{0:T(1024)}, u32[]{:S(2)}) %copy-start.6) | copy-done | bytes 4120
  4.7 0.7 %copy-done.8 = bf16[128]{0:T(256)(128)(2,1)S(1)} copy-done((bf16[128]{0:T(256)(128)(2,1)S(1)}, bf16[128]{0:T(256)(128)(2,1)}, u32[]{:S(2)}) %copy-start.8) | copy-done | bytes 280
  5.4 1.6 %uptake.1 = (f32[8,32,512]{2,1,0:T(8,128)S(1)}, f32[8,1024]{1,0:T(8,128)S(1)}, bf16[4,16,512]{2,1,0:T(8,128)(2,1)S(1)}, bf16[4,16,512]{2,1,0:T(8,128)(2,1)S(1)},...) custom-call(f32[8,32,512]{2,1,0:T(8,128)S(1)} %copy-done, s32[1,1024]{1,0:T(1,128)S(1)} %bitcast.8, ...), custom_call_target="tpu_custom_call" | custom-call | tf_op jit(solution)/shard_map/uptake/pallas_call | solution.py:376
  7.0 2.5 %collective-permute-start = (bf16[4,16,512]{2,1,0:T(8,128)(2,1)S(1)}, bf16[4,16,512]{2,1,0:T(8,128)(2,1)S(1)}, u32[]{:S(2)}, u32[]{:S(2)}) collective-permute-start(bf16[4,16,512]{2,1,0:T(8,128)(2,1)S(1)} %get-tuple-element.21), channel_id=1, source_target_pairs={{0,3},{1,0},{2,1},{3,2},{4,7},{5,4},{6,5},{7,6},{8,11},{9,8},{10,9... | collective-permute-start | bytes 196616 | tf_op jit(solution)/shard_map/ppermute | solution.py:38
  9.5 0.0 collective-permute-start.1
  9.5 2.4 %collective-permute-done.above_ref = bf16[4,16,512]{2,1,0:T(8,128)(2,1)S(1)} collective-permute-done((bf16[4,16,512]{2,1,0:T(8,128)(2,1)S(1)}, bf16[4,16,512]{2,1,0:T(8,128)(2,1)S(1)}, u32[]{:S(2)}, u32[]{:S(2)}) %collective-permute-start) | collective-permute-done | bytes 65568 | tf_op jit(solution)/shard_map/ppermute | solution.py:38
  11.9 1.2 %collective-permute-done.1.below_ref = bf16[4,16,512]{2,1,0:T(8,128)(2,1)S(1)} collective-permute-done((bf16[4,16,512]{2,1,0:T(8,128)(2,1)S(1)}, bf16[4,16,512]{2,1,0:T(8,128)(2,1)S(1)}, u32[]{:S(2)}, u32[]{:S(2)}) %collective-permute-start.1) | collective-permute-done | bytes 65568 | tf_op jit(solution)/shard_map/ppermute | solution.py:38
  13.2 4.6 %collective-permute-start.3 = (bf16[18,16,512]{2,1,0:T(8,128)(2,1)S(1)}, bf16[18,16,512]{2,1,0:T(8,128)(2,1)S(1)}, u32[]{:S(2)}, u32[]{:S(2)}) collective-permute-start(bf16[18,16,512]{2,1,0:T(8,128)(2,1)S(1)} %pad_maximum_fusion.1), channel_id=1, source_target_pairs={{0,28},{4,0},{8,4},{12,8},{16,12},{20,16},{24,20},{28,24},{1,29},{... | collective-permute-start | bytes 884744 | tf_op jit(solution)/shard_map/ppermute | solution.py:38
  17.8 0.0 copy-start.1
  17.8 0.1 collective-permute-start.2
  17.9 0.0 copy-done.7
  17.9 0.0 copy-done.12
  17.9 0.0 copy-done.3
  17.9 0.0 copy-done.9
  18.0 0.0 copy-done.10
  18.0 0.0 copy-done.11
  18.0 1.8 %network.1 = (bf16[512,128]{1,0:T(8,128)(2,1)S(1)}, bf16[512,128]{1,0:T(8,128)(2,1)S(1)}, bf16[512,128]{1,0:T(8,128)(2,1)S(1)}, bf16[512,128]{1,0:T(8,128)(2,1)S...) custom-call(s32[1]{0:T(128)} %bitcast.me_ref, bf16[1024,128]{1,0:T(8,128)(2,1)S(1)} %copy-done.3, ...), custom_call_target="tpu_custom_call" | custom-call | flops 603979776 | bytes 1048576 | tf_op jit(solution)/shard_map/network/pallas_call | solution.py:393
  19.8 0.7 %collective-permute-start.10 = (bf16[512,128]{1,0:T(8,128)(2,1)S(1)}, bf16[512,128]{1,0:T(8,128)(2,1)S(1)}, u32[]{:S(2)}, u32[]{:S(2)}) collective-permute-start(bf16[512,128]{1,0:T(8,128)(2,1)S(1)} %get-tuple-element.35), channel_id=1, source_target_pairs={{0,3},{1,0},{2,1},{3,2},{4,7},{5,4},{6,5},{7,6},{8,11},{9,8},{10,9... | collective-permute-start | bytes 393224 | tf_op jit(solution)/shard_map/ppermute | solution.py:38
  20.5 0.0 collective-permute-start.8
  20.5 1.1 %collective-permute-start.9 = (bf16[512,128]{1,0:T(8,128)(2,1)S(1)}, bf16[512,128]{1,0:T(8,128)(2,1)S(1)}, u32[]{:S(2)}, u32[]{:S(2)}) collective-permute-start(bf16[512,128]{1,0:T(8,128)(2,1)S(1)} %get-tuple-element.34), channel_id=1, source_target_pairs={{0,2},{1,3},{2,0},{3,1},{4,6},{5,7},{6,4},{7,5},{8,10},{9,11},{10,... | collective-permute-start | bytes 393224 | tf_op jit(solution)/shard_map/ppermute | solution.py:38
  21.6 1.6 %collective-permute-done.3.after_ref = bf16[18,16,512]{2,1,0:T(8,128)(2,1)S(1)} collective-permute-done((bf16[18,16,512]{2,1,0:T(8,128)(2,1)S(1)}, bf16[18,16,512]{2,1,0:T(8,128)(2,1)S(1)}, u32[]{:S(2)}, u32[]{:S(2)}) %collective-permute-start.3) | collective-permute-done | bytes 294944 | tf_op jit(solution)/shard_map/ppermute | solution.py:38
  23.2 0.4 collective-permute-start.11
  23.6 4.6 %collective-permute-done.2.before_ref = bf16[18,16,512]{2,1,0:T(8,128)(2,1)S(1)} collective-permute-done((bf16[18,16,512]{2,1,0:T(8,128)(2,1)S(1)}, bf16[18,16,512]{2,1,0:T(8,128)(2,1)S(1)}, u32[]{:S(2)}, u32[]{:S(2)}) %collective-permute-start.2) | collective-permute-done | bytes 294944 | tf_op jit(solution)/shard_map/ppermute | solution.py:38
  28.2 0.0 copy-done.1
  28.2 4.0 %smooth.1 = (f32[12,40,512]{2,1,0:T(8,128)S(1)}, f32[14,40,512]{2,1,0:T(8,128)S(1)}, f32[4,16,256]{2,1,0:T(8,128)S(1)}, bf16[4,16,256]{2,1,0:T(8,128)(2,1)S(1)},...) custom-call(s32[1]{0:T(128)} %bitcast.me_ref, f32[8,32,512]{2,1,0:T(8,128)S(1)} %copy-done.1, ...), custom_call_target="tpu_custom_call" | custom-call | tf_op jit(solution)/shard_map/smooth/pallas_call | solution.py:413
  32.2 1.3 %collective-permute-start.4 = (bf16[1,16,256]{2,1,0:T(8,128)(2,1)S(1)}, bf16[1,16,256]{2,1,0:T(8,128)(2,1)S(1)}, u32[]{:S(2)}, u32[]{:S(2)}) collective-permute-start(bf16[1,16,256]{2,1,0:T(8,128)(2,1)S(1)} %get-tuple-element.26), channel_id=1, source_target_pairs={{0,3},{1,0},{2,1},{3,2},{4,7},{5,4},{6,5},{7,6},{8,11},{9,8},{10,9... | collective-permute-start | bytes 24584 | tf_op jit(solution)/shard_map/ppermute | solution.py:38
  33.5 1.4 %collective-permute-done.4.above_ref = bf16[1,16,256]{2,1,0:T(8,128)(2,1)S(1)} collective-permute-done((bf16[1,16,256]{2,1,0:T(8,128)(2,1)S(1)}, bf16[1,16,256]{2,1,0:T(8,128)(2,1)S(1)}, u32[]{:S(2)}, u32[]{:S(2)}) %collective-permute-start.4) | collective-permute-done | bytes 8224 | tf_op jit(solution)/shard_map/ppermute | solution.py:38
  34.9 1.3 %collective-permute-start.5 = (bf16[1,16,256]{2,1,0:T(8,128)(2,1)S(1)}, bf16[1,16,256]{2,1,0:T(8,128)(2,1)S(1)}, u32[]{:S(2)}, u32[]{:S(2)}) collective-permute-start(bf16[1,16,256]{2,1,0:T(8,128)(2,1)S(1)} %get-tuple-element.27), channel_id=1, source_target_pairs={{0,1},{1,2},{2,3},{3,0},{4,5},{5,6},{6,7},{7,4},{8,9},{9,10},{10,1... | collective-permute-start | bytes 24584 | tf_op jit(solution)/shard_map/ppermute | solution.py:38
  36.1 1.8 %collective-permute-done.5.below_ref = bf16[1,16,256]{2,1,0:T(8,128)(2,1)S(1)} collective-permute-done((bf16[1,16,256]{2,1,0:T(8,128)(2,1)S(1)}, bf16[1,16,256]{2,1,0:T(8,128)(2,1)S(1)}, u32[]{:S(2)}, u32[]{:S(2)}) %collective-permute-start.5) | collective-permute-done | bytes 8224 | tf_op jit(solution)/shard_map/ppermute | solution.py:38
  37.9 3.8 %collective-permute-start.12 = (bf16[128,128]{1,0:T(8,128)(2,1)S(1)}, bf16[128,128]{1,0:T(8,128)(2,1)S(1)}, u32[]{:S(2)}, u32[]{:S(2)}) collective-permute-start(bf16[128,128]{1,0:T(8,128)(2,1)S(1)} %get-tuple-element.37), channel_id=1, source_target_pairs={{0,28},{4,0},{8,4},{12,8},{16,12},{20,16},{24,20},{28,24},{1,29},{... | collective-permute-start | bytes 98312 | tf_op jit(solution)/shard_map/ppermute | solution.py:38
  41.8 0.0 collective-permute-done.11.rest_4_
  41.8 0.0 collective-permute-start.6
  41.8 1.6 %collective-permute-done.12.rest_5_ = bf16[128,128]{1,0:T(8,128)(2,1)S(1)} collective-permute-done((bf16[128,128]{1,0:T(8,128)(2,1)S(1)}, bf16[128,128]{1,0:T(8,128)(2,1)S(1)}, u32[]{:S(2)}, u32[]{:S(2)}) %collective-permute-start.12) | collective-permute-done | bytes 32800 | tf_op jit(solution)/shard_map/ppermute | solution.py:38
  43.4 5.0 %collective-permute-start.7 = (bf16[6,16,256]{2,1,0:T(8,128)(2,1)S(1)}, bf16[6,16,256]{2,1,0:T(8,128)(2,1)S(1)}, u32[]{:S(2)}, u32[]{:S(2)}) collective-permute-start(bf16[6,16,256]{2,1,0:T(8,128)(2,1)S(1)} %constant_dynamic-update-slice_fusion), channel_id=1, source_target_pairs={{0,28},{4,0},{8,4},{12,8},{16,12},{20,16},{24,20},{28,24},{1,29},{... | collective-permute-start | bytes 147464 | tf_op jit(solution)/shard_map/ppermute | solution.py:38
  48.4 0.0 collective-permute-done.10.rest_3_
  48.4 0.0 collective-permute-done.8.rest_1_
  48.4 0.0 collective-permute-done.9.rest_2_
  48.4 0.2 collective-permute-done.6.before_ref
  48.6 1.6 %collective-permute-done.7.after_ref = bf16[6,16,256]{2,1,0:T(8,128)(2,1)S(1)} collective-permute-done((bf16[6,16,256]{2,1,0:T(8,128)(2,1)S(1)}, bf16[6,16,256]{2,1,0:T(8,128)(2,1)S(1)}, u32[]{:S(2)}, u32[]{:S(2)}) %collective-permute-start.7) | collective-permute-done | bytes 49184 | tf_op jit(solution)/shard_map/ppermute | solution.py:38
  50.1 3.8 %correct.1 = (f32[8,32,512]{2,1,0:T(8,128)}, bf16[2304,128]{1,0:T(8,128)(2,1)}) custom-call(s32[1]{0:T(128)} %bitcast.me_ref, f32[4,16,256]{2,1,0:T(8,128)S(1)} %get-tuple-element.25.ct_ref, bf16[1,16,256]{2,1,0:T(8,128)(2,1)S(1)} %collective-permute-done.4.above_ref, bf16[1,16,256]{2,1,0:T(8,128)(2,1)S(1)} %collective-permute-done.5.below_ref, ...), custom_call_target="tpu_custom_call" | custom-call | tf_op jit(solution)/shard_map/correct/pallas_call | solution.py:438
  (15 shorter events, 0.1 us)
Async XLA Ops:
  0.6 17.3 %copy-start.7 = (s32[1024]{0:T(1024)S(1)}, s32[1024]{0:T(1024)}, u32[]{:S(2)}) copy-start(s32[1024]{0:T(1024)} %param.13) | copy-start | bytes 12292
  0.6 17.3 %copy-start.12 = (f32[128]{0:T(128)S(1)}, f32[128]{0:T(128)}, u32[]{:S(2)}) copy-start(f32[128]{0:T(128)} %param.18) | copy-start | bytes 1540
  0.7 1.1 %copy-start = (f32[8,32,512]{2,1,0:T(8,128)S(1)}, f32[8,32,512]{2,1,0:T(8,128)}, u32[]{:S(2)}) copy-start(f32[8,32,512]{2,1,0:T(8,128)} %u_ref.3) | copy-start | bytes 1572868
  1.7 0.9 %copy-start.2 = (bf16[1024,128]{1,0:T(8,128)(2,1)S(1)}, bf16[1024,128]{1,0:T(8,128)(2,1)}, u32[]{:S(2)}) copy-start(bf16[1024,128]{1,0:T(8,128)(2,1)} %species_ref.3) | copy-start | bytes 786436
  2.7 0.7 %copy-start.4 = (s32[1024]{0:T(1024)S(1)}, s32[1024]{0:T(1024)}, u32[]{:S(2)}) copy-start(s32[1024]{0:T(1024)} %param.12) | copy-start | bytes 12292
  3.3 0.7 %copy-start.5 = (s32[1024]{0:T(1024)S(1)}, s32[1024]{0:T(1024)}, u32[]{:S(2)}) copy-start(s32[1024]{0:T(1024)} %param.14) | copy-start | bytes 12292
  4.0 0.7 %copy-start.6 = (s32[1024]{0:T(1024)S(1)}, s32[1024]{0:T(1024)}, u32[]{:S(2)}) copy-start(s32[1024]{0:T(1024)} %param.13) | copy-start | bytes 12292
  4.7 0.7 %copy-start.8 = (bf16[128]{0:T(256)(128)(2,1)S(1)}, bf16[128]{0:T(256)(128)(2,1)}, u32[]{:S(2)}) copy-start(bf16[128]{0:T(256)(128)(2,1)} %param.19) | copy-start | bytes 772
  5.4 12.6 %copy-start.3 = (bf16[1024,128]{1,0:T(8,128)(2,1)S(1)}, bf16[1024,128]{1,0:T(8,128)(2,1)}, u32[]{:S(2)}) copy-start(bf16[1024,128]{1,0:T(8,128)(2,1)} %species_ref.3) | copy-start | bytes 786436
  5.4 12.6 %copy-start.9 = (bf16[128,128]{1,0:T(8,128)(2,1)S(1)}, bf16[128,128]{1,0:T(8,128)(2,1)}, u32[]{:S(2)}) copy-start(bf16[128,128]{1,0:T(8,128)(2,1)} %net_ref.1) | copy-start | bytes 98308
  5.4 12.6 %copy-start.10 = (s32[1024]{0:T(1024)S(1)}, s32[1024]{0:T(1024)}, u32[]{:S(2)}) copy-start(s32[1024]{0:T(1024)} %param.15) | copy-start | bytes 12292
  5.4 12.6 %copy-start.11 = (s32[1024,1]{0,1:T(1,128)S(1)}, s32[1024,1]{0,1:T(1,128)}, u32[]{:S(2)}) copy-start(s32[1024,1]{0,1:T(1,128)} %param.16) | copy-start | bytes 12292
  7.0 4.9 %collective-permute-start = (bf16[4,16,512]{2,1,0:T(8,128)(2,1)S(1)}, bf16[4,16,512]{2,1,0:T(8,128)(2,1)S(1)}, u32[]{:S(2)}, u32[]{:S(2)}) collective-permute-start(bf16[4,16,512]{2,1,0:T(8,128)(2,1)S(1)} %get-tuple-element.21), channel_id=1, source_target_pairs={{0,3},{1,0},{2,1},{3,2},{4,7},{5,4},{6,5},{7,6},{8,11},{9,8},{10,9... | collective-permute-start | bytes 196616 | tf_op jit(solution)/shard_map/ppermute | solution.py:38
  9.5 3.7 %collective-permute-start.1 = (bf16[4,16,512]{2,1,0:T(8,128)(2,1)S(1)}, bf16[4,16,512]{2,1,0:T(8,128)(2,1)S(1)}, u32[]{:S(2)}, u32[]{:S(2)}) collective-permute-start(bf16[4,16,512]{2,1,0:T(8,128)(2,1)S(1)} %get-tuple-element.22), channel_id=1, source_target_pairs={{0,1},{1,2},{2,3},{3,0},{4,5},{5,6},{6,7},{7,4},{8,9},{9,10},{10,1... | collective-permute-start | bytes 196616 | tf_op jit(solution)/shard_map/ppermute | solution.py:38
  13.2 10.0 %collective-permute-start.3 = (bf16[18,16,512]{2,1,0:T(8,128)(2,1)S(1)}, bf16[18,16,512]{2,1,0:T(8,128)(2,1)S(1)}, u32[]{:S(2)}, u32[]{:S(2)}) collective-permute-start(bf16[18,16,512]{2,1,0:T(8,128)(2,1)S(1)} %pad_maximum_fusion.1), channel_id=1, source_target_pairs={{0,28},{4,0},{8,4},{12,8},{16,12},{20,16},{24,20},{28,24},{1,29},{... | collective-permute-start | bytes 884744 | tf_op jit(solution)/shard_map/ppermute | solution.py:38
  17.8 10.4 %copy-start.1 = (f32[8,32,512]{2,1,0:T(8,128)S(1)}, f32[8,32,512]{2,1,0:T(8,128)}, u32[]{:S(2)}) copy-start(f32[8,32,512]{2,1,0:T(8,128)} %u_ref.3) | copy-start | bytes 1572868
  17.8 10.3 %collective-permute-start.2 = (bf16[18,16,512]{2,1,0:T(8,128)(2,1)S(1)}, bf16[18,16,512]{2,1,0:T(8,128)(2,1)S(1)}, u32[]{:S(2)}, u32[]{:S(2)}) collective-permute-start(bf16[18,16,512]{2,1,0:T(8,128)(2,1)S(1)} %pad_maximum_fusion), channel_id=1, source_target_pairs={{0,4},{4,8},{8,12},{12,16},{16,20},{20,24},{24,28},{28,0},{1,5},{5... | collective-permute-start | bytes 884744 | tf_op jit(solution)/shard_map/ppermute | solution.py:38
  19.8 28.6 %collective-permute-start.10 = (bf16[512,128]{1,0:T(8,128)(2,1)S(1)}, bf16[512,128]{1,0:T(8,128)(2,1)S(1)}, u32[]{:S(2)}, u32[]{:S(2)}) collective-permute-start(bf16[512,128]{1,0:T(8,128)(2,1)S(1)} %get-tuple-element.35), channel_id=1, source_target_pairs={{0,3},{1,0},{2,1},{3,2},{4,7},{5,4},{6,5},{7,6},{8,11},{9,8},{10,9... | collective-permute-start | bytes 393224 | tf_op jit(solution)/shard_map/ppermute | solution.py:38
  20.5 27.9 %collective-permute-start.8 = (bf16[512,128]{1,0:T(8,128)(2,1)S(1)}, bf16[512,128]{1,0:T(8,128)(2,1)S(1)}, u32[]{:S(2)}, u32[]{:S(2)}) collective-permute-start(bf16[512,128]{1,0:T(8,128)(2,1)S(1)} %get-tuple-element.33), channel_id=1, source_target_pairs={{0,1},{1,2},{2,3},{3,0},{4,5},{5,6},{6,7},{7,4},{8,9},{9,10},{10,1... | collective-permute-start | bytes 393224 | tf_op jit(solution)/shard_map/ppermute | solution.py:38
  20.5 27.9 %collective-permute-start.9 = (bf16[512,128]{1,0:T(8,128)(2,1)S(1)}, bf16[512,128]{1,0:T(8,128)(2,1)S(1)}, u32[]{:S(2)}, u32[]{:S(2)}) collective-permute-start(bf16[512,128]{1,0:T(8,128)(2,1)S(1)} %get-tuple-element.34), channel_id=1, source_target_pairs={{0,2},{1,3},{2,0},{3,1},{4,6},{5,7},{6,4},{7,5},{8,10},{9,11},{10,... | collective-permute-start | bytes 393224 | tf_op jit(solution)/shard_map/ppermute | solution.py:38
  23.2 18.6 %collective-permute-start.11 = (bf16[128,128]{1,0:T(8,128)(2,1)S(1)}, bf16[128,128]{1,0:T(8,128)(2,1)S(1)}, u32[]{:S(2)}, u32[]{:S(2)}) collective-permute-start(bf16[128,128]{1,0:T(8,128)(2,1)S(1)} %get-tuple-element.36), channel_id=1, source_target_pairs={{0,4},{4,8},{8,12},{12,16},{16,20},{20,24},{24,28},{28,0},{1,5},{5... | collective-permute-start | bytes 98312 | tf_op jit(solution)/shard_map/ppermute | solution.py:38
  32.2 2.6 %collective-permute-start.4 = (bf16[1,16,256]{2,1,0:T(8,128)(2,1)S(1)}, bf16[1,16,256]{2,1,0:T(8,128)(2,1)S(1)}, u32[]{:S(2)}, u32[]{:S(2)}) collective-permute-start(bf16[1,16,256]{2,1,0:T(8,128)(2,1)S(1)} %get-tuple-element.26), channel_id=1, source_target_pairs={{0,3},{1,0},{2,1},{3,2},{4,7},{5,4},{6,5},{7,6},{8,11},{9,8},{10,9... | collective-permute-start | bytes 24584 | tf_op jit(solution)/shard_map/ppermute | solution.py:38
  34.9 3.1 %collective-permute-start.5 = (bf16[1,16,256]{2,1,0:T(8,128)(2,1)S(1)}, bf16[1,16,256]{2,1,0:T(8,128)(2,1)S(1)}, u32[]{:S(2)}, u32[]{:S(2)}) collective-permute-start(bf16[1,16,256]{2,1,0:T(8,128)(2,1)S(1)} %get-tuple-element.27), channel_id=1, source_target_pairs={{0,1},{1,2},{2,3},{3,0},{4,5},{5,6},{6,7},{7,4},{8,9},{9,10},{10,1... | collective-permute-start | bytes 24584 | tf_op jit(solution)/shard_map/ppermute | solution.py:38
  37.9 5.4 %collective-permute-start.12 = (bf16[128,128]{1,0:T(8,128)(2,1)S(1)}, bf16[128,128]{1,0:T(8,128)(2,1)S(1)}, u32[]{:S(2)}, u32[]{:S(2)}) collective-permute-start(bf16[128,128]{1,0:T(8,128)(2,1)S(1)} %get-tuple-element.37), channel_id=1, source_target_pairs={{0,28},{4,0},{8,4},{12,8},{16,12},{20,16},{24,20},{28,24},{1,29},{... | collective-permute-start | bytes 98312 | tf_op jit(solution)/shard_map/ppermute | solution.py:38
  41.8 6.8 %collective-permute-start.6 = (bf16[6,16,256]{2,1,0:T(8,128)(2,1)S(1)}, bf16[6,16,256]{2,1,0:T(8,128)(2,1)S(1)}, u32[]{:S(2)}, u32[]{:S(2)}) collective-permute-start(bf16[6,16,256]{2,1,0:T(8,128)(2,1)S(1)} %constant_dynamic-update-slice_fusion), channel_id=1, source_target_pairs={{0,4},{4,8},{8,12},{12,16},{16,20},{20,24},{24,28},{28,0},{1,5},{5... | collective-permute-start | bytes 147464 | tf_op jit(solution)/shard_map/ppermute | solution.py:38
  43.4 6.8 %collective-permute-start.7 = (bf16[6,16,256]{2,1,0:T(8,128)(2,1)S(1)}, bf16[6,16,256]{2,1,0:T(8,128)(2,1)S(1)}, u32[]{:S(2)}, u32[]{:S(2)}) collective-permute-start(bf16[6,16,256]{2,1,0:T(8,128)(2,1)S(1)} %constant_dynamic-update-slice_fusion), channel_id=1, source_target_pairs={{0,28},{4,0},{8,4},{12,8},{16,12},{20,16},{24,20},{28,24},{1,29},{... | collective-permute-start | bytes 147464 | tf_op jit(solution)/shard_map/ppermute | solution.py:38

commit v2 on v1

v2 whole, which is shorter than its diff:
```python
import functools

import jax
import jax.numpy as jnp
from jax import lax
from jax.experimental import pallas as pl
from jax.experimental.pallas import tpu as pltpu
from jax.sharding import PartitionSpec as P

MIG = 128
SCREENING = 0.05
DAMPING = 2.0 / 3.0
CENTRE = 6.0 + SCREENING
COARSE_CENTRE = 6.0 + 4.0 * SCREENING
HALO = 4
F32, BF16 = jnp.float32, jnp.bfloat16
VMEM_SPEC = pl.BlockSpec(memory_space=pltpu.VMEM)
ANY_SPEC = pl.BlockSpec(memory_space=pl.ANY)
HBM_SPEC = pl.BlockSpec(memory_space=pltpu.HBM)
SMEM_SPEC = pl.BlockSpec(memory_space=pltpu.SMEM)
PARAMS = pltpu.CompilerParams(vmem_limit_bytes=40 * 1024 * 1024)


def dot(a, b, ca, cb):
    return lax.dot_general(a, b, (((ca,), (cb,)), ((), ())), preferred_element_type=F32)


def halves(x):
    high = x.astype(BF16)
    return high, (x - high.astype(F32)).astype(BF16)


def iota(shape, dim):
    return lax.broadcasted_iota(jnp.int32, shape, dim)


def cyclic(x, axis, by):
    count = lax.axis_size(axis)
    return lax.ppermute(x, axis, [(i, (i + by) % count) for i in range(count)])


def swapped(x, axis, which):
    count = lax.axis_size(axis)
    if count % 2:
        raise ValueError("odd axis")
    first = 0 if which == "a" else 1
    pairs = []
    for i in range(first, count, 2):
        j = (i + 1) % count
        pairs += [(i, j), (j, i)]
    return lax.ppermute(x, axis, sorted(pairs))


def is_even(x):
    return lax.rem(x, 2) == 0


def load_kernel(slab_ref, *refs):
    count = (len(refs) - 3) // 2
    sources, targets = refs[:count], refs[count : 2 * count]
    slab_a, slab_b, sem = refs[2 * count :]
    copies = [
        pltpu.make_async_copy(source, target, sem.at[i])
        for i, (source, target) in enumerate(zip(sources, targets))
    ]
    for copy in copies:
        copy.start()
    copies[0].wait()
    u_ref = targets[0]
    nx, ny, nz = u_ref.shape
    half = ny // 16
    even = is_even(slab_ref[0])
    for ref, front in ((slab_a, even), (slab_b, jnp.logical_not(even))):
        start = jnp.where(front, nx - HALO, 0)
        for k in range(HALO):
            ref[k * half : (k + 1) * half] = u_ref[start + k].astype(BF16).reshape(half, 16, nz)
    for copy in copies[1:]:
        copy.wait()


def uptake_kernel(
    me_ref, slab_ref, u_ref, cell_ref, death_ref, divide_ref, species_ref, weight_ref,
    t_ref, sensed_ref, depth_a, depth_b, slab_a, slab_b,
):
    nx, ny, nz = u_ref.shape
    agents = species_ref.shape[0]
    rows = nx * ny
    u = u_ref[...].reshape(rows, nz)
    cell = cell_ref[...].reshape(1, agents)
    cell_row = cell // nz
    cell_z = cell - cell_row * nz
    one_z = (iota((nz, agents), 0) == cell_z).astype(F32).astype(BF16)
    in_row = iota((rows, agents), 0) == cell_row
    high, low = halves(u)
    picked = dot(high, one_z, 1, 0) + dot(low, one_z, 1, 0)
    sample = jnp.sum(jnp.where(in_row, picked, 0.0), axis=0, keepdims=True)
    sensed_ref[...] = jnp.broadcast_to(sample, (8, agents)).astype(BF16).astype(F32)
    weight = jnp.broadcast_to(weight_ref[...].reshape(1, -1), (8, species_ref.shape[1]))
    score = dot(weight, species_ref[...], 1, 1)[0:1]
    softplus = jnp.maximum(score, 0.0) + jnp.log1p(jnp.exp(-jnp.abs(score)))
    alive = (1 - death_ref[...].reshape(1, agents)).astype(F32)
    divide = divide_ref[...].reshape(1, agents).astype(F32)
    uptake = alive * (1.0 + divide) * softplus * sample / (0.5 + sample)
    up_high = uptake.astype(BF16).astype(F32)
    a_high = jnp.where(in_row, up_high, 0.0).astype(BF16)
    a_low = jnp.where(in_row, uptake - up_high, 0.0).astype(BF16)
    source = dot(a_high, one_z, 1, 1) + dot(a_low, one_z, 1, 1)
    t_ref[...] = (SCREENING * u - source).reshape(nx, ny, nz)
    even = is_even(me_ref[0])
    for pair in range(nx // 2):
        parts = []
        for start in (0, ny - HALO):
            for plane in (2 * pair, 2 * pair + 1):
                parts.append(u_ref[plane, start : start + HALO])
                parts.append(t_ref[plane, start : start + HALO])
        low = jnp.concatenate(parts[:4], axis=0)
        high = jnp.concatenate(parts[4:], axis=0)
        depth_a[pair] = jnp.where(even, high, low).astype(BF16)
        depth_b[pair] = jnp.where(even, low, high).astype(BF16)
    half = ny // 16
    count = HALO - 1
    even = is_even(slab_ref[0])
    for ref, front in ((slab_a, even), (slab_b, jnp.logical_not(even))):
        start = jnp.where(front, nx - count, 0)
        for k in range(count):
            ref[k * half : (k + 1) * half] = t_ref[start + k].astype(BF16).reshape(half, 16, nz)


def network_kernel(
    me_ref, slab_ref, species_ref, sensed_ref, death_ref, move_ref, route_ref, net_ref, sensing_ref, *outs
):
    agents, width = species_ref.shape
    depths = len(outs) - 2
    capacity = outs[0].shape[0]
    species = species_ref[...]
    sensing = sensing_ref[...].reshape(1, width)
    first = sensing.astype(BF16)
    rest = sensing - first.astype(F32)
    second = rest.astype(BF16)
    third = (rest - second.astype(F32)).astype(BF16)
    line = iota((8, width), 0)
    terms = jnp.where(
        line == 0, first.astype(F32),
        jnp.where(line == 1, second.astype(F32), jnp.where(line == 2, third.astype(F32), 0.0)),
    ).astype(BF16)
    activation = dot(species, net_ref[...], 1, 0) + dot(sensed_ref[...].astype(BF16), terms, 0, 0)
    updated = (0.5 * species.astype(F32) + jnp.tanh(activation)).astype(BF16)
    lanes = 128
    lines = -(-(depths + 2) // 8) * 8
    line = iota((lines, lanes), 0)
    square = iota((lanes, 2 * lanes), 0)
    column = iota((lanes, 2 * lanes), 1)
    counter = jnp.where(jnp.logical_or(column >= lanes, square < column), 1.0, 0.0).astype(BF16)
    blocks = agents // lanes
    route = route_ref[...].reshape(1, agents)
    move = move_ref[...].reshape(1, agents)
    death = death_ref[...].reshape(1, agents)
    hits = []
    for block in range(blocks):
        cut = slice(block * lanes, (block + 1) * lanes)
        wanted = jnp.where(line < depths, route[:, cut], jnp.where(line < depths + 2, move[:, cut] + (depths - 1), -1))
        hits.append((wanted == line).astype(F32))
    counts = dot(jnp.concatenate(hits, axis=0).astype(BF16), counter, 1, 0)
    me = me_ref[0]
    to_a = jnp.where(is_even(slab_ref[0]), 1, 2)
    running = jnp.zeros((lines, lanes), F32)
    keys = []
    for block in range(blocks):
        cut = slice(block * lanes, (block + 1) * lanes)
        own = slice(block * lines, (block + 1) * lines)
        before = (counts[own, :lanes] + running) * hits[block]
        running = running + counts[own, lanes:]
        slot = jnp.sum(jnp.where(line < depths, before, 0.0), axis=0, keepdims=True).astype(jnp.int32)
        rank = jnp.sum(jnp.where(line < depths, 0.0, before), axis=0, keepdims=True).astype(jnp.int32)
        hop = route[:, cut] - me
        hop = jnp.where(hop < 0, hop + depths, hop)
        key = jnp.where(
            move[:, cut] == 0,
            hop * capacity + slot,
            depths * capacity + jnp.where(move[:, cut] == to_a, 0, MIG) + rank,
        )
        keys.append(jnp.where(death[:, cut] == 0, key, -1))
    key = jnp.concatenate(keys, axis=1)
    start = 0
    for index, out in enumerate(outs):
        size = capacity if index < depths else MIG
        chosen = (iota((size, agents), 0) == key - start).astype(F32).astype(BF16)
        placed = dot(chosen, updated, 1, 0).astype(BF16)
        start += size
        if index < depths:
            out[...] = placed
        else:
            tiles = out.shape[2] // width
            for i in range(MIG // 16):
                at = (i % tiles) * width
                out[i // tiles, :, at : at + width] = placed[i * 16 : (i + 1) * 16]


def third_sum(x):
    width = 128
    tiles = x.shape[1] // width
    lane = iota((x.shape[0], width), 1)
    parts = [x[:, i * width : (i + 1) * width] for i in range(tiles)]
    ups = [pltpu.roll(part, 1, 1) for part in parts]
    downs = [pltpu.roll(part, width - 1, 1) for part in parts]
    sums = []
    for i in range(tiles):
        before = ups[i - 1] if i else 0.0
        after = downs[i + 1] if i < tiles - 1 else 0.0
        sums.append(jnp.where(lane == 0, before, ups[i]) + jnp.where(lane == width - 1, after, downs[i]))
    return jnp.concatenate(sums, axis=1)


def neighbour_total(before, plane, after):
    rows = plane.shape[0]
    second = pltpu.roll(plane, 1, 0) + pltpu.roll(plane, rows - 1, 0)
    return before + after + second + third_sum(plane)


def relaxed(before, plane, after, target, centre):
    return (1.0 - DAMPING) * plane + (DAMPING / centre) * (
        target + neighbour_total(before, plane, after)
    )


def edge_mask(me, depths, halo):
    row = iota((2 * halo, 1), 0)
    return jnp.where(
        row < halo, (me < depths - 1).astype(F32), (me > 0).astype(F32)
    )


def masked(plane, own, mask):
    return jnp.concatenate([plane[:own], plane[own:] * mask], axis=0)


def halo_rows(side_a, side_b, even, plane, mask):
    at = 2 * HALO * (plane % 2)
    side_a = side_a[at : at + 2 * HALO].astype(F32)
    side_b = side_b[at : at + 2 * HALO].astype(F32)
    high = jnp.where(even, side_a, side_b)
    low = jnp.where(even, side_b, side_a)
    return (
        jnp.concatenate([high[:HALO], low[:HALO]], axis=0) * mask,
        jnp.concatenate([high[HALO:], low[HALO:]], axis=0),
    )


def inner_kernel(
    depths, me_ref, u_ref, t_ref, side_a, side_b, u0, text_ref, u1, u2_ref, inside
):
    nx, ny, nz = u_ref.shape
    even = is_even(me_ref[0])
    mask = edge_mask(me_ref[0], depths, HALO)
    for plane in range(nx):
        u0[HALO + plane, :ny] = u_ref[plane]
        text_ref[HALO - 1 + plane, :ny] = t_ref[plane]
        uh, th = halo_rows(side_a[plane // 2], side_b[plane // 2], even, plane, mask)
        u0[HALO + plane, ny:] = uh
        text_ref[HALO - 1 + plane, ny:] = th

    def first(p, carry):
        v = relaxed(u0[p], u0[p + 1], u0[p + 2], text_ref[p], CENTRE)
        u1[p] = masked(v, ny, mask)
        return carry

    lax.fori_loop(HALO, nx + HALO - 2, first, 0)

    def second(p, carry):
        v = relaxed(u1[p], u1[p + 1], u1[p + 2], text_ref[p + 1], CENTRE)
        u2_ref[p] = masked(v, ny, mask)
        return carry

    lax.fori_loop(HALO, nx, second, 0)
    for p in range(3, nx - 3):
        inside[p - 3] = residual(u2_ref, text_ref, p, ny)


def residual(u2_ref, text_ref, p, ny):
    v = u2_ref[p + 2]
    total = neighbour_total(u2_ref[p + 1], v, u2_ref[p + 3])
    return (text_ref[p + 3] - CENTRE * v + total)[:ny]


def smooth_kernel(
    depths, me_ref, slab_ref, u0_in, text_in, u1_in, u2_in, inside, field_a, field_b, slab_a, slab_b,
    u0, text_ref, u1, u2_ref, coarse_ref, coarse_all_ref, coarse_a, coarse_b, paired,
):
    nx = u0.shape[0] - 2 * HALO
    ny, nz = u0.shape[1] - 2 * HALO, u0.shape[2]
    mask = edge_mask(me_ref[0], depths, HALO)
    half = ny // 16
    pairs = HALO // 2
    own = (HALO - 1) * half
    even = is_even(me_ref[0])
    slab_even = is_even(slab_ref[0])
    for field, ref, after in (
        (field_a, slab_a, slab_even), (field_b, slab_b, jnp.logical_not(slab_even))
    ):
        u_at = jnp.where(after, HALO + nx, 0)
        t_at = jnp.where(after, HALO - 1 + nx, 0)
        sides = []
        for k in range(HALO):
            u0[u_at + k, :ny] = field[k * half : (k + 1) * half].astype(F32).reshape(ny, nz)
            uh, th = halo_rows(ref[own + k // 2], ref[own + pairs + k // 2], even, k, mask)
            u0[u_at + k, ny:] = uh
            sides.append(th)
        for k in range(HALO - 1):
            text_ref[t_at + k, :ny] = ref[k * half : (k + 1) * half].astype(F32).reshape(ny, nz)
            text_ref[t_at + k, ny:] = jnp.where(after, sides[k], sides[k + 1])

    def first(i, carry):
        for p in (i, nx + 2 + i):
            v = relaxed(u0[p], u0[p + 1], u0[p + 2], text_ref[p], CENTRE)
            u1[p] = masked(v, ny, mask)
        return carry

    lax.fori_loop(0, HALO, first, 0)

    def second(i, carry):
        for p in (i, nx + i):
            v = relaxed(u1[p], u1[p + 1], u1[p + 2], text_ref[p + 1], CENTRE)
            u2_ref[p] = masked(v, ny, mask)
        return carry

    lax.fori_loop(0, HALO, second, 0)
    for q in range(nx // 2):
        both = 0.0
        for p in (2 * q, 2 * q + 1):
            known = 3 <= p < nx - 3
            both = both + (inside[p - 3] if known else residual(u2_ref, text_ref, p, ny))
        for i in range(nz // 128):
            paired[q, i] = both[:, i * 128 : (i + 1) * 128]
    cx, cy, cz = coarse_ref.shape
    flat = jnp.concatenate(
        [
            jnp.concatenate(
                [
                    paired[q, i, pl.ds(0, cy, 2), :] + paired[q, i, pl.ds(1, cy, 2), :]
                    for i in range(nz // 128)
                ],
                axis=1,
            )
            for q in range(cx)
        ],
        axis=0,
    )
    fold = ((iota((nz, cz), 0) >> 1) == iota((nz, cz), 1)).astype(F32).astype(BF16)
    high, low = halves(flat)
    coarse = 0.5 * (dot(high, fold, 1, 0) + dot(low, fold, 1, 0))
    coarse_ref[...] = coarse.reshape(cx, cy, cz)
    coarse_all_ref[...] = coarse.astype(BF16).reshape(cx, cy, cz)
    low, high = (
        jnp.concatenate([coarse_ref[q, start : start + HALO] for q in range(cx)], axis=0)
        for start in (0, cy - HALO)
    )
    coarse_a[0] = jnp.where(even, high, low).astype(BF16)
    coarse_b[0] = jnp.where(even, low, high).astype(BF16)


def post_kernel(depths, me_ref, u2_ref, text_ref, out_ref, v1):
    nx, ny, nz = out_ref.shape
    mask = edge_mask(me_ref[0], depths, HALO)

    def first(p, carry):
        v = relaxed(u2_ref[p], u2_ref[p + 1], u2_ref[p + 2], text_ref[p + 2], CENTRE)
        v1[p] = masked(v, ny, mask)
        return carry

    lax.fori_loop(0, nx + 2, first, 0)

    def second(p, carry):
        v = relaxed(v1[p], v1[p + 1], v1[p + 2], text_ref[p + 3], CENTRE)
        out_ref[p] = v[:ny]
        return carry

    lax.fori_loop(0, nx, second, 0)


def correct_kernel(
    depths, me_ref, slab_ref, ct_ref, side_a, side_b, slab_a, slab_b, base_ref, *rest
):
    packed = rest[:depths]
    out_ref, agents_ref, fine, sem = rest[depths:]
    nx, ny, nz = out_ref.shape
    cx, cy, cz = ct_ref.shape
    me = me_ref[0]
    even = is_even(me)
    slab_even = is_even(slab_ref[0])
    capacity = packed[0].shape[0]
    width = agents_ref.shape[1]
    copies = []
    for k in range(depths):
        origin = me - k
        origin = jnp.where(origin < 0, origin + depths, origin)
        place = pl.ds(pl.multiple_of(origin * capacity, capacity), capacity)
        copies.append(pltpu.make_async_copy(packed[k], agents_ref.at[place], sem.at[len(copies)]))
    tiles = cz // width
    for ref, late in ((slab_a, slab_even), (slab_b, jnp.logical_not(slab_even))):
        start = depths * capacity + jnp.where(late, MIG, 0)
        for i in range(MIG // 16):
            place = pl.ds(pl.multiple_of(start + i * 16, 16), 16)
            source = ref.at[cx + 2 + i // tiles, :, pl.ds((i % tiles) * width, width)]
            copies.append(pltpu.make_async_copy(source, agents_ref.at[place], sem.at[len(copies)]))
    for copy in copies:
        copy.start()
    mask = edge_mask(me, depths, HALO)

    def chosen(condition, x, y):
        return jnp.where(condition, x.astype(F32), y.astype(F32))

    planes = []
    for p in range(cx + 2 * HALO):
        if HALO <= p < HALO + cx:
            k = p - HALO
            own, one, two = ct_ref[k], side_a[0].astype(F32), side_b[0].astype(F32)
        else:
            before = p < HALO
            k = p + cx - HALO if before else p - HALO - cx
            x, y = (slab_b, slab_a) if before else (slab_a, slab_b)
            own, one, two = (chosen(slab_even, x[i], y[i]) for i in (k, cx, cx + 1))
        rows = slice(HALO * k, HALO * (k + 1))
        one, two = one[rows], two[rows]
        sides = jnp.concatenate([jnp.where(even, one, two), jnp.where(even, two, one)], axis=0)
        planes.append(jnp.concatenate([own, sides * mask], axis=0))
    values = [(DAMPING / COARSE_CENTRE) * plane for plane in planes]
    for sweep in range(1, HALO):
        values = [
            masked(
                relaxed(values[i - 1], values[i], values[i + 1], planes[i + sweep - 1], COARSE_CENTRE),
                cy,
                mask,
            )
            for i in range(1, len(values) - 1)
        ]
    wide = cy + 4
    for q, value in enumerate(values):
        value = jnp.concatenate([value[: cy + 2], value[cy + 2 * HALO - 2 :]], axis=0)
        for i in range(cz // 128):
            part = value[:, i * 128 : (i + 1) * 128]
            fine[q, i, pl.ds(0, wide, 2), :] = part
            fine[q, i, pl.ds(1, wide, 2), :] = part
    keep, pull = 1.0 - DAMPING, DAMPING / CENTRE

    def second_total(plane):
        rows = plane.shape[0]
        return pltpu.roll(plane, 1, 0) + pltpu.roll(plane, rows - 1, 0)

    spread = [jnp.concatenate([fine[q, i] for i in range(cz // 128)], axis=1) for q in range(cx + 2)]
    still = [keep * plane + pull * second_total(plane) for plane in spread]
    once = []
    for p in range(-1, nx + 1):
        q = (p + 2) // 2
        if p % 2 == 0:
            others = spread[q - 1] + spread[q]
        else:
            others = spread[q] + spread[q + 1]
        once.append(masked(still[q] + pull * others, ny, mask))
    none, one, two = [], [], []
    for p in range(nx):
        plane = once[p + 1]
        total = once[p] + once[p + 2] + second_total(plane)
        none.append((keep * plane + pull * total)[:ny])
        one.append(plane[:ny])
        two.append(spread[(p + 2) // 2][:ny])
    z = iota((cz, nz), 1)
    k = iota((cz, nz), 0)

    def hit(shift):
        moved = z + shift
        inside = jnp.logical_and(moved >= 0, moved < nz)
        return jnp.logical_and((moved >> 1) == k, inside).astype(F32)

    here, left, right = hit(0), hit(-1), hit(1)
    paths = jnp.where(jnp.logical_or(z == 0, z == nz - 1), here, 2.0 * here)
    spread_none = here.astype(BF16)
    spread_one = ((left + right) * 1.0).astype(BF16)
    spread_two = (hit(-2) + hit(2) + paths).astype(BF16)
    total = base_ref[...].reshape(nx * ny, nz)
    for parts, scale, matrix in (
        (none, 1.0, spread_none), (one, 2.0 * pull, spread_one), (two, pull * pull, spread_two)
    ):
        high, low = halves(scale * jnp.concatenate(parts, axis=0))
        total = total + dot(high, matrix, 1, 0) + dot(low, matrix, 1, 0)
    out_ref[...] = total.reshape(nx, ny, nz)
    for copy in copies:
        copy.wait()


def local(
    nutrient, species, agent_cell, death_flag, divide_flag, slab_move, depth_route, net_weight, sensing, uptake_weight
):
    depths = lax.axis_size("depth")
    nx, ny, nz = nutrient.shape
    agents, width = species.shape
    capacity = 2 * agents // depths
    me = lax.axis_index("depth").astype(jnp.int32).reshape(1)
    slab = lax.axis_index("slab").astype(jnp.int32).reshape(1)
    shape = jax.ShapeDtypeStruct
    cells, death, divide = (x.reshape(1, agents) for x in (agent_cell, death_flag, divide_flag))
    move, route = slab_move.reshape(1, agents), depth_route.reshape(1, agents)
    half = ny // 16
    arguments = (
        nutrient, cells, species, uptake_weight.reshape(1, width), death, divide,
        move, route, net_weight, sensing.reshape(1, width),
    )
    loaded = pl.pallas_call(
        load_kernel,
        out_shape=tuple(shape(x.shape, x.dtype) for x in arguments)
        + tuple(shape((HALO * half, 16, nz), BF16) for _ in range(2)),
        in_specs=[SMEM_SPEC] + [HBM_SPEC] * len(arguments),
        out_specs=[VMEM_SPEC] * (len(arguments) + 2),
        scratch_shapes=[pltpu.SemaphoreType.DMA((len(arguments),))],
        compiler_params=PARAMS,
        name="load",
    )(slab, *(pltpu.with_memory_space_constraint(x, pltpu.HBM) for x in arguments))
    nutrient, cells, species, weight, death, divide, move, route, net_weight, sensing = loaded[:-2]
    target, sensed, depth_a, depth_b, slab_a, slab_b = pl.pallas_call(
        uptake_kernel,
        out_shape=(
            shape((nx, ny, nz), F32),
            shape((8, agents), F32),
            shape((nx // 2, 16, nz), BF16),
            shape((nx // 2, 16, nz), BF16),
            shape(((HALO - 1) * half, 16, nz), BF16),
            shape(((HALO - 1) * half, 16, nz), BF16),
        ),
        in_specs=[SMEM_SPEC] * 2 + [VMEM_SPEC] * 6,
        out_specs=[VMEM_SPEC] * 6,
        compiler_params=PARAMS,
        name="uptake",
    )(me, slab, nutrient, cells, death, divide, species, weight)
    field_a, field_b, depth_a, depth_b = lax.optimization_barrier(
        (loaded[-2], loaded[-1], depth_a, depth_b)
    )
    side_a = swapped(depth_a, "depth", "a")
    side_b = swapped(depth_b, "depth", "b")
    field_a = swapped(field_a, "slab", "a")
    field_b = swapped(field_b, "slab", "b")
    pairs = HALO // 2
    slab_even = is_even(slab[0])
    last = nx // 2 - pairs

    def with_sides(own, start):
        parts = [lax.dynamic_slice_in_dim(side, start, pairs, 0) for side in (side_a, side_b)]
        return jnp.concatenate([own] + parts, axis=0)

    slab_a = swapped(with_sides(slab_a, jnp.where(slab_even, last, 0)), "slab", "a")
    slab_b = swapped(with_sides(slab_b, jnp.where(slab_even, 0, last)), "slab", "b")
    cx, cy, cz = nx // 2, ny // 2, nz // 2
    ext = ny + 2 * HALO
    sent = pl.pallas_call(
        network_kernel,
        out_shape=tuple(shape((capacity, width), BF16) for _ in range(depths))
        + tuple(shape((MIG * width // (16 * cz), 16, cz), BF16) for _ in range(2)),
        in_specs=[SMEM_SPEC] * 2 + [VMEM_SPEC] * 7,
        out_specs=[VMEM_SPEC] * (depths + 2),
        compiler_params=PARAMS,
        cost_estimate=pl.CostEstimate(
            flops=2 * 2304 * agents * width, bytes_accessed=1 << 20, transcendentals=agents * width
        ),
        name="network",
    )(me, slab, species, sensed, death, move, route, net_weight, sensing)
    arrived = [sent[0]] + [cyclic(sent[k], "depth", k) for k in range(1, depths)]
    u0, text, u1, u2, inside = pl.pallas_call(
        functools.partial(inner_kernel, depths),
        out_shape=(
            shape((nx + 2 * HALO, ext, nz), F32),
            shape((nx + 2 * HALO - 2, ext, nz), F32),
            shape((nx + 2 * HALO - 2, ext, nz), F32),
            shape((nx + 4, ext, nz), F32),
            shape((nx - 6, ny, nz), F32),
        ),
        in_specs=[SMEM_SPEC] + [VMEM_SPEC] * 4,
        out_specs=[VMEM_SPEC] * 5,
        compiler_params=PARAMS,
        cost_estimate=pl.CostEstimate(flops=1 << 30, bytes_accessed=1 << 22, transcendentals=0),
        name="inner",
    )(me, nutrient, target, side_a, side_b)
    _, text, _, u2, ct, ct_all, coarse_a, coarse_b = pl.pallas_call(
        functools.partial(smooth_kernel, depths),
        out_shape=(
            shape(u0.shape, F32),
            shape(text.shape, F32),
            shape(u1.shape, F32),
            shape(u2.shape, F32),
            shape((cx, cy, cz), F32),
            shape((cx, cy, cz), BF16),
            shape((1, cx * HALO, cz), BF16),
            shape((1, cx * HALO, cz), BF16),
        ),
        in_specs=[SMEM_SPEC] * 2 + [VMEM_SPEC] * 9,
        out_specs=[VMEM_SPEC] * 8,
        scratch_shapes=[pltpu.VMEM((cx, nz // 128, ny, 128), F32)],
        input_output_aliases={2: 0, 3: 1, 4: 2, 5: 3},
        compiler_params=PARAMS,
        name="smooth",
    )(me, slab, u0, text, u1, u2, inside, field_a, field_b, slab_a, slab_b)
    coarse_a = swapped(coarse_a, "depth", "a")
    coarse_b = swapped(coarse_b, "depth", "b")
    tail_a, tail_b = (
        swapped(jnp.concatenate([ct_all, coarse_a, coarse_b, movers], axis=0), "slab", which)
        for which, movers in (("a", sent[depths]), ("b", sent[depths + 1]))
    )
    base = pl.pallas_call(
        functools.partial(post_kernel, depths),
        out_shape=shape((nx, ny, nz), F32),
        in_specs=[SMEM_SPEC] + [VMEM_SPEC] * 2,
        out_specs=VMEM_SPEC,
        scratch_shapes=[pltpu.VMEM((nx + 2, ext, nz), F32)],
        compiler_params=PARAMS,
        cost_estimate=pl.CostEstimate(flops=1 << 30, bytes_accessed=1 << 22, transcendentals=0),
        name="post",
    )(me, u2, text)
    return pl.pallas_call(
        functools.partial(correct_kernel, depths),
        out_shape=(
            shape((nx, ny, nz), F32),
            shape((depths * capacity + 2 * MIG, width), BF16),
        ),
        in_specs=[SMEM_SPEC] * 2 + [VMEM_SPEC] * 6 + [ANY_SPEC] * depths,
        out_specs=[VMEM_SPEC, ANY_SPEC],
        scratch_shapes=[
            pltpu.VMEM((cx + 2, cz // 128, ext, 128), F32),
            pltpu.SemaphoreType.DMA((depths + 2 * (MIG // 16),)),
        ],
        compiler_params=PARAMS,
        name="correct",
    )(me, slab, ct, coarse_a, coarse_b, tail_a, tail_b, base, *arrived)


def solution(mesh):
    rows = P(("slab", "depth"))
    in_specs = (
        P("slab", "depth", None),
        P(("slab", "depth"), None),
        rows,
        rows,
        rows,
        rows,
        P(("slab", "depth"), None),
        P(),
        P(),
        P(),
    )
    out_specs = (P("slab", "depth", None), P(("slab", "depth"), None))
    return jax.shard_map(local, mesh=mesh, in_specs=in_specs, out_specs=out_specs, check_vma=False)
```

time: 54.3 us -> 43.5 us (0.80)
  waiting for transfers between devices: 16.3 us -> 11.4 us
  local copies, waits for them, and re-layouts: 4.76 us -> 0.01 us
  starting transfers between devices: 20.8 us -> 18.6 us
  Pallas kernels: 11.3 us -> 12.6 us
    ppermute x13 -> x3, starting transfers between devices: 20.8 us -> 2.02 us  [cyclic(): return lax.ppermute(x, axis, [(i, (i + by) % count) for i in range(count)])]
    ppermute x0 -> x10, starting transfers between devices: none -> 16.5 us  [swapped(): return lax.ppermute(x, axis, sorted(pairs))]
    ppermute x13 -> x3, waiting for transfers between devices: 16.3 us -> 0.01 us  [cyclic(): return lax.ppermute(x, axis, [(i, (i + by) % count) for i in range(count)])]
    ppermute x0 -> x10, waiting for transfers between devices: none -> 11.4 us  [swapped(): return lax.ppermute(x, axis, sorted(pairs))]
    unnamed x28 -> x0, local copies, waits for them, and re-layouts: 4.74 us -> none
    pallas_call x0 -> x3, Pallas kernels: none -> 4.7 us  [the longest x1 2.06 us: local(): pl.pallas_call(functools.partial(post_kernel, depths), out_shape=shape((n...]
    pallas_call x1, Pallas kernels: 4.02 us -> 1.94 us  [local(): pl.pallas_call(functools.partial(smooth_kernel, depths), out_shape=(shape...]
    pallas_call x1, Pallas kernels: 3.84 us -> 2.44 us  [local(): pl.pallas_call(functools.partial(correct_kernel, depths), out_shape=(shap...]
  transfers between devices with their start and end apart: 13 -> 13, of which waited for: 9 -> 3; matrix products, arithmetic and copies ran while one was open for 0% -> 0% of each run, Pallas kernels for 11% -> 12%
where the time goes in v2:
time: 43.5 us; the launch traced here: 43.4 us
  starting transfers between devices  18.6 us (43%)
  Pallas kernels  12.6 us (29%)
  waiting for transfers between devices  11.4 us (26%)
  between operations  0.74 us (2%)
    ppermute x10, starting transfers between devices, swapped(): return lax.ppermute(x, axis, sorted(pairs))  16.5 us
    ppermute x10, waiting for transfers between devices, swapped(): return lax.ppermute(x, axis, sorted(pairs))  11.4 us
    pallas_call x1, Pallas kernels, local(): pl.pallas_call(functools.partial(correct_kernel, depths), out_shape=(shap...  2.44 us
    pallas_call x1, Pallas kernels, local(): pl.pallas_call(functools.partial(post_kernel, depths), out_shape=shape((n...  2.06 us
    ppermute x3, starting transfers between devices, cyclic(): return lax.ppermute(x, axis, [(i, (i + by) % count) for i in range(count)])  2.02 us
    pallas_call x1, Pallas kernels, local(): pl.pallas_call(functools.partial(smooth_kernel, depths), out_shape=(shape...  1.94 us
    pallas_call x1, Pallas kernels, local(): pl.pallas_call(network_kernel, out_shape=tuple((shape((capacity, width),...  1.79 us
    pallas_call x1, Pallas kernels, local(): pl.pallas_call(uptake_kernel, out_shape=(shape((nx, ny, nz), F32), shape(...  1.68 us
  transfers between devices with their start and end apart: 13, of which 3 were waited for; matrix products, arithmetic and copies ran while one was open for 0% of the time, Pallas kernels for 12%

profile of v2, /device:TPU:0, one launch (start us, length us, event | category | flops | bytes accessed | tf_op | source)
XLA Modules:
  0.0 43.4 jit_solution(16736830224691920021)
XLA Ops:
  0.6 1.2 %load.1 = (f32[8,32,512]{2,1,0:T(8,128)S(1)}, s32[1,1024]{1,0:T(1,128)S(1)}, bf16[1024,128]{1,0:T(8,128)(2,1)S(1)}, bf16[1,128]{1,0:T(2,128)(2,1)S(1)}, s32[1,10...) custom-call(s32[1]{0:T(128)} %bitcast.1.slab_ref, ...), custom_call_target="tpu_custom_call" | custom-call | tf_op jit(solution)/shard_map/load/pallas_call | solution.py:507
  1.9 1.7 %uptake.1 = (f32[8,32,512]{2,1,0:T(8,128)S(1)}, f32[8,1024]{1,0:T(8,128)S(1)}, bf16[4,16,512]{2,1,0:T(8,128)(2,1)S(1)}, bf16[4,16,512]{2,1,0:T(8,128)(2,1)S(1)},...) custom-call(s32[1]{0:T(128)} %bitcast.me_ref, s32[1]{0:T(128)} %bitcast.1.slab_ref, ...), custom_call_target="tpu_custom_call" | custom-call | tf_op jit(solution)/shard_map/uptake/pallas_call | solution.py:518
  3.6 0.5 %collective-permute-start = (bf16[4,16,512]{2,1,0:T(8,128)(2,1)S(1)}, bf16[4,16,512]{2,1,0:T(8,128)(2,1)S(1)}, u32[]{:S(2)}, u32[]{:S(2)}) collective-permute-start(bf16[4,16,512]{2,1,0:T(8,128)(2,1)S(1)} %get-tuple-element.52), channel_id=1, source_target_pairs={{0,1},{1,0},{2,3},{3,2},{4,5},{5,4},{6,7},{7,6},{8,9},{9,8},{10,11... | collective-permute-start | bytes 196616 | tf_op jit(solution)/shard_map/ppermute | solution.py:51
  4.1 2.6 %collective-permute-start.1 = (bf16[4,16,512]{2,1,0:T(8,128)(2,1)S(1)}, bf16[4,16,512]{2,1,0:T(8,128)(2,1)S(1)}, u32[]{:S(2)}, u32[]{:S(2)}) collective-permute-start(bf16[4,16,512]{2,1,0:T(8,128)(2,1)S(1)} %get-tuple-element.53), channel_id=1, source_target_pairs={{0,3},{1,2},{2,1},{3,0},{4,7},{5,6},{6,5},{7,4},{8,11},{9,10},{10,... | collective-permute-start | bytes 196616 | tf_op jit(solution)/shard_map/ppermute | solution.py:51
  6.7 0.0 collective-permute-done.side_a
  6.7 2.4 %collective-permute-done.1.side_b = bf16[4,16,512]{2,1,0:T(8,128)(2,1)S(1)} collective-permute-done((bf16[4,16,512]{2,1,0:T(8,128)(2,1)S(1)}, bf16[4,16,512]{2,1,0:T(8,128)(2,1)S(1)}, u32[]{:S(2)}, u32[]{:S(2)}) %collective-permute-start.1) | collective-permute-done | bytes 65568 | tf_op jit(solution)/shard_map/ppermute | solution.py:51
  9.1 1.5 %collective-permute-start.4 = (bf16[10,16,512]{2,1,0:T(8,128)(2,1)S(1)}, bf16[10,16,512]{2,1,0:T(8,128)(2,1)S(1)}, u32[]{:S(2)}, u32[]{:S(2)}) collective-permute-start(bf16[10,16,512]{2,1,0:T(8,128)(2,1)S(1)} %pad_maximum_fusion), channel_id=1, source_target_pairs={{0,4},{4,0},{8,12},{12,8},{16,20},{20,16},{24,28},{28,24},{1,5},{5... | collective-permute-start | bytes 491528 | tf_op jit(solution)/shard_map/ppermute | solution.py:51
  10.6 3.6 %collective-permute-start.5 = (bf16[10,16,512]{2,1,0:T(8,128)(2,1)S(1)}, bf16[10,16,512]{2,1,0:T(8,128)(2,1)S(1)}, u32[]{:S(2)}, u32[]{:S(2)}) collective-permute-start(bf16[10,16,512]{2,1,0:T(8,128)(2,1)S(1)} %pad_maximum_fusion.1), channel_id=1, source_target_pairs={{0,28},{4,8},{8,4},{12,16},{16,12},{20,24},{24,20},{28,0},{1,29},{... | collective-permute-start | bytes 491528 | tf_op jit(solution)/shard_map/ppermute | solution.py:51
  14.3 0.0 collective-permute-start.2
  14.3 1.9 %collective-permute-start.3 = (bf16[8,16,512]{2,1,0:T(8,128)(2,1)S(1)}, bf16[8,16,512]{2,1,0:T(8,128)(2,1)S(1)}, u32[]{:S(2)}, u32[]{:S(2)}) collective-permute-start(bf16[8,16,512]{2,1,0:T(8,128)(2,1)S(1)} %get-tuple-element.60), channel_id=1, source_target_pairs={{0,28},{4,8},{8,4},{12,16},{16,12},{20,24},{24,20},{28,0},{1,29},{... | collective-permute-start | bytes 393224 | tf_op jit(solution)/shard_map/ppermute | solution.py:51
  16.2 1.4 %inner.1 = (f32[16,40,512]{2,1,0:T(8,128)S(1)}, f32[14,40,512]{2,1,0:T(8,128)S(1)}, f32[14,40,512]{2,1,0:T(8,128)S(1)}, f32[12,40,512]{2,1,0:T(8,128)S(1)}, f32[2,32,512]{2,1,0:T(8,128)S(1)}) custom-call(s32[1]{0:T(128)} %bitcast.me_ref, f32[8,32,512]{2,1,0:T(8,128)S(1)} %get-tuple-element.41.u_ref, f32[8,32,512]{2,1,0:T(8,128)S(1)} %get-tuple-element.47.t_ref, ...), custom_call_target="tpu_custom_call" | custom-call | flops 1073741824 | bytes 4194304 | tf_op jit(solution)/shard_map/inner/pallas_call | solution.py:565
  17.6 7.6 %collective-permute-done.2.field_a = bf16[8,16,512]{2,1,0:T(8,128)(2,1)S(1)} collective-permute-done((bf16[8,16,512]{2,1,0:T(8,128)(2,1)S(1)}, bf16[8,16,512]{2,1,0:T(8,128)(2,1)S(1)}, u32[]{:S(2)}, u32[]{:S(2)}) %collective-permute-start.2) | collective-permute-done | bytes 131104 | tf_op jit(solution)/shard_map/ppermute | solution.py:51
  25.2 0.0 collective-permute-done.3.field_b
  25.2 0.0 collective-permute-done.4.slab_a
  25.2 0.0 collective-permute-done.5.slab_b
  25.2 1.9 %smooth.1 = (f32[16,40,512]{2,1,0:T(8,128)S(1)}, f32[14,40,512]{2,1,0:T(8,128)S(1)}, f32[14,40,512]{2,1,0:T(8,128)S(1)}, f32[12,40,512]{2,1,0:T(8,128)S(1)}, f32...) custom-call(s32[1]{0:T(128)} %bitcast.me_ref, ...), custom_call_target="tpu_custom_call", output_to_operand_aliasing={{0}: (2, {}), {1}: (3, {}), {2}: (4, {}), {3}: (5, {})} | custom-call | tf_op jit(solution)/shard_map/smooth/pallas_call | solution.py:580
  27.1 0.1 collective-permute-start.6
  27.2 1.6 %collective-permute-start.7 = (bf16[1,16,256]{2,1,0:T(8,128)(2,1)S(1)}, bf16[1,16,256]{2,1,0:T(8,128)(2,1)S(1)}, u32[]{:S(2)}, u32[]{:S(2)}) collective-permute-start(bf16[1,16,256]{2,1,0:T(8,128)(2,1)S(1)} %get-tuple-element.65), channel_id=1, source_target_pairs={{0,3},{1,2},{2,1},{3,0},{4,7},{5,6},{6,5},{7,4},{8,11},{9,10},{10,... | collective-permute-start | bytes 24584 | tf_op jit(solution)/shard_map/ppermute | solution.py:51
  28.9 1.8 %network.1 = (bf16[512,128]{1,0:T(8,128)(2,1)S(1)}, bf16[512,128]{1,0:T(8,128)(2,1)S(1)}, bf16[512,128]{1,0:T(8,128)(2,1)S(1)}, bf16[512,128]{1,0:T(8,128)(2,1)S...) custom-call(s32[1]{0:T(128)} %bitcast.me_ref, s32[1]{0:T(128)} %bitcast.1.slab_ref, ...), custom_call_target="tpu_custom_call" | custom-call | flops 603979776 | bytes 1048576 | tf_op jit(solution)/shard_map/network/pallas_call | solution.py:552
  30.7 0.1 collective-permute-start.10
  30.8 0.5 %collective-permute-start.11 = (bf16[512,128]{1,0:T(8,128)(2,1)S(1)}, bf16[512,128]{1,0:T(8,128)(2,1)S(1)}, u32[]{:S(2)}, u32[]{:S(2)}) collective-permute-start(bf16[512,128]{1,0:T(8,128)(2,1)S(1)} %get-tuple-element.78), channel_id=1, source_target_pairs={{0,2},{1,3},{2,0},{3,1},{4,6},{5,7},{6,4},{7,5},{8,10},{9,11},{10,... | collective-permute-start | bytes 393224 | tf_op jit(solution)/shard_map/ppermute | solution.py:39
  31.3 1.4 %collective-permute-start.12 = (bf16[512,128]{1,0:T(8,128)(2,1)S(1)}, bf16[512,128]{1,0:T(8,128)(2,1)S(1)}, u32[]{:S(2)}, u32[]{:S(2)}) collective-permute-start(bf16[512,128]{1,0:T(8,128)(2,1)S(1)} %get-tuple-element.79), channel_id=1, source_target_pairs={{0,3},{1,0},{2,1},{3,2},{4,7},{5,4},{6,5},{7,6},{8,11},{9,8},{10,9... | collective-permute-start | bytes 393224 | tf_op jit(solution)/shard_map/ppermute | solution.py:39
  32.7 0.0 collective-permute-done.6.side_a
  32.7 0.0 collective-permute-done.7.side_b
  32.7 1.1 %collective-permute-start.8 = (bf16[10,16,256]{2,1,0:T(8,128)(2,1)S(1)}, bf16[10,16,256]{2,1,0:T(8,128)(2,1)S(1)}, u32[]{:S(2)}, u32[]{:S(2)}) collective-permute-start(bf16[10,16,256]{2,1,0:T(8,128)(2,1)S(1)} %get-tuple-element.85), channel_id=1, source_target_pairs={{0,4},{4,0},{8,12},{12,8},{16,20},{20,16},{24,28},{28,24},{1,5},{5... | collective-permute-start | bytes 245768 | tf_op jit(solution)/shard_map/ppermute | solution.py:51
  33.8 3.6 %collective-permute-start.9 = (bf16[10,16,256]{2,1,0:T(8,128)(2,1)S(1)}, bf16[10,16,256]{2,1,0:T(8,128)(2,1)S(1)}, u32[]{:S(2)}, u32[]{:S(2)}) collective-permute-start(bf16[10,16,256]{2,1,0:T(8,128)(2,1)S(1)} %get-tuple-element.84), channel_id=1, source_target_pairs={{0,28},{4,8},{8,4},{12,16},{16,12},{20,24},{24,20},{28,0},{1,29},{... | collective-permute-start | bytes 245768 | tf_op jit(solution)/shard_map/ppermute | solution.py:51
  37.4 2.1 %post.1.base_ref = f32[8,32,512]{2,1,0:T(8,128)S(1)} custom-call(s32[1]{0:T(128)} %bitcast.me_ref, f32[12,40,512]{2,1,0:T(8,128)S(1)} %get-tuple-element.74.u2_ref, f32[14,40,512]{2,1,0:T(8,128)S(1)} %get-tuple-element.75.text_ref), custom_call_target="tpu_custom_call" | custom-call | flops 1073741824 | bytes 4194304 | tf_op jit(solution)/shard_map/post/pallas_call | solution.py:605
  39.4 0.0 collective-permute-done.10.rest_1_
  39.4 0.0 collective-permute-done.11.rest_2_
  39.5 0.0 collective-permute-done.12.rest_3_
  39.5 0.0 collective-permute-done.8.slab_a
  39.5 1.4 %collective-permute-done.9.slab_b = bf16[10,16,256]{2,1,0:T(8,128)(2,1)S(1)} collective-permute-done((bf16[10,16,256]{2,1,0:T(8,128)(2,1)S(1)}, bf16[10,16,256]{2,1,0:T(8,128)(2,1)S(1)}, u32[]{:S(2)}, u32[]{:S(2)}) %collective-permute-start.9) | collective-permute-done | bytes 81952 | tf_op jit(solution)/shard_map/ppermute | solution.py:51
  40.9 2.4 %correct.1 = (f32[8,32,512]{2,1,0:T(8,128)}, bf16[2304,128]{1,0:T(8,128)(2,1)}) custom-call(s32[1]{0:T(128)} %bitcast.me_ref, s32[1]{0:T(128)} %bitcast.1.slab_ref, f32[4,16,256]{2,1,0:T(8,128)S(1)} %get-tuple-element.63.ct_ref, bf16[1,16,256]{2,1,0:T(8,128)(2,1)S(1)} %collective-permute-done.6.side_a, ...), custom_call_target="tpu_custom_call" | custom-call | tf_op jit(solution)/shard_map/correct/pallas_call | solution.py:615
  (5 shorter events, 0.1 us)
Async XLA Ops:
  3.6 3.2 %collective-permute-start = (bf16[4,16,512]{2,1,0:T(8,128)(2,1)S(1)}, bf16[4,16,512]{2,1,0:T(8,128)(2,1)S(1)}, u32[]{:S(2)}, u32[]{:S(2)}) collective-permute-start(bf16[4,16,512]{2,1,0:T(8,128)(2,1)S(1)} %get-tuple-element.52), channel_id=1, source_target_pairs={{0,1},{1,0},{2,3},{3,2},{4,5},{5,4},{6,7},{7,6},{8,9},{9,8},{10,11... | collective-permute-start | bytes 196616 | tf_op jit(solution)/shard_map/ppermute | solution.py:51
  4.1 5.0 %collective-permute-start.1 = (bf16[4,16,512]{2,1,0:T(8,128)(2,1)S(1)}, bf16[4,16,512]{2,1,0:T(8,128)(2,1)S(1)}, u32[]{:S(2)}, u32[]{:S(2)}) collective-permute-start(bf16[4,16,512]{2,1,0:T(8,128)(2,1)S(1)} %get-tuple-element.53), channel_id=1, source_target_pairs={{0,3},{1,2},{2,1},{3,0},{4,7},{5,6},{6,5},{7,4},{8,11},{9,10},{10,... | collective-permute-start | bytes 196616 | tf_op jit(solution)/shard_map/ppermute | solution.py:51
  9.1 16.1 %collective-permute-start.4 = (bf16[10,16,512]{2,1,0:T(8,128)(2,1)S(1)}, bf16[10,16,512]{2,1,0:T(8,128)(2,1)S(1)}, u32[]{:S(2)}, u32[]{:S(2)}) collective-permute-start(bf16[10,16,512]{2,1,0:T(8,128)(2,1)S(1)} %pad_maximum_fusion), channel_id=1, source_target_pairs={{0,4},{4,0},{8,12},{12,8},{16,20},{20,16},{24,28},{28,24},{1,5},{5... | collective-permute-start | bytes 491528 | tf_op jit(solution)/shard_map/ppermute | solution.py:51
  10.6 14.6 %collective-permute-start.5 = (bf16[10,16,512]{2,1,0:T(8,128)(2,1)S(1)}, bf16[10,16,512]{2,1,0:T(8,128)(2,1)S(1)}, u32[]{:S(2)}, u32[]{:S(2)}) collective-permute-start(bf16[10,16,512]{2,1,0:T(8,128)(2,1)S(1)} %pad_maximum_fusion.1), channel_id=1, source_target_pairs={{0,28},{4,8},{8,4},{12,16},{16,12},{20,24},{24,20},{28,0},{1,29},{... | collective-permute-start | bytes 491528 | tf_op jit(solution)/shard_map/ppermute | solution.py:51
  14.3 10.9 %collective-permute-start.2 = (bf16[8,16,512]{2,1,0:T(8,128)(2,1)S(1)}, bf16[8,16,512]{2,1,0:T(8,128)(2,1)S(1)}, u32[]{:S(2)}, u32[]{:S(2)}) collective-permute-start(bf16[8,16,512]{2,1,0:T(8,128)(2,1)S(1)} %get-tuple-element.59), channel_id=1, source_target_pairs={{0,4},{4,0},{8,12},{12,8},{16,20},{20,16},{24,28},{28,24},{1,5},{5... | collective-permute-start | bytes 393224 | tf_op jit(solution)/shard_map/ppermute | solution.py:51
  14.3 10.9 %collective-permute-start.3 = (bf16[8,16,512]{2,1,0:T(8,128)(2,1)S(1)}, bf16[8,16,512]{2,1,0:T(8,128)(2,1)S(1)}, u32[]{:S(2)}, u32[]{:S(2)}) collective-permute-start(bf16[8,16,512]{2,1,0:T(8,128)(2,1)S(1)} %get-tuple-element.60), channel_id=1, source_target_pairs={{0,28},{4,8},{8,4},{12,16},{16,12},{20,24},{24,20},{28,0},{1,29},{... | collective-permute-start | bytes 393224 | tf_op jit(solution)/shard_map/ppermute | solution.py:51
  27.1 5.5 %collective-permute-start.6 = (bf16[1,16,256]{2,1,0:T(8,128)(2,1)S(1)}, bf16[1,16,256]{2,1,0:T(8,128)(2,1)S(1)}, u32[]{:S(2)}, u32[]{:S(2)}) collective-permute-start(bf16[1,16,256]{2,1,0:T(8,128)(2,1)S(1)} %get-tuple-element.64), channel_id=1, source_target_pairs={{0,1},{1,0},{2,3},{3,2},{4,5},{5,4},{6,7},{7,6},{8,9},{9,8},{10,11... | collective-permute-start | bytes 24584 | tf_op jit(solution)/shard_map/ppermute | solution.py:51
  27.2 5.5 %collective-permute-start.7 = (bf16[1,16,256]{2,1,0:T(8,128)(2,1)S(1)}, bf16[1,16,256]{2,1,0:T(8,128)(2,1)S(1)}, u32[]{:S(2)}, u32[]{:S(2)}) collective-permute-start(bf16[1,16,256]{2,1,0:T(8,128)(2,1)S(1)} %get-tuple-element.65), channel_id=1, source_target_pairs={{0,3},{1,2},{2,1},{3,0},{4,7},{5,6},{6,5},{7,4},{8,11},{9,10},{10,... | collective-permute-start | bytes 24584 | tf_op jit(solution)/shard_map/ppermute | solution.py:51
  30.7 8.8 %collective-permute-start.10 = (bf16[512,128]{1,0:T(8,128)(2,1)S(1)}, bf16[512,128]{1,0:T(8,128)(2,1)S(1)}, u32[]{:S(2)}, u32[]{:S(2)}) collective-permute-start(bf16[512,128]{1,0:T(8,128)(2,1)S(1)} %get-tuple-element.77), channel_id=1, source_target_pairs={{0,1},{1,2},{2,3},{3,0},{4,5},{5,6},{6,7},{7,4},{8,9},{9,10},{10,1... | collective-permute-start | bytes 393224 | tf_op jit(solution)/shard_map/ppermute | solution.py:39
  30.8 8.7 %collective-permute-start.11 = (bf16[512,128]{1,0:T(8,128)(2,1)S(1)}, bf16[512,128]{1,0:T(8,128)(2,1)S(1)}, u32[]{:S(2)}, u32[]{:S(2)}) collective-permute-start(bf16[512,128]{1,0:T(8,128)(2,1)S(1)} %get-tuple-element.78), channel_id=1, source_target_pairs={{0,2},{1,3},{2,0},{3,1},{4,6},{5,7},{6,4},{7,5},{8,10},{9,11},{10,... | collective-permute-start | bytes 393224 | tf_op jit(solution)/shard_map/ppermute | solution.py:39
  31.3 8.2 %collective-permute-start.12 = (bf16[512,128]{1,0:T(8,128)(2,1)S(1)}, bf16[512,128]{1,0:T(8,128)(2,1)S(1)}, u32[]{:S(2)}, u32[]{:S(2)}) collective-permute-start(bf16[512,128]{1,0:T(8,128)(2,1)S(1)} %get-tuple-element.79), channel_id=1, source_target_pairs={{0,3},{1,0},{2,1},{3,2},{4,7},{5,4},{6,5},{7,6},{8,11},{9,8},{10,9... | collective-permute-start | bytes 393224 | tf_op jit(solution)/shard_map/ppermute | solution.py:39
  32.7 6.8 %collective-permute-start.8 = (bf16[10,16,256]{2,1,0:T(8,128)(2,1)S(1)}, bf16[10,16,256]{2,1,0:T(8,128)(2,1)S(1)}, u32[]{:S(2)}, u32[]{:S(2)}) collective-permute-start(bf16[10,16,256]{2,1,0:T(8,128)(2,1)S(1)} %get-tuple-element.85), channel_id=1, source_target_pairs={{0,4},{4,0},{8,12},{12,8},{16,20},{20,16},{24,28},{28,24},{1,5},{5... | collective-permute-start | bytes 245768 | tf_op jit(solution)/shard_map/ppermute | solution.py:51
  33.8 7.1 %collective-permute-start.9 = (bf16[10,16,256]{2,1,0:T(8,128)(2,1)S(1)}, bf16[10,16,256]{2,1,0:T(8,128)(2,1)S(1)}, u32[]{:S(2)}, u32[]{:S(2)}) collective-permute-start(bf16[10,16,256]{2,1,0:T(8,128)(2,1)S(1)} %get-tuple-element.84), channel_id=1, source_target_pairs={{0,28},{4,8},{8,4},{12,16},{16,12},{20,24},{24,20},{28,0},{1,29},{... | collective-permute-start | bytes 245768 | tf_op jit(solution)/shard_map/ppermute | solution.py:51

commit v3 on v2

--- a/solution.py
+++ b/solution.py
@@ -246,12 +246,65 @@
     )
 
 
+def corner_kernel(me_ref, slab_ref, side_a, side_b, in_a, in_b, slab_a, slab_b):
+    layers = 2 * side_a.shape[0]
+    nz = side_a.shape[2]
+    own = slab_a.shape[0] - 2
+    even = is_even(me_ref[0])
+    slab_even = is_even(slab_ref[0])
+
+    def layer(side, plane):
+        at = 2 * HALO * (plane % 2)
+        return side[plane // 2].astype(F32)[at : at + 2 * HALO]
+
+    for index, (side, high) in enumerate(((side_a, even), (side_b, jnp.logical_not(even)))):
+        for ref, front in ((slab_a, slab_even), (slab_b, jnp.logical_not(slab_even))):
+            fields, targets = [], []
+            for i in range(1, HALO):
+                x = jnp.where(front, layer(side, layers - i), layer(side, i - 1))
+                fields.append(jnp.where(high, x[: HALO - i], x[i:HALO]))
+                if i < HALO - 1:
+                    targets.append(
+                        jnp.where(high, x[HALO : 2 * HALO - 1 - i], x[HALO + 1 + i :])
+                    )
+            rows = jnp.concatenate(fields + targets, axis=0)
+            rest = jnp.zeros((16 - rows.shape[0], nz), F32)
+            ref[own + index] = jnp.concatenate([rows, rest], axis=0).astype(BF16)
+
+
+def corner_rows(block_a, block_b, even, mask):
+    block_a, block_b = block_a.astype(F32), block_b.astype(F32)
+    high = jnp.where(even, block_a, block_b)
+    low = jnp.where(even, block_b, block_a)
+    nz = high.shape[1]
+    fields, targets = [], []
+    at = 0
+    for rows, out in ((HALO, fields), (HALO - 1, targets)):
+        for i in range(1, rows):
+            count = rows - i
+            gap = jnp.zeros((2 * (HALO - count), nz), F32)
+            cut = slice(at, at + count)
+            out.append(jnp.concatenate([high[cut], gap, low[cut]], axis=0) * mask)
+            at += count
+    return fields, targets + [jnp.zeros_like(fields[0])]
+
+
+KEEP, PULL = 1.0 - DAMPING, DAMPING / CENTRE
+
+
 def inner_kernel(
-    depths, me_ref, u_ref, t_ref, side_a, side_b, u0, text_ref, u1, u2_ref, inside
+    depths, me_ref, slab_ref, u_ref, t_ref, side_a, side_b, field_a, field_b, u0, text_ref, u1, u2_ref, inside
 ):
     nx, ny, nz = u_ref.shape
     even = is_even(me_ref[0])
+    slab_even = is_even(slab_ref[0])
+    half = ny // 16
     mask = edge_mask(me_ref[0], depths, HALO)
+    for field, after in ((field_a, slab_even), (field_b, jnp.logical_not(slab_even))):
+        u_at = jnp.where(after, HALO + nx, 0)
+        for k in range(HALO):
+            u0[u_at + k, :ny] = field[k * half : (k + 1) * half].astype(F32).reshape(ny, nz)
+            u0[u_at + k, ny:] = jnp.zeros((2 * HALO, nz), F32)
     for plane in range(nx):
         u0[HALO + plane, :ny] = u_ref[plane]
         text_ref[HALO - 1 + plane, :ny] = t_ref[plane]
@@ -259,21 +312,28 @@
         u0[HALO + plane, ny:] = uh
         text_ref[HALO - 1 + plane, ny:] = th
 
+    def outer(i, carry):
+        for p in (i, nx + HALO - 1 + i):
+            u1[p] = KEEP * u0[p + 1] + PULL * neighbour_total(u0[p], u0[p + 1], u0[p + 2])
+        return carry
+
+    lax.fori_loop(0, HALO - 1, outer, 0)
+
     def first(p, carry):
         v = relaxed(u0[p], u0[p + 1], u0[p + 2], text_ref[p], CENTRE)
         u1[p] = masked(v, ny, mask)
         return carry
 
-    lax.fori_loop(HALO, nx + HALO - 2, first, 0)
+    lax.fori_loop(HALO - 1, nx + HALO - 1, first, 0)
 
     def second(p, carry):
         v = relaxed(u1[p], u1[p + 1], u1[p + 2], text_ref[p + 1], CENTRE)
         u2_ref[p] = masked(v, ny, mask)
         return carry
 
-    lax.fori_loop(HALO, nx, second, 0)
-    for p in range(3, nx - 3):
-        inside[p - 3] = residual(u2_ref, text_ref, p, ny)
+    lax.fori_loop(HALO - 1, nx + 1, second, 0)
+    for p in range(2, nx - 2):
+        inside[p - 2] = residual(u2_ref, text_ref, p, ny)
 
 
 def residual(u2_ref, text_ref, p, ny):
@@ -283,52 +343,56 @@
 
 
 def smooth_kernel(
-    depths, me_ref, slab_ref, u0_in, text_in, u1_in, u2_in, inside, field_a, field_b, slab_a, slab_b,
-    u0, text_ref, u1, u2_ref, coarse_ref, coarse_all_ref, coarse_a, coarse_b, paired,
+    depths, me_ref, slab_ref, u0, text_in, u1_in, u2_in, inside, slab_a, slab_b,
+    text_ref, u1, u2_ref, coarse_ref, coarse_all_ref, coarse_a, coarse_b, paired,
 ):
     nx = u0.shape[0] - 2 * HALO
     ny, nz = u0.shape[1] - 2 * HALO, u0.shape[2]
     mask = edge_mask(me_ref[0], depths, HALO)
     half = ny // 16
-    pairs = HALO // 2
     own = (HALO - 1) * half
     even = is_even(me_ref[0])
     slab_even = is_even(slab_ref[0])
-    for field, ref, after in (
-        (field_a, slab_a, slab_even), (field_b, slab_b, jnp.logical_not(slab_even))
-    ):
-        u_at = jnp.where(after, HALO + nx, 0)
-        t_at = jnp.where(after, HALO - 1 + nx, 0)
-        sides = []
-        for k in range(HALO):
-            u0[u_at + k, :ny] = field[k * half : (k + 1) * half].astype(F32).reshape(ny, nz)
-            uh, th = halo_rows(ref[own + k // 2], ref[own + pairs + k // 2], even, k, mask)
-            u0[u_at + k, ny:] = uh
-            sides.append(th)
-        for k in range(HALO - 1):
-            text_ref[t_at + k, :ny] = ref[k * half : (k + 1) * half].astype(F32).reshape(ny, nz)
-            text_ref[t_at + k, ny:] = jnp.where(after, sides[k], sides[k + 1])
-
-    def first(i, carry):
-        for p in (i, nx + 2 + i):
-            v = relaxed(u0[p], u0[p + 1], u0[p + 2], text_ref[p], CENTRE)
-            u1[p] = masked(v, ny, mask)
-        return carry
-
-    lax.fori_loop(0, HALO, first, 0)
+    row = iota((8, 1), 0)
+    first, last = (row == 0).astype(F32), (row == 7).astype(F32)
+    for ref, after in ((slab_a, slab_even), (slab_b, jnp.logical_not(slab_even))):
+        fields, targets = corner_rows(ref[own], ref[own + 1], even, mask)
+        sign = jnp.where(after, 1, -1)
+        edge = jnp.where(after, nx - 1, 0)
+        for i in range(1, HALO):
+            p = edge + sign * i
+            index = jnp.where(after, i - 1, HALO - 1 - i)
+            t = ref[pl.ds(index * half, half)].astype(F32).reshape(ny, nz)
+            text_ref[p + 3, :ny] = t
+            text_ref[p + 3, ny:] = targets[i - 1]
+            x = fields[i - 1]
+            nearer = u0[p + 4 - sign, ny:] if i == 1 else fields[i - 2]
+            total = nearer + third_sum(x)
+            if i < HALO - 1:
+                total = total + fields[i]
+            beyond = u0[p + 4]
+            up = jnp.where(row == 0, beyond[ny - 1 : ny], pltpu.roll(x, 1, 0))
+            down = jnp.where(row == 7, beyond[0:1], pltpu.roll(x, 7, 0))
+            u1[p + 3, ny:] = (KEEP * x + PULL * (targets[i - 1] + total + up + down)) * mask
+            v = u1[p + 3, :ny] + PULL * t
+            u1[p + 3, :ny] = v
+            u1[p + 3, 0:8] = v[0:8] + (PULL * first) * x[7:8]
+            u1[p + 3, ny - 8 : ny] = v[ny - 8 :] + (PULL * last) * x[0:1]
+        u1[edge + 3, ny:] = u1[edge + 3, ny:] + PULL * fields[0]
+        u2_ref[edge - sign + 2, ny:] = u2_ref[edge - sign + 2, ny:] + (PULL * PULL) * fields[0]
 
     def second(i, carry):
-        for p in (i, nx + i):
+        for p in (i, nx + 1 + i):
             v = relaxed(u1[p], u1[p + 1], u1[p + 2], text_ref[p + 1], CENTRE)
             u2_ref[p] = masked(v, ny, mask)
         return carry
 
-    lax.fori_loop(0, HALO, second, 0)
+    lax.fori_loop(0, HALO - 1, second, 0)
     for q in range(nx // 2):
         both = 0.0
         for p in (2 * q, 2 * q + 1):
-            known = 3 <= p < nx - 3
-            both = both + (inside[p - 3] if known else residual(u2_ref, text_ref, p, ny))
+            known = 2 <= p < nx - 2
+            both = both + (inside[p - 2] if known else residual(u2_ref, text_ref, p, ny))
         for i in range(nz // 128):
             paired[q, i] = both[:, i * 128 : (i + 1) * 128]
     cx, cy, cz = coarse_ref.shape
@@ -440,14 +504,12 @@
             part = value[:, i * 128 : (i + 1) * 128]
             fine[q, i, pl.ds(0, wide, 2), :] = part
             fine[q, i, pl.ds(1, wide, 2), :] = part
-    keep, pull = 1.0 - DAMPING, DAMPING / CENTRE
-
     def second_total(plane):
         rows = plane.shape[0]
         return pltpu.roll(plane, 1, 0) + pltpu.roll(plane, rows - 1, 0)
 
     spread = [jnp.concatenate([fine[q, i] for i in range(cz // 128)], axis=1) for q in range(cx + 2)]
-    still = [keep * plane + pull * second_total(plane) for plane in spread]
+    still = [KEEP * plane + PULL * second_total(plane) for plane in spread]
     once = []
     for p in range(-1, nx + 1):
         q = (p + 2) // 2
@@ -455,12 +517,12 @@
             others = spread[q - 1] + spread[q]
         else:
             others = spread[q] + spread[q + 1]
-        once.append(masked(still[q] + pull * others, ny, mask))
+        once.append(masked(still[q] + PULL * others, ny, mask))
     none, one, two = [], [], []
     for p in range(nx):
         plane = once[p + 1]
         total = once[p] + once[p + 2] + second_total(plane)
-        none.append((keep * plane + pull * total)[:ny])
+        none.append((KEEP * plane + PULL * total)[:ny])
         one.append(plane[:ny])
         two.append(spread[(p + 2) // 2][:ny])
     z = iota((cz, nz), 1)
@@ -478,7 +540,7 @@
     spread_two = (hit(-2) + hit(2) + paths).astype(BF16)
     total = base_ref[...].reshape(nx * ny, nz)
     for parts, scale, matrix in (
-        (none, 1.0, spread_none), (one, 2.0 * pull, spread_one), (two, pull * pull, spread_two)
+        (none, 1.0, spread_none), (one, 2.0 * PULL, spread_one), (two, PULL * PULL, spread_two)
     ):
         high, low = halves(scale * jnp.concatenate(parts, axis=0))
         total = total + dot(high, matrix, 1, 0) + dot(low, matrix, 1, 0)
@@ -522,8 +584,8 @@
             shape((8, agents), F32),
             shape((nx // 2, 16, nz), BF16),
             shape((nx // 2, 16, nz), BF16),
-            shape(((HALO - 1) * half, 16, nz), BF16),
-            shape(((HALO - 1) * half, 16, nz), BF16),
+            shape(((HALO - 1) * half + 2, 16, nz), BF16),
+            shape(((HALO - 1) * half + 2, 16, nz), BF16),
         ),
         in_specs=[SMEM_SPEC] * 2 + [VMEM_SPEC] * 6,
         out_specs=[VMEM_SPEC] * 6,
@@ -537,16 +599,17 @@
     side_b = swapped(depth_b, "depth", "b")
     field_a = swapped(field_a, "slab", "a")
     field_b = swapped(field_b, "slab", "b")
-    pairs = HALO // 2
-    slab_even = is_even(slab[0])
-    last = nx // 2 - pairs
-
-    def with_sides(own, start):
-        parts = [lax.dynamic_slice_in_dim(side, start, pairs, 0) for side in (side_a, side_b)]
-        return jnp.concatenate([own] + parts, axis=0)
-
-    slab_a = swapped(with_sides(slab_a, jnp.where(slab_even, last, 0)), "slab", "a")
-    slab_b = swapped(with_sides(slab_b, jnp.where(slab_even, 0, last)), "slab", "b")
+    slab_a, slab_b = pl.pallas_call(
+        corner_kernel,
+        out_shape=tuple(shape(x.shape, BF16) for x in (slab_a, slab_b)),
+        in_specs=[SMEM_SPEC] * 2 + [VMEM_SPEC] * 4,
+        out_specs=[VMEM_SPEC] * 2,
+        input_output_aliases={4: 0, 5: 1},
+        compiler_params=PARAMS,
+        name="corner",
+    )(me, slab, side_a, side_b, slab_a, slab_b)
+    slab_a = swapped(slab_a, "slab", "a")
+    slab_b = swapped(slab_b, "slab", "b")
     cx, cy, cz = nx // 2, ny // 2, nz // 2
     ext = ny + 2 * HALO
     sent = pl.pallas_call(
@@ -561,7 +624,6 @@
         ),
         name="network",
     )(me, slab, species, sensed, death, move, route, net_weight, sensing)
-    arrived = [sent[0]] + [cyclic(sent[k], "depth", k) for k in range(1, depths)]
     u0, text, u1, u2, inside = pl.pallas_call(
         functools.partial(inner_kernel, depths),
         out_shape=(
@@ -569,18 +631,18 @@
             shape((nx + 2 * HALO - 2, ext, nz), F32),
             shape((nx + 2 * HALO - 2, ext, nz), F32),
             shape((nx + 4, ext, nz), F32),
-            shape((nx - 6, ny, nz), F32),
+            shape((nx - 4, ny, nz), F32),
         ),
-        in_specs=[SMEM_SPEC] + [VMEM_SPEC] * 4,
+        in_specs=[SMEM_SPEC] * 2 + [VMEM_SPEC] * 6,
         out_specs=[VMEM_SPEC] * 5,
         compiler_params=PARAMS,
         cost_estimate=pl.CostEstimate(flops=1 << 30, bytes_accessed=1 << 22, transcendentals=0),
         name="inner",
-    )(me, nutrient, target, side_a, side_b)
-    _, text, _, u2, ct, ct_all, coarse_a, coarse_b = pl.pallas_call(
+    )(me, slab, nutrient, target, side_a, side_b, field_a, field_b)
+    slab_a, slab_b, *sent = lax.optimization_barrier((slab_a, slab_b, *sent))
+    text, _, u2, ct, ct_all, coarse_a, coarse_b = pl.pallas_call(
         functools.partial(smooth_kernel, depths),
         out_shape=(
-            shape(u0.shape, F32),
             shape(text.shape, F32),
             shape(u1.shape, F32),
             shape(u2.shape, F32),
@@ -589,13 +651,14 @@
             shape((1, cx * HALO, cz), BF16),
             shape((1, cx * HALO, cz), BF16),
         ),
-        in_specs=[SMEM_SPEC] * 2 + [VMEM_SPEC] * 9,
-        out_specs=[VMEM_SPEC] * 8,
+        in_specs=[SMEM_SPEC] * 2 + [VMEM_SPEC] * 7,
+        out_specs=[VMEM_SPEC] * 7,
         scratch_shapes=[pltpu.VMEM((cx, nz // 128, ny, 128), F32)],
-        input_output_aliases={2: 0, 3: 1, 4: 2, 5: 3},
+        input_output_aliases={3: 0, 4: 1, 5: 2},
         compiler_params=PARAMS,
         name="smooth",
-    )(me, slab, u0, text, u1, u2, inside, field_a, field_b, slab_a, slab_b)
+    )(me, slab, u0, text, u1, u2, inside, slab_a, slab_b)
+    arrived = [sent[0]] + [cyclic(sent[k], "depth", k) for k in range(1, depths)]
     coarse_a = swapped(coarse_a, "depth", "a")
     coarse_b = swapped(coarse_b, "depth", "b")
     tail_a, tail_b = (

time: 43.5 us -> 38.1 us (0.88)
  starting transfers between devices: 18.6 us -> 15.7 us
  waiting for transfers between devices: 11.4 us -> 8.54 us
    ppermute x10, waiting for transfers between devices: 11.4 us -> 8.54 us  [swapped(): return lax.ppermute(x, axis, sorted(pairs))]
    ppermute x10, starting transfers between devices: 16.5 us -> 13.8 us  [swapped(): return lax.ppermute(x, axis, sorted(pairs))]
    pallas_call x1, Pallas kernels: 1.41 us -> 2.52 us  [local(): pl.pallas_call(functools.partial(inner_kernel, depths), out_shape=(shape(...]
    pallas_call x1, Pallas kernels: 1.94 us -> 1.11 us  [local(): pl.pallas_call(functools.partial(smooth_kernel, depths), out_shape=(shape...]
  transfers between devices with their start and end apart: 13 -> 13, of which waited for: 3 -> 5; matrix products, arithmetic and copies ran while one was open for 0% -> 0% of each run, Pallas kernels for 12% -> 17%
where the time goes in v3:
time: 38.1 us; the launch traced here: 38 us
  starting transfers between devices  15.7 us (41%)
  Pallas kernels  12.9 us (34%)
  waiting for transfers between devices  8.54 us (22%)
  between operations  0.73 us (2%)
    ppermute x10, starting transfers between devices, swapped(): return lax.ppermute(x, axis, sorted(pairs))  13.8 us
    ppermute x10, waiting for transfers between devices, swapped(): return lax.ppermute(x, axis, sorted(pairs))  8.54 us
    pallas_call x1, Pallas kernels, local(): pl.pallas_call(functools.partial(inner_kernel, depths), out_shape=(shape(...  2.52 us
    pallas_call x1, Pallas kernels, local(): pl.pallas_call(functools.partial(correct_kernel, depths), out_shape=(shap...  2.45 us
    pallas_call x1, Pallas kernels, local(): pl.pallas_call(functools.partial(post_kernel, depths), out_shape=shape((n...  2.07 us
    ppermute x3, starting transfers between devices, cyclic(): return lax.ppermute(x, axis, [(i, (i + by) % count) for i in range(count)])  1.97 us
    pallas_call x1, Pallas kernels, local(): pl.pallas_call(network_kernel, out_shape=tuple((shape((capacity, width),...  1.79 us
    pallas_call x1, Pallas kernels, local(): pl.pallas_call(uptake_kernel, out_shape=(shape((nx, ny, nz), F32), shape(...  1.67 us
  transfers between devices with their start and end apart: 13, of which 5 were waited for; matrix products, arithmetic and copies ran while one was open for 0% of the time, Pallas kernels for 17%

profile of v3, /device:TPU:0, one launch (start us, length us, event | category | flops | bytes accessed | tf_op | source)
XLA Modules:
  0.0 38.0 jit_solution(9006699088353685408)
XLA Ops:
  0.6 1.2 %load.1 = (f32[8,32,512]{2,1,0:T(8,128)S(1)}, s32[1,1024]{1,0:T(1,128)S(1)}, bf16[1024,128]{1,0:T(8,128)(2,1)S(1)}, bf16[1,128]{1,0:T(2,128)(2,1)S(1)}, s32[1,10...) custom-call(s32[1]{0:T(128)} %bitcast.1.slab_ref, ...), custom_call_target="tpu_custom_call" | custom-call | tf_op jit(solution)/shard_map/load/pallas_call | solution.py:569
  1.9 1.7 %uptake.1 = (f32[8,32,512]{2,1,0:T(8,128)S(1)}, f32[8,1024]{1,0:T(8,128)S(1)}, bf16[4,16,512]{2,1,0:T(8,128)(2,1)S(1)}, bf16[4,16,512]{2,1,0:T(8,128)(2,1)S(1)},...) custom-call(s32[1]{0:T(128)} %bitcast.me_ref, s32[1]{0:T(128)} %bitcast.1.slab_ref, ...), custom_call_target="tpu_custom_call" | custom-call | tf_op jit(solution)/shard_map/uptake/pallas_call | solution.py:580
  3.6 3.0 %collective-permute-start.2 = (bf16[8,16,512]{2,1,0:T(8,128)(2,1)S(1)}, bf16[8,16,512]{2,1,0:T(8,128)(2,1)S(1)}, u32[]{:S(2)}, u32[]{:S(2)}) collective-permute-start(bf16[8,16,512]{2,1,0:T(8,128)(2,1)S(1)} %get-tuple-element.64), channel_id=1, source_target_pairs={{0,4},{4,0},{8,12},{12,8},{16,20},{20,16},{24,28},{28,24},{1,5},{5... | collective-permute-start | bytes 393224 | tf_op jit(solution)/shard_map/ppermute | solution.py:51
  6.6 3.6 %collective-permute-start.3 = (bf16[8,16,512]{2,1,0:T(8,128)(2,1)S(1)}, bf16[8,16,512]{2,1,0:T(8,128)(2,1)S(1)}, u32[]{:S(2)}, u32[]{:S(2)}) collective-permute-start(bf16[8,16,512]{2,1,0:T(8,128)(2,1)S(1)} %get-tuple-element.65), channel_id=1, source_target_pairs={{0,28},{4,8},{8,4},{12,16},{16,12},{20,24},{24,20},{28,0},{1,29},{... | collective-permute-start | bytes 393224 | tf_op jit(solution)/shard_map/ppermute | solution.py:51
  10.1 0.0 collective-permute-start
  10.1 1.6 %collective-permute-start.1 = (bf16[4,16,512]{2,1,0:T(8,128)(2,1)S(1)}, bf16[4,16,512]{2,1,0:T(8,128)(2,1)S(1)}, u32[]{:S(2)}, u32[]{:S(2)}) collective-permute-start(bf16[4,16,512]{2,1,0:T(8,128)(2,1)S(1)} %get-tuple-element.63), channel_id=1, source_target_pairs={{0,3},{1,2},{2,1},{3,0},{4,7},{5,6},{6,5},{7,4},{8,11},{9,10},{10,... | collective-permute-start | bytes 196616 | tf_op jit(solution)/shard_map/ppermute | solution.py:51
  11.8 0.0 collective-permute-done.side_a
  11.8 2.1 %collective-permute-done.1.side_b = bf16[4,16,512]{2,1,0:T(8,128)(2,1)S(1)} collective-permute-done((bf16[4,16,512]{2,1,0:T(8,128)(2,1)S(1)}, bf16[4,16,512]{2,1,0:T(8,128)(2,1)S(1)}, u32[]{:S(2)}, u32[]{:S(2)}) %collective-permute-start.1) | collective-permute-done | bytes 65568 | tf_op jit(solution)/shard_map/ppermute | solution.py:51
  13.9 0.1 corner.1
  14.0 0.1 collective-permute-start.4
  14.0 1.9 %collective-permute-start.5 = (bf16[8,16,512]{2,1,0:T(8,128)(2,1)S(1)}, bf16[8,16,512]{2,1,0:T(8,128)(2,1)S(1)}, u32[]{:S(2)}, u32[]{:S(2)}) collective-permute-start(bf16[8,16,512]{2,1,0:T(8,128)(2,1)S(1)} %get-tuple-element.74), channel_id=1, source_target_pairs={{0,28},{4,8},{8,4},{12,16},{16,12},{20,24},{24,20},{28,0},{1,29},{... | collective-permute-start | bytes 393224 | tf_op jit(solution)/shard_map/ppermute | solution.py:51
  15.9 1.8 %network.1 = (bf16[512,128]{1,0:T(8,128)(2,1)S(1)}, bf16[512,128]{1,0:T(8,128)(2,1)S(1)}, bf16[512,128]{1,0:T(8,128)(2,1)S(1)}, bf16[512,128]{1,0:T(8,128)(2,1)S...) custom-call(s32[1]{0:T(128)} %bitcast.me_ref, s32[1]{0:T(128)} %bitcast.1.slab_ref, ...), custom_call_target="tpu_custom_call" | custom-call | flops 603979776 | bytes 1048576 | tf_op jit(solution)/shard_map/network/pallas_call | solution.py:615
  17.7 0.0 collective-permute-done.2.field_a
  17.7 0.0 collective-permute-done.3.field_b
  17.8 2.5 %inner.1 = (f32[16,40,512]{2,1,0:T(8,128)S(1)}, f32[14,40,512]{2,1,0:T(8,128)S(1)}, f32[14,40,512]{2,1,0:T(8,128)S(1)}, f32[12,40,512]{2,1,0:T(8,128)S(1)}, f32[4,32,512]{2,1,0:T(8,128)S(1)}) custom-call(s32[1]{0:T(128)} %bitcast.me_ref, s32[1]{0:T(128)} %bitcast.1.slab_ref, f32[8,32,512]{2,1,0:T(8,128)S(1)} %get-tuple-element.51.u_ref, ...), custom_call_target="tpu_custom_call" | custom-call | flops 1073741824 | bytes 4194304 | tf_op jit(solution)/shard_map/inner/pallas_call | solution.py:627
  20.3 0.3 collective-permute-done.4.slab_a
  20.5 2.2 %collective-permute-done.5.slab_b = bf16[8,16,512]{2,1,0:T(8,128)(2,1)S(1)} collective-permute-done((bf16[8,16,512]{2,1,0:T(8,128)(2,1)S(1)}, bf16[8,16,512]{2,1,0:T(8,128)(2,1)S(1)}, u32[]{:S(2)}, u32[]{:S(2)}) %collective-permute-start.5) | collective-permute-done | bytes 131104 | tf_op jit(solution)/shard_map/ppermute | solution.py:51
  22.7 1.1 %smooth.1 = (f32[14,40,512]{2,1,0:T(8,128)S(1)}, f32[14,40,512]{2,1,0:T(8,128)S(1)}, f32[12,40,512]{2,1,0:T(8,128)S(1)}, f32[4,16,256]{2,1,0:T(8,128)S(1)}, bf16...) custom-call(s32[1]{0:T(128)} %bitcast.me_ref, ...), custom_call_target="tpu_custom_call", output_to_operand_aliasing={{0}: (3, {}), {1}: (4, {}), {2}: (5, {})} | custom-call | tf_op jit(solution)/shard_map/smooth/pallas_call | solution.py:643
  23.8 0.1 collective-permute-start.6
  23.9 1.6 %collective-permute-start.7 = (bf16[1,16,256]{2,1,0:T(8,128)(2,1)S(1)}, bf16[1,16,256]{2,1,0:T(8,128)(2,1)S(1)}, u32[]{:S(2)}, u32[]{:S(2)}) collective-permute-start(bf16[1,16,256]{2,1,0:T(8,128)(2,1)S(1)} %get-tuple-element.90), channel_id=1, source_target_pairs={{0,3},{1,2},{2,1},{3,0},{4,7},{5,6},{6,5},{7,4},{8,11},{9,10},{10,... | collective-permute-start | bytes 24584 | tf_op jit(solution)/shard_map/ppermute | solution.py:51
  25.5 0.1 collective-permute-start.10
  25.6 0.5 %collective-permute-start.11 = (bf16[512,128]{1,0:T(8,128)(2,1)S(1)}, bf16[512,128]{1,0:T(8,128)(2,1)S(1)}, u32[]{:S(2)}, u32[]{:S(2)}) collective-permute-start(bf16[512,128]{1,0:T(8,128)(2,1)S(1)} %get-tuple-element.98), channel_id=1, source_target_pairs={{0,2},{1,3},{2,0},{3,1},{4,6},{5,7},{6,4},{7,5},{8,10},{9,11},{10,... | collective-permute-start | bytes 393224 | tf_op jit(solution)/shard_map/ppermute | solution.py:39
  26.1 1.4 %collective-permute-start.12 = (bf16[512,128]{1,0:T(8,128)(2,1)S(1)}, bf16[512,128]{1,0:T(8,128)(2,1)S(1)}, u32[]{:S(2)}, u32[]{:S(2)}) collective-permute-start(bf16[512,128]{1,0:T(8,128)(2,1)S(1)} %get-tuple-element.99), channel_id=1, source_target_pairs={{0,3},{1,0},{2,1},{3,2},{4,7},{5,4},{6,5},{7,6},{8,11},{9,8},{10,9... | collective-permute-start | bytes 393224 | tf_op jit(solution)/shard_map/ppermute | solution.py:39
  27.5 0.0 collective-permute-done.6.side_a
  27.5 0.0 collective-permute-done.7.side_b
  27.5 1.9 %collective-permute-start.9 = (bf16[10,16,256]{2,1,0:T(8,128)(2,1)S(1)}, bf16[10,16,256]{2,1,0:T(8,128)(2,1)S(1)}, u32[]{:S(2)}, u32[]{:S(2)}) collective-permute-start(bf16[10,16,256]{2,1,0:T(8,128)(2,1)S(1)} %get-tuple-element.100), channel_id=1, source_target_pairs={{0,28},{4,8},{8,4},{12,16},{16,12},{20,24},{24,20},{28,0},{1,29},{... | collective-permute-start | bytes 245768 | tf_op jit(solution)/shard_map/ppermute | solution.py:51
  29.4 0.0 collective-permute-start.8
  29.4 2.1 %post.1.base_ref = f32[8,32,512]{2,1,0:T(8,128)S(1)} custom-call(s32[1]{0:T(128)} %bitcast.me_ref, f32[12,40,512]{2,1,0:T(8,128)S(1)} %get-tuple-element.94.u2_ref, f32[14,40,512]{2,1,0:T(8,128)S(1)} %get-tuple-element.95.text_ref), custom_call_target="tpu_custom_call" | custom-call | flops 1073741824 | bytes 4194304 | tf_op jit(solution)/shard_map/post/pallas_call | solution.py:668
  31.5 3.3 %collective-permute-done.9.slab_b = bf16[10,16,256]{2,1,0:T(8,128)(2,1)S(1)} collective-permute-done((bf16[10,16,256]{2,1,0:T(8,128)(2,1)S(1)}, bf16[10,16,256]{2,1,0:T(8,128)(2,1)S(1)}, u32[]{:S(2)}, u32[]{:S(2)}) %collective-permute-start.9) | collective-permute-done | bytes 81952 | tf_op jit(solution)/shard_map/ppermute | solution.py:51
  34.8 0.7 %collective-permute-done.8.slab_a = bf16[10,16,256]{2,1,0:T(8,128)(2,1)S(1)} collective-permute-done((bf16[10,16,256]{2,1,0:T(8,128)(2,1)S(1)}, bf16[10,16,256]{2,1,0:T(8,128)(2,1)S(1)}, u32[]{:S(2)}, u32[]{:S(2)}) %collective-permute-start.8) | collective-permute-done | bytes 81952 | tf_op jit(solution)/shard_map/ppermute | solution.py:51
  35.5 0.0 collective-permute-done.10.rest_1_
  35.5 0.0 collective-permute-done.11.rest_2_
  35.5 0.0 collective-permute-done.12.rest_3_
  35.5 2.4 %correct.1 = (f32[8,32,512]{2,1,0:T(8,128)}, bf16[2304,128]{1,0:T(8,128)(2,1)}) custom-call(s32[1]{0:T(128)} %bitcast.me_ref, s32[1]{0:T(128)} %bitcast.1.slab_ref, f32[4,16,256]{2,1,0:T(8,128)S(1)} %get-tuple-element.88.ct_ref, bf16[1,16,256]{2,1,0:T(8,128)(2,1)S(1)} %collective-permute-done.6.side_a, ...), custom_call_target="tpu_custom_call" | custom-call | tf_op jit(solution)/shard_map/correct/pallas_call | solution.py:678
  (1 shorter events, 0.0 us)
Async XLA Ops:
  3.6 14.2 %collective-permute-start.2 = (bf16[8,16,512]{2,1,0:T(8,128)(2,1)S(1)}, bf16[8,16,512]{2,1,0:T(8,128)(2,1)S(1)}, u32[]{:S(2)}, u32[]{:S(2)}) collective-permute-start(bf16[8,16,512]{2,1,0:T(8,128)(2,1)S(1)} %get-tuple-element.64), channel_id=1, source_target_pairs={{0,4},{4,0},{8,12},{12,8},{16,20},{20,16},{24,28},{28,24},{1,5},{5... | collective-permute-start | bytes 393224 | tf_op jit(solution)/shard_map/ppermute | solution.py:51
  6.6 11.2 %collective-permute-start.3 = (bf16[8,16,512]{2,1,0:T(8,128)(2,1)S(1)}, bf16[8,16,512]{2,1,0:T(8,128)(2,1)S(1)}, u32[]{:S(2)}, u32[]{:S(2)}) collective-permute-start(bf16[8,16,512]{2,1,0:T(8,128)(2,1)S(1)} %get-tuple-element.65), channel_id=1, source_target_pairs={{0,28},{4,8},{8,4},{12,16},{16,12},{20,24},{24,20},{28,0},{1,29},{... | collective-permute-start | bytes 393224 | tf_op jit(solution)/shard_map/ppermute | solution.py:51
  10.1 1.6 %collective-permute-start = (bf16[4,16,512]{2,1,0:T(8,128)(2,1)S(1)}, bf16[4,16,512]{2,1,0:T(8,128)(2,1)S(1)}, u32[]{:S(2)}, u32[]{:S(2)}) collective-permute-start(bf16[4,16,512]{2,1,0:T(8,128)(2,1)S(1)} %get-tuple-element.62), channel_id=1, source_target_pairs={{0,1},{1,0},{2,3},{3,2},{4,5},{5,4},{6,7},{7,6},{8,9},{9,8},{10,11... | collective-permute-start | bytes 196616 | tf_op jit(solution)/shard_map/ppermute | solution.py:51
  10.1 3.7 %collective-permute-start.1 = (bf16[4,16,512]{2,1,0:T(8,128)(2,1)S(1)}, bf16[4,16,512]{2,1,0:T(8,128)(2,1)S(1)}, u32[]{:S(2)}, u32[]{:S(2)}) collective-permute-start(bf16[4,16,512]{2,1,0:T(8,128)(2,1)S(1)} %get-tuple-element.63), channel_id=1, source_target_pairs={{0,3},{1,2},{2,1},{3,0},{4,7},{5,6},{6,5},{7,4},{8,11},{9,10},{10,... | collective-permute-start | bytes 196616 | tf_op jit(solution)/shard_map/ppermute | solution.py:51
  14.0 6.6 %collective-permute-start.4 = (bf16[8,16,512]{2,1,0:T(8,128)(2,1)S(1)}, bf16[8,16,512]{2,1,0:T(8,128)(2,1)S(1)}, u32[]{:S(2)}, u32[]{:S(2)}) collective-permute-start(bf16[8,16,512]{2,1,0:T(8,128)(2,1)S(1)} %get-tuple-element.73), channel_id=1, source_target_pairs={{0,4},{4,0},{8,12},{12,8},{16,20},{20,16},{24,28},{28,24},{1,5},{5... | collective-permute-start | bytes 393224 | tf_op jit(solution)/shard_map/ppermute | solution.py:51
  14.0 8.7 %collective-permute-start.5 = (bf16[8,16,512]{2,1,0:T(8,128)(2,1)S(1)}, bf16[8,16,512]{2,1,0:T(8,128)(2,1)S(1)}, u32[]{:S(2)}, u32[]{:S(2)}) collective-permute-start(bf16[8,16,512]{2,1,0:T(8,128)(2,1)S(1)} %get-tuple-element.74), channel_id=1, source_target_pairs={{0,28},{4,8},{8,4},{12,16},{16,12},{20,24},{24,20},{28,0},{1,29},{... | collective-permute-start | bytes 393224 | tf_op jit(solution)/shard_map/ppermute | solution.py:51
  23.8 3.7 %collective-permute-start.6 = (bf16[1,16,256]{2,1,0:T(8,128)(2,1)S(1)}, bf16[1,16,256]{2,1,0:T(8,128)(2,1)S(1)}, u32[]{:S(2)}, u32[]{:S(2)}) collective-permute-start(bf16[1,16,256]{2,1,0:T(8,128)(2,1)S(1)} %get-tuple-element.89), channel_id=1, source_target_pairs={{0,1},{1,0},{2,3},{3,2},{4,5},{5,4},{6,7},{7,6},{8,9},{9,8},{10,11... | collective-permute-start | bytes 24584 | tf_op jit(solution)/shard_map/ppermute | solution.py:51
  23.9 3.6 %collective-permute-start.7 = (bf16[1,16,256]{2,1,0:T(8,128)(2,1)S(1)}, bf16[1,16,256]{2,1,0:T(8,128)(2,1)S(1)}, u32[]{:S(2)}, u32[]{:S(2)}) collective-permute-start(bf16[1,16,256]{2,1,0:T(8,128)(2,1)S(1)} %get-tuple-element.90), channel_id=1, source_target_pairs={{0,3},{1,2},{2,1},{3,0},{4,7},{5,6},{6,5},{7,4},{8,11},{9,10},{10,... | collective-permute-start | bytes 24584 | tf_op jit(solution)/shard_map/ppermute | solution.py:51
  25.5 10.0 %collective-permute-start.10 = (bf16[512,128]{1,0:T(8,128)(2,1)S(1)}, bf16[512,128]{1,0:T(8,128)(2,1)S(1)}, u32[]{:S(2)}, u32[]{:S(2)}) collective-permute-start(bf16[512,128]{1,0:T(8,128)(2,1)S(1)} %get-tuple-element.97), channel_id=1, source_target_pairs={{0,1},{1,2},{2,3},{3,0},{4,5},{5,6},{6,7},{7,4},{8,9},{9,10},{10,1... | collective-permute-start | bytes 393224 | tf_op jit(solution)/shard_map/ppermute | solution.py:39
  25.6 9.9 %collective-permute-start.11 = (bf16[512,128]{1,0:T(8,128)(2,1)S(1)}, bf16[512,128]{1,0:T(8,128)(2,1)S(1)}, u32[]{:S(2)}, u32[]{:S(2)}) collective-permute-start(bf16[512,128]{1,0:T(8,128)(2,1)S(1)} %get-tuple-element.98), channel_id=1, source_target_pairs={{0,2},{1,3},{2,0},{3,1},{4,6},{5,7},{6,4},{7,5},{8,10},{9,11},{10,... | collective-permute-start | bytes 393224 | tf_op jit(solution)/shard_map/ppermute | solution.py:39
  26.1 9.4 %collective-permute-start.12 = (bf16[512,128]{1,0:T(8,128)(2,1)S(1)}, bf16[512,128]{1,0:T(8,128)(2,1)S(1)}, u32[]{:S(2)}, u32[]{:S(2)}) collective-permute-start(bf16[512,128]{1,0:T(8,128)(2,1)S(1)} %get-tuple-element.99), channel_id=1, source_target_pairs={{0,3},{1,0},{2,1},{3,2},{4,7},{5,4},{6,5},{7,6},{8,11},{9,8},{10,9... | collective-permute-start | bytes 393224 | tf_op jit(solution)/shard_map/ppermute | solution.py:39
  27.5 7.3 %collective-permute-start.9 = (bf16[10,16,256]{2,1,0:T(8,128)(2,1)S(1)}, bf16[10,16,256]{2,1,0:T(8,128)(2,1)S(1)}, u32[]{:S(2)}, u32[]{:S(2)}) collective-permute-start(bf16[10,16,256]{2,1,0:T(8,128)(2,1)S(1)} %get-tuple-element.100), channel_id=1, source_target_pairs={{0,28},{4,8},{8,4},{12,16},{16,12},{20,24},{24,20},{28,0},{1,29},{... | collective-permute-start | bytes 245768 | tf_op jit(solution)/shard_map/ppermute | solution.py:51
  29.4 6.1 %collective-permute-start.8 = (bf16[10,16,256]{2,1,0:T(8,128)(2,1)S(1)}, bf16[10,16,256]{2,1,0:T(8,128)(2,1)S(1)}, u32[]{:S(2)}, u32[]{:S(2)}) collective-permute-start(bf16[10,16,256]{2,1,0:T(8,128)(2,1)S(1)} %get-tuple-element.101), channel_id=1, source_target_pairs={{0,4},{4,0},{8,12},{12,8},{16,20},{20,16},{24,28},{28,24},{1,5},{5... | collective-permute-start | bytes 245768 | tf_op jit(solution)/shard_map/ppermute | solution.py:51

commit v4 on v3

--- a/solution.py
+++ b/solution.py
@@ -79,8 +79,8 @@
 
 
 def uptake_kernel(
-    me_ref, slab_ref, u_ref, cell_ref, death_ref, divide_ref, species_ref, weight_ref,
-    t_ref, sensed_ref, depth_a, depth_b, slab_a, slab_b,
+    me_ref, u_ref, cell_ref, death_ref, divide_ref, species_ref, weight_ref,
+    t_ref, sensed_ref, depth_a, depth_b, list_ref,
 ):
     nx, ny, nz = u_ref.shape
     agents = species_ref.shape[0]
@@ -117,13 +117,11 @@
         high = jnp.concatenate(parts[4:], axis=0)
         depth_a[pair] = jnp.where(even, high, low).astype(BF16)
         depth_b[pair] = jnp.where(even, low, high).astype(BF16)
-    half = ny // 16
-    count = HALO - 1
-    even = is_even(slab_ref[0])
-    for ref, front in ((slab_a, even), (slab_b, jnp.logical_not(even))):
-        start = jnp.where(front, nx - count, 0)
-        for k in range(count):
-            ref[k * half : (k + 1) * half] = t_ref[start + k].astype(BF16).reshape(half, 16, nz)
+    half_z = cell_z // 2
+    values = (cell_row.astype(F32), half_z.astype(F32), (cell_z - 2 * half_z).astype(F32), up_high)
+    list_ref[...] = jnp.concatenate(
+        [x[:, i * nz : (i + 1) * nz] for x in values for i in range(agents // nz)], axis=0
+    )
 
 
 def network_kernel(
@@ -246,10 +244,9 @@
     )
 
 
-def corner_kernel(me_ref, slab_ref, side_a, side_b, in_a, in_b, slab_a, slab_b):
+def corner_kernel(me_ref, slab_ref, side_a, side_b, list_ref, slab_a, slab_b):
     layers = 2 * side_a.shape[0]
     nz = side_a.shape[2]
-    own = slab_a.shape[0] - 2
     even = is_even(me_ref[0])
     slab_even = is_even(slab_ref[0])
 
@@ -257,23 +254,26 @@
         at = 2 * HALO * (plane % 2)
         return side[plane // 2].astype(F32)[at : at + 2 * HALO]
 
-    for index, (side, high) in enumerate(((side_a, even), (side_b, jnp.logical_not(even)))):
-        for ref, front in ((slab_a, slab_even), (slab_b, jnp.logical_not(slab_even))):
-            fields, targets = [], []
+    for ref, front in ((slab_a, slab_even), (slab_b, jnp.logical_not(slab_even))):
+        parts = []
+        for side, high in ((side_a, even), (side_b, jnp.logical_not(even))):
+            targets = []
             for i in range(1, HALO):
                 x = jnp.where(front, layer(side, layers - i), layer(side, i - 1))
-                fields.append(jnp.where(high, x[: HALO - i], x[i:HALO]))
+                parts.append(jnp.where(high, x[: HALO - i], x[i:HALO]))
                 if i < HALO - 1:
                     targets.append(
                         jnp.where(high, x[HALO : 2 * HALO - 1 - i], x[HALO + 1 + i :])
                     )
-            rows = jnp.concatenate(fields + targets, axis=0)
-            rest = jnp.zeros((16 - rows.shape[0], nz), F32)
-            ref[own + index] = jnp.concatenate([rows, rest], axis=0).astype(BF16)
+            parts += targets
+        parts.append(list_ref[...])
+        used = sum(part.shape[0] for part in parts)
+        total = ref.shape[0] * ref.shape[1]
+        parts.append(jnp.zeros((total - used, nz), F32))
+        ref[...] = jnp.concatenate(parts, axis=0).astype(BF16).reshape(ref.shape)
 
 
 def corner_rows(block_a, block_b, even, mask):
-    block_a, block_b = block_a.astype(F32), block_b.astype(F32)
     high = jnp.where(even, block_a, block_b)
     low = jnp.where(even, block_b, block_a)
     nz = high.shape[1]
@@ -343,26 +343,37 @@
 
 
 def smooth_kernel(
-    depths, me_ref, slab_ref, u0, text_in, u1_in, u2_in, inside, slab_a, slab_b,
-    text_ref, u1, u2_ref, coarse_ref, coarse_all_ref, coarse_a, coarse_b, paired,
+    depths, agents, me_ref, slab_ref, u0, text_in, u1_in, u2_in, inside, slab_a, slab_b,
+    text_ref, u1, u2_ref, coarse_ref, coarse_all_ref, coarse_a, coarse_b, paired, foreign,
 ):
     nx = u0.shape[0] - 2 * HALO
     ny, nz = u0.shape[1] - 2 * HALO, u0.shape[2]
     mask = edge_mask(me_ref[0], depths, HALO)
-    half = ny // 16
-    own = (HALO - 1) * half
     even = is_even(me_ref[0])
     slab_even = is_even(slab_ref[0])
+    near = HALO - 1
+    corner = HALO * near // 2 + near * (near - 1) // 2
     row = iota((8, 1), 0)
     first, last = (row == 0).astype(F32), (row == 7).astype(F32)
     for ref, after in ((slab_a, slab_even), (slab_b, jnp.logical_not(slab_even))):
-        fields, targets = corner_rows(ref[own], ref[own + 1], even, mask)
+        message = ref[...].astype(F32).reshape(-1, nz)
+        fields, targets = corner_rows(message[:corner], message[corner : 2 * corner], even, mask)
         sign = jnp.where(after, 1, -1)
         edge = jnp.where(after, nx - 1, 0)
+        lines = agents // nz
+        cell_row, half_z, bit, uptake = (
+            jnp.concatenate([message[at + i : at + i + 1] for i in range(lines)], axis=1)
+            for at in range(2 * corner, 2 * corner + 4 * lines, lines)
+        )
+        cell_row = cell_row.astype(jnp.int32) - jnp.where(after, 0, (nx - near) * ny)
+        cell_z = (2.0 * half_z + bit).astype(jnp.int32)
+        one_z = (iota((nz, agents), 0) == cell_z).astype(F32).astype(BF16)
+        taken = jnp.where(iota((near * ny, agents), 0) == cell_row, uptake, 0.0).astype(BF16)
+        foreign[...] = dot(taken, one_z, 1, 1)
         for i in range(1, HALO):
             p = edge + sign * i
             index = jnp.where(after, i - 1, HALO - 1 - i)
-            t = ref[pl.ds(index * half, half)].astype(F32).reshape(ny, nz)
+            t = SCREENING * u0[p + 4, :ny] - foreign[pl.ds(index * ny, ny)]
             text_ref[p + 3, :ny] = t
             text_ref[p + 3, ny:] = targets[i - 1]
             x = fields[i - 1]
@@ -562,6 +573,8 @@
     cells, death, divide = (x.reshape(1, agents) for x in (agent_cell, death_flag, divide_flag))
     move, route = slab_move.reshape(1, agents), depth_route.reshape(1, agents)
     half = ny // 16
+    if agents % nz or nx * ny > 256 or nz > 512:
+        raise ValueError("list digits")
     arguments = (
         nutrient, cells, species, uptake_weight.reshape(1, width), death, divide,
         move, route, net_weight, sensing.reshape(1, width),
@@ -577,21 +590,20 @@
         name="load",
     )(slab, *(pltpu.with_memory_space_constraint(x, pltpu.HBM) for x in arguments))
     nutrient, cells, species, weight, death, divide, move, route, net_weight, sensing = loaded[:-2]
-    target, sensed, depth_a, depth_b, slab_a, slab_b = pl.pallas_call(
+    target, sensed, depth_a, depth_b, agent_list = pl.pallas_call(
         uptake_kernel,
         out_shape=(
             shape((nx, ny, nz), F32),
             shape((8, agents), F32),
             shape((nx // 2, 16, nz), BF16),
             shape((nx // 2, 16, nz), BF16),
-            shape(((HALO - 1) * half + 2, 16, nz), BF16),
-            shape(((HALO - 1) * half + 2, 16, nz), BF16),
+            shape((4 * agents // nz, nz), F32),
         ),
-        in_specs=[SMEM_SPEC] * 2 + [VMEM_SPEC] * 6,
-        out_specs=[VMEM_SPEC] * 6,
+        in_specs=[SMEM_SPEC] + [VMEM_SPEC] * 6,
+        out_specs=[VMEM_SPEC] * 5,
         compiler_params=PARAMS,
         name="uptake",
-    )(me, slab, nutrient, cells, death, divide, species, weight)
+    )(me, nutrient, cells, death, divide, species, weight)
     field_a, field_b, depth_a, depth_b = lax.optimization_barrier(
         (loaded[-2], loaded[-1], depth_a, depth_b)
     )
@@ -599,15 +611,16 @@
     side_b = swapped(depth_b, "depth", "b")
     field_a = swapped(field_a, "slab", "a")
     field_b = swapped(field_b, "slab", "b")
+    rows = 2 * (HALO - 1) ** 2 + agent_list.shape[0]
+    rows = -(-rows // 16) * 16
     slab_a, slab_b = pl.pallas_call(
         corner_kernel,
-        out_shape=tuple(shape(x.shape, BF16) for x in (slab_a, slab_b)),
-        in_specs=[SMEM_SPEC] * 2 + [VMEM_SPEC] * 4,
+        out_shape=tuple(shape((rows // 16, 16, nz), BF16) for _ in range(2)),
+        in_specs=[SMEM_SPEC] * 2 + [VMEM_SPEC] * 3,
         out_specs=[VMEM_SPEC] * 2,
-        input_output_aliases={4: 0, 5: 1},
         compiler_params=PARAMS,
         name="corner",
-    )(me, slab, side_a, side_b, slab_a, slab_b)
+    )(me, slab, side_a, side_b, agent_list)
     slab_a = swapped(slab_a, "slab", "a")
     slab_b = swapped(slab_b, "slab", "b")
     cx, cy, cz = nx // 2, ny // 2, nz // 2
@@ -619,9 +632,7 @@
         in_specs=[SMEM_SPEC] * 2 + [VMEM_SPEC] * 7,
         out_specs=[VMEM_SPEC] * (depths + 2),
         compiler_params=PARAMS,
-        cost_estimate=pl.CostEstimate(
-            flops=2 * 2304 * agents * width, bytes_accessed=1 << 20, transcendentals=agents * width
-        ),
+        cost_estimate=pl.CostEstimate(flops=1 << 31, bytes_accessed=1<<20, transcendentals=0),
         name="network",
     )(me, slab, species, sensed, death, move, route, net_weight, sensing)
     u0, text, u1, u2, inside = pl.pallas_call(
@@ -636,12 +647,12 @@
         in_specs=[SMEM_SPEC] * 2 + [VMEM_SPEC] * 6,
         out_specs=[VMEM_SPEC] * 5,
         compiler_params=PARAMS,
-        cost_estimate=pl.CostEstimate(flops=1 << 30, bytes_accessed=1 << 22, transcendentals=0),
+        cost_estimate=pl.CostEstimate(flops=1 << 20, bytes_accessed=1<<20, transcendentals=0),
         name="inner",
     )(me, slab, nutrient, target, side_a, side_b, field_a, field_b)
-    slab_a, slab_b, *sent = lax.optimization_barrier((slab_a, slab_b, *sent))
+    slab_a, slab_b, inside, *sent = lax.optimization_barrier((slab_a, slab_b, inside, *sent))
     text, _, u2, ct, ct_all, coarse_a, coarse_b = pl.pallas_call(
-        functools.partial(smooth_kernel, depths),
+        functools.partial(smooth_kernel, depths, agents),
         out_shape=(
             shape(text.shape, F32),
             shape(u1.shape, F32),
@@ -653,7 +664,10 @@
         ),
         in_specs=[SMEM_SPEC] * 2 + [VMEM_SPEC] * 7,
         out_specs=[VMEM_SPEC] * 7,
-        scratch_shapes=[pltpu.VMEM((cx, nz // 128, ny, 128), F32)],
+        scratch_shapes=[
+            pltpu.VMEM((cx, nz // 128, ny, 128), F32),
+            pltpu.VMEM(((HALO - 1) * ny, nz), F32),
+        ],
         input_output_aliases={3: 0, 4: 1, 5: 2},
         compiler_params=PARAMS,
         name="smooth",

time: 38.1 us -> 36 us (0.945)
  waiting for transfers between devices: 8.54 us -> 3.41 us
  starting transfers between devices: 15.7 us -> 17.9 us
  Pallas kernels: 12.9 us -> 13.7 us
    ppermute x10, waiting for transfers between devices: 8.54 us -> 3.4 us  [swapped(): return lax.ppermute(x, axis, sorted(pairs))]
    ppermute x10, starting transfers between devices: 13.8 us -> 15.7 us  [swapped(): return lax.ppermute(x, axis, sorted(pairs))]
    pallas_call x2, Pallas kernels: 1.18 us -> 2.05 us  [the longest x1 1.98 us: local(): pl.pallas_call(functools.partial(smooth_kernel, depths, agents), out_shap...]
  transfers between devices with their start and end apart: 13 -> 13, of which waited for: 5 -> 3; matrix products, arithmetic and copies ran while one was open for 0% -> 0% of each run, Pallas kernels for 17% -> 18%
where the time goes in v4:
time: 36 us; the launch traced here: 35.8 us
  starting transfers between devices  17.9 us (50%)
  Pallas kernels  13.7 us (38%)
  waiting for transfers between devices  3.41 us (9%)
  between operations  0.74 us (2%)
    ppermute x10, starting transfers between devices, swapped(): return lax.ppermute(x, axis, sorted(pairs))  15.7 us
    ppermute x10, waiting for transfers between devices, swapped(): return lax.ppermute(x, axis, sorted(pairs))  3.4 us
    pallas_call x1, Pallas kernels, local(): pl.pallas_call(functools.partial(inner_kernel, depths), out_shape=(shape(...  2.51 us
    pallas_call x1, Pallas kernels, local(): pl.pallas_call(functools.partial(correct_kernel, depths), out_shape=(shap...  2.45 us
    ppermute x3, starting transfers between devices, cyclic(): return lax.ppermute(x, axis, [(i, (i + by) % count) for i in range(count)])  2.18 us
    pallas_call x1, Pallas kernels, local(): pl.pallas_call(functools.partial(post_kernel, depths), out_shape=shape((n...  2.08 us
    pallas_call x1, Pallas kernels, local(): pl.pallas_call(functools.partial(smooth_kernel, depths, agents), out_shap...  1.98 us
    pallas_call x1, Pallas kernels, local(): pl.pallas_call(network_kernel, out_shape=tuple((shape((capacity, width),...  1.79 us
  transfers between devices with their start and end apart: 13, of which 3 were waited for; matrix products, arithmetic and copies ran while one was open for 0% of the time, Pallas kernels for 18%

profile of v4, /device:TPU:0, one launch (start us, length us, event | category | flops | bytes accessed | tf_op | source)
XLA Modules:
  0.0 35.8 jit_solution(3858990171102628720)
XLA Ops:
  0.6 1.2 %load.1 = (f32[8,32,512]{2,1,0:T(8,128)S(1)}, s32[1,1024]{1,0:T(1,128)S(1)}, bf16[1024,128]{1,0:T(8,128)(2,1)S(1)}, bf16[1,128]{1,0:T(2,128)(2,1)S(1)}, s32[1,10...) custom-call(s32[1]{0:T(128)} %bitcast.1.slab_ref, ...), custom_call_target="tpu_custom_call" | custom-call | tf_op jit(solution)/shard_map/load/pallas_call | solution.py:582
  1.9 1.6 %uptake.1 = (f32[8,32,512]{2,1,0:T(8,128)S(1)}, f32[8,1024]{1,0:T(8,128)S(1)}, bf16[4,16,512]{2,1,0:T(8,128)(2,1)S(1)}, bf16[4,16,512]{2,1,0:T(8,128)(2,1)S(1)}, f32[8,512]{1,0:T(8,128)S(1)}) custom-call(s32[1]{0:T(128)} %bitcast.me_ref, f32[8,32,512]{2,1,0:T(8,128)S(1)} %get-tuple-element.51.u_ref, s32[1,1024]{1,0:T(1,128)S(1)} %get-tuple-element.52.cell_ref, ...), custom_call_target="tpu_custom_call" | custom-call | tf_op jit(solution)/shard_map/uptake/pallas_call | solution.py:593
  3.5 0.5 %collective-permute-start = (bf16[4,16,512]{2,1,0:T(8,128)(2,1)S(1)}, bf16[4,16,512]{2,1,0:T(8,128)(2,1)S(1)}, u32[]{:S(2)}, u32[]{:S(2)}) collective-permute-start(bf16[4,16,512]{2,1,0:T(8,128)(2,1)S(1)} %get-tuple-element.62), channel_id=1, source_target_pairs={{0,1},{1,0},{2,3},{3,2},{4,5},{5,4},{6,7},{7,6},{8,9},{9,8},{10,11... | collective-permute-start | bytes 196616 | tf_op jit(solution)/shard_map/ppermute | solution.py:51
  4.0 2.6 %collective-permute-start.1 = (bf16[4,16,512]{2,1,0:T(8,128)(2,1)S(1)}, bf16[4,16,512]{2,1,0:T(8,128)(2,1)S(1)}, u32[]{:S(2)}, u32[]{:S(2)}) collective-permute-start(bf16[4,16,512]{2,1,0:T(8,128)(2,1)S(1)} %get-tuple-element.63), channel_id=1, source_target_pairs={{0,3},{1,2},{2,1},{3,0},{4,7},{5,6},{6,5},{7,4},{8,11},{9,10},{10,... | collective-permute-start | bytes 196616 | tf_op jit(solution)/shard_map/ppermute | solution.py:51
  6.7 1.5 %collective-permute-start.2 = (bf16[8,16,512]{2,1,0:T(8,128)(2,1)S(1)}, bf16[8,16,512]{2,1,0:T(8,128)(2,1)S(1)}, u32[]{:S(2)}, u32[]{:S(2)}) collective-permute-start(bf16[8,16,512]{2,1,0:T(8,128)(2,1)S(1)} %get-tuple-element.64), channel_id=1, source_target_pairs={{0,4},{4,0},{8,12},{12,8},{16,20},{20,16},{24,28},{28,24},{1,5},{5... | collective-permute-start | bytes 393224 | tf_op jit(solution)/shard_map/ppermute | solution.py:51
  8.2 3.6 %collective-permute-start.3 = (bf16[8,16,512]{2,1,0:T(8,128)(2,1)S(1)}, bf16[8,16,512]{2,1,0:T(8,128)(2,1)S(1)}, u32[]{:S(2)}, u32[]{:S(2)}) collective-permute-start(bf16[8,16,512]{2,1,0:T(8,128)(2,1)S(1)} %get-tuple-element.65), channel_id=1, source_target_pairs={{0,28},{4,8},{8,4},{12,16},{16,12},{20,24},{24,20},{28,0},{1,29},{... | collective-permute-start | bytes 393224 | tf_op jit(solution)/shard_map/ppermute | solution.py:51
  11.7 0.0 collective-permute-done.side_a
  11.7 0.0 collective-permute-done.1.side_b
  11.7 0.1 corner.1
  11.8 0.1 collective-permute-start.4
  11.9 2.3 %collective-permute-start.5 = (bf16[2,16,512]{2,1,0:T(8,128)(2,1)S(1)}, bf16[2,16,512]{2,1,0:T(8,128)(2,1)S(1)}, u32[]{:S(2)}, u32[]{:S(2)}) collective-permute-start(bf16[2,16,512]{2,1,0:T(8,128)(2,1)S(1)} %get-tuple-element.72), channel_id=1, source_target_pairs={{0,28},{4,8},{8,4},{12,16},{16,12},{20,24},{24,20},{28,0},{1,29},{... | collective-permute-start | bytes 98312 | tf_op jit(solution)/shard_map/ppermute | solution.py:51
  14.1 1.8 %network.1 = (bf16[512,128]{1,0:T(8,128)(2,1)S(1)}, bf16[512,128]{1,0:T(8,128)(2,1)S(1)}, bf16[512,128]{1,0:T(8,128)(2,1)S(1)}, bf16[512,128]{1,0:T(8,128)(2,1)S...) custom-call(s32[1]{0:T(128)} %bitcast.me_ref, s32[1]{0:T(128)} %bitcast.1.slab_ref, ...), custom_call_target="tpu_custom_call" | custom-call | flops 2147483648 | bytes 1048576 | tf_op jit(solution)/shard_map/network/pallas_call | solution.py:628
  15.9 0.0 collective-permute-done.2.field_a
  16.0 0.2 collective-permute-done.3.field_b
  16.1 2.5 %inner.1 = (f32[16,40,512]{2,1,0:T(8,128)S(1)}, f32[14,40,512]{2,1,0:T(8,128)S(1)}, f32[14,40,512]{2,1,0:T(8,128)S(1)}, f32[12,40,512]{2,1,0:T(8,128)S(1)}, f32[4,32,512]{2,1,0:T(8,128)S(1)}) custom-call(s32[1]{0:T(128)} %bitcast.me_ref, s32[1]{0:T(128)} %bitcast.1.slab_ref, f32[8,32,512]{2,1,0:T(8,128)S(1)} %get-tuple-element.51.u_ref, ...), custom_call_target="tpu_custom_call" | custom-call | flops 1048576 | bytes 1048576 | tf_op jit(solution)/shard_map/inner/pallas_call | solution.py:638
  18.7 0.0 collective-permute-done.4.slab_a
  18.7 0.0 collective-permute-done.5.slab_b
  18.7 2.0 %smooth.1 = (f32[14,40,512]{2,1,0:T(8,128)S(1)}, f32[14,40,512]{2,1,0:T(8,128)S(1)}, f32[12,40,512]{2,1,0:T(8,128)S(1)}, f32[4,16,256]{2,1,0:T(8,128)S(1)}, bf16...) custom-call(s32[1]{0:T(128)} %bitcast.me_ref, ...), custom_call_target="tpu_custom_call", output_to_operand_aliasing={{0}: (3, {}), {1}: (4, {}), {2}: (5, {})} | custom-call | tf_op jit(solution)/shard_map/smooth/pallas_call | solution.py:654
  20.7 0.1 collective-permute-start.6
  20.7 1.4 %collective-permute-start.7 = (bf16[1,16,256]{2,1,0:T(8,128)(2,1)S(1)}, bf16[1,16,256]{2,1,0:T(8,128)(2,1)S(1)}, u32[]{:S(2)}, u32[]{:S(2)}) collective-permute-start(bf16[1,16,256]{2,1,0:T(8,128)(2,1)S(1)} %get-tuple-element.90), channel_id=1, source_target_pairs={{0,3},{1,2},{2,1},{3,0},{4,7},{5,6},{6,5},{7,4},{8,11},{9,10},{10,... | collective-permute-start | bytes 24584 | tf_op jit(solution)/shard_map/ppermute | solution.py:51
  22.2 0.2 collective-permute-start.10
  22.3 0.6 %collective-permute-start.11 = (bf16[512,128]{1,0:T(8,128)(2,1)S(1)}, bf16[512,128]{1,0:T(8,128)(2,1)S(1)}, u32[]{:S(2)}, u32[]{:S(2)}) collective-permute-start(bf16[512,128]{1,0:T(8,128)(2,1)S(1)} %get-tuple-element.98), channel_id=1, source_target_pairs={{0,2},{1,3},{2,0},{3,1},{4,6},{5,7},{6,4},{7,5},{8,10},{9,11},{10,... | collective-permute-start | bytes 393224 | tf_op jit(solution)/shard_map/ppermute | solution.py:39
  23.0 1.4 %collective-permute-start.12 = (bf16[512,128]{1,0:T(8,128)(2,1)S(1)}, bf16[512,128]{1,0:T(8,128)(2,1)S(1)}, u32[]{:S(2)}, u32[]{:S(2)}) collective-permute-start(bf16[512,128]{1,0:T(8,128)(2,1)S(1)} %get-tuple-element.99), channel_id=1, source_target_pairs={{0,3},{1,0},{2,1},{3,2},{4,7},{5,4},{6,5},{7,6},{8,11},{9,8},{10,9... | collective-permute-start | bytes 393224 | tf_op jit(solution)/shard_map/ppermute | solution.py:39
  24.4 0.0 collective-permute-done.6.side_a
  24.4 0.0 collective-permute-done.7.side_b
  24.4 3.7 %collective-permute-start.9 = (bf16[10,16,256]{2,1,0:T(8,128)(2,1)S(1)}, bf16[10,16,256]{2,1,0:T(8,128)(2,1)S(1)}, u32[]{:S(2)}, u32[]{:S(2)}) collective-permute-start(bf16[10,16,256]{2,1,0:T(8,128)(2,1)S(1)} %get-tuple-element.100), channel_id=1, source_target_pairs={{0,28},{4,8},{8,4},{12,16},{16,12},{20,24},{24,20},{28,0},{1,29},{... | collective-permute-start | bytes 245768 | tf_op jit(solution)/shard_map/ppermute | solution.py:51
  28.1 0.0 collective-permute-start.8
  28.1 2.1 %post.1.base_ref = f32[8,32,512]{2,1,0:T(8,128)S(1)} custom-call(s32[1]{0:T(128)} %bitcast.me_ref, f32[12,40,512]{2,1,0:T(8,128)S(1)} %get-tuple-element.94.u2_ref, f32[14,40,512]{2,1,0:T(8,128)S(1)} %get-tuple-element.95.text_ref), custom_call_target="tpu_custom_call" | custom-call | flops 1073741824 | bytes 4194304 | tf_op jit(solution)/shard_map/post/pallas_call | solution.py:682
  30.1 1.5 %collective-permute-done.9.slab_b = bf16[10,16,256]{2,1,0:T(8,128)(2,1)S(1)} collective-permute-done((bf16[10,16,256]{2,1,0:T(8,128)(2,1)S(1)}, bf16[10,16,256]{2,1,0:T(8,128)(2,1)S(1)}, u32[]{:S(2)}, u32[]{:S(2)}) %collective-permute-start.9) | collective-permute-done | bytes 81952 | tf_op jit(solution)/shard_map/ppermute | solution.py:51
  31.7 1.7 %collective-permute-done.8.slab_a = bf16[10,16,256]{2,1,0:T(8,128)(2,1)S(1)} collective-permute-done((bf16[10,16,256]{2,1,0:T(8,128)(2,1)S(1)}, bf16[10,16,256]{2,1,0:T(8,128)(2,1)S(1)}, u32[]{:S(2)}, u32[]{:S(2)}) %collective-permute-start.8) | collective-permute-done | bytes 81952 | tf_op jit(solution)/shard_map/ppermute | solution.py:51
  33.3 0.0 collective-permute-done.10.rest_1_
  33.3 0.0 collective-permute-done.11.rest_2_
  33.3 0.0 collective-permute-done.12.rest_3_
  33.4 2.4 %correct.1 = (f32[8,32,512]{2,1,0:T(8,128)}, bf16[2304,128]{1,0:T(8,128)(2,1)}) custom-call(s32[1]{0:T(128)} %bitcast.me_ref, s32[1]{0:T(128)} %bitcast.1.slab_ref, f32[4,16,256]{2,1,0:T(8,128)S(1)} %get-tuple-element.88.ct_ref, bf16[1,16,256]{2,1,0:T(8,128)(2,1)S(1)} %collective-permute-done.6.side_a, ...), custom_call_target="tpu_custom_call" | custom-call | tf_op jit(solution)/shard_map/correct/pallas_call | solution.py:692
  (1 shorter events, 0.0 us)
Async XLA Ops:
  3.5 8.2 %collective-permute-start = (bf16[4,16,512]{2,1,0:T(8,128)(2,1)S(1)}, bf16[4,16,512]{2,1,0:T(8,128)(2,1)S(1)}, u32[]{:S(2)}, u32[]{:S(2)}) collective-permute-start(bf16[4,16,512]{2,1,0:T(8,128)(2,1)S(1)} %get-tuple-element.62), channel_id=1, source_target_pairs={{0,1},{1,0},{2,3},{3,2},{4,5},{5,4},{6,7},{7,6},{8,9},{9,8},{10,11... | collective-permute-start | bytes 196616 | tf_op jit(solution)/shard_map/ppermute | solution.py:51
  4.0 7.7 %collective-permute-start.1 = (bf16[4,16,512]{2,1,0:T(8,128)(2,1)S(1)}, bf16[4,16,512]{2,1,0:T(8,128)(2,1)S(1)}, u32[]{:S(2)}, u32[]{:S(2)}) collective-permute-start(bf16[4,16,512]{2,1,0:T(8,128)(2,1)S(1)} %get-tuple-element.63), channel_id=1, source_target_pairs={{0,3},{1,2},{2,1},{3,0},{4,7},{5,6},{6,5},{7,4},{8,11},{9,10},{10,... | collective-permute-start | bytes 196616 | tf_op jit(solution)/shard_map/ppermute | solution.py:51
  6.7 9.3 %collective-permute-start.2 = (bf16[8,16,512]{2,1,0:T(8,128)(2,1)S(1)}, bf16[8,16,512]{2,1,0:T(8,128)(2,1)S(1)}, u32[]{:S(2)}, u32[]{:S(2)}) collective-permute-start(bf16[8,16,512]{2,1,0:T(8,128)(2,1)S(1)} %get-tuple-element.64), channel_id=1, source_target_pairs={{0,4},{4,0},{8,12},{12,8},{16,20},{20,16},{24,28},{28,24},{1,5},{5... | collective-permute-start | bytes 393224 | tf_op jit(solution)/shard_map/ppermute | solution.py:51
  8.2 8.0 %collective-permute-start.3 = (bf16[8,16,512]{2,1,0:T(8,128)(2,1)S(1)}, bf16[8,16,512]{2,1,0:T(8,128)(2,1)S(1)}, u32[]{:S(2)}, u32[]{:S(2)}) collective-permute-start(bf16[8,16,512]{2,1,0:T(8,128)(2,1)S(1)} %get-tuple-element.65), channel_id=1, source_target_pairs={{0,28},{4,8},{8,4},{12,16},{16,12},{20,24},{24,20},{28,0},{1,29},{... | collective-permute-start | bytes 393224 | tf_op jit(solution)/shard_map/ppermute | solution.py:51
  11.8 6.8 %collective-permute-start.4 = (bf16[2,16,512]{2,1,0:T(8,128)(2,1)S(1)}, bf16[2,16,512]{2,1,0:T(8,128)(2,1)S(1)}, u32[]{:S(2)}, u32[]{:S(2)}) collective-permute-start(bf16[2,16,512]{2,1,0:T(8,128)(2,1)S(1)} %get-tuple-element.71), channel_id=1, source_target_pairs={{0,4},{4,0},{8,12},{12,8},{16,20},{20,16},{24,28},{28,24},{1,5},{5... | collective-permute-start | bytes 98312 | tf_op jit(solution)/shard_map/ppermute | solution.py:51
  11.9 6.8 %collective-permute-start.5 = (bf16[2,16,512]{2,1,0:T(8,128)(2,1)S(1)}, bf16[2,16,512]{2,1,0:T(8,128)(2,1)S(1)}, u32[]{:S(2)}, u32[]{:S(2)}) collective-permute-start(bf16[2,16,512]{2,1,0:T(8,128)(2,1)S(1)} %get-tuple-element.72), channel_id=1, source_target_pairs={{0,28},{4,8},{8,4},{12,16},{16,12},{20,24},{24,20},{28,0},{1,29},{... | collective-permute-start | bytes 98312 | tf_op jit(solution)/shard_map/ppermute | solution.py:51
  20.7 3.7 %collective-permute-start.6 = (bf16[1,16,256]{2,1,0:T(8,128)(2,1)S(1)}, bf16[1,16,256]{2,1,0:T(8,128)(2,1)S(1)}, u32[]{:S(2)}, u32[]{:S(2)}) collective-permute-start(bf16[1,16,256]{2,1,0:T(8,128)(2,1)S(1)} %get-tuple-element.89), channel_id=1, source_target_pairs={{0,1},{1,0},{2,3},{3,2},{4,5},{5,4},{6,7},{7,6},{8,9},{9,8},{10,11... | collective-permute-start | bytes 24584 | tf_op jit(solution)/shard_map/ppermute | solution.py:51
  20.7 3.6 %collective-permute-start.7 = (bf16[1,16,256]{2,1,0:T(8,128)(2,1)S(1)}, bf16[1,16,256]{2,1,0:T(8,128)(2,1)S(1)}, u32[]{:S(2)}, u32[]{:S(2)}) collective-permute-start(bf16[1,16,256]{2,1,0:T(8,128)(2,1)S(1)} %get-tuple-element.90), channel_id=1, source_target_pairs={{0,3},{1,2},{2,1},{3,0},{4,7},{5,6},{6,5},{7,4},{8,11},{9,10},{10,... | collective-permute-start | bytes 24584 | tf_op jit(solution)/shard_map/ppermute | solution.py:51
  22.2 11.2 %collective-permute-start.10 = (bf16[512,128]{1,0:T(8,128)(2,1)S(1)}, bf16[512,128]{1,0:T(8,128)(2,1)S(1)}, u32[]{:S(2)}, u32[]{:S(2)}) collective-permute-start(bf16[512,128]{1,0:T(8,128)(2,1)S(1)} %get-tuple-element.97), channel_id=1, source_target_pairs={{0,1},{1,2},{2,3},{3,0},{4,5},{5,6},{6,7},{7,4},{8,9},{9,10},{10,1... | collective-permute-start | bytes 393224 | tf_op jit(solution)/shard_map/ppermute | solution.py:39
  22.3 11.0 %collective-permute-start.11 = (bf16[512,128]{1,0:T(8,128)(2,1)S(1)}, bf16[512,128]{1,0:T(8,128)(2,1)S(1)}, u32[]{:S(2)}, u32[]{:S(2)}) collective-permute-start(bf16[512,128]{1,0:T(8,128)(2,1)S(1)} %get-tuple-element.98), channel_id=1, source_target_pairs={{0,2},{1,3},{2,0},{3,1},{4,6},{5,7},{6,4},{7,5},{8,10},{9,11},{10,... | collective-permute-start | bytes 393224 | tf_op jit(solution)/shard_map/ppermute | solution.py:39
  23.0 10.4 %collective-permute-start.12 = (bf16[512,128]{1,0:T(8,128)(2,1)S(1)}, bf16[512,128]{1,0:T(8,128)(2,1)S(1)}, u32[]{:S(2)}, u32[]{:S(2)}) collective-permute-start(bf16[512,128]{1,0:T(8,128)(2,1)S(1)} %get-tuple-element.99), channel_id=1, source_target_pairs={{0,3},{1,0},{2,1},{3,2},{4,7},{5,4},{6,5},{7,6},{8,11},{9,8},{10,9... | collective-permute-start | bytes 393224 | tf_op jit(solution)/shard_map/ppermute | solution.py:39
  24.4 7.3 %collective-permute-start.9 = (bf16[10,16,256]{2,1,0:T(8,128)(2,1)S(1)}, bf16[10,16,256]{2,1,0:T(8,128)(2,1)S(1)}, u32[]{:S(2)}, u32[]{:S(2)}) collective-permute-start(bf16[10,16,256]{2,1,0:T(8,128)(2,1)S(1)} %get-tuple-element.100), channel_id=1, source_target_pairs={{0,28},{4,8},{8,4},{12,16},{16,12},{20,24},{24,20},{28,0},{1,29},{... | collective-permute-start | bytes 245768 | tf_op jit(solution)/shard_map/ppermute | solution.py:51
  28.1 5.3 %collective-permute-start.8 = (bf16[10,16,256]{2,1,0:T(8,128)(2,1)S(1)}, bf16[10,16,256]{2,1,0:T(8,128)(2,1)S(1)}, u32[]{:S(2)}, u32[]{:S(2)}) collective-permute-start(bf16[10,16,256]{2,1,0:T(8,128)(2,1)S(1)} %get-tuple-element.101), channel_id=1, source_target_pairs={{0,4},{4,0},{8,12},{12,8},{16,20},{20,16},{24,28},{28,24},{1,5},{5... | collective-permute-start | bytes 245768 | tf_op jit(solution)/shard_map/ppermute | solution.py:51

commit v5 on v4

--- a/solution.py
+++ b/solution.py
@@ -8,6 +8,7 @@
 from jax.sharding import PartitionSpec as P
 
 MIG = 128
+PART = 256
 SCREENING = 0.05
 DAMPING = 2.0 / 3.0
 CENTRE = 6.0 + SCREENING
@@ -55,46 +56,57 @@
     return lax.rem(x, 2) == 0
 
 
-def load_kernel(slab_ref, *refs):
-    count = (len(refs) - 3) // 2
-    sources, targets = refs[:count], refs[count : 2 * count]
-    slab_a, slab_b, sem = refs[2 * count :]
+LANES = 128
+
+
+def shuffle(nz, back):
+    one, two = iota((nz, nz), 0), iota((nz, nz), 1)
+    if back:
+        one, two = two, one
+    return (one == (two % LANES) * (nz // LANES) + two // LANES).astype(F32).astype(BF16)
+
+
+def begin_kernel(me_ref, slab_ref, *refs):
+    count = 10
+    sources, refs = refs[:count], refs[count:]
+    u_ref, t_ref, sensed_ref, depth_a, depth_b, field_a, field_b, list_ref, *targets = refs[:-5]
+    raw, weight_ref, cell_ref, divide_ref, sem = refs[-5:]
+    targets = [cell_ref, raw, divide_ref, weight_ref] + targets
+    species_ref, death_ref = targets[4:6]
     copies = [
         pltpu.make_async_copy(source, target, sem.at[i])
-        for i, (source, target) in enumerate(zip(sources, targets))
+        for i, (source, target) in enumerate(zip(sources, targets, strict=True))
     ]
     for copy in copies:
         copy.start()
+    nx, ny, nz = u_ref.shape
+    agents = species_ref.shape[0]
+    rows = nx * ny
+    tiles = nz // LANES
+    order = shuffle(nz, False)
     copies[0].wait()
-    u_ref = targets[0]
-    nx, ny, nz = u_ref.shape
+    cell = cell_ref[...]
+    cell_row = cell // nz
+    cell_z = cell - cell_row * nz
+    cell_z = (cell_z % tiles) * LANES + cell_z // tiles
+    one_z = (iota((nz, agents), 0) == cell_z).astype(F32).astype(BF16)
+    in_row = iota((rows, agents), 0) == cell_row
+    copies[1].wait()
+    high, low = halves(raw[...].reshape(rows, nz))
+    high = dot(high, order, 1, 0)
+    u = high + dot(low, order, 1, 0)
+    u_ref[...] = u.reshape(nx, ny, nz)
     half = ny // 16
-    even = is_even(slab_ref[0])
-    for ref, front in ((slab_a, even), (slab_b, jnp.logical_not(even))):
+    slab_even = is_even(slab_ref[0])
+    for ref, front in ((field_a, slab_even), (field_b, jnp.logical_not(slab_even))):
         start = jnp.where(front, nx - HALO, 0)
         for k in range(HALO):
             ref[k * half : (k + 1) * half] = u_ref[start + k].astype(BF16).reshape(half, 16, nz)
-    for copy in copies[1:]:
+    for copy in copies[2:]:
         copy.wait()
-
-
-def uptake_kernel(
-    me_ref, u_ref, cell_ref, death_ref, divide_ref, species_ref, weight_ref,
-    t_ref, sensed_ref, depth_a, depth_b, list_ref,
-):
-    nx, ny, nz = u_ref.shape
-    agents = species_ref.shape[0]
-    rows = nx * ny
-    u = u_ref[...].reshape(rows, nz)
-    cell = cell_ref[...].reshape(1, agents)
-    cell_row = cell // nz
-    cell_z = cell - cell_row * nz
-    one_z = (iota((nz, agents), 0) == cell_z).astype(F32).astype(BF16)
-    in_row = iota((rows, agents), 0) == cell_row
-    high, low = halves(u)
-    picked = dot(high, one_z, 1, 0) + dot(low, one_z, 1, 0)
+    picked = dot(high.astype(BF16), one_z, 1, 0)
     sample = jnp.sum(jnp.where(in_row, picked, 0.0), axis=0, keepdims=True)
-    sensed_ref[...] = jnp.broadcast_to(sample, (8, agents)).astype(BF16).astype(F32)
+    sensed_ref[...] = jnp.broadcast_to(sample, (8, agents))
     weight = jnp.broadcast_to(weight_ref[...].reshape(1, -1), (8, species_ref.shape[1]))
     score = dot(weight, species_ref[...], 1, 1)[0:1]
     softplus = jnp.maximum(score, 0.0) + jnp.log1p(jnp.exp(-jnp.abs(score)))
@@ -117,8 +129,8 @@
         high = jnp.concatenate(parts[4:], axis=0)
         depth_a[pair] = jnp.where(even, high, low).astype(BF16)
         depth_b[pair] = jnp.where(even, low, high).astype(BF16)
-    half_z = cell_z // 2
-    values = (cell_row.astype(F32), half_z.astype(F32), (cell_z - 2 * half_z).astype(F32), up_high)
+    part = cell_z // PART
+    values = (cell_row.astype(F32), (cell_z - part * PART).astype(F32), part.astype(F32), up_high)
     list_ref[...] = jnp.concatenate(
         [x[:, i * nz : (i + 1) * nz] for x in values for i in range(agents // nz)], axis=0
     )
@@ -194,19 +206,17 @@
                 out[i // tiles, :, at : at + width] = placed[i * 16 : (i + 1) * 16]
 
 
+def tiles_of(x):
+    return [x[:, i : i + LANES] for i in range(0, x.shape[1], LANES)]
+
+
 def third_sum(x):
-    width = 128
-    tiles = x.shape[1] // width
-    lane = iota((x.shape[0], width), 1)
-    parts = [x[:, i * width : (i + 1) * width] for i in range(tiles)]
-    ups = [pltpu.roll(part, 1, 1) for part in parts]
-    downs = [pltpu.roll(part, width - 1, 1) for part in parts]
-    sums = []
-    for i in range(tiles):
-        before = ups[i - 1] if i else 0.0
-        after = downs[i + 1] if i < tiles - 1 else 0.0
-        sums.append(jnp.where(lane == 0, before, ups[i]) + jnp.where(lane == width - 1, after, downs[i]))
-    return jnp.concatenate(sums, axis=1)
+    parts = tiles_of(x)
+    lane = iota((x.shape[0], LANES), 1)
+    before = jnp.where(lane == 0, 0.0, pltpu.roll(parts[-1], 1, 1))
+    after = jnp.where(lane == LANES - 1, 0.0, pltpu.roll(parts[0], LANES - 1, 1))
+    padded = [before] + parts + [after]
+    return jnp.concatenate([x + y for x, y in zip(padded[:-2], padded[2:])], axis=1)
 
 
 def neighbour_total(before, plane, after):
@@ -324,14 +334,14 @@
         u1[p] = masked(v, ny, mask)
         return carry
 
-    lax.fori_loop(HALO - 1, nx + HALO - 1, first, 0)
+    lax.fori_loop(HALO - 1, nx + HALO - 1, first, 0, unroll=2)
 
     def second(p, carry):
         v = relaxed(u1[p], u1[p + 1], u1[p + 2], text_ref[p + 1], CENTRE)
         u2_ref[p] = masked(v, ny, mask)
         return carry
 
-    lax.fori_loop(HALO - 1, nx + 1, second, 0)
+    lax.fori_loop(HALO - 1, nx + 1, second, 0, unroll=2)
     for p in range(2, nx - 2):
         inside[p - 2] = residual(u2_ref, text_ref, p, ny)
 
@@ -361,15 +371,19 @@
         sign = jnp.where(after, 1, -1)
         edge = jnp.where(after, nx - 1, 0)
         lines = agents // nz
-        cell_row, half_z, bit, uptake = (
+        cell_row, place, part, uptake = (
             jnp.concatenate([message[at + i : at + i + 1] for i in range(lines)], axis=1)
             for at in range(2 * corner, 2 * corner + 4 * lines, lines)
         )
         cell_row = cell_row.astype(jnp.int32) - jnp.where(after, 0, (nx - near) * ny)
-        cell_z = (2.0 * half_z + bit).astype(jnp.int32)
-        one_z = (iota((nz, agents), 0) == cell_z).astype(F32).astype(BF16)
-        taken = jnp.where(iota((near * ny, agents), 0) == cell_row, uptake, 0.0).astype(BF16)
-        foreign[...] = dot(taken, one_z, 1, 1)
+        wanted = jnp.logical_and(cell_row >= 0, cell_row < near * ny)
+        key = jnp.where(wanted, part.astype(jnp.int32) * (near * ny) + cell_row, -1)
+        one_z = (iota((PART, agents), 0) == place.astype(jnp.int32)).astype(F32).astype(BF16)
+        key_rows = iota((near * ny * (nz // PART), agents), 0)
+        taken = jnp.where(key_rows == key, uptake, 0.0).astype(BF16)
+        source = dot(taken, one_z, 1, 1)
+        for i in range(nz // PART):
+            foreign[:, i * PART : (i + 1) * PART] = source[i * near * ny : (i + 1) * near * ny]
         for i in range(1, HALO):
             p = edge + sign * i
             index = jnp.where(after, i - 1, HALO - 1 - i)
@@ -404,15 +418,16 @@
         for p in (2 * q, 2 * q + 1):
             known = 2 <= p < nx - 2
             both = both + (inside[p - 2] if known else residual(u2_ref, text_ref, p, ny))
-        for i in range(nz // 128):
-            paired[q, i] = both[:, i * 128 : (i + 1) * 128]
+        parts = tiles_of(both)
+        for i in range(len(parts) // 2):
+            paired[q, i] = parts[2 * i] + parts[2 * i + 1]
     cx, cy, cz = coarse_ref.shape
-    flat = jnp.concatenate(
+    coarse = jnp.concatenate(
         [
             jnp.concatenate(
                 [
                     paired[q, i, pl.ds(0, cy, 2), :] + paired[q, i, pl.ds(1, cy, 2), :]
-                    for i in range(nz // 128)
+                    for i in range(cz // LANES)
                 ],
                 axis=1,
             )
@@ -420,9 +435,7 @@
         ],
         axis=0,
     )
-    fold = ((iota((nz, cz), 0) >> 1) == iota((nz, cz), 1)).astype(F32).astype(BF16)
-    high, low = halves(flat)
-    coarse = 0.5 * (dot(high, fold, 1, 0) + dot(low, fold, 1, 0))
+    coarse = 0.5 * coarse
     coarse_ref[...] = coarse.reshape(cx, cy, cz)
     coarse_all_ref[...] = coarse.astype(BF16).reshape(cx, cy, cz)
     low, high = (
@@ -433,8 +446,9 @@
     coarse_b[0] = jnp.where(even, low, high).astype(BF16)
 
 
-def post_kernel(depths, me_ref, u2_ref, text_ref, out_ref, v1):
+def post_kernel(depths, me_ref, u2_ref, text_ref, out_ref, back_ref, v1):
     nx, ny, nz = out_ref.shape
+    back_ref[...] = shuffle(nz, True)
     mask = edge_mask(me_ref[0], depths, HALO)
 
     def first(p, carry):
@@ -442,21 +456,21 @@
         v1[p] = masked(v, ny, mask)
         return carry
 
-    lax.fori_loop(0, nx + 2, first, 0)
+    lax.fori_loop(0, nx + 2, first, 0, unroll=2)
 
     def second(p, carry):
         v = relaxed(v1[p], v1[p + 1], v1[p + 2], text_ref[p + 3], CENTRE)
         out_ref[p] = v[:ny]
         return carry
 
-    lax.fori_loop(0, nx, second, 0)
+    lax.fori_loop(0, nx, second, 0, unroll=2)
 
 
 def correct_kernel(
-    depths, me_ref, slab_ref, ct_ref, side_a, side_b, slab_a, slab_b, base_ref, *rest
+    depths, me_ref, slab_ref, ct_ref, side_a, side_b, slab_a, slab_b, base_ref, back_ref, *rest
 ):
     packed = rest[:depths]
-    out_ref, agents_ref, fine, sem = rest[depths:]
+    out_any, agents_ref, fine, out_ref, sem = rest[depths:]
     nx, ny, nz = out_ref.shape
     cx, cy, cz = ct_ref.shape
     me = me_ref[0]
@@ -511,15 +525,14 @@
     wide = cy + 4
     for q, value in enumerate(values):
         value = jnp.concatenate([value[: cy + 2], value[cy + 2 * HALO - 2 :]], axis=0)
-        for i in range(cz // 128):
-            part = value[:, i * 128 : (i + 1) * 128]
+        for i, part in enumerate(tiles_of(value)):
             fine[q, i, pl.ds(0, wide, 2), :] = part
             fine[q, i, pl.ds(1, wide, 2), :] = part
     def second_total(plane):
         rows = plane.shape[0]
         return pltpu.roll(plane, 1, 0) + pltpu.roll(plane, rows - 1, 0)
 
-    spread = [jnp.concatenate([fine[q, i] for i in range(cz // 128)], axis=1) for q in range(cx + 2)]
+    spread = [jnp.concatenate([fine[q, i] for i in range(cz // LANES)], axis=1) for q in range(cx + 2)]
     still = [KEEP * plane + PULL * second_total(plane) for plane in spread]
     once = []
     for p in range(-1, nx + 1):
@@ -529,33 +542,27 @@
         else:
             others = spread[q] + spread[q + 1]
         once.append(masked(still[q] + PULL * others, ny, mask))
-    none, one, two = [], [], []
-    for p in range(nx):
-        plane = once[p + 1]
-        total = once[p] + once[p + 2] + second_total(plane)
-        none.append((KEEP * plane + PULL * total)[:ny])
-        one.append(plane[:ny])
-        two.append(spread[(p + 2) // 2][:ny])
-    z = iota((cz, nz), 1)
-    k = iota((cz, nz), 0)
-
-    def hit(shift):
-        moved = z + shift
-        inside = jnp.logical_and(moved >= 0, moved < nz)
-        return jnp.logical_and((moved >> 1) == k, inside).astype(F32)
-
-    here, left, right = hit(0), hit(-1), hit(1)
-    paths = jnp.where(jnp.logical_or(z == 0, z == nz - 1), here, 2.0 * here)
-    spread_none = here.astype(BF16)
-    spread_one = ((left + right) * 1.0).astype(BF16)
-    spread_two = (hit(-2) + hit(2) + paths).astype(BF16)
-    total = base_ref[...].reshape(nx * ny, nz)
-    for parts, scale, matrix in (
-        (none, 1.0, spread_none), (one, 2.0 * PULL, spread_one), (two, PULL * PULL, spread_two)
-    ):
-        high, low = halves(scale * jnp.concatenate(parts, axis=0))
-        total = total + dot(high, matrix, 1, 0) + dot(low, matrix, 1, 0)
-    out_ref[...] = total.reshape(nx, ny, nz)
+
+    def twice(plane):
+        return jnp.concatenate([part for part in tiles_of(plane) for _ in range(2)], axis=1)
+
+    back = back_ref[...]
+    step = 2
+    for start in range(0, nx, step):
+        planes = []
+        for p in range(start, start + step):
+            plane = once[p + 1]
+            total = once[p] + once[p + 2] + second_total(plane)
+            none = (KEEP * plane + PULL * total)[:ny]
+            one = (2.0 * PULL) * plane[:ny]
+            two = (PULL * PULL) * spread[(p + 2) // 2][:ny]
+            planes.append(base_ref[p] + twice(none) + third_sum(twice(one) + third_sum(twice(two))))
+        high, low = halves(jnp.concatenate(planes, axis=0))
+        done = dot(high, back, 1, 0) + dot(low, back, 1, 0)
+        out_ref[start : start + step] = done.reshape(step, ny, nz)
+        cut = pl.ds(start, step)
+        copies.append(pltpu.make_async_copy(out_ref.at[cut], out_any.at[cut], sem.at[len(copies)]))
+        copies[-1].start()
     for copy in copies:
         copy.wait()
 
@@ -573,39 +580,42 @@
     cells, death, divide = (x.reshape(1, agents) for x in (agent_cell, death_flag, divide_flag))
     move, route = slab_move.reshape(1, agents), depth_route.reshape(1, agents)
     half = ny // 16
-    if agents % nz or nx * ny > 256 or nz > 512:
+    if agents % nz or nx * ny > PART or nz % PART:
         raise ValueError("list digits")
     arguments = (
-        nutrient, cells, species, uptake_weight.reshape(1, width), death, divide,
+        cells, nutrient, divide, uptake_weight.reshape(1, width), species, death,
         move, route, net_weight, sensing.reshape(1, width),
     )
-    loaded = pl.pallas_call(
-        load_kernel,
-        out_shape=tuple(shape(x.shape, x.dtype) for x in arguments)
-        + tuple(shape((HALO * half, 16, nz), BF16) for _ in range(2)),
-        in_specs=[SMEM_SPEC] + [HBM_SPEC] * len(arguments),
-        out_specs=[VMEM_SPEC] * (len(arguments) + 2),
-        scratch_shapes=[pltpu.SemaphoreType.DMA((len(arguments),))],
-        compiler_params=PARAMS,
-        name="load",
-    )(slab, *(pltpu.with_memory_space_constraint(x, pltpu.HBM) for x in arguments))
-    nutrient, cells, species, weight, death, divide, move, route, net_weight, sensing = loaded[:-2]
-    target, sensed, depth_a, depth_b, agent_list = pl.pallas_call(
-        uptake_kernel,
+    (
+        nutrient, target, sensed, depth_a, depth_b, field_a, field_b, agent_list,
+        species, death, move, route, net_weight, sensing,
+    ) = pl.pallas_call(
+        begin_kernel,
         out_shape=(
+            shape((nx, ny, nz), F32),
             shape((nx, ny, nz), F32),
             shape((8, agents), F32),
             shape((nx // 2, 16, nz), BF16),
             shape((nx // 2, 16, nz), BF16),
+            shape((HALO * half, 16, nz), BF16),
+            shape((HALO * half, 16, nz), BF16),
             shape((4 * agents // nz, nz), F32),
-        ),
-        in_specs=[SMEM_SPEC] + [VMEM_SPEC] * 6,
-        out_specs=[VMEM_SPEC] * 5,
+        )
+        + tuple(shape(x.shape, x.dtype) for x in arguments[4:]),
+        in_specs=[SMEM_SPEC] * 2 + [HBM_SPEC] * len(arguments),
+        out_specs=[VMEM_SPEC] * (8 + len(arguments) - 4),
+        scratch_shapes=[
+            pltpu.VMEM((nx, ny, nz), F32),
+            pltpu.VMEM((1, width), BF16),
+            pltpu.VMEM((1, agents), jnp.int32),
+            pltpu.VMEM((1, agents), jnp.int32),
+            pltpu.SemaphoreType.DMA((len(arguments),)),
+        ],
         compiler_params=PARAMS,
-        name="uptake",
-    )(me, nutrient, cells, death, divide, species, weight)
+        name="begin",
+    )(me, slab, *(pltpu.with_memory_space_constraint(x, pltpu.HBM) for x in arguments))
     field_a, field_b, depth_a, depth_b = lax.optimization_barrier(
-        (loaded[-2], loaded[-1], depth_a, depth_b)
+        (field_a, field_b, depth_a, depth_b)
     )
     side_a = swapped(depth_a, "depth", "a")
     side_b = swapped(depth_b, "depth", "b")
@@ -665,7 +675,7 @@
         in_specs=[SMEM_SPEC] * 2 + [VMEM_SPEC] * 7,
         out_specs=[VMEM_SPEC] * 7,
         scratch_shapes=[
-            pltpu.VMEM((cx, nz // 128, ny, 128), F32),
+            pltpu.VMEM((cx, cz // LANES, ny, LANES), F32),
             pltpu.VMEM(((HALO - 1) * ny, nz), F32),
         ],
         input_output_aliases={3: 0, 4: 1, 5: 2},
@@ -679,11 +689,11 @@
         swapped(jnp.concatenate([ct_all, coarse_a, coarse_b, movers], axis=0), "slab", which)
         for which, movers in (("a", sent[depths]), ("b", sent[depths + 1]))
     )
-    base = pl.pallas_call(
+    base, back = pl.pallas_call(
         functools.partial(post_kernel, depths),
-        out_shape=shape((nx, ny, nz), F32),
+        out_shape=(shape((nx, ny, nz), F32), shape((nz, nz), BF16)),
         in_specs=[SMEM_SPEC] + [VMEM_SPEC] * 2,
-        out_specs=VMEM_SPEC,
+        out_specs=[VMEM_SPEC] * 2,
         scratch_shapes=[pltpu.VMEM((nx + 2, ext, nz), F32)],
         compiler_params=PARAMS,
         cost_estimate=pl.CostEstimate(flops=1 << 30, bytes_accessed=1 << 22, transcendentals=0),
@@ -695,15 +705,16 @@
             shape((nx, ny, nz), F32),
             shape((depths * capacity + 2 * MIG, width), BF16),
         ),
-        in_specs=[SMEM_SPEC] * 2 + [VMEM_SPEC] * 6 + [ANY_SPEC] * depths,
-        out_specs=[VMEM_SPEC, ANY_SPEC],
+        in_specs=[SMEM_SPEC] * 2 + [VMEM_SPEC] * 7 + [ANY_SPEC] * depths,
+        out_specs=[HBM_SPEC, ANY_SPEC],
         scratch_shapes=[
-            pltpu.VMEM((cx + 2, cz // 128, ext, 128), F32),
-            pltpu.SemaphoreType.DMA((depths + 2 * (MIG // 16),)),
+            pltpu.VMEM((cx + 2, cz // LANES, ext, LANES), F32),
+            pltpu.VMEM((nx, ny, nz), F32),
+            pltpu.SemaphoreType.DMA((depths + 2 * (MIG // 16) + nx // 2,)),
         ],
         compiler_params=PARAMS,
         name="correct",
-    )(me, slab, ct, coarse_a, coarse_b, tail_a, tail_b, base, *arrived)
+    )(me, slab, ct, coarse_a, coarse_b, tail_a, tail_b, base, back, *arrived)
 
 
 def solution(mesh):

time: 36 us -> 34.4 us (0.956)
  Pallas kernels: 13.7 us -> 10.5 us
  waiting for transfers between devices: 3.41 us -> 6.28 us
  starting transfers between devices: 17.9 us -> 16.7 us
    ppermute x10, waiting for transfers between devices: 3.4 us -> 6.27 us  [swapped(): return lax.ppermute(x, axis, sorted(pairs))]
    ppermute x10, starting transfers between devices: 15.7 us -> 13.7 us  [swapped(): return lax.ppermute(x, axis, sorted(pairs))]
    pallas_call x1, Pallas kernels: 2.51 us -> 1.21 us  [local(): pl.pallas_call(functools.partial(inner_kernel, depths), out_shape=(shape(...]
    pallas_call x3 -> x2, Pallas kernels: 4.93 us -> 4.01 us  [the longest x1 3.03 us: local(): pl.pallas_call(begin_kernel, out_shape=(shape((nx, ny, nz), F32), shape((...]
    ppermute x3, starting transfers between devices: 2.18 us -> 2.99 us  [cyclic(): return lax.ppermute(x, axis, [(i, (i + by) % count) for i in range(count)])]
    pallas_call x1, Pallas kernels: 1.98 us -> 1.19 us  [local(): pl.pallas_call(functools.partial(smooth_kernel, depths, agents), out_shap...]
  transfers between devices with their start and end apart: 13 -> 13, of which waited for: 3 -> 4; matrix products, arithmetic and copies ran while one was open for 0% -> 0% of each run, Pallas kernels for 18% -> 12%
where the time goes in v5:
time: 34.4 us; the launch traced here: 34.2 us
  starting transfers between devices  16.7 us (49%)
  Pallas kernels  10.5 us (31%)
  waiting for transfers between devices  6.28 us (18%)
  between operations  0.72 us (2%)
    ppermute x10, starting transfers between devices, swapped(): return lax.ppermute(x, axis, sorted(pairs))  13.7 us
    ppermute x10, waiting for transfers between devices, swapped(): return lax.ppermute(x, axis, sorted(pairs))  6.27 us
    pallas_call x1, Pallas kernels, local(): pl.pallas_call(begin_kernel, out_shape=(shape((nx, ny, nz), F32), shape((...  3.03 us
    ppermute x3, starting transfers between devices, cyclic(): return lax.ppermute(x, axis, [(i, (i + by) % count) for i in range(count)])  2.99 us
    pallas_call x1, Pallas kernels, local(): pl.pallas_call(functools.partial(correct_kernel, depths), out_shape=(shap...  2.25 us
    pallas_call x1, Pallas kernels, local(): pl.pallas_call(network_kernel, out_shape=tuple((shape((capacity, width),...  1.8 us
    pallas_call x1, Pallas kernels, local(): pl.pallas_call(functools.partial(inner_kernel, depths), out_shape=(shape(...  1.21 us
    pallas_call x1, Pallas kernels, local(): pl.pallas_call(functools.partial(smooth_kernel, depths, agents), out_shap...  1.19 us
  transfers between devices with their start and end apart: 13, of which 4 were waited for; matrix products, arithmetic and copies ran while one was open for 0% of the time, Pallas kernels for 12%

profile of v5, /device:TPU:0, one launch (start us, length us, event | category | flops | bytes accessed | tf_op | source)
XLA Modules:
  0.0 34.2 jit_solution(5249465774465889184)
XLA Ops:
  0.6 3.0 %begin.1 = (f32[8,32,512]{2,1,0:T(8,128)S(1)}, f32[8,32,512]{2,1,0:T(8,128)S(1)}, f32[8,1024]{1,0:T(8,128)S(1)}, bf16[4,16,512]{2,1,0:T(8,128)(2,1)S(1)}, bf16[4...) custom-call(s32[1]{0:T(128)} %bitcast.me_ref, ...), custom_call_target="tpu_custom_call" | custom-call | tf_op jit(solution)/shard_map/begin/pallas_call | solution.py:592
  3.7 0.5 %collective-permute-start = (bf16[4,16,512]{2,1,0:T(8,128)(2,1)S(1)}, bf16[4,16,512]{2,1,0:T(8,128)(2,1)S(1)}, u32[]{:S(2)}, u32[]{:S(2)}) collective-permute-start(bf16[4,16,512]{2,1,0:T(8,128)(2,1)S(1)} %get-tuple-element.56), channel_id=1, source_target_pairs={{0,1},{1,0},{2,3},{3,2},{4,5},{5,4},{6,7},{7,6},{8,9},{9,8},{10,11... | collective-permute-start | bytes 196616 | tf_op jit(solution)/shard_map/ppermute | solution.py:52
  4.2 2.6 %collective-permute-start.1 = (bf16[4,16,512]{2,1,0:T(8,128)(2,1)S(1)}, bf16[4,16,512]{2,1,0:T(8,128)(2,1)S(1)}, u32[]{:S(2)}, u32[]{:S(2)}) collective-permute-start(bf16[4,16,512]{2,1,0:T(8,128)(2,1)S(1)} %get-tuple-element.57), channel_id=1, source_target_pairs={{0,3},{1,2},{2,1},{3,0},{4,7},{5,6},{6,5},{7,4},{8,11},{9,10},{10,... | collective-permute-start | bytes 196616 | tf_op jit(solution)/shard_map/ppermute | solution.py:52
  6.8 1.5 %collective-permute-start.2 = (bf16[8,16,512]{2,1,0:T(8,128)(2,1)S(1)}, bf16[8,16,512]{2,1,0:T(8,128)(2,1)S(1)}, u32[]{:S(2)}, u32[]{:S(2)}) collective-permute-start(bf16[8,16,512]{2,1,0:T(8,128)(2,1)S(1)} %get-tuple-element.58), channel_id=1, source_target_pairs={{0,4},{4,0},{8,12},{12,8},{16,20},{20,16},{24,28},{28,24},{1,5},{5... | collective-permute-start | bytes 393224 | tf_op jit(solution)/shard_map/ppermute | solution.py:52
  8.3 3.6 %collective-permute-start.3 = (bf16[8,16,512]{2,1,0:T(8,128)(2,1)S(1)}, bf16[8,16,512]{2,1,0:T(8,128)(2,1)S(1)}, u32[]{:S(2)}, u32[]{:S(2)}) collective-permute-start(bf16[8,16,512]{2,1,0:T(8,128)(2,1)S(1)} %get-tuple-element.59), channel_id=1, source_target_pairs={{0,28},{4,8},{8,4},{12,16},{16,12},{20,24},{24,20},{28,0},{1,29},{... | collective-permute-start | bytes 393224 | tf_op jit(solution)/shard_map/ppermute | solution.py:52
  11.9 0.0 collective-permute-done.side_a
  11.9 0.0 collective-permute-done.1.side_b
  11.9 0.1 corner.1
  12.0 0.1 collective-permute-start.4
  12.1 2.3 %collective-permute-start.5 = (bf16[2,16,512]{2,1,0:T(8,128)(2,1)S(1)}, bf16[2,16,512]{2,1,0:T(8,128)(2,1)S(1)}, u32[]{:S(2)}, u32[]{:S(2)}) collective-permute-start(bf16[2,16,512]{2,1,0:T(8,128)(2,1)S(1)} %get-tuple-element.66), channel_id=1, source_target_pairs={{0,28},{4,8},{8,4},{12,16},{16,12},{20,24},{24,20},{28,0},{1,29},{... | collective-permute-start | bytes 98312 | tf_op jit(solution)/shard_map/ppermute | solution.py:52
  14.3 1.8 %network.1 = (bf16[512,128]{1,0:T(8,128)(2,1)S(1)}, bf16[512,128]{1,0:T(8,128)(2,1)S(1)}, bf16[512,128]{1,0:T(8,128)(2,1)S(1)}, bf16[512,128]{1,0:T(8,128)(2,1)S...) custom-call(s32[1]{0:T(128)} %bitcast.me_ref, s32[1]{0:T(128)} %bitcast.1.slab_ref, ...), custom_call_target="tpu_custom_call" | custom-call | flops 2147483648 | bytes 1048576 | tf_op jit(solution)/shard_map/network/pallas_call | solution.py:638
  16.1 0.0 collective-permute-done.2.field_a
  16.1 0.2 collective-permute-done.3.field_b
  16.3 1.2 %inner.1 = (f32[16,40,512]{2,1,0:T(8,128)S(1)}, f32[14,40,512]{2,1,0:T(8,128)S(1)}, f32[14,40,512]{2,1,0:T(8,128)S(1)}, f32[12,40,512]{2,1,0:T(8,128)S(1)}, f32[4,32,512]{2,1,0:T(8,128)S(1)}) custom-call(s32[1]{0:T(128)} %bitcast.me_ref, s32[1]{0:T(128)} %bitcast.1.slab_ref, f32[8,32,512]{2,1,0:T(8,128)S(1)} %get-tuple-element.50.u_ref, ...), custom_call_target="tpu_custom_call" | custom-call | flops 1048576 | bytes 1048576 | tf_op jit(solution)/shard_map/inner/pallas_call | solution.py:648
  17.5 0.0 collective-permute-done.4.slab_a
  17.5 1.2 %collective-permute-done.5.slab_b = bf16[2,16,512]{2,1,0:T(8,128)(2,1)S(1)} collective-permute-done((bf16[2,16,512]{2,1,0:T(8,128)(2,1)S(1)}, bf16[2,16,512]{2,1,0:T(8,128)(2,1)S(1)}, u32[]{:S(2)}, u32[]{:S(2)}) %collective-permute-start.5) | collective-permute-done | bytes 32800 | tf_op jit(solution)/shard_map/ppermute | solution.py:52
  18.7 1.2 %smooth.1 = (f32[14,40,512]{2,1,0:T(8,128)S(1)}, f32[14,40,512]{2,1,0:T(8,128)S(1)}, f32[12,40,512]{2,1,0:T(8,128)S(1)}, f32[4,16,256]{2,1,0:T(8,128)S(1)}, bf16...) custom-call(s32[1]{0:T(128)} %bitcast.me_ref, ...), custom_call_target="tpu_custom_call", output_to_operand_aliasing={{0}: (3, {}), {1}: (4, {}), {2}: (5, {})} | custom-call | tf_op jit(solution)/shard_map/smooth/pallas_call | solution.py:664
  19.9 0.1 collective-permute-start.6
  20.0 0.6 %collective-permute-start.7 = (bf16[1,16,256]{2,1,0:T(8,128)(2,1)S(1)}, bf16[1,16,256]{2,1,0:T(8,128)(2,1)S(1)}, u32[]{:S(2)}, u32[]{:S(2)}) collective-permute-start(bf16[1,16,256]{2,1,0:T(8,128)(2,1)S(1)} %get-tuple-element.86), channel_id=1, source_target_pairs={{0,3},{1,2},{2,1},{3,0},{4,7},{5,6},{6,5},{7,4},{8,11},{9,10},{10,... | collective-permute-start | bytes 24584 | tf_op jit(solution)/shard_map/ppermute | solution.py:52
  20.6 0.1 collective-permute-start.10
  20.7 1.5 %collective-permute-start.11 = (bf16[512,128]{1,0:T(8,128)(2,1)S(1)}, bf16[512,128]{1,0:T(8,128)(2,1)S(1)}, u32[]{:S(2)}, u32[]{:S(2)}) collective-permute-start(bf16[512,128]{1,0:T(8,128)(2,1)S(1)} %get-tuple-element.96), channel_id=1, source_target_pairs={{0,2},{1,3},{2,0},{3,1},{4,6},{5,7},{6,4},{7,5},{8,10},{9,11},{10,... | collective-permute-start | bytes 393224 | tf_op jit(solution)/shard_map/ppermute | solution.py:40
  22.2 1.4 %collective-permute-start.12 = (bf16[512,128]{1,0:T(8,128)(2,1)S(1)}, bf16[512,128]{1,0:T(8,128)(2,1)S(1)}, u32[]{:S(2)}, u32[]{:S(2)}) collective-permute-start(bf16[512,128]{1,0:T(8,128)(2,1)S(1)} %get-tuple-element.97), channel_id=1, source_target_pairs={{0,3},{1,0},{2,1},{3,2},{4,7},{5,4},{6,5},{7,6},{8,11},{9,8},{10,9... | collective-permute-start | bytes 393224 | tf_op jit(solution)/shard_map/ppermute | solution.py:40
  23.6 0.0 collective-permute-done.6.side_a
  23.6 0.0 collective-permute-done.7.side_b
  23.6 2.5 %collective-permute-start.9 = (bf16[10,16,256]{2,1,0:T(8,128)(2,1)S(1)}, bf16[10,16,256]{2,1,0:T(8,128)(2,1)S(1)}, u32[]{:S(2)}, u32[]{:S(2)}) collective-permute-start(bf16[10,16,256]{2,1,0:T(8,128)(2,1)S(1)} %get-tuple-element.98), channel_id=1, source_target_pairs={{0,28},{4,8},{8,4},{12,16},{16,12},{20,24},{24,20},{28,0},{1,29},{... | collective-permute-start | bytes 245768 | tf_op jit(solution)/shard_map/ppermute | solution.py:52
  26.1 0.0 collective-permute-start.8
  26.1 1.0 %post.1 = (f32[8,32,512]{2,1,0:T(8,128)S(1)}, bf16[512,512]{1,0:T(8,128)(2,1)S(1)}) custom-call(s32[1]{0:T(128)} %bitcast.me_ref, f32[12,40,512]{2,1,0:T(8,128)S(1)} %get-tuple-element.90.u2_ref, f32[14,40,512]{2,1,0:T(8,128)S(1)} %get-tuple-element.91.text_ref), custom_call_target="tpu_custom_call" | custom-call | flops 1073741824 | bytes 4194304 | tf_op jit(solution)/shard_map/post/pallas_call | solution.py:692
  27.1 4.1 %collective-permute-done.9.slab_b = bf16[10,16,256]{2,1,0:T(8,128)(2,1)S(1)} collective-permute-done((bf16[10,16,256]{2,1,0:T(8,128)(2,1)S(1)}, bf16[10,16,256]{2,1,0:T(8,128)(2,1)S(1)}, u32[]{:S(2)}, u32[]{:S(2)}) %collective-permute-start.9) | collective-permute-done | bytes 81952 | tf_op jit(solution)/shard_map/ppermute | solution.py:52
  31.2 0.8 %collective-permute-done.8.slab_a = bf16[10,16,256]{2,1,0:T(8,128)(2,1)S(1)} collective-permute-done((bf16[10,16,256]{2,1,0:T(8,128)(2,1)S(1)}, bf16[10,16,256]{2,1,0:T(8,128)(2,1)S(1)}, u32[]{:S(2)}, u32[]{:S(2)}) %collective-permute-start.8) | collective-permute-done | bytes 81952 | tf_op jit(solution)/shard_map/ppermute | solution.py:52
  32.0 0.0 collective-permute-done.10.rest_1_
  32.0 0.0 collective-permute-done.11.rest_2_
  32.0 0.0 collective-permute-done.12.rest_3_
  32.0 2.3 %correct.1 = (f32[8,32,512]{2,1,0:T(8,128)}, bf16[2304,128]{1,0:T(8,128)(2,1)}) custom-call(s32[1]{0:T(128)} %bitcast.me_ref, s32[1]{0:T(128)} %bitcast.1.slab_ref, f32[4,16,256]{2,1,0:T(8,128)S(1)} %get-tuple-element.84.ct_ref, bf16[1,16,256]{2,1,0:T(8,128)(2,1)S(1)} %collective-permute-done.6.side_a, ...), custom_call_target="tpu_custom_call" | custom-call | tf_op jit(solution)/shard_map/correct/pallas_call | solution.py:702
  (1 shorter events, 0.0 us)
Async XLA Ops:
  3.7 8.2 %collective-permute-start = (bf16[4,16,512]{2,1,0:T(8,128)(2,1)S(1)}, bf16[4,16,512]{2,1,0:T(8,128)(2,1)S(1)}, u32[]{:S(2)}, u32[]{:S(2)}) collective-permute-start(bf16[4,16,512]{2,1,0:T(8,128)(2,1)S(1)} %get-tuple-element.56), channel_id=1, source_target_pairs={{0,1},{1,0},{2,3},{3,2},{4,5},{5,4},{6,7},{7,6},{8,9},{9,8},{10,11... | collective-permute-start | bytes 196616 | tf_op jit(solution)/shard_map/ppermute | solution.py:52
  4.2 7.7 %collective-permute-start.1 = (bf16[4,16,512]{2,1,0:T(8,128)(2,1)S(1)}, bf16[4,16,512]{2,1,0:T(8,128)(2,1)S(1)}, u32[]{:S(2)}, u32[]{:S(2)}) collective-permute-start(bf16[4,16,512]{2,1,0:T(8,128)(2,1)S(1)} %get-tuple-element.57), channel_id=1, source_target_pairs={{0,3},{1,2},{2,1},{3,0},{4,7},{5,6},{6,5},{7,4},{8,11},{9,10},{10,... | collective-permute-start | bytes 196616 | tf_op jit(solution)/shard_map/ppermute | solution.py:52
  6.8 9.3 %collective-permute-start.2 = (bf16[8,16,512]{2,1,0:T(8,128)(2,1)S(1)}, bf16[8,16,512]{2,1,0:T(8,128)(2,1)S(1)}, u32[]{:S(2)}, u32[]{:S(2)}) collective-permute-start(bf16[8,16,512]{2,1,0:T(8,128)(2,1)S(1)} %get-tuple-element.58), channel_id=1, source_target_pairs={{0,4},{4,0},{8,12},{12,8},{16,20},{20,16},{24,28},{28,24},{1,5},{5... | collective-permute-start | bytes 393224 | tf_op jit(solution)/shard_map/ppermute | solution.py:52
  8.3 8.0 %collective-permute-start.3 = (bf16[8,16,512]{2,1,0:T(8,128)(2,1)S(1)}, bf16[8,16,512]{2,1,0:T(8,128)(2,1)S(1)}, u32[]{:S(2)}, u32[]{:S(2)}) collective-permute-start(bf16[8,16,512]{2,1,0:T(8,128)(2,1)S(1)} %get-tuple-element.59), channel_id=1, source_target_pairs={{0,28},{4,8},{8,4},{12,16},{16,12},{20,24},{24,20},{28,0},{1,29},{... | collective-permute-start | bytes 393224 | tf_op jit(solution)/shard_map/ppermute | solution.py:52
  12.0 5.5 %collective-permute-start.4 = (bf16[2,16,512]{2,1,0:T(8,128)(2,1)S(1)}, bf16[2,16,512]{2,1,0:T(8,128)(2,1)S(1)}, u32[]{:S(2)}, u32[]{:S(2)}) collective-permute-start(bf16[2,16,512]{2,1,0:T(8,128)(2,1)S(1)} %get-tuple-element.65), channel_id=1, source_target_pairs={{0,4},{4,0},{8,12},{12,8},{16,20},{20,16},{24,28},{28,24},{1,5},{5... | collective-permute-start | bytes 98312 | tf_op jit(solution)/shard_map/ppermute | solution.py:52
  12.1 6.7 %collective-permute-start.5 = (bf16[2,16,512]{2,1,0:T(8,128)(2,1)S(1)}, bf16[2,16,512]{2,1,0:T(8,128)(2,1)S(1)}, u32[]{:S(2)}, u32[]{:S(2)}) collective-permute-start(bf16[2,16,512]{2,1,0:T(8,128)(2,1)S(1)} %get-tuple-element.66), channel_id=1, source_target_pairs={{0,28},{4,8},{8,4},{12,16},{16,12},{20,24},{24,20},{28,0},{1,29},{... | collective-permute-start | bytes 98312 | tf_op jit(solution)/shard_map/ppermute | solution.py:52
  19.9 3.7 %collective-permute-start.6 = (bf16[1,16,256]{2,1,0:T(8,128)(2,1)S(1)}, bf16[1,16,256]{2,1,0:T(8,128)(2,1)S(1)}, u32[]{:S(2)}, u32[]{:S(2)}) collective-permute-start(bf16[1,16,256]{2,1,0:T(8,128)(2,1)S(1)} %get-tuple-element.85), channel_id=1, source_target_pairs={{0,1},{1,0},{2,3},{3,2},{4,5},{5,4},{6,7},{7,6},{8,9},{9,8},{10,11... | collective-permute-start | bytes 24584 | tf_op jit(solution)/shard_map/ppermute | solution.py:52
  20.0 3.6 %collective-permute-start.7 = (bf16[1,16,256]{2,1,0:T(8,128)(2,1)S(1)}, bf16[1,16,256]{2,1,0:T(8,128)(2,1)S(1)}, u32[]{:S(2)}, u32[]{:S(2)}) collective-permute-start(bf16[1,16,256]{2,1,0:T(8,128)(2,1)S(1)} %get-tuple-element.86), channel_id=1, source_target_pairs={{0,3},{1,2},{2,1},{3,0},{4,7},{5,6},{6,5},{7,4},{8,11},{9,10},{10,... | collective-permute-start | bytes 24584 | tf_op jit(solution)/shard_map/ppermute | solution.py:52
  20.6 11.4 %collective-permute-start.10 = (bf16[512,128]{1,0:T(8,128)(2,1)S(1)}, bf16[512,128]{1,0:T(8,128)(2,1)S(1)}, u32[]{:S(2)}, u32[]{:S(2)}) collective-permute-start(bf16[512,128]{1,0:T(8,128)(2,1)S(1)} %get-tuple-element.95), channel_id=1, source_target_pairs={{0,1},{1,2},{2,3},{3,0},{4,5},{5,6},{6,7},{7,4},{8,9},{9,10},{10,1... | collective-permute-start | bytes 393224 | tf_op jit(solution)/shard_map/ppermute | solution.py:40
  20.7 11.3 %collective-permute-start.11 = (bf16[512,128]{1,0:T(8,128)(2,1)S(1)}, bf16[512,128]{1,0:T(8,128)(2,1)S(1)}, u32[]{:S(2)}, u32[]{:S(2)}) collective-permute-start(bf16[512,128]{1,0:T(8,128)(2,1)S(1)} %get-tuple-element.96), channel_id=1, source_target_pairs={{0,2},{1,3},{2,0},{3,1},{4,6},{5,7},{6,4},{7,5},{8,10},{9,11},{10,... | collective-permute-start | bytes 393224 | tf_op jit(solution)/shard_map/ppermute | solution.py:40
  22.2 9.8 %collective-permute-start.12 = (bf16[512,128]{1,0:T(8,128)(2,1)S(1)}, bf16[512,128]{1,0:T(8,128)(2,1)S(1)}, u32[]{:S(2)}, u32[]{:S(2)}) collective-permute-start(bf16[512,128]{1,0:T(8,128)(2,1)S(1)} %get-tuple-element.97), channel_id=1, source_target_pairs={{0,3},{1,0},{2,1},{3,2},{4,7},{5,4},{6,5},{7,6},{8,11},{9,8},{10,9... | collective-permute-start | bytes 393224 | tf_op jit(solution)/shard_map/ppermute | solution.py:40
  23.6 7.6 %collective-permute-start.9 = (bf16[10,16,256]{2,1,0:T(8,128)(2,1)S(1)}, bf16[10,16,256]{2,1,0:T(8,128)(2,1)S(1)}, u32[]{:S(2)}, u32[]{:S(2)}) collective-permute-start(bf16[10,16,256]{2,1,0:T(8,128)(2,1)S(1)} %get-tuple-element.98), channel_id=1, source_target_pairs={{0,28},{4,8},{8,4},{12,16},{16,12},{20,24},{24,20},{28,0},{1,29},{... | collective-permute-start | bytes 245768 | tf_op jit(solution)/shard_map/ppermute | solution.py:52
  26.1 5.9 %collective-permute-start.8 = (bf16[10,16,256]{2,1,0:T(8,128)(2,1)S(1)}, bf16[10,16,256]{2,1,0:T(8,128)(2,1)S(1)}, u32[]{:S(2)}, u32[]{:S(2)}) collective-permute-start(bf16[10,16,256]{2,1,0:T(8,128)(2,1)S(1)} %get-tuple-element.99), channel_id=1, source_target_pairs={{0,4},{4,0},{8,12},{12,8},{16,20},{20,16},{24,28},{28,24},{1,5},{5... | collective-permute-start | bytes 245768 | tf_op jit(solution)/shard_map/ppermute | solution.py:52

commit v6 on v5

--- a/solution.py
+++ b/solution.py
@@ -66,13 +66,13 @@
     return (one == (two % LANES) * (nz // LANES) + two // LANES).astype(F32).astype(BF16)
 
 
-def begin_kernel(me_ref, slab_ref, *refs):
+def load_kernel(slab_ref, *refs):
     count = 10
     sources, refs = refs[:count], refs[count:]
-    u_ref, t_ref, sensed_ref, depth_a, depth_b, field_a, field_b, list_ref, *targets = refs[:-5]
-    raw, weight_ref, cell_ref, divide_ref, sem = refs[-5:]
-    targets = [cell_ref, raw, divide_ref, weight_ref] + targets
-    species_ref, death_ref = targets[4:6]
+    u_ref, place_ref, field_a, field_b, *targets = refs[:-2]
+    raw, sem = refs[-2:]
+    cell_ref = targets[0]
+    targets.insert(1, raw)
     copies = [
         pltpu.make_async_copy(source, target, sem.at[i])
         for i, (source, target) in enumerate(zip(sources, targets, strict=True))
@@ -80,22 +80,17 @@
     for copy in copies:
         copy.start()
     nx, ny, nz = u_ref.shape
-    agents = species_ref.shape[0]
     rows = nx * ny
     tiles = nz // LANES
     order = shuffle(nz, False)
     copies[0].wait()
-    cell = cell_ref[...]
-    cell_row = cell // nz
-    cell_z = cell - cell_row * nz
+    cell_z = cell_ref[...] % nz
     cell_z = (cell_z % tiles) * LANES + cell_z // tiles
-    one_z = (iota((nz, agents), 0) == cell_z).astype(F32).astype(BF16)
-    in_row = iota((rows, agents), 0) == cell_row
+    place_ref[...] = (iota(place_ref.shape, 0) == cell_z).astype(F32).astype(BF16)
     copies[1].wait()
     high, low = halves(raw[...].reshape(rows, nz))
-    high = dot(high, order, 1, 0)
-    u = high + dot(low, order, 1, 0)
-    u_ref[...] = u.reshape(nx, ny, nz)
+    both = dot(jnp.concatenate([high, low], axis=0), order, 1, 0)
+    u_ref[...] = (both[:rows] + both[rows:]).reshape(nx, ny, nz)
     half = ny // 16
     slab_even = is_even(slab_ref[0])
     for ref, front in ((field_a, slab_even), (field_b, jnp.logical_not(slab_even))):
@@ -104,7 +99,24 @@
             ref[k * half : (k + 1) * half] = u_ref[start + k].astype(BF16).reshape(half, 16, nz)
     for copy in copies[2:]:
         copy.wait()
-    picked = dot(high.astype(BF16), one_z, 1, 0)
+
+
+def uptake_kernel(
+    me_ref, u_ref, place_ref, cell_ref, divide_ref, weight_ref, species_ref, death_ref,
+    t_ref, sensed_ref, depth_a, depth_b, list_ref,
+):
+    nx, ny, nz = u_ref.shape
+    agents = species_ref.shape[0]
+    rows = nx * ny
+    tiles = nz // LANES
+    cell = cell_ref[...]
+    cell_row = cell // nz
+    cell_z = cell - cell_row * nz
+    cell_z = (cell_z % tiles) * LANES + cell_z // tiles
+    one_z = place_ref[...]
+    in_row = iota((rows, agents), 0) == cell_row
+    u = u_ref[...].reshape(rows, nz)
+    picked = dot(u.astype(BF16), one_z, 1, 0)
     sample = jnp.sum(jnp.where(in_row, picked, 0.0), axis=0, keepdims=True)
     sensed_ref[...] = jnp.broadcast_to(sample, (8, agents))
     weight = jnp.broadcast_to(weight_ref[...].reshape(1, -1), (8, species_ref.shape[1]))
@@ -114,9 +126,7 @@
     divide = divide_ref[...].reshape(1, agents).astype(F32)
     uptake = alive * (1.0 + divide) * softplus * sample / (0.5 + sample)
     up_high = uptake.astype(BF16).astype(F32)
-    a_high = jnp.where(in_row, up_high, 0.0).astype(BF16)
-    a_low = jnp.where(in_row, uptake - up_high, 0.0).astype(BF16)
-    source = dot(a_high, one_z, 1, 1) + dot(a_low, one_z, 1, 1)
+    source = dot(jnp.where(in_row, up_high, 0.0).astype(BF16), one_z, 1, 1)
     t_ref[...] = (SCREENING * u - source).reshape(nx, ny, nz)
     even = is_even(me_ref[0])
     for pair in range(nx // 2):
@@ -141,7 +151,7 @@
 ):
     agents, width = species_ref.shape
     depths = len(outs) - 2
-    capacity = outs[0].shape[0]
+    capacity = outs[0].shape[0] * 16
     species = species_ref[...]
     sensing = sensing_ref[...].reshape(1, width)
     first = sensing.astype(BF16)
@@ -173,6 +183,7 @@
     counts = dot(jnp.concatenate(hits, axis=0).astype(BF16), counter, 1, 0)
     me = me_ref[0]
     to_a = jnp.where(is_even(slab_ref[0]), 1, 2)
+    hop_a = jnp.where(is_even(me), 1, depths - 1)
     running = jnp.zeros((lines, lanes), F32)
     keys = []
     for block in range(blocks):
@@ -184,6 +195,7 @@
         rank = jnp.sum(jnp.where(line < depths, 0.0, before), axis=0, keepdims=True).astype(jnp.int32)
         hop = route[:, cut] - me
         hop = jnp.where(hop < 0, hop + depths, hop)
+        hop = jnp.where(hop == hop_a, 1, jnp.where(hop == depths - hop_a, 2, jnp.where(hop == 0, 0, hop + 1)))
         key = jnp.where(
             move[:, cut] == 0,
             hop * capacity + slot,
@@ -197,13 +209,10 @@
         chosen = (iota((size, agents), 0) == key - start).astype(F32).astype(BF16)
         placed = dot(chosen, updated, 1, 0).astype(BF16)
         start += size
-        if index < depths:
-            out[...] = placed
-        else:
-            tiles = out.shape[2] // width
-            for i in range(MIG // 16):
-                at = (i % tiles) * width
-                out[i // tiles, :, at : at + width] = placed[i * 16 : (i + 1) * 16]
+        blocks = out.shape[0]
+        for i in range(0, out.shape[2], width):
+            part = placed[i // width * blocks * 16 :][: blocks * 16]
+            out[:, :, i : i + width] = part.reshape(blocks, 16, width)
 
 
 def tiles_of(x):
@@ -448,7 +457,8 @@
 
 def post_kernel(depths, me_ref, u2_ref, text_ref, out_ref, back_ref, v1):
     nx, ny, nz = out_ref.shape
-    back_ref[...] = shuffle(nz, True)
+    back = shuffle(nz, True)
+    back_ref[...] = back
     mask = edge_mask(me_ref[0], depths, HALO)
 
     def first(p, carry):
@@ -464,35 +474,46 @@
         return carry
 
     lax.fori_loop(0, nx, second, 0, unroll=2)
+    high, low = halves(out_ref[...].reshape(nx * ny, nz))
+    both = dot(jnp.concatenate([high, low], axis=0), back, 1, 0)
+    out_ref[...] = (both[: nx * ny] + both[nx * ny :]).reshape(nx, ny, nz)
 
 
 def correct_kernel(
     depths, me_ref, slab_ref, ct_ref, side_a, side_b, slab_a, slab_b, base_ref, back_ref, *rest
 ):
-    packed = rest[:depths]
-    out_any, agents_ref, fine, out_ref, sem = rest[depths:]
+    packed = rest[: depths - 1]
+    out_any, agents_ref, fine, out_ref, sem = rest[depths - 1 :]
     nx, ny, nz = out_ref.shape
     cx, cy, cz = ct_ref.shape
     me = me_ref[0]
     even = is_even(me)
     slab_even = is_even(slab_ref[0])
-    capacity = packed[0].shape[0]
-    width = agents_ref.shape[1]
+    blocks = packed[0].shape[0]
+    width = agents_ref.shape[2]
     copies = []
-    for k in range(depths):
+
+    def place(source, start):
+        target = agents_ref.at[pl.ds(start, source.shape[0])]
+        copies.append(pltpu.make_async_copy(source, target, sem.at[len(copies)]))
+        copies[-1].start()
+
+    def place_wide(source, start):
+        for i in range(source.shape[2] // width):
+            part = source.at[:, :, pl.ds(i * width, width)]
+            place(part, start + i * source.shape[0])
+
+    up = jnp.where(me == depths - 1, 0, me + 1)
+    down = jnp.where(me == 0, depths - 1, me - 1)
+    place(packed[0], me * blocks)
+    place_wide(side_a.at[pl.ds(1, side_a.shape[0] - 1)], jnp.where(even, up, down) * blocks)
+    place(packed[1], jnp.where(even, down, up) * blocks)
+    for k in range(2, depths - 1):
         origin = me - k
-        origin = jnp.where(origin < 0, origin + depths, origin)
-        place = pl.ds(pl.multiple_of(origin * capacity, capacity), capacity)
-        copies.append(pltpu.make_async_copy(packed[k], agents_ref.at[place], sem.at[len(copies)]))
-    tiles = cz // width
+        place(packed[k], jnp.where(origin < 0, origin + depths, origin) * blocks)
     for ref, late in ((slab_a, slab_even), (slab_b, jnp.logical_not(slab_even))):
-        start = depths * capacity + jnp.where(late, MIG, 0)
-        for i in range(MIG // 16):
-            place = pl.ds(pl.multiple_of(start + i * 16, 16), 16)
-            source = ref.at[cx + 2 + i // tiles, :, pl.ds((i % tiles) * width, width)]
-            copies.append(pltpu.make_async_copy(source, agents_ref.at[place], sem.at[len(copies)]))
-    for copy in copies:
-        copy.start()
+        start = depths * blocks + jnp.where(late, MIG // 16, 0)
+        place_wide(ref.at[pl.ds(cx + 2, ref.shape[0] - cx - 2)], start)
     mask = edge_mask(me, depths, HALO)
 
     def chosen(condition, x, y):
@@ -547,7 +568,7 @@
         return jnp.concatenate([part for part in tiles_of(plane) for _ in range(2)], axis=1)
 
     back = back_ref[...]
-    step = 2
+    step = 4
     for start in range(0, nx, step):
         planes = []
         for p in range(start, start + step):
@@ -556,10 +577,9 @@
             none = (KEEP * plane + PULL * total)[:ny]
             one = (2.0 * PULL) * plane[:ny]
             two = (PULL * PULL) * spread[(p + 2) // 2][:ny]
-            planes.append(base_ref[p] + twice(none) + third_sum(twice(one) + third_sum(twice(two))))
-        high, low = halves(jnp.concatenate(planes, axis=0))
-        done = dot(high, back, 1, 0) + dot(low, back, 1, 0)
-        out_ref[start : start + step] = done.reshape(step, ny, nz)
+            planes.append(twice(none) + third_sum(twice(one) + third_sum(twice(two))))
+        done = dot(jnp.concatenate(planes, axis=0).astype(BF16), back, 1, 0)
+        out_ref[start : start + step] = base_ref[start : start + step] + done.reshape(step, ny, nz)
         cut = pl.ds(start, step)
         copies.append(pltpu.make_async_copy(out_ref.at[cut], out_any.at[cut], sem.at[len(copies)]))
         copies[-1].start()
@@ -580,43 +600,48 @@
     cells, death, divide = (x.reshape(1, agents) for x in (agent_cell, death_flag, divide_flag))
     move, route = slab_move.reshape(1, agents), depth_route.reshape(1, agents)
     half = ny // 16
-    if agents % nz or nx * ny > PART or nz % PART:
+    if agents % nz or nx * ny > PART or nz % PART or depths < 4:
         raise ValueError("list digits")
     arguments = (
         cells, nutrient, divide, uptake_weight.reshape(1, width), species, death,
         move, route, net_weight, sensing.reshape(1, width),
     )
     (
-        nutrient, target, sensed, depth_a, depth_b, field_a, field_b, agent_list,
-        species, death, move, route, net_weight, sensing,
+        nutrient, places, field_a, field_b, cells, divide, weight, species, death, move, route, net_weight, sensing
     ) = pl.pallas_call(
-        begin_kernel,
+        load_kernel,
         out_shape=(
             shape((nx, ny, nz), F32),
+            shape((nz, agents), BF16),
+            shape((HALO * half, 16, nz), BF16),
+            shape((HALO * half, 16, nz), BF16),
+        )
+        + tuple(shape(x.shape, x.dtype) for i, x in enumerate(arguments) if i != 1),
+        in_specs=[SMEM_SPEC] + [HBM_SPEC] * len(arguments),
+        out_specs=[VMEM_SPEC] * (4 + len(arguments) - 1),
+        scratch_shapes=[
+            pltpu.VMEM((nx, ny, nz), F32),
+            pltpu.SemaphoreType.DMA((len(arguments),)),
+        ],
+        compiler_params=PARAMS,
+        name="load",
+    )(slab, *(pltpu.with_memory_space_constraint(x, pltpu.HBM) for x in arguments))
+    target, sensed, depth_a, depth_b, agent_list = pl.pallas_call(
+        uptake_kernel,
+        out_shape=(
             shape((nx, ny, nz), F32),
             shape((8, agents), F32),
             shape((nx // 2, 16, nz), BF16),
             shape((nx // 2, 16, nz), BF16),
-            shape((HALO * half, 16, nz), BF16),
-            shape((HALO * half, 16, nz), BF16),
             shape((4 * agents // nz, nz), F32),
-        )
-        + tuple(shape(x.shape, x.dtype) for x in arguments[4:]),
-        in_specs=[SMEM_SPEC] * 2 + [HBM_SPEC] * len(arguments),
-        out_specs=[VMEM_SPEC] * (8 + len(arguments) - 4),
-        scratch_shapes=[
-            pltpu.VMEM((nx, ny, nz), F32),
-            pltpu.VMEM((1, width), BF16),
-            pltpu.VMEM((1, agents), jnp.int32),
-            pltpu.VMEM((1, agents), jnp.int32),
-            pltpu.SemaphoreType.DMA((len(arguments),)),
-        ],
+        ),
+        in_specs=[SMEM_SPEC] + [VMEM_SPEC] * 7,
+        out_specs=[VMEM_SPEC] * 5,
         compiler_params=PARAMS,
-        name="begin",
-    )(me, slab, *(pltpu.with_memory_space_constraint(x, pltpu.HBM) for x in arguments))
-    field_a, field_b, depth_a, depth_b = lax.optimization_barrier(
-        (field_a, field_b, depth_a, depth_b)
-    )
+        cost_estimate=pl.CostEstimate(flops=1 << 31, bytes_accessed=1 << 20, transcendentals=0),
+        name="uptake",
+    )(me, nutrient, places, cells, divide, weight, species, death)
+    field_a, field_b, depth_a, depth_b = lax.optimization_barrier((field_a, field_b, depth_a, depth_b))
     side_a = swapped(depth_a, "depth", "a")
     side_b = swapped(depth_b, "depth", "b")
     field_a = swapped(field_a, "slab", "a")
@@ -637,7 +662,10 @@
     ext = ny + 2 * HALO
     sent = pl.pallas_call(
         network_kernel,
-        out_shape=tuple(shape((capacity, width), BF16) for _ in range(depths))
+        out_shape=tuple(
+            shape((capacity // 32, 16, 2 * width) if k == 1 else (capacity // 16, 16, width), BF16)
+            for k in range(depths)
+        )
         + tuple(shape((MIG * width // (16 * cz), 16, cz), BF16) for _ in range(2)),
         in_specs=[SMEM_SPEC] * 2 + [VMEM_SPEC] * 7,
         out_specs=[VMEM_SPEC] * (depths + 2),
@@ -682,11 +710,12 @@
         compiler_params=PARAMS,
         name="smooth",
     )(me, slab, u0, text, u1, u2, inside, slab_a, slab_b)
-    arrived = [sent[0]] + [cyclic(sent[k], "depth", k) for k in range(1, depths)]
-    coarse_a = swapped(coarse_a, "depth", "a")
+    coarse_a = swapped(jnp.concatenate([coarse_a, sent[1]], axis=0), "depth", "a")
     coarse_b = swapped(coarse_b, "depth", "b")
+    arrived = [sent[0], swapped(sent[2], "depth", "b")]
+    arrived += [cyclic(sent[k + 1], "depth", k) for k in range(2, depths - 1)]
     tail_a, tail_b = (
-        swapped(jnp.concatenate([ct_all, coarse_a, coarse_b, movers], axis=0), "slab", which)
+        swapped(jnp.concatenate([ct_all, coarse_a[:1], coarse_b, movers], axis=0), "slab", which)
         for which, movers in (("a", sent[depths]), ("b", sent[depths + 1]))
     )
     base, back = pl.pallas_call(
@@ -699,22 +728,23 @@
         cost_estimate=pl.CostEstimate(flops=1 << 30, bytes_accessed=1 << 22, transcendentals=0),
         name="post",
     )(me, u2, text)
-    return pl.pallas_call(
+    grid_field, agents_out = pl.pallas_call(
         functools.partial(correct_kernel, depths),
         out_shape=(
             shape((nx, ny, nz), F32),
-            shape((depths * capacity + 2 * MIG, width), BF16),
+            shape(((depths * capacity + 2 * MIG) // 16, 16, width), BF16),
         ),
-        in_specs=[SMEM_SPEC] * 2 + [VMEM_SPEC] * 7 + [ANY_SPEC] * depths,
+        in_specs=[SMEM_SPEC] * 2 + [VMEM_SPEC] * 7 + [ANY_SPEC] * (depths - 1),
         out_specs=[HBM_SPEC, ANY_SPEC],
         scratch_shapes=[
             pltpu.VMEM((cx + 2, cz // LANES, ext, LANES), F32),
             pltpu.VMEM((nx, ny, nz), F32),
-            pltpu.SemaphoreType.DMA((depths + 2 * (MIG // 16) + nx // 2,)),
+            pltpu.SemaphoreType.DMA((depths + 5 + nx,)),
         ],
         compiler_params=PARAMS,
         name="correct",
     )(me, slab, ct, coarse_a, coarse_b, tail_a, tail_b, base, back, *arrived)
+    return grid_field, agents_out.reshape(-1, width)
 
 
 def solution(mesh):

time: 34.4 us -> 33.6 us (0.977)
  starting transfers between devices: 16.7 us -> 15.4 us
  waiting for transfers between devices: 6.28 us -> 6.97 us
    ppermute x3 -> x1, starting transfers between devices: 2.99 us -> 0.5 us  [cyclic(): return lax.ppermute(x, axis, [(i, (i + by) % count) for i in range(count)])]
    ppermute x3 -> x1, waiting for transfers between devices: 0.01 us -> 2.15 us  [cyclic(): return lax.ppermute(x, axis, [(i, (i + by) % count) for i in range(count)])]
    ppermute x10 -> x11, waiting for transfers between devices: 6.27 us -> 4.82 us  [swapped(): return lax.ppermute(x, axis, sorted(pairs))]
    ppermute x10 -> x11, starting transfers between devices: 13.7 us -> 14.9 us  [swapped(): return lax.ppermute(x, axis, sorted(pairs))]
    pallas_call x1, Pallas kernels: 0.98 us -> 1.5 us  [local(): pl.pallas_call(functools.partial(post_kernel, depths), out_shape=(shape((...]
    pallas_call x1, Pallas kernels: 2.25 us -> 1.84 us  [local(): pl.pallas_call(functools.partial(correct_kernel, depths), out_shape=(shap...]
    pallas_call x2 -> x3, Pallas kernels: 4.83 us -> 4.45 us  [the longest x1 1.79 us: local(): pl.pallas_call(network_kernel, out_shape=tuple((shape((capacity // 32, 16...]
  transfers between devices with their start and end apart: 13 -> 12, of which waited for: 4 -> 6; matrix products, arithmetic and copies ran while one was open for 0% -> 0% of each run, Pallas kernels for 12% -> 14%
where the time goes in v6:
time: 33.6 us; the launch traced here: 33.4 us
  starting transfers between devices  15.4 us (46%)
  Pallas kernels  10.2 us (30%)
  waiting for transfers between devices  6.97 us (21%)
  between operations  0.73 us (2%)
    ppermute x11, starting transfers between devices, swapped(): return lax.ppermute(x, axis, sorted(pairs))  14.9 us
    ppermute x11, waiting for transfers between devices, swapped(): return lax.ppermute(x, axis, sorted(pairs))  4.82 us
    ppermute x1, waiting for transfers between devices, cyclic(): return lax.ppermute(x, axis, [(i, (i + by) % count) for i in range(count)])  2.15 us
    pallas_call x1, Pallas kernels, local(): pl.pallas_call(functools.partial(correct_kernel, depths), out_shape=(shap...  1.84 us
    pallas_call x1, Pallas kernels, local(): pl.pallas_call(network_kernel, out_shape=tuple((shape((capacity // 32, 16...  1.79 us
    pallas_call x1, Pallas kernels, local(): pl.pallas_call(load_kernel, out_shape=(shape((nx, ny, nz), F32), shape((n...  1.65 us
    pallas_call x1, Pallas kernels, local(): pl.pallas_call(functools.partial(post_kernel, depths), out_shape=(shape((...  1.5 us
    pallas_call x1, Pallas kernels, local(): pl.pallas_call(functools.partial(inner_kernel, depths), out_shape=(shape(...  1.21 us
  transfers between devices with their start and end apart: 12, of which 6 were waited for; matrix products, arithmetic and copies ran while one was open for 0% of the time, Pallas kernels for 14%

profile of v6, /device:TPU:0, one launch (start us, length us, event | category | flops | bytes accessed | tf_op | source)
XLA Modules:
  0.0 33.4 jit_solution(5563461406603624494)
XLA Ops:
  0.6 1.7 %load.1 = (f32[8,32,512]{2,1,0:T(8,128)S(1)}, bf16[512,1024]{1,0:T(8,128)(2,1)S(1)}, bf16[8,16,512]{2,1,0:T(8,128)(2,1)S(1)}, bf16[8,16,512]{2,1,0:T(8,128)(2,1)...) custom-call(s32[1]{0:T(128)} %bitcast.1.slab_ref, ...), custom_call_target="tpu_custom_call" | custom-call | tf_op jit(solution)/shard_map/load/pallas_call | solution.py:611
  2.3 1.0 %uptake.1 = (f32[8,32,512]{2,1,0:T(8,128)S(1)}, f32[8,1024]{1,0:T(8,128)S(1)}, bf16[4,16,512]{2,1,0:T(8,128)(2,1)S(1)}, bf16[4,16,512]{2,1,0:T(8,128)(2,1)S(1)}, f32[8,512]{1,0:T(8,128)S(1)}) custom-call(s32[1]{0:T(128)} %bitcast.me_ref, f32[8,32,512]{2,1,0:T(8,128)S(1)} %get-tuple-element.56.u_ref, bf16[512,1024]{1,0:T(8,128)(2,1)S(1)} %get-tuple-element.57.place_ref, ...), custom_call_target="tpu_custom_call" | custom-call | flops 2147483648 | bytes 1048576 | tf_op jit(solution)/shard_map/uptake/pallas_call | solution.py:629
  3.3 0.5 %collective-permute-start = (bf16[4,16,512]{2,1,0:T(8,128)(2,1)S(1)}, bf16[4,16,512]{2,1,0:T(8,128)(2,1)S(1)}, u32[]{:S(2)}, u32[]{:S(2)}) collective-permute-start(bf16[4,16,512]{2,1,0:T(8,128)(2,1)S(1)} %get-tuple-element.68), channel_id=1, source_target_pairs={{0,1},{1,0},{2,3},{3,2},{4,5},{5,4},{6,7},{7,6},{8,9},{9,8},{10,11... | collective-permute-start | bytes 196616 | tf_op jit(solution)/shard_map/ppermute | solution.py:52
  3.8 2.6 %collective-permute-start.1 = (bf16[4,16,512]{2,1,0:T(8,128)(2,1)S(1)}, bf16[4,16,512]{2,1,0:T(8,128)(2,1)S(1)}, u32[]{:S(2)}, u32[]{:S(2)}) collective-permute-start(bf16[4,16,512]{2,1,0:T(8,128)(2,1)S(1)} %get-tuple-element.69), channel_id=1, source_target_pairs={{0,3},{1,2},{2,1},{3,0},{4,7},{5,6},{6,5},{7,4},{8,11},{9,10},{10,... | collective-permute-start | bytes 196616 | tf_op jit(solution)/shard_map/ppermute | solution.py:52
  6.5 1.5 %collective-permute-start.2 = (bf16[8,16,512]{2,1,0:T(8,128)(2,1)S(1)}, bf16[8,16,512]{2,1,0:T(8,128)(2,1)S(1)}, u32[]{:S(2)}, u32[]{:S(2)}) collective-permute-start(bf16[8,16,512]{2,1,0:T(8,128)(2,1)S(1)} %get-tuple-element.70), channel_id=1, source_target_pairs={{0,4},{4,0},{8,12},{12,8},{16,20},{20,16},{24,28},{28,24},{1,5},{5... | collective-permute-start | bytes 393224 | tf_op jit(solution)/shard_map/ppermute | solution.py:52
  8.0 3.6 %collective-permute-start.3 = (bf16[8,16,512]{2,1,0:T(8,128)(2,1)S(1)}, bf16[8,16,512]{2,1,0:T(8,128)(2,1)S(1)}, u32[]{:S(2)}, u32[]{:S(2)}) collective-permute-start(bf16[8,16,512]{2,1,0:T(8,128)(2,1)S(1)} %get-tuple-element.71), channel_id=1, source_target_pairs={{0,28},{4,8},{8,4},{12,16},{16,12},{20,24},{24,20},{28,0},{1,29},{... | collective-permute-start | bytes 393224 | tf_op jit(solution)/shard_map/ppermute | solution.py:52
  11.5 0.0 collective-permute-done.side_a
  11.5 0.0 collective-permute-done.1.side_b
  11.5 0.1 corner.1
  11.6 0.1 collective-permute-start.4
  11.7 2.3 %collective-permute-start.5 = (bf16[2,16,512]{2,1,0:T(8,128)(2,1)S(1)}, bf16[2,16,512]{2,1,0:T(8,128)(2,1)S(1)}, u32[]{:S(2)}, u32[]{:S(2)}) collective-permute-start(bf16[2,16,512]{2,1,0:T(8,128)(2,1)S(1)} %get-tuple-element.78), channel_id=1, source_target_pairs={{0,28},{4,8},{8,4},{12,16},{16,12},{20,24},{24,20},{28,0},{1,29},{... | collective-permute-start | bytes 98312 | tf_op jit(solution)/shard_map/ppermute | solution.py:52
  13.9 1.8 %network.1 = (bf16[32,16,128]{2,1,0:T(8,128)(2,1)S(1)}, bf16[16,16,256]{2,1,0:T(8,128)(2,1)S(1)}, bf16[32,16,128]{2,1,0:T(8,128)(2,1)S(1)}, bf16[32,16,128]{2,1,...) custom-call(s32[1]{0:T(128)} %bitcast.me_ref, s32[1]{0:T(128)} %bitcast.1.slab_ref, ...), custom_call_target="tpu_custom_call" | custom-call | flops 2147483648 | bytes 1048576 | tf_op jit(solution)/shard_map/network/pallas_call | solution.py:663
  15.7 0.0 collective-permute-done.2.field_a
  15.8 0.2 collective-permute-done.3.field_b
  15.9 1.2 %inner.1 = (f32[16,40,512]{2,1,0:T(8,128)S(1)}, f32[14,40,512]{2,1,0:T(8,128)S(1)}, f32[14,40,512]{2,1,0:T(8,128)S(1)}, f32[12,40,512]{2,1,0:T(8,128)S(1)}, f32[4,32,512]{2,1,0:T(8,128)S(1)}) custom-call(s32[1]{0:T(128)} %bitcast.me_ref, s32[1]{0:T(128)} %bitcast.1.slab_ref, f32[8,32,512]{2,1,0:T(8,128)S(1)} %get-tuple-element.56.u_ref, ...), custom_call_target="tpu_custom_call" | custom-call | flops 1048576 | bytes 1048576 | tf_op jit(solution)/shard_map/inner/pallas_call | solution.py:676
  17.2 0.0 collective-permute-done.4.slab_a
  17.2 1.2 %collective-permute-done.5.slab_b = bf16[2,16,512]{2,1,0:T(8,128)(2,1)S(1)} collective-permute-done((bf16[2,16,512]{2,1,0:T(8,128)(2,1)S(1)}, bf16[2,16,512]{2,1,0:T(8,128)(2,1)S(1)}, u32[]{:S(2)}, u32[]{:S(2)}) %collective-permute-start.5) | collective-permute-done | bytes 32800 | tf_op jit(solution)/shard_map/ppermute | solution.py:52
  18.4 1.2 %smooth.1 = (f32[14,40,512]{2,1,0:T(8,128)S(1)}, f32[14,40,512]{2,1,0:T(8,128)S(1)}, f32[12,40,512]{2,1,0:T(8,128)S(1)}, f32[4,16,256]{2,1,0:T(8,128)S(1)}, bf16...) custom-call(s32[1]{0:T(128)} %bitcast.me_ref, ...), custom_call_target="tpu_custom_call", output_to_operand_aliasing={{0}: (3, {}), {1}: (4, {}), {2}: (5, {})} | custom-call | tf_op jit(solution)/shard_map/smooth/pallas_call | solution.py:692
  19.6 0.1 collective-permute-start.6
  19.7 0.6 %collective-permute-start.7 = (bf16[1,16,256]{2,1,0:T(8,128)(2,1)S(1)}, bf16[1,16,256]{2,1,0:T(8,128)(2,1)S(1)}, u32[]{:S(2)}, u32[]{:S(2)}) collective-permute-start(bf16[1,16,256]{2,1,0:T(8,128)(2,1)S(1)} %get-tuple-element.97), channel_id=1, source_target_pairs={{0,3},{1,2},{2,1},{3,0},{4,7},{5,6},{6,5},{7,4},{8,11},{9,10},{10,... | collective-permute-start | bytes 24584 | tf_op jit(solution)/shard_map/ppermute | solution.py:52
  20.3 1.2 %collective-permute-start.10 = (bf16[32,16,128]{2,1,0:T(8,128)(2,1)S(1)}, bf16[32,16,128]{2,1,0:T(8,128)(2,1)S(1)}, u32[]{:S(2)}, u32[]{:S(2)}) collective-permute-start(bf16[32,16,128]{2,1,0:T(8,128)(2,1)S(1)} %get-tuple-element.106), channel_id=1, source_target_pairs={{0,3},{1,2},{2,1},{3,0},{4,7},{5,6},{6,5},{7,4},{8,11},{9,10},{10,... | collective-permute-start | bytes 393224 | tf_op jit(solution)/shard_map/ppermute | solution.py:52
  21.5 0.5 %collective-permute-start.11 = (bf16[32,16,128]{2,1,0:T(8,128)(2,1)S(1)}, bf16[32,16,128]{2,1,0:T(8,128)(2,1)S(1)}, u32[]{:S(2)}, u32[]{:S(2)}) collective-permute-start(bf16[32,16,128]{2,1,0:T(8,128)(2,1)S(1)} %get-tuple-element.107), channel_id=1, source_target_pairs={{0,2},{1,3},{2,0},{3,1},{4,6},{5,7},{6,4},{7,5},{8,10},{9,11},{10,... | collective-permute-start | bytes 393224 | tf_op jit(solution)/shard_map/ppermute | solution.py:40
  22.0 0.0 collective-permute-done.6.side_a
  22.0 0.8 %collective-permute-done.7.side_b = bf16[1,16,256]{2,1,0:T(8,128)(2,1)S(1)} collective-permute-done((bf16[1,16,256]{2,1,0:T(8,128)(2,1)S(1)}, bf16[1,16,256]{2,1,0:T(8,128)(2,1)S(1)}, u32[]{:S(2)}, u32[]{:S(2)}) %collective-permute-start.7) | collective-permute-done | bytes 8224 | tf_op jit(solution)/shard_map/ppermute | solution.py:52
  22.8 2.5 %collective-permute-start.9 = (bf16[10,16,256]{2,1,0:T(8,128)(2,1)S(1)}, bf16[10,16,256]{2,1,0:T(8,128)(2,1)S(1)}, u32[]{:S(2)}, u32[]{:S(2)}) collective-permute-start(bf16[10,16,256]{2,1,0:T(8,128)(2,1)S(1)} %get-tuple-element.110), channel_id=1, source_target_pairs={{0,28},{4,8},{8,4},{12,16},{16,12},{20,24},{24,20},{28,0},{1,29},{... | collective-permute-start | bytes 245768 | tf_op jit(solution)/shard_map/ppermute | solution.py:52
  25.3 0.0 collective-permute-start.8
  25.3 1.5 %post.1 = (f32[8,32,512]{2,1,0:T(8,128)S(1)}, bf16[512,512]{1,0:T(8,128)(2,1)S(1)}) custom-call(s32[1]{0:T(128)} %bitcast.me_ref, f32[12,40,512]{2,1,0:T(8,128)S(1)} %get-tuple-element.101.u2_ref, f32[14,40,512]{2,1,0:T(8,128)S(1)} %get-tuple-element.102.text_ref), custom_call_target="tpu_custom_call" | custom-call | flops 1073741824 | bytes 4194304 | tf_op jit(solution)/shard_map/post/pallas_call | solution.py:721
  26.8 0.0 collective-permute-done.10.rest_1_
  26.8 2.1 %collective-permute-done.11.rest_2_ = bf16[32,16,128]{2,1,0:T(8,128)(2,1)S(1)} collective-permute-done((bf16[32,16,128]{2,1,0:T(8,128)(2,1)S(1)}, bf16[32,16,128]{2,1,0:T(8,128)(2,1)S(1)}, u32[]{:S(2)}, u32[]{:S(2)}) %collective-permute-start.11) | collective-permute-done | bytes 131104 | tf_op jit(solution)/shard_map/ppermute | solution.py:40
  29.0 1.9 %collective-permute-done.9.slab_b = bf16[10,16,256]{2,1,0:T(8,128)(2,1)S(1)} collective-permute-done((bf16[10,16,256]{2,1,0:T(8,128)(2,1)S(1)}, bf16[10,16,256]{2,1,0:T(8,128)(2,1)S(1)}, u32[]{:S(2)}, u32[]{:S(2)}) %collective-permute-start.9) | collective-permute-done | bytes 81952 | tf_op jit(solution)/shard_map/ppermute | solution.py:52
  30.9 0.7 %collective-permute-done.8.slab_a = bf16[10,16,256]{2,1,0:T(8,128)(2,1)S(1)} collective-permute-done((bf16[10,16,256]{2,1,0:T(8,128)(2,1)S(1)}, bf16[10,16,256]{2,1,0:T(8,128)(2,1)S(1)}, u32[]{:S(2)}, u32[]{:S(2)}) %collective-permute-start.8) | collective-permute-done | bytes 81952 | tf_op jit(solution)/shard_map/ppermute | solution.py:52
  31.6 1.8 %correct.1 = (f32[8,32,512]{2,1,0:T(8,128)}, bf16[144,16,128]{2,1,0:T(8,128)(2,1)}) custom-call(s32[1]{0:T(128)} %bitcast.me_ref, s32[1]{0:T(128)} %bitcast.1.slab_ref, f32[4,16,256]{2,1,0:T(8,128)S(1)} %get-tuple-element.94.ct_ref, bf16[17,16,256]{2,1,0:T(8,128)(2,1)S(1)} %collective-permute-done.6.side_a, ...), custom_call_target="tpu_custom_call" | custom-call | tf_op jit(solution)/shard_map/correct/pallas_call | solution.py:731
  (3 shorter events, 0.0 us)
Async XLA Ops:
  3.3 8.2 %collective-permute-start = (bf16[4,16,512]{2,1,0:T(8,128)(2,1)S(1)}, bf16[4,16,512]{2,1,0:T(8,128)(2,1)S(1)}, u32[]{:S(2)}, u32[]{:S(2)}) collective-permute-start(bf16[4,16,512]{2,1,0:T(8,128)(2,1)S(1)} %get-tuple-element.68), channel_id=1, source_target_pairs={{0,1},{1,0},{2,3},{3,2},{4,5},{5,4},{6,7},{7,6},{8,9},{9,8},{10,11... | collective-permute-start | bytes 196616 | tf_op jit(solution)/shard_map/ppermute | solution.py:52
  3.8 7.7 %collective-permute-start.1 = (bf16[4,16,512]{2,1,0:T(8,128)(2,1)S(1)}, bf16[4,16,512]{2,1,0:T(8,128)(2,1)S(1)}, u32[]{:S(2)}, u32[]{:S(2)}) collective-permute-start(bf16[4,16,512]{2,1,0:T(8,128)(2,1)S(1)} %get-tuple-element.69), channel_id=1, source_target_pairs={{0,3},{1,2},{2,1},{3,0},{4,7},{5,6},{6,5},{7,4},{8,11},{9,10},{10,... | collective-permute-start | bytes 196616 | tf_op jit(solution)/shard_map/ppermute | solution.py:52
  6.5 9.3 %collective-permute-start.2 = (bf16[8,16,512]{2,1,0:T(8,128)(2,1)S(1)}, bf16[8,16,512]{2,1,0:T(8,128)(2,1)S(1)}, u32[]{:S(2)}, u32[]{:S(2)}) collective-permute-start(bf16[8,16,512]{2,1,0:T(8,128)(2,1)S(1)} %get-tuple-element.70), channel_id=1, source_target_pairs={{0,4},{4,0},{8,12},{12,8},{16,20},{20,16},{24,28},{28,24},{1,5},{5... | collective-permute-start | bytes 393224 | tf_op jit(solution)/shard_map/ppermute | solution.py:52
  8.0 8.0 %collective-permute-start.3 = (bf16[8,16,512]{2,1,0:T(8,128)(2,1)S(1)}, bf16[8,16,512]{2,1,0:T(8,128)(2,1)S(1)}, u32[]{:S(2)}, u32[]{:S(2)}) collective-permute-start(bf16[8,16,512]{2,1,0:T(8,128)(2,1)S(1)} %get-tuple-element.71), channel_id=1, source_target_pairs={{0,28},{4,8},{8,4},{12,16},{16,12},{20,24},{24,20},{28,0},{1,29},{... | collective-permute-start | bytes 393224 | tf_op jit(solution)/shard_map/ppermute | solution.py:52
  11.6 5.6 %collective-permute-start.4 = (bf16[2,16,512]{2,1,0:T(8,128)(2,1)S(1)}, bf16[2,16,512]{2,1,0:T(8,128)(2,1)S(1)}, u32[]{:S(2)}, u32[]{:S(2)}) collective-permute-start(bf16[2,16,512]{2,1,0:T(8,128)(2,1)S(1)} %get-tuple-element.77), channel_id=1, source_target_pairs={{0,4},{4,0},{8,12},{12,8},{16,20},{20,16},{24,28},{28,24},{1,5},{5... | collective-permute-start | bytes 98312 | tf_op jit(solution)/shard_map/ppermute | solution.py:52
  11.7 6.7 %collective-permute-start.5 = (bf16[2,16,512]{2,1,0:T(8,128)(2,1)S(1)}, bf16[2,16,512]{2,1,0:T(8,128)(2,1)S(1)}, u32[]{:S(2)}, u32[]{:S(2)}) collective-permute-start(bf16[2,16,512]{2,1,0:T(8,128)(2,1)S(1)} %get-tuple-element.78), channel_id=1, source_target_pairs={{0,28},{4,8},{8,4},{12,16},{16,12},{20,24},{24,20},{28,0},{1,29},{... | collective-permute-start | bytes 98312 | tf_op jit(solution)/shard_map/ppermute | solution.py:52
  19.6 2.4 %collective-permute-start.6 = (bf16[17,16,256]{2,1,0:T(8,128)(2,1)S(1)}, bf16[17,16,256]{2,1,0:T(8,128)(2,1)S(1)}, u32[]{:S(2)}, u32[]{:S(2)}) collective-permute-start(bf16[17,16,256]{2,1,0:T(8,128)(2,1)S(1)} %pad_maximum_fusion), channel_id=1, source_target_pairs={{0,1},{1,0},{2,3},{3,2},{4,5},{5,4},{6,7},{7,6},{8,9},{9,8},{10,11... | collective-permute-start | bytes 417800 | tf_op jit(solution)/shard_map/ppermute | solution.py:52
  19.7 3.1 %collective-permute-start.7 = (bf16[1,16,256]{2,1,0:T(8,128)(2,1)S(1)}, bf16[1,16,256]{2,1,0:T(8,128)(2,1)S(1)}, u32[]{:S(2)}, u32[]{:S(2)}) collective-permute-start(bf16[1,16,256]{2,1,0:T(8,128)(2,1)S(1)} %get-tuple-element.97), channel_id=1, source_target_pairs={{0,3},{1,2},{2,1},{3,0},{4,7},{5,6},{6,5},{7,4},{8,11},{9,10},{10,... | collective-permute-start | bytes 24584 | tf_op jit(solution)/shard_map/ppermute | solution.py:52
  20.3 6.5 %collective-permute-start.10 = (bf16[32,16,128]{2,1,0:T(8,128)(2,1)S(1)}, bf16[32,16,128]{2,1,0:T(8,128)(2,1)S(1)}, u32[]{:S(2)}, u32[]{:S(2)}) collective-permute-start(bf16[32,16,128]{2,1,0:T(8,128)(2,1)S(1)} %get-tuple-element.106), channel_id=1, source_target_pairs={{0,3},{1,2},{2,1},{3,0},{4,7},{5,6},{6,5},{7,4},{8,11},{9,10},{10,... | collective-permute-start | bytes 393224 | tf_op jit(solution)/shard_map/ppermute | solution.py:52
  21.5 7.5 %collective-permute-start.11 = (bf16[32,16,128]{2,1,0:T(8,128)(2,1)S(1)}, bf16[32,16,128]{2,1,0:T(8,128)(2,1)S(1)}, u32[]{:S(2)}, u32[]{:S(2)}) collective-permute-start(bf16[32,16,128]{2,1,0:T(8,128)(2,1)S(1)} %get-tuple-element.107), channel_id=1, source_target_pairs={{0,2},{1,3},{2,0},{3,1},{4,6},{5,7},{6,4},{7,5},{8,10},{9,11},{10,... | collective-permute-start | bytes 393224 | tf_op jit(solution)/shard_map/ppermute | solution.py:40
  22.8 8.0 %collective-permute-start.9 = (bf16[10,16,256]{2,1,0:T(8,128)(2,1)S(1)}, bf16[10,16,256]{2,1,0:T(8,128)(2,1)S(1)}, u32[]{:S(2)}, u32[]{:S(2)}) collective-permute-start(bf16[10,16,256]{2,1,0:T(8,128)(2,1)S(1)} %get-tuple-element.110), channel_id=1, source_target_pairs={{0,28},{4,8},{8,4},{12,16},{16,12},{20,24},{24,20},{28,0},{1,29},{... | collective-permute-start | bytes 245768 | tf_op jit(solution)/shard_map/ppermute | solution.py:52
  25.3 6.3 %collective-permute-start.8 = (bf16[10,16,256]{2,1,0:T(8,128)(2,1)S(1)}, bf16[10,16,256]{2,1,0:T(8,128)(2,1)S(1)}, u32[]{:S(2)}, u32[]{:S(2)}) collective-permute-start(bf16[10,16,256]{2,1,0:T(8,128)(2,1)S(1)} %get-tuple-element.111), channel_id=1, source_target_pairs={{0,4},{4,0},{8,12},{12,8},{16,20},{20,16},{24,28},{28,24},{1,5},{5... | collective-permute-start | bytes 245768 | tf_op jit(solution)/shard_map/ppermute | solution.py:52

commit v7 on v6

--- a/solution.py
+++ b/solution.py
@@ -374,12 +374,12 @@
     corner = HALO * near // 2 + near * (near - 1) // 2
     row = iota((8, 1), 0)
     first, last = (row == 0).astype(F32), (row == 7).astype(F32)
-    for ref, after in ((slab_a, slab_even), (slab_b, jnp.logical_not(slab_even))):
+    sides = ((slab_a, slab_even), (slab_b, jnp.logical_not(slab_even)))
+    messages = []
+    lines = agents // nz
+    for side, (ref, after) in enumerate(sides):
         message = ref[...].astype(F32).reshape(-1, nz)
-        fields, targets = corner_rows(message[:corner], message[corner : 2 * corner], even, mask)
-        sign = jnp.where(after, 1, -1)
-        edge = jnp.where(after, nx - 1, 0)
-        lines = agents // nz
+        messages.append(message)
         cell_row, place, part, uptake = (
             jnp.concatenate([message[at + i : at + i + 1] for i in range(lines)], axis=1)
             for at in range(2 * corner, 2 * corner + 4 * lines, lines)
@@ -392,11 +392,16 @@
         taken = jnp.where(key_rows == key, uptake, 0.0).astype(BF16)
         source = dot(taken, one_z, 1, 1)
         for i in range(nz // PART):
-            foreign[:, i * PART : (i + 1) * PART] = source[i * near * ny : (i + 1) * near * ny]
+            foreign[side, :, i * PART : (i + 1) * PART] = source[i * near * ny : (i + 1) * near * ny]
+    for side, (_, after) in enumerate(sides):
+        message = messages[side]
+        fields, targets = corner_rows(message[:corner], message[corner : 2 * corner], even, mask)
+        sign = jnp.where(after, 1, -1)
+        edge = jnp.where(after, nx - 1, 0)
         for i in range(1, HALO):
             p = edge + sign * i
             index = jnp.where(after, i - 1, HALO - 1 - i)
-            t = SCREENING * u0[p + 4, :ny] - foreign[pl.ds(index * ny, ny)]
+            t = SCREENING * u0[p + 4, :ny] - foreign[side, pl.ds(index * ny, ny)]
             text_ref[p + 3, :ny] = t
             text_ref[p + 3, ny:] = targets[i - 1]
             x = fields[i - 1]
@@ -429,7 +434,7 @@
             both = both + (inside[p - 2] if known else residual(u2_ref, text_ref, p, ny))
         parts = tiles_of(both)
         for i in range(len(parts) // 2):
-            paired[q, i] = parts[2 * i] + parts[2 * i + 1]
+            paired[q, i, :ny] = parts[2 * i] + parts[2 * i + 1]
     cx, cy, cz = coarse_ref.shape
     coarse = jnp.concatenate(
         [
@@ -553,7 +558,7 @@
         rows = plane.shape[0]
         return pltpu.roll(plane, 1, 0) + pltpu.roll(plane, rows - 1, 0)
 
-    spread = [jnp.concatenate([fine[q, i] for i in range(cz // LANES)], axis=1) for q in range(cx + 2)]
+    spread = [jnp.concatenate([fine[q, i, : 2 * wide] for i in range(cz // LANES)], axis=1) for q in range(cx + 2)]
     still = [KEEP * plane + PULL * second_total(plane) for plane in spread]
     once = []
     for p in range(-1, nx + 1):
@@ -568,10 +573,10 @@
         return jnp.concatenate([part for part in tiles_of(plane) for _ in range(2)], axis=1)
 
     back = back_ref[...]
-    step = 4
-    for start in range(0, nx, step):
+    bounds = (0, nx // 2, nx // 4 * 3, nx)
+    for start, end in zip(bounds, bounds[1:]):
         planes = []
-        for p in range(start, start + step):
+        for p in range(start, end):
             plane = once[p + 1]
             total = once[p] + once[p + 2] + second_total(plane)
             none = (KEEP * plane + PULL * total)[:ny]
@@ -579,10 +584,10 @@
             two = (PULL * PULL) * spread[(p + 2) // 2][:ny]
             planes.append(twice(none) + third_sum(twice(one) + third_sum(twice(two))))
         done = dot(jnp.concatenate(planes, axis=0).astype(BF16), back, 1, 0)
-        out_ref[start : start + step] = base_ref[start : start + step] + done.reshape(step, ny, nz)
-        cut = pl.ds(start, step)
-        copies.append(pltpu.make_async_copy(out_ref.at[cut], out_any.at[cut], sem.at[len(copies)]))
-        copies[-1].start()
+        out_ref[start:end] = base_ref[start:end] + done.reshape(end - start, ny, nz)
+        for p in range(start, end):
+            copies.append(pltpu.make_async_copy(out_ref.at[p], out_any.at[p], sem.at[len(copies)]))
+            copies[-1].start()
     for copy in copies:
         copy.wait()
 
@@ -703,8 +708,8 @@
         in_specs=[SMEM_SPEC] * 2 + [VMEM_SPEC] * 7,
         out_specs=[VMEM_SPEC] * 7,
         scratch_shapes=[
-            pltpu.VMEM((cx, cz // LANES, ny, LANES), F32),
-            pltpu.VMEM(((HALO - 1) * ny, nz), F32),
+            pltpu.VMEM((cx, cz // LANES, ny + 8, LANES), F32),
+            pltpu.VMEM((2, (HALO - 1) * ny, nz), F32),
         ],
         input_output_aliases={3: 0, 4: 1, 5: 2},
         compiler_params=PARAMS,
@@ -737,7 +742,7 @@
         in_specs=[SMEM_SPEC] * 2 + [VMEM_SPEC] * 7 + [ANY_SPEC] * (depths - 1),
         out_specs=[HBM_SPEC, ANY_SPEC],
         scratch_shapes=[
-            pltpu.VMEM((cx + 2, cz // LANES, ext, LANES), F32),
+            pltpu.VMEM((cx + 2, cz // LANES, ext + 8, LANES), F32),
             pltpu.VMEM((nx, ny, nz), F32),
             pltpu.SemaphoreType.DMA((depths + 5 + nx,)),
         ],

time: 33.6 us -> 33.6 us (level)
  no operation moved by 1% of the time
where the time goes in v7:
time: 33.6 us; the launch traced here: 33.4 us
  starting transfers between devices  15.4 us (46%)
  Pallas kernels  10.2 us (30%)
  waiting for transfers between devices  6.97 us (21%)
  between operations  0.73 us (2%)
    ppermute x11, starting transfers between devices, swapped(): return lax.ppermute(x, axis, sorted(pairs))  14.9 us
    ppermute x11, waiting for transfers between devices, swapped(): return lax.ppermute(x, axis, sorted(pairs))  4.82 us
    ppermute x1, waiting for transfers between devices, cyclic(): return lax.ppermute(x, axis, [(i, (i + by) % count) for i in range(count)])  2.14 us
    pallas_call x1, Pallas kernels, local(): pl.pallas_call(functools.partial(correct_kernel, depths), out_shape=(shap...  1.8 us
    pallas_call x1, Pallas kernels, local(): pl.pallas_call(network_kernel, out_shape=tuple((shape((capacity // 32, 16...  1.79 us
    pallas_call x1, Pallas kernels, local(): pl.pallas_call(load_kernel, out_shape=(shape((nx, ny, nz), F32), shape((n...  1.65 us
    pallas_call x1, Pallas kernels, local(): pl.pallas_call(functools.partial(post_kernel, depths), out_shape=(shape((...  1.5 us
    pallas_call x1, Pallas kernels, local(): pl.pallas_call(functools.partial(smooth_kernel, depths, agents), out_shap...  1.21 us
  transfers between devices with their start and end apart: 12, of which 6 were waited for; matrix products, arithmetic and copies ran while one was open for 0% of the time, Pallas kernels for 14%

profile of v7, /device:TPU:0, one launch (start us, length us, event | category | flops | bytes accessed | tf_op | source)
XLA Modules:
  0.0 33.4 jit_solution(9834309173552897833)
XLA Ops:
  0.6 1.7 %load.1 = (f32[8,32,512]{2,1,0:T(8,128)S(1)}, bf16[512,1024]{1,0:T(8,128)(2,1)S(1)}, bf16[8,16,512]{2,1,0:T(8,128)(2,1)S(1)}, bf16[8,16,512]{2,1,0:T(8,128)(2,1)...) custom-call(s32[1]{0:T(128)} %bitcast.1.slab_ref, ...), custom_call_target="tpu_custom_call" | custom-call | tf_op jit(solution)/shard_map/load/pallas_call | solution.py:616
  2.3 1.0 %uptake.1 = (f32[8,32,512]{2,1,0:T(8,128)S(1)}, f32[8,1024]{1,0:T(8,128)S(1)}, bf16[4,16,512]{2,1,0:T(8,128)(2,1)S(1)}, bf16[4,16,512]{2,1,0:T(8,128)(2,1)S(1)}, f32[8,512]{1,0:T(8,128)S(1)}) custom-call(s32[1]{0:T(128)} %bitcast.me_ref, f32[8,32,512]{2,1,0:T(8,128)S(1)} %get-tuple-element.56.u_ref, bf16[512,1024]{1,0:T(8,128)(2,1)S(1)} %get-tuple-element.57.place_ref, ...), custom_call_target="tpu_custom_call" | custom-call | flops 2147483648 | bytes 1048576 | tf_op jit(solution)/shard_map/uptake/pallas_call | solution.py:634
  3.3 0.5 %collective-permute-start = (bf16[4,16,512]{2,1,0:T(8,128)(2,1)S(1)}, bf16[4,16,512]{2,1,0:T(8,128)(2,1)S(1)}, u32[]{:S(2)}, u32[]{:S(2)}) collective-permute-start(bf16[4,16,512]{2,1,0:T(8,128)(2,1)S(1)} %get-tuple-element.68), channel_id=1, source_target_pairs={{0,1},{1,0},{2,3},{3,2},{4,5},{5,4},{6,7},{7,6},{8,9},{9,8},{10,11... | collective-permute-start | bytes 196616 | tf_op jit(solution)/shard_map/ppermute | solution.py:52
  3.8 2.6 %collective-permute-start.1 = (bf16[4,16,512]{2,1,0:T(8,128)(2,1)S(1)}, bf16[4,16,512]{2,1,0:T(8,128)(2,1)S(1)}, u32[]{:S(2)}, u32[]{:S(2)}) collective-permute-start(bf16[4,16,512]{2,1,0:T(8,128)(2,1)S(1)} %get-tuple-element.69), channel_id=1, source_target_pairs={{0,3},{1,2},{2,1},{3,0},{4,7},{5,6},{6,5},{7,4},{8,11},{9,10},{10,... | collective-permute-start | bytes 196616 | tf_op jit(solution)/shard_map/ppermute | solution.py:52
  6.5 1.5 %collective-permute-start.2 = (bf16[8,16,512]{2,1,0:T(8,128)(2,1)S(1)}, bf16[8,16,512]{2,1,0:T(8,128)(2,1)S(1)}, u32[]{:S(2)}, u32[]{:S(2)}) collective-permute-start(bf16[8,16,512]{2,1,0:T(8,128)(2,1)S(1)} %get-tuple-element.70), channel_id=1, source_target_pairs={{0,4},{4,0},{8,12},{12,8},{16,20},{20,16},{24,28},{28,24},{1,5},{5... | collective-permute-start | bytes 393224 | tf_op jit(solution)/shard_map/ppermute | solution.py:52
  8.0 3.6 %collective-permute-start.3 = (bf16[8,16,512]{2,1,0:T(8,128)(2,1)S(1)}, bf16[8,16,512]{2,1,0:T(8,128)(2,1)S(1)}, u32[]{:S(2)}, u32[]{:S(2)}) collective-permute-start(bf16[8,16,512]{2,1,0:T(8,128)(2,1)S(1)} %get-tuple-element.71), channel_id=1, source_target_pairs={{0,28},{4,8},{8,4},{12,16},{16,12},{20,24},{24,20},{28,0},{1,29},{... | collective-permute-start | bytes 393224 | tf_op jit(solution)/shard_map/ppermute | solution.py:52
  11.5 0.0 collective-permute-done.side_a
  11.5 0.0 collective-permute-done.1.side_b
  11.5 0.1 corner.1
  11.6 0.1 collective-permute-start.4
  11.7 2.3 %collective-permute-start.5 = (bf16[2,16,512]{2,1,0:T(8,128)(2,1)S(1)}, bf16[2,16,512]{2,1,0:T(8,128)(2,1)S(1)}, u32[]{:S(2)}, u32[]{:S(2)}) collective-permute-start(bf16[2,16,512]{2,1,0:T(8,128)(2,1)S(1)} %get-tuple-element.78), channel_id=1, source_target_pairs={{0,28},{4,8},{8,4},{12,16},{16,12},{20,24},{24,20},{28,0},{1,29},{... | collective-permute-start | bytes 98312 | tf_op jit(solution)/shard_map/ppermute | solution.py:52
  13.9 1.8 %network.1 = (bf16[32,16,128]{2,1,0:T(8,128)(2,1)S(1)}, bf16[16,16,256]{2,1,0:T(8,128)(2,1)S(1)}, bf16[32,16,128]{2,1,0:T(8,128)(2,1)S(1)}, bf16[32,16,128]{2,1,...) custom-call(s32[1]{0:T(128)} %bitcast.me_ref, s32[1]{0:T(128)} %bitcast.1.slab_ref, ...), custom_call_target="tpu_custom_call" | custom-call | flops 2147483648 | bytes 1048576 | tf_op jit(solution)/shard_map/network/pallas_call | solution.py:668
  15.7 0.0 collective-permute-done.2.field_a
  15.8 0.2 collective-permute-done.3.field_b
  15.9 1.2 %inner.1 = (f32[16,40,512]{2,1,0:T(8,128)S(1)}, f32[14,40,512]{2,1,0:T(8,128)S(1)}, f32[14,40,512]{2,1,0:T(8,128)S(1)}, f32[12,40,512]{2,1,0:T(8,128)S(1)}, f32[4,32,512]{2,1,0:T(8,128)S(1)}) custom-call(s32[1]{0:T(128)} %bitcast.me_ref, s32[1]{0:T(128)} %bitcast.1.slab_ref, f32[8,32,512]{2,1,0:T(8,128)S(1)} %get-tuple-element.56.u_ref, ...), custom_call_target="tpu_custom_call" | custom-call | flops 1048576 | bytes 1048576 | tf_op jit(solution)/shard_map/inner/pallas_call | solution.py:681
  17.2 0.0 collective-permute-done.4.slab_a
  17.2 1.2 %collective-permute-done.5.slab_b = bf16[2,16,512]{2,1,0:T(8,128)(2,1)S(1)} collective-permute-done((bf16[2,16,512]{2,1,0:T(8,128)(2,1)S(1)}, bf16[2,16,512]{2,1,0:T(8,128)(2,1)S(1)}, u32[]{:S(2)}, u32[]{:S(2)}) %collective-permute-start.5) | collective-permute-done | bytes 32800 | tf_op jit(solution)/shard_map/ppermute | solution.py:52
  18.4 1.2 %smooth.1 = (f32[14,40,512]{2,1,0:T(8,128)S(1)}, f32[14,40,512]{2,1,0:T(8,128)S(1)}, f32[12,40,512]{2,1,0:T(8,128)S(1)}, f32[4,16,256]{2,1,0:T(8,128)S(1)}, bf16...) custom-call(s32[1]{0:T(128)} %bitcast.me_ref, ...), custom_call_target="tpu_custom_call", output_to_operand_aliasing={{0}: (3, {}), {1}: (4, {}), {2}: (5, {})} | custom-call | tf_op jit(solution)/shard_map/smooth/pallas_call | solution.py:697
  19.6 0.1 collective-permute-start.6
  19.7 0.6 %collective-permute-start.7 = (bf16[1,16,256]{2,1,0:T(8,128)(2,1)S(1)}, bf16[1,16,256]{2,1,0:T(8,128)(2,1)S(1)}, u32[]{:S(2)}, u32[]{:S(2)}) collective-permute-start(bf16[1,16,256]{2,1,0:T(8,128)(2,1)S(1)} %get-tuple-element.97), channel_id=1, source_target_pairs={{0,3},{1,2},{2,1},{3,0},{4,7},{5,6},{6,5},{7,4},{8,11},{9,10},{10,... | collective-permute-start | bytes 24584 | tf_op jit(solution)/shard_map/ppermute | solution.py:52
  20.3 1.2 %collective-permute-start.10 = (bf16[32,16,128]{2,1,0:T(8,128)(2,1)S(1)}, bf16[32,16,128]{2,1,0:T(8,128)(2,1)S(1)}, u32[]{:S(2)}, u32[]{:S(2)}) collective-permute-start(bf16[32,16,128]{2,1,0:T(8,128)(2,1)S(1)} %get-tuple-element.106), channel_id=1, source_target_pairs={{0,3},{1,2},{2,1},{3,0},{4,7},{5,6},{6,5},{7,4},{8,11},{9,10},{10,... | collective-permute-start | bytes 393224 | tf_op jit(solution)/shard_map/ppermute | solution.py:52
  21.5 0.5 %collective-permute-start.11 = (bf16[32,16,128]{2,1,0:T(8,128)(2,1)S(1)}, bf16[32,16,128]{2,1,0:T(8,128)(2,1)S(1)}, u32[]{:S(2)}, u32[]{:S(2)}) collective-permute-start(bf16[32,16,128]{2,1,0:T(8,128)(2,1)S(1)} %get-tuple-element.107), channel_id=1, source_target_pairs={{0,2},{1,3},{2,0},{3,1},{4,6},{5,7},{6,4},{7,5},{8,10},{9,11},{10,... | collective-permute-start | bytes 393224 | tf_op jit(solution)/shard_map/ppermute | solution.py:40
  22.0 0.0 collective-permute-done.6.side_a
  22.0 0.8 %collective-permute-done.7.side_b = bf16[1,16,256]{2,1,0:T(8,128)(2,1)S(1)} collective-permute-done((bf16[1,16,256]{2,1,0:T(8,128)(2,1)S(1)}, bf16[1,16,256]{2,1,0:T(8,128)(2,1)S(1)}, u32[]{:S(2)}, u32[]{:S(2)}) %collective-permute-start.7) | collective-permute-done | bytes 8224 | tf_op jit(solution)/shard_map/ppermute | solution.py:52
  22.8 2.5 %collective-permute-start.9 = (bf16[10,16,256]{2,1,0:T(8,128)(2,1)S(1)}, bf16[10,16,256]{2,1,0:T(8,128)(2,1)S(1)}, u32[]{:S(2)}, u32[]{:S(2)}) collective-permute-start(bf16[10,16,256]{2,1,0:T(8,128)(2,1)S(1)} %get-tuple-element.110), channel_id=1, source_target_pairs={{0,28},{4,8},{8,4},{12,16},{16,12},{20,24},{24,20},{28,0},{1,29},{... | collective-permute-start | bytes 245768 | tf_op jit(solution)/shard_map/ppermute | solution.py:52
  25.3 0.0 collective-permute-start.8
  25.3 1.5 %post.1 = (f32[8,32,512]{2,1,0:T(8,128)S(1)}, bf16[512,512]{1,0:T(8,128)(2,1)S(1)}) custom-call(s32[1]{0:T(128)} %bitcast.me_ref, f32[12,40,512]{2,1,0:T(8,128)S(1)} %get-tuple-element.101.u2_ref, f32[14,40,512]{2,1,0:T(8,128)S(1)} %get-tuple-element.102.text_ref), custom_call_target="tpu_custom_call" | custom-call | flops 1073741824 | bytes 4194304 | tf_op jit(solution)/shard_map/post/pallas_call | solution.py:726
  26.8 0.0 collective-permute-done.10.rest_1_
  26.8 2.1 %collective-permute-done.11.rest_2_ = bf16[32,16,128]{2,1,0:T(8,128)(2,1)S(1)} collective-permute-done((bf16[32,16,128]{2,1,0:T(8,128)(2,1)S(1)}, bf16[32,16,128]{2,1,0:T(8,128)(2,1)S(1)}, u32[]{:S(2)}, u32[]{:S(2)}) %collective-permute-start.11) | collective-permute-done | bytes 131104 | tf_op jit(solution)/shard_map/ppermute | solution.py:40
  29.0 1.9 %collective-permute-done.9.slab_b = bf16[10,16,256]{2,1,0:T(8,128)(2,1)S(1)} collective-permute-done((bf16[10,16,256]{2,1,0:T(8,128)(2,1)S(1)}, bf16[10,16,256]{2,1,0:T(8,128)(2,1)S(1)}, u32[]{:S(2)}, u32[]{:S(2)}) %collective-permute-start.9) | collective-permute-done | bytes 81952 | tf_op jit(solution)/shard_map/ppermute | solution.py:52
  30.9 0.7 %collective-permute-done.8.slab_a = bf16[10,16,256]{2,1,0:T(8,128)(2,1)S(1)} collective-permute-done((bf16[10,16,256]{2,1,0:T(8,128)(2,1)S(1)}, bf16[10,16,256]{2,1,0:T(8,128)(2,1)S(1)}, u32[]{:S(2)}, u32[]{:S(2)}) %collective-permute-start.8) | collective-permute-done | bytes 81952 | tf_op jit(solution)/shard_map/ppermute | solution.py:52
  31.6 1.8 %correct.1 = (f32[8,32,512]{2,1,0:T(8,128)}, bf16[144,16,128]{2,1,0:T(8,128)(2,1)}) custom-call(s32[1]{0:T(128)} %bitcast.me_ref, s32[1]{0:T(128)} %bitcast.1.slab_ref, f32[4,16,256]{2,1,0:T(8,128)S(1)} %get-tuple-element.94.ct_ref, bf16[17,16,256]{2,1,0:T(8,128)(2,1)S(1)} %collective-permute-done.6.side_a, ...), custom_call_target="tpu_custom_call" | custom-call | tf_op jit(solution)/shard_map/correct/pallas_call | solution.py:736
  (3 shorter events, 0.0 us)
Async XLA Ops:
  3.3 8.2 %collective-permute-start = (bf16[4,16,512]{2,1,0:T(8,128)(2,1)S(1)}, bf16[4,16,512]{2,1,0:T(8,128)(2,1)S(1)}, u32[]{:S(2)}, u32[]{:S(2)}) collective-permute-start(bf16[4,16,512]{2,1,0:T(8,128)(2,1)S(1)} %get-tuple-element.68), channel_id=1, source_target_pairs={{0,1},{1,0},{2,3},{3,2},{4,5},{5,4},{6,7},{7,6},{8,9},{9,8},{10,11... | collective-permute-start | bytes 196616 | tf_op jit(solution)/shard_map/ppermute | solution.py:52
  3.8 7.7 %collective-permute-start.1 = (bf16[4,16,512]{2,1,0:T(8,128)(2,1)S(1)}, bf16[4,16,512]{2,1,0:T(8,128)(2,1)S(1)}, u32[]{:S(2)}, u32[]{:S(2)}) collective-permute-start(bf16[4,16,512]{2,1,0:T(8,128)(2,1)S(1)} %get-tuple-element.69), channel_id=1, source_target_pairs={{0,3},{1,2},{2,1},{3,0},{4,7},{5,6},{6,5},{7,4},{8,11},{9,10},{10,... | collective-permute-start | bytes 196616 | tf_op jit(solution)/shard_map/ppermute | solution.py:52
  6.5 9.3 %collective-permute-start.2 = (bf16[8,16,512]{2,1,0:T(8,128)(2,1)S(1)}, bf16[8,16,512]{2,1,0:T(8,128)(2,1)S(1)}, u32[]{:S(2)}, u32[]{:S(2)}) collective-permute-start(bf16[8,16,512]{2,1,0:T(8,128)(2,1)S(1)} %get-tuple-element.70), channel_id=1, source_target_pairs={{0,4},{4,0},{8,12},{12,8},{16,20},{20,16},{24,28},{28,24},{1,5},{5... | collective-permute-start | bytes 393224 | tf_op jit(solution)/shard_map/ppermute | solution.py:52
  8.0 8.0 %collective-permute-start.3 = (bf16[8,16,512]{2,1,0:T(8,128)(2,1)S(1)}, bf16[8,16,512]{2,1,0:T(8,128)(2,1)S(1)}, u32[]{:S(2)}, u32[]{:S(2)}) collective-permute-start(bf16[8,16,512]{2,1,0:T(8,128)(2,1)S(1)} %get-tuple-element.71), channel_id=1, source_target_pairs={{0,28},{4,8},{8,4},{12,16},{16,12},{20,24},{24,20},{28,0},{1,29},{... | collective-permute-start | bytes 393224 | tf_op jit(solution)/shard_map/ppermute | solution.py:52
  11.6 5.6 %collective-permute-start.4 = (bf16[2,16,512]{2,1,0:T(8,128)(2,1)S(1)}, bf16[2,16,512]{2,1,0:T(8,128)(2,1)S(1)}, u32[]{:S(2)}, u32[]{:S(2)}) collective-permute-start(bf16[2,16,512]{2,1,0:T(8,128)(2,1)S(1)} %get-tuple-element.77), channel_id=1, source_target_pairs={{0,4},{4,0},{8,12},{12,8},{16,20},{20,16},{24,28},{28,24},{1,5},{5... | collective-permute-start | bytes 98312 | tf_op jit(solution)/shard_map/ppermute | solution.py:52
  11.7 6.7 %collective-permute-start.5 = (bf16[2,16,512]{2,1,0:T(8,128)(2,1)S(1)}, bf16[2,16,512]{2,1,0:T(8,128)(2,1)S(1)}, u32[]{:S(2)}, u32[]{:S(2)}) collective-permute-start(bf16[2,16,512]{2,1,0:T(8,128)(2,1)S(1)} %get-tuple-element.78), channel_id=1, source_target_pairs={{0,28},{4,8},{8,4},{12,16},{16,12},{20,24},{24,20},{28,0},{1,29},{... | collective-permute-start | bytes 98312 | tf_op jit(solution)/shard_map/ppermute | solution.py:52
  19.6 2.4 %collective-permute-start.6 = (bf16[17,16,256]{2,1,0:T(8,128)(2,1)S(1)}, bf16[17,16,256]{2,1,0:T(8,128)(2,1)S(1)}, u32[]{:S(2)}, u32[]{:S(2)}) collective-permute-start(bf16[17,16,256]{2,1,0:T(8,128)(2,1)S(1)} %pad_maximum_fusion), channel_id=1, source_target_pairs={{0,1},{1,0},{2,3},{3,2},{4,5},{5,4},{6,7},{7,6},{8,9},{9,8},{10,11... | collective-permute-start | bytes 417800 | tf_op jit(solution)/shard_map/ppermute | solution.py:52
  19.7 3.1 %collective-permute-start.7 = (bf16[1,16,256]{2,1,0:T(8,128)(2,1)S(1)}, bf16[1,16,256]{2,1,0:T(8,128)(2,1)S(1)}, u32[]{:S(2)}, u32[]{:S(2)}) collective-permute-start(bf16[1,16,256]{2,1,0:T(8,128)(2,1)S(1)} %get-tuple-element.97), channel_id=1, source_target_pairs={{0,3},{1,2},{2,1},{3,0},{4,7},{5,6},{6,5},{7,4},{8,11},{9,10},{10,... | collective-permute-start | bytes 24584 | tf_op jit(solution)/shard_map/ppermute | solution.py:52
  20.3 6.5 %collective-permute-start.10 = (bf16[32,16,128]{2,1,0:T(8,128)(2,1)S(1)}, bf16[32,16,128]{2,1,0:T(8,128)(2,1)S(1)}, u32[]{:S(2)}, u32[]{:S(2)}) collective-permute-start(bf16[32,16,128]{2,1,0:T(8,128)(2,1)S(1)} %get-tuple-element.106), channel_id=1, source_target_pairs={{0,3},{1,2},{2,1},{3,0},{4,7},{5,6},{6,5},{7,4},{8,11},{9,10},{10,... | collective-permute-start | bytes 393224 | tf_op jit(solution)/shard_map/ppermute | solution.py:52
  21.5 7.5 %collective-permute-start.11 = (bf16[32,16,128]{2,1,0:T(8,128)(2,1)S(1)}, bf16[32,16,128]{2,1,0:T(8,128)(2,1)S(1)}, u32[]{:S(2)}, u32[]{:S(2)}) collective-permute-start(bf16[32,16,128]{2,1,0:T(8,128)(2,1)S(1)} %get-tuple-element.107), channel_id=1, source_target_pairs={{0,2},{1,3},{2,0},{3,1},{4,6},{5,7},{6,4},{7,5},{8,10},{9,11},{10,... | collective-permute-start | bytes 393224 | tf_op jit(solution)/shard_map/ppermute | solution.py:40
  22.8 8.0 %collective-permute-start.9 = (bf16[10,16,256]{2,1,0:T(8,128)(2,1)S(1)}, bf16[10,16,256]{2,1,0:T(8,128)(2,1)S(1)}, u32[]{:S(2)}, u32[]{:S(2)}) collective-permute-start(bf16[10,16,256]{2,1,0:T(8,128)(2,1)S(1)} %get-tuple-element.110), channel_id=1, source_target_pairs={{0,28},{4,8},{8,4},{12,16},{16,12},{20,24},{24,20},{28,0},{1,29},{... | collective-permute-start | bytes 245768 | tf_op jit(solution)/shard_map/ppermute | solution.py:52
  25.3 6.3 %collective-permute-start.8 = (bf16[10,16,256]{2,1,0:T(8,128)(2,1)S(1)}, bf16[10,16,256]{2,1,0:T(8,128)(2,1)S(1)}, u32[]{:S(2)}, u32[]{:S(2)}) collective-permute-start(bf16[10,16,256]{2,1,0:T(8,128)(2,1)S(1)} %get-tuple-element.111), channel_id=1, source_target_pairs={{0,4},{4,0},{8,12},{12,8},{16,20},{20,16},{24,28},{28,24},{1,5},{5... | collective-permute-start | bytes 245768 | tf_op jit(solution)/shard_map/ppermute | solution.py:52

commit v8 on v7

--- a/solution.py
+++ b/solution.py
@@ -420,13 +420,9 @@
         u1[edge + 3, ny:] = u1[edge + 3, ny:] + PULL * fields[0]
         u2_ref[edge - sign + 2, ny:] = u2_ref[edge - sign + 2, ny:] + (PULL * PULL) * fields[0]
 
-    def second(i, carry):
-        for p in (i, nx + 1 + i):
-            v = relaxed(u1[p], u1[p + 1], u1[p + 2], text_ref[p + 1], CENTRE)
-            u2_ref[p] = masked(v, ny, mask)
-        return carry
-
-    lax.fori_loop(0, HALO - 1, second, 0)
+    for p in (1, 2, nx + 1, nx + 2):
+        v = relaxed(u1[p], u1[p + 1], u1[p + 2], text_ref[p + 1], CENTRE)
+        u2_ref[p] = masked(v, ny, mask)
     for q in range(nx // 2):
         both = 0.0
         for p in (2 * q, 2 * q + 1):
@@ -460,11 +456,17 @@
     coarse_b[0] = jnp.where(even, low, high).astype(BF16)
 
 
-def post_kernel(depths, me_ref, u2_ref, text_ref, out_ref, back_ref, v1):
+def post_kernel(depths, me_ref, u1, u2_in, text_ref, out_ref, back_ref, v1, u2_ref):
     nx, ny, nz = out_ref.shape
     back = shuffle(nz, True)
     back_ref[...] = back
     mask = edge_mask(me_ref[0], depths, HALO)
+    last = nx + 3
+    for p in range(1, last):
+        u2_ref[p] = u2_in[p]
+    for p in (0, last):
+        v = relaxed(u1[p], u1[p + 1], u1[p + 2], text_ref[p + 1], CENTRE)
+        u2_ref[p] = masked(v, ny, mask)
 
     def first(p, carry):
         v = relaxed(u2_ref[p], u2_ref[p + 1], u2_ref[p + 2], text_ref[p + 2], CENTRE)
@@ -694,7 +696,7 @@
         name="inner",
     )(me, slab, nutrient, target, side_a, side_b, field_a, field_b)
     slab_a, slab_b, inside, *sent = lax.optimization_barrier((slab_a, slab_b, inside, *sent))
-    text, _, u2, ct, ct_all, coarse_a, coarse_b = pl.pallas_call(
+    text, u1, u2, ct, ct_all, coarse_a, coarse_b = pl.pallas_call(
         functools.partial(smooth_kernel, depths, agents),
         out_shape=(
             shape(text.shape, F32),
@@ -726,13 +728,13 @@
     base, back = pl.pallas_call(
         functools.partial(post_kernel, depths),
         out_shape=(shape((nx, ny, nz), F32), shape((nz, nz), BF16)),
-        in_specs=[SMEM_SPEC] + [VMEM_SPEC] * 2,
+        in_specs=[SMEM_SPEC] + [VMEM_SPEC] * 3,
         out_specs=[VMEM_SPEC] * 2,
-        scratch_shapes=[pltpu.VMEM((nx + 2, ext, nz), F32)],
+        scratch_shapes=[pltpu.VMEM((nx + 2, ext, nz), F32), pltpu.VMEM((nx + 4, ext, nz), F32)],
         compiler_params=PARAMS,
         cost_estimate=pl.CostEstimate(flops=1 << 30, bytes_accessed=1 << 22, transcendentals=0),
         name="post",
-    )(me, u2, text)
+    )(me, u1, u2, text)
     grid_field, agents_out = pl.pallas_call(
         functools.partial(correct_kernel, depths),
         out_shape=(

time: 33.6 us -> 33.5 us (level)
  no operation moved by 1% of the time
where the time goes in v8:
time: 33.5 us; the launch traced here: 33.3 us
  starting transfers between devices  15.4 us (46%)
  Pallas kernels  10.3 us (31%)
  waiting for transfers between devices  6.81 us (20%)
  between operations  0.74 us (2%)
    ppermute x11, starting transfers between devices, swapped(): return lax.ppermute(x, axis, sorted(pairs))  14.9 us
    ppermute x11, waiting for transfers between devices, swapped(): return lax.ppermute(x, axis, sorted(pairs))  4.77 us
    ppermute x1, waiting for transfers between devices, cyclic(): return lax.ppermute(x, axis, [(i, (i + by) % count) for i in range(count)])  2.04 us
    pallas_call x1, Pallas kernels, local(): pl.pallas_call(functools.partial(correct_kernel, depths), out_shape=(shap...  1.8 us
    pallas_call x1, Pallas kernels, local(): pl.pallas_call(network_kernel, out_shape=tuple((shape((capacity // 32, 16...  1.79 us
    pallas_call x1, Pallas kernels, local(): pl.pallas_call(load_kernel, out_shape=(shape((nx, ny, nz), F32), shape((n...  1.65 us
    pallas_call x1, Pallas kernels, local(): pl.pallas_call(functools.partial(post_kernel, depths), out_shape=(shape((...  1.63 us
    pallas_call x1, Pallas kernels, local(): pl.pallas_call(functools.partial(inner_kernel, depths), out_shape=(shape(...  1.21 us
  transfers between devices with their start and end apart: 12, of which 6 were waited for; matrix products, arithmetic and copies ran while one was open for 0% of the time, Pallas kernels for 14%

profile of v8, /device:TPU:0, one launch (start us, length us, event | category | flops | bytes accessed | tf_op | source)
XLA Modules:
  0.0 33.3 jit_solution(9376618531079260957)
XLA Ops:
  0.6 1.7 %load.1 = (f32[8,32,512]{2,1,0:T(8,128)S(1)}, bf16[512,1024]{1,0:T(8,128)(2,1)S(1)}, bf16[8,16,512]{2,1,0:T(8,128)(2,1)S(1)}, bf16[8,16,512]{2,1,0:T(8,128)(2,1)...) custom-call(s32[1]{0:T(128)} %bitcast.1.slab_ref, ...), custom_call_target="tpu_custom_call" | custom-call | tf_op jit(solution)/shard_map/load/pallas_call | solution.py:618
  2.3 1.0 %uptake.1 = (f32[8,32,512]{2,1,0:T(8,128)S(1)}, f32[8,1024]{1,0:T(8,128)S(1)}, bf16[4,16,512]{2,1,0:T(8,128)(2,1)S(1)}, bf16[4,16,512]{2,1,0:T(8,128)(2,1)S(1)}, f32[8,512]{1,0:T(8,128)S(1)}) custom-call(s32[1]{0:T(128)} %bitcast.me_ref, f32[8,32,512]{2,1,0:T(8,128)S(1)} %get-tuple-element.57.u_ref, bf16[512,1024]{1,0:T(8,128)(2,1)S(1)} %get-tuple-element.58.place_ref, ...), custom_call_target="tpu_custom_call" | custom-call | flops 2147483648 | bytes 1048576 | tf_op jit(solution)/shard_map/uptake/pallas_call | solution.py:636
  3.3 0.5 %collective-permute-start = (bf16[4,16,512]{2,1,0:T(8,128)(2,1)S(1)}, bf16[4,16,512]{2,1,0:T(8,128)(2,1)S(1)}, u32[]{:S(2)}, u32[]{:S(2)}) collective-permute-start(bf16[4,16,512]{2,1,0:T(8,128)(2,1)S(1)} %get-tuple-element.69), channel_id=1, source_target_pairs={{0,1},{1,0},{2,3},{3,2},{4,5},{5,4},{6,7},{7,6},{8,9},{9,8},{10,11... | collective-permute-start | bytes 196616 | tf_op jit(solution)/shard_map/ppermute | solution.py:52
  3.8 2.6 %collective-permute-start.1 = (bf16[4,16,512]{2,1,0:T(8,128)(2,1)S(1)}, bf16[4,16,512]{2,1,0:T(8,128)(2,1)S(1)}, u32[]{:S(2)}, u32[]{:S(2)}) collective-permute-start(bf16[4,16,512]{2,1,0:T(8,128)(2,1)S(1)} %get-tuple-element.70), channel_id=1, source_target_pairs={{0,3},{1,2},{2,1},{3,0},{4,7},{5,6},{6,5},{7,4},{8,11},{9,10},{10,... | collective-permute-start | bytes 196616 | tf_op jit(solution)/shard_map/ppermute | solution.py:52
  6.5 1.5 %collective-permute-start.2 = (bf16[8,16,512]{2,1,0:T(8,128)(2,1)S(1)}, bf16[8,16,512]{2,1,0:T(8,128)(2,1)S(1)}, u32[]{:S(2)}, u32[]{:S(2)}) collective-permute-start(bf16[8,16,512]{2,1,0:T(8,128)(2,1)S(1)} %get-tuple-element.71), channel_id=1, source_target_pairs={{0,4},{4,0},{8,12},{12,8},{16,20},{20,16},{24,28},{28,24},{1,5},{5... | collective-permute-start | bytes 393224 | tf_op jit(solution)/shard_map/ppermute | solution.py:52
  8.0 3.6 %collective-permute-start.3 = (bf16[8,16,512]{2,1,0:T(8,128)(2,1)S(1)}, bf16[8,16,512]{2,1,0:T(8,128)(2,1)S(1)}, u32[]{:S(2)}, u32[]{:S(2)}) collective-permute-start(bf16[8,16,512]{2,1,0:T(8,128)(2,1)S(1)} %get-tuple-element.72), channel_id=1, source_target_pairs={{0,28},{4,8},{8,4},{12,16},{16,12},{20,24},{24,20},{28,0},{1,29},{... | collective-permute-start | bytes 393224 | tf_op jit(solution)/shard_map/ppermute | solution.py:52
  11.5 0.0 collective-permute-done.side_a
  11.5 0.0 collective-permute-done.1.side_b
  11.5 0.1 corner.1
  11.6 0.1 collective-permute-start.4
  11.7 2.3 %collective-permute-start.5 = (bf16[2,16,512]{2,1,0:T(8,128)(2,1)S(1)}, bf16[2,16,512]{2,1,0:T(8,128)(2,1)S(1)}, u32[]{:S(2)}, u32[]{:S(2)}) collective-permute-start(bf16[2,16,512]{2,1,0:T(8,128)(2,1)S(1)} %get-tuple-element.79), channel_id=1, source_target_pairs={{0,28},{4,8},{8,4},{12,16},{16,12},{20,24},{24,20},{28,0},{1,29},{... | collective-permute-start | bytes 98312 | tf_op jit(solution)/shard_map/ppermute | solution.py:52
  14.0 1.8 %network.1 = (bf16[32,16,128]{2,1,0:T(8,128)(2,1)S(1)}, bf16[16,16,256]{2,1,0:T(8,128)(2,1)S(1)}, bf16[32,16,128]{2,1,0:T(8,128)(2,1)S(1)}, bf16[32,16,128]{2,1,...) custom-call(s32[1]{0:T(128)} %bitcast.me_ref, s32[1]{0:T(128)} %bitcast.1.slab_ref, ...), custom_call_target="tpu_custom_call" | custom-call | flops 2147483648 | bytes 1048576 | tf_op jit(solution)/shard_map/network/pallas_call | solution.py:670
  15.8 0.0 collective-permute-done.2.field_a
  15.8 0.2 collective-permute-done.3.field_b
  15.9 1.2 %inner.1 = (f32[16,40,512]{2,1,0:T(8,128)S(1)}, f32[14,40,512]{2,1,0:T(8,128)S(1)}, f32[14,40,512]{2,1,0:T(8,128)S(1)}, f32[12,40,512]{2,1,0:T(8,128)S(1)}, f32[4,32,512]{2,1,0:T(8,128)S(1)}) custom-call(s32[1]{0:T(128)} %bitcast.me_ref, s32[1]{0:T(128)} %bitcast.1.slab_ref, f32[8,32,512]{2,1,0:T(8,128)S(1)} %get-tuple-element.57.u_ref, ...), custom_call_target="tpu_custom_call" | custom-call | flops 1048576 | bytes 1048576 | tf_op jit(solution)/shard_map/inner/pallas_call | solution.py:683
  17.2 0.0 collective-permute-done.4.slab_a
  17.2 1.2 %collective-permute-done.5.slab_b = bf16[2,16,512]{2,1,0:T(8,128)(2,1)S(1)} collective-permute-done((bf16[2,16,512]{2,1,0:T(8,128)(2,1)S(1)}, bf16[2,16,512]{2,1,0:T(8,128)(2,1)S(1)}, u32[]{:S(2)}, u32[]{:S(2)}) %collective-permute-start.5) | collective-permute-done | bytes 32800 | tf_op jit(solution)/shard_map/ppermute | solution.py:52
  18.4 1.1 %smooth.1 = (f32[14,40,512]{2,1,0:T(8,128)S(1)}, f32[14,40,512]{2,1,0:T(8,128)S(1)}, f32[12,40,512]{2,1,0:T(8,128)S(1)}, f32[4,16,256]{2,1,0:T(8,128)S(1)}, bf16...) custom-call(s32[1]{0:T(128)} %bitcast.me_ref, ...), custom_call_target="tpu_custom_call", output_to_operand_aliasing={{0}: (3, {}), {1}: (4, {}), {2}: (5, {})} | custom-call | tf_op jit(solution)/shard_map/smooth/pallas_call | solution.py:699
  19.5 0.1 collective-permute-start.6
  19.6 0.6 %collective-permute-start.7 = (bf16[1,16,256]{2,1,0:T(8,128)(2,1)S(1)}, bf16[1,16,256]{2,1,0:T(8,128)(2,1)S(1)}, u32[]{:S(2)}, u32[]{:S(2)}) collective-permute-start(bf16[1,16,256]{2,1,0:T(8,128)(2,1)S(1)} %get-tuple-element.98), channel_id=1, source_target_pairs={{0,3},{1,2},{2,1},{3,0},{4,7},{5,6},{6,5},{7,4},{8,11},{9,10},{10,... | collective-permute-start | bytes 24584 | tf_op jit(solution)/shard_map/ppermute | solution.py:52
  20.2 1.2 %collective-permute-start.10 = (bf16[32,16,128]{2,1,0:T(8,128)(2,1)S(1)}, bf16[32,16,128]{2,1,0:T(8,128)(2,1)S(1)}, u32[]{:S(2)}, u32[]{:S(2)}) collective-permute-start(bf16[32,16,128]{2,1,0:T(8,128)(2,1)S(1)} %get-tuple-element.108), channel_id=1, source_target_pairs={{0,3},{1,2},{2,1},{3,0},{4,7},{5,6},{6,5},{7,4},{8,11},{9,10},{10,... | collective-permute-start | bytes 393224 | tf_op jit(solution)/shard_map/ppermute | solution.py:52
  21.4 0.5 %collective-permute-start.11 = (bf16[32,16,128]{2,1,0:T(8,128)(2,1)S(1)}, bf16[32,16,128]{2,1,0:T(8,128)(2,1)S(1)}, u32[]{:S(2)}, u32[]{:S(2)}) collective-permute-start(bf16[32,16,128]{2,1,0:T(8,128)(2,1)S(1)} %get-tuple-element.109), channel_id=1, source_target_pairs={{0,2},{1,3},{2,0},{3,1},{4,6},{5,7},{6,4},{7,5},{8,10},{9,11},{10,... | collective-permute-start | bytes 393224 | tf_op jit(solution)/shard_map/ppermute | solution.py:40
  21.9 0.0 collective-permute-done.6.side_a
  21.9 0.8 %collective-permute-done.7.side_b = bf16[1,16,256]{2,1,0:T(8,128)(2,1)S(1)} collective-permute-done((bf16[1,16,256]{2,1,0:T(8,128)(2,1)S(1)}, bf16[1,16,256]{2,1,0:T(8,128)(2,1)S(1)}, u32[]{:S(2)}, u32[]{:S(2)}) %collective-permute-start.7) | collective-permute-done | bytes 8224 | tf_op jit(solution)/shard_map/ppermute | solution.py:52
  22.8 2.5 %collective-permute-start.9 = (bf16[10,16,256]{2,1,0:T(8,128)(2,1)S(1)}, bf16[10,16,256]{2,1,0:T(8,128)(2,1)S(1)}, u32[]{:S(2)}, u32[]{:S(2)}) collective-permute-start(bf16[10,16,256]{2,1,0:T(8,128)(2,1)S(1)} %get-tuple-element.112), channel_id=1, source_target_pairs={{0,28},{4,8},{8,4},{12,16},{16,12},{20,24},{24,20},{28,0},{1,29},{... | collective-permute-start | bytes 245768 | tf_op jit(solution)/shard_map/ppermute | solution.py:52
  25.2 0.0 collective-permute-start.8
  25.2 1.6 %post.1 = (f32[8,32,512]{2,1,0:T(8,128)S(1)}, bf16[512,512]{1,0:T(8,128)(2,1)S(1)}) custom-call(s32[1]{0:T(128)} %bitcast.me_ref, f32[14,40,512]{2,1,0:T(8,128)S(1)} %get-tuple-element.102.u1, f32[12,40,512]{2,1,0:T(8,128)S(1)} %get-tuple-element.103.u2_in, f32[14,40,512]{2,1,0:T(8,128)S(1)} %get-tuple-element.104.text_ref), custom_call_target="tpu_custom_call" | custom-call | flops 1073741824 | bytes 4194304 | tf_op jit(solution)/shard_map/post/pallas_call | solution.py:728
  26.9 0.0 collective-permute-done.10.rest_1_
  26.9 2.0 %collective-permute-done.11.rest_2_ = bf16[32,16,128]{2,1,0:T(8,128)(2,1)S(1)} collective-permute-done((bf16[32,16,128]{2,1,0:T(8,128)(2,1)S(1)}, bf16[32,16,128]{2,1,0:T(8,128)(2,1)S(1)}, u32[]{:S(2)}, u32[]{:S(2)}) %collective-permute-start.11) | collective-permute-done | bytes 131104 | tf_op jit(solution)/shard_map/ppermute | solution.py:40
  28.9 1.9 %collective-permute-done.9.slab_b = bf16[10,16,256]{2,1,0:T(8,128)(2,1)S(1)} collective-permute-done((bf16[10,16,256]{2,1,0:T(8,128)(2,1)S(1)}, bf16[10,16,256]{2,1,0:T(8,128)(2,1)S(1)}, u32[]{:S(2)}, u32[]{:S(2)}) %collective-permute-start.9) | collective-permute-done | bytes 81952 | tf_op jit(solution)/shard_map/ppermute | solution.py:52
  30.8 0.7 %collective-permute-done.8.slab_a = bf16[10,16,256]{2,1,0:T(8,128)(2,1)S(1)} collective-permute-done((bf16[10,16,256]{2,1,0:T(8,128)(2,1)S(1)}, bf16[10,16,256]{2,1,0:T(8,128)(2,1)S(1)}, u32[]{:S(2)}, u32[]{:S(2)}) %collective-permute-start.8) | collective-permute-done | bytes 81952 | tf_op jit(solution)/shard_map/ppermute | solution.py:52
  31.5 1.8 %correct.1 = (f32[8,32,512]{2,1,0:T(8,128)}, bf16[144,16,128]{2,1,0:T(8,128)(2,1)}) custom-call(s32[1]{0:T(128)} %bitcast.me_ref, s32[1]{0:T(128)} %bitcast.1.slab_ref, f32[4,16,256]{2,1,0:T(8,128)S(1)} %get-tuple-element.95.ct_ref, bf16[17,16,256]{2,1,0:T(8,128)(2,1)S(1)} %collective-permute-done.6.side_a, ...), custom_call_target="tpu_custom_call" | custom-call | tf_op jit(solution)/shard_map/correct/pallas_call | solution.py:738
  (3 shorter events, 0.0 us)
Async XLA Ops:
  3.3 8.2 %collective-permute-start = (bf16[4,16,512]{2,1,0:T(8,128)(2,1)S(1)}, bf16[4,16,512]{2,1,0:T(8,128)(2,1)S(1)}, u32[]{:S(2)}, u32[]{:S(2)}) collective-permute-start(bf16[4,16,512]{2,1,0:T(8,128)(2,1)S(1)} %get-tuple-element.69), channel_id=1, source_target_pairs={{0,1},{1,0},{2,3},{3,2},{4,5},{5,4},{6,7},{7,6},{8,9},{9,8},{10,11... | collective-permute-start | bytes 196616 | tf_op jit(solution)/shard_map/ppermute | solution.py:52
  3.8 7.7 %collective-permute-start.1 = (bf16[4,16,512]{2,1,0:T(8,128)(2,1)S(1)}, bf16[4,16,512]{2,1,0:T(8,128)(2,1)S(1)}, u32[]{:S(2)}, u32[]{:S(2)}) collective-permute-start(bf16[4,16,512]{2,1,0:T(8,128)(2,1)S(1)} %get-tuple-element.70), channel_id=1, source_target_pairs={{0,3},{1,2},{2,1},{3,0},{4,7},{5,6},{6,5},{7,4},{8,11},{9,10},{10,... | collective-permute-start | bytes 196616 | tf_op jit(solution)/shard_map/ppermute | solution.py:52
  6.5 9.3 %collective-permute-start.2 = (bf16[8,16,512]{2,1,0:T(8,128)(2,1)S(1)}, bf16[8,16,512]{2,1,0:T(8,128)(2,1)S(1)}, u32[]{:S(2)}, u32[]{:S(2)}) collective-permute-start(bf16[8,16,512]{2,1,0:T(8,128)(2,1)S(1)} %get-tuple-element.71), channel_id=1, source_target_pairs={{0,4},{4,0},{8,12},{12,8},{16,20},{20,16},{24,28},{28,24},{1,5},{5... | collective-permute-start | bytes 393224 | tf_op jit(solution)/shard_map/ppermute | solution.py:52
  8.0 8.0 %collective-permute-start.3 = (bf16[8,16,512]{2,1,0:T(8,128)(2,1)S(1)}, bf16[8,16,512]{2,1,0:T(8,128)(2,1)S(1)}, u32[]{:S(2)}, u32[]{:S(2)}) collective-permute-start(bf16[8,16,512]{2,1,0:T(8,128)(2,1)S(1)} %get-tuple-element.72), channel_id=1, source_target_pairs={{0,28},{4,8},{8,4},{12,16},{16,12},{20,24},{24,20},{28,0},{1,29},{... | collective-permute-start | bytes 393224 | tf_op jit(solution)/shard_map/ppermute | solution.py:52
  11.6 5.6 %collective-permute-start.4 = (bf16[2,16,512]{2,1,0:T(8,128)(2,1)S(1)}, bf16[2,16,512]{2,1,0:T(8,128)(2,1)S(1)}, u32[]{:S(2)}, u32[]{:S(2)}) collective-permute-start(bf16[2,16,512]{2,1,0:T(8,128)(2,1)S(1)} %get-tuple-element.78), channel_id=1, source_target_pairs={{0,4},{4,0},{8,12},{12,8},{16,20},{20,16},{24,28},{28,24},{1,5},{5... | collective-permute-start | bytes 98312 | tf_op jit(solution)/shard_map/ppermute | solution.py:52
  11.7 6.7 %collective-permute-start.5 = (bf16[2,16,512]{2,1,0:T(8,128)(2,1)S(1)}, bf16[2,16,512]{2,1,0:T(8,128)(2,1)S(1)}, u32[]{:S(2)}, u32[]{:S(2)}) collective-permute-start(bf16[2,16,512]{2,1,0:T(8,128)(2,1)S(1)} %get-tuple-element.79), channel_id=1, source_target_pairs={{0,28},{4,8},{8,4},{12,16},{16,12},{20,24},{24,20},{28,0},{1,29},{... | collective-permute-start | bytes 98312 | tf_op jit(solution)/shard_map/ppermute | solution.py:52
  19.5 2.4 %collective-permute-start.6 = (bf16[17,16,256]{2,1,0:T(8,128)(2,1)S(1)}, bf16[17,16,256]{2,1,0:T(8,128)(2,1)S(1)}, u32[]{:S(2)}, u32[]{:S(2)}) collective-permute-start(bf16[17,16,256]{2,1,0:T(8,128)(2,1)S(1)} %pad_maximum_fusion), channel_id=1, source_target_pairs={{0,1},{1,0},{2,3},{3,2},{4,5},{5,4},{6,7},{7,6},{8,9},{9,8},{10,11... | collective-permute-start | bytes 417800 | tf_op jit(solution)/shard_map/ppermute | solution.py:52
  19.6 3.1 %collective-permute-start.7 = (bf16[1,16,256]{2,1,0:T(8,128)(2,1)S(1)}, bf16[1,16,256]{2,1,0:T(8,128)(2,1)S(1)}, u32[]{:S(2)}, u32[]{:S(2)}) collective-permute-start(bf16[1,16,256]{2,1,0:T(8,128)(2,1)S(1)} %get-tuple-element.98), channel_id=1, source_target_pairs={{0,3},{1,2},{2,1},{3,0},{4,7},{5,6},{6,5},{7,4},{8,11},{9,10},{10,... | collective-permute-start | bytes 24584 | tf_op jit(solution)/shard_map/ppermute | solution.py:52
  20.2 6.6 %collective-permute-start.10 = (bf16[32,16,128]{2,1,0:T(8,128)(2,1)S(1)}, bf16[32,16,128]{2,1,0:T(8,128)(2,1)S(1)}, u32[]{:S(2)}, u32[]{:S(2)}) collective-permute-start(bf16[32,16,128]{2,1,0:T(8,128)(2,1)S(1)} %get-tuple-element.108), channel_id=1, source_target_pairs={{0,3},{1,2},{2,1},{3,0},{4,7},{5,6},{6,5},{7,4},{8,11},{9,10},{10,... | collective-permute-start | bytes 393224 | tf_op jit(solution)/shard_map/ppermute | solution.py:52
  21.4 7.5 %collective-permute-start.11 = (bf16[32,16,128]{2,1,0:T(8,128)(2,1)S(1)}, bf16[32,16,128]{2,1,0:T(8,128)(2,1)S(1)}, u32[]{:S(2)}, u32[]{:S(2)}) collective-permute-start(bf16[32,16,128]{2,1,0:T(8,128)(2,1)S(1)} %get-tuple-element.109), channel_id=1, source_target_pairs={{0,2},{1,3},{2,0},{3,1},{4,6},{5,7},{6,4},{7,5},{8,10},{9,11},{10,... | collective-permute-start | bytes 393224 | tf_op jit(solution)/shard_map/ppermute | solution.py:40
  22.8 8.0 %collective-permute-start.9 = (bf16[10,16,256]{2,1,0:T(8,128)(2,1)S(1)}, bf16[10,16,256]{2,1,0:T(8,128)(2,1)S(1)}, u32[]{:S(2)}, u32[]{:S(2)}) collective-permute-start(bf16[10,16,256]{2,1,0:T(8,128)(2,1)S(1)} %get-tuple-element.112), channel_id=1, source_target_pairs={{0,28},{4,8},{8,4},{12,16},{16,12},{20,24},{24,20},{28,0},{1,29},{... | collective-permute-start | bytes 245768 | tf_op jit(solution)/shard_map/ppermute | solution.py:52
  25.2 6.3 %collective-permute-start.8 = (bf16[10,16,256]{2,1,0:T(8,128)(2,1)S(1)}, bf16[10,16,256]{2,1,0:T(8,128)(2,1)S(1)}, u32[]{:S(2)}, u32[]{:S(2)}) collective-permute-start(bf16[10,16,256]{2,1,0:T(8,128)(2,1)S(1)} %get-tuple-element.113), channel_id=1, source_target_pairs={{0,4},{4,0},{8,12},{12,8},{16,20},{20,16},{24,28},{28,24},{1,5},{5... | collective-permute-start | bytes 245768 | tf_op jit(solution)/shard_map/ppermute | solution.py:52

commit v9 on v8

--- a/solution.py
+++ b/solution.py
@@ -336,21 +336,21 @@
             u1[p] = KEEP * u0[p + 1] + PULL * neighbour_total(u0[p], u0[p + 1], u0[p + 2])
         return carry
 
-    lax.fori_loop(0, HALO - 1, outer, 0)
+    lax.fori_loop(0, HALO - 1, outer, 0, unroll=True)
 
     def first(p, carry):
         v = relaxed(u0[p], u0[p + 1], u0[p + 2], text_ref[p], CENTRE)
         u1[p] = masked(v, ny, mask)
         return carry
 
-    lax.fori_loop(HALO - 1, nx + HALO - 1, first, 0, unroll=2)
+    lax.fori_loop(HALO - 1, nx + HALO - 1, first, 0, unroll=4)
 
     def second(p, carry):
         v = relaxed(u1[p], u1[p + 1], u1[p + 2], text_ref[p + 1], CENTRE)
         u2_ref[p] = masked(v, ny, mask)
         return carry
 
-    lax.fori_loop(HALO - 1, nx + 1, second, 0, unroll=2)
+    lax.fori_loop(HALO - 1, nx + 1, second, 0, unroll=3)
     for p in range(2, nx - 2):
         inside[p - 2] = residual(u2_ref, text_ref, p, ny)
 

time: 33.5 us -> 33.4 us (level)
  no operation moved by 1% of the time
where the time goes in v9:
time: 33.4 us; the launch traced here: 33.3 us
  starting transfers between devices  15.4 us (46%)
  Pallas kernels  10.2 us (31%)
  waiting for transfers between devices  6.86 us (21%)
  between operations  0.74 us (2%)
    ppermute x11, starting transfers between devices, swapped(): return lax.ppermute(x, axis, sorted(pairs))  14.9 us
    ppermute x11, waiting for transfers between devices, swapped(): return lax.ppermute(x, axis, sorted(pairs))  4.79 us
    ppermute x1, waiting for transfers between devices, cyclic(): return lax.ppermute(x, axis, [(i, (i + by) % count) for i in range(count)])  2.07 us
    pallas_call x1, Pallas kernels, local(): pl.pallas_call(functools.partial(correct_kernel, depths), out_shape=(shap...  1.8 us
    pallas_call x1, Pallas kernels, local(): pl.pallas_call(network_kernel, out_shape=tuple((shape((capacity // 32, 16...  1.79 us
    pallas_call x1, Pallas kernels, local(): pl.pallas_call(load_kernel, out_shape=(shape((nx, ny, nz), F32), shape((n...  1.65 us
    pallas_call x1, Pallas kernels, local(): pl.pallas_call(functools.partial(post_kernel, depths), out_shape=(shape((...  1.63 us
    pallas_call x1, Pallas kernels, local(): pl.pallas_call(functools.partial(inner_kernel, depths), out_shape=(shape(...  1.14 us
  transfers between devices with their start and end apart: 12, of which 6 were waited for; matrix products, arithmetic and copies ran while one was open for 0% of the time, Pallas kernels for 14%

profile of v9, /device:TPU:0, one launch (start us, length us, event | category | flops | bytes accessed | tf_op | source)
XLA Modules:
  0.0 33.3 jit_solution(15378341712634002596)
XLA Ops:
  0.6 1.7 %load.1 = (f32[8,32,512]{2,1,0:T(8,128)S(1)}, bf16[512,1024]{1,0:T(8,128)(2,1)S(1)}, bf16[8,16,512]{2,1,0:T(8,128)(2,1)S(1)}, bf16[8,16,512]{2,1,0:T(8,128)(2,1)...) custom-call(s32[1]{0:T(128)} %bitcast.1.slab_ref, ...), custom_call_target="tpu_custom_call" | custom-call | tf_op jit(solution)/shard_map/load/pallas_call | solution.py:618
  2.3 1.0 %uptake.1 = (f32[8,32,512]{2,1,0:T(8,128)S(1)}, f32[8,1024]{1,0:T(8,128)S(1)}, bf16[4,16,512]{2,1,0:T(8,128)(2,1)S(1)}, bf16[4,16,512]{2,1,0:T(8,128)(2,1)S(1)}, f32[8,512]{1,0:T(8,128)S(1)}) custom-call(s32[1]{0:T(128)} %bitcast.me_ref, f32[8,32,512]{2,1,0:T(8,128)S(1)} %get-tuple-element.57.u_ref, bf16[512,1024]{1,0:T(8,128)(2,1)S(1)} %get-tuple-element.58.place_ref, ...), custom_call_target="tpu_custom_call" | custom-call | flops 2147483648 | bytes 1048576 | tf_op jit(solution)/shard_map/uptake/pallas_call | solution.py:636
  3.3 0.5 %collective-permute-start = (bf16[4,16,512]{2,1,0:T(8,128)(2,1)S(1)}, bf16[4,16,512]{2,1,0:T(8,128)(2,1)S(1)}, u32[]{:S(2)}, u32[]{:S(2)}) collective-permute-start(bf16[4,16,512]{2,1,0:T(8,128)(2,1)S(1)} %get-tuple-element.69), channel_id=1, source_target_pairs={{0,1},{1,0},{2,3},{3,2},{4,5},{5,4},{6,7},{7,6},{8,9},{9,8},{10,11... | collective-permute-start | bytes 196616 | tf_op jit(solution)/shard_map/ppermute | solution.py:52
  3.8 2.6 %collective-permute-start.1 = (bf16[4,16,512]{2,1,0:T(8,128)(2,1)S(1)}, bf16[4,16,512]{2,1,0:T(8,128)(2,1)S(1)}, u32[]{:S(2)}, u32[]{:S(2)}) collective-permute-start(bf16[4,16,512]{2,1,0:T(8,128)(2,1)S(1)} %get-tuple-element.70), channel_id=1, source_target_pairs={{0,3},{1,2},{2,1},{3,0},{4,7},{5,6},{6,5},{7,4},{8,11},{9,10},{10,... | collective-permute-start | bytes 196616 | tf_op jit(solution)/shard_map/ppermute | solution.py:52
  6.5 1.5 %collective-permute-start.2 = (bf16[8,16,512]{2,1,0:T(8,128)(2,1)S(1)}, bf16[8,16,512]{2,1,0:T(8,128)(2,1)S(1)}, u32[]{:S(2)}, u32[]{:S(2)}) collective-permute-start(bf16[8,16,512]{2,1,0:T(8,128)(2,1)S(1)} %get-tuple-element.71), channel_id=1, source_target_pairs={{0,4},{4,0},{8,12},{12,8},{16,20},{20,16},{24,28},{28,24},{1,5},{5... | collective-permute-start | bytes 393224 | tf_op jit(solution)/shard_map/ppermute | solution.py:52
  8.0 3.6 %collective-permute-start.3 = (bf16[8,16,512]{2,1,0:T(8,128)(2,1)S(1)}, bf16[8,16,512]{2,1,0:T(8,128)(2,1)S(1)}, u32[]{:S(2)}, u32[]{:S(2)}) collective-permute-start(bf16[8,16,512]{2,1,0:T(8,128)(2,1)S(1)} %get-tuple-element.72), channel_id=1, source_target_pairs={{0,28},{4,8},{8,4},{12,16},{16,12},{20,24},{24,20},{28,0},{1,29},{... | collective-permute-start | bytes 393224 | tf_op jit(solution)/shard_map/ppermute | solution.py:52
  11.5 0.0 collective-permute-done.side_a
  11.5 0.0 collective-permute-done.1.side_b
  11.5 0.1 corner.1
  11.6 0.1 collective-permute-start.4
  11.7 2.3 %collective-permute-start.5 = (bf16[2,16,512]{2,1,0:T(8,128)(2,1)S(1)}, bf16[2,16,512]{2,1,0:T(8,128)(2,1)S(1)}, u32[]{:S(2)}, u32[]{:S(2)}) collective-permute-start(bf16[2,16,512]{2,1,0:T(8,128)(2,1)S(1)} %get-tuple-element.79), channel_id=1, source_target_pairs={{0,28},{4,8},{8,4},{12,16},{16,12},{20,24},{24,20},{28,0},{1,29},{... | collective-permute-start | bytes 98312 | tf_op jit(solution)/shard_map/ppermute | solution.py:52
  14.0 1.8 %network.1 = (bf16[32,16,128]{2,1,0:T(8,128)(2,1)S(1)}, bf16[16,16,256]{2,1,0:T(8,128)(2,1)S(1)}, bf16[32,16,128]{2,1,0:T(8,128)(2,1)S(1)}, bf16[32,16,128]{2,1,...) custom-call(s32[1]{0:T(128)} %bitcast.me_ref, s32[1]{0:T(128)} %bitcast.1.slab_ref, ...), custom_call_target="tpu_custom_call" | custom-call | flops 2147483648 | bytes 1048576 | tf_op jit(solution)/shard_map/network/pallas_call | solution.py:670
  15.8 0.0 collective-permute-done.2.field_a
  15.8 0.2 collective-permute-done.3.field_b
  15.9 1.1 %inner.1 = (f32[16,40,512]{2,1,0:T(8,128)S(1)}, f32[14,40,512]{2,1,0:T(8,128)S(1)}, f32[14,40,512]{2,1,0:T(8,128)S(1)}, f32[12,40,512]{2,1,0:T(8,128)S(1)}, f32[4,32,512]{2,1,0:T(8,128)S(1)}) custom-call(s32[1]{0:T(128)} %bitcast.me_ref, s32[1]{0:T(128)} %bitcast.1.slab_ref, f32[8,32,512]{2,1,0:T(8,128)S(1)} %get-tuple-element.57.u_ref, ...), custom_call_target="tpu_custom_call" | custom-call | flops 1048576 | bytes 1048576 | tf_op jit(solution)/shard_map/inner/pallas_call | solution.py:683
  17.1 0.0 collective-permute-done.4.slab_a
  17.1 1.3 %collective-permute-done.5.slab_b = bf16[2,16,512]{2,1,0:T(8,128)(2,1)S(1)} collective-permute-done((bf16[2,16,512]{2,1,0:T(8,128)(2,1)S(1)}, bf16[2,16,512]{2,1,0:T(8,128)(2,1)S(1)}, u32[]{:S(2)}, u32[]{:S(2)}) %collective-permute-start.5) | collective-permute-done | bytes 32800 | tf_op jit(solution)/shard_map/ppermute | solution.py:52
  18.4 1.1 %smooth.1 = (f32[14,40,512]{2,1,0:T(8,128)S(1)}, f32[14,40,512]{2,1,0:T(8,128)S(1)}, f32[12,40,512]{2,1,0:T(8,128)S(1)}, f32[4,16,256]{2,1,0:T(8,128)S(1)}, bf16...) custom-call(s32[1]{0:T(128)} %bitcast.me_ref, ...), custom_call_target="tpu_custom_call", output_to_operand_aliasing={{0}: (3, {}), {1}: (4, {}), {2}: (5, {})} | custom-call | tf_op jit(solution)/shard_map/smooth/pallas_call | solution.py:699
  19.5 0.1 collective-permute-start.6
  19.6 0.6 %collective-permute-start.7 = (bf16[1,16,256]{2,1,0:T(8,128)(2,1)S(1)}, bf16[1,16,256]{2,1,0:T(8,128)(2,1)S(1)}, u32[]{:S(2)}, u32[]{:S(2)}) collective-permute-start(bf16[1,16,256]{2,1,0:T(8,128)(2,1)S(1)} %get-tuple-element.98), channel_id=1, source_target_pairs={{0,3},{1,2},{2,1},{3,0},{4,7},{5,6},{6,5},{7,4},{8,11},{9,10},{10,... | collective-permute-start | bytes 24584 | tf_op jit(solution)/shard_map/ppermute | solution.py:52
  20.2 1.2 %collective-permute-start.10 = (bf16[32,16,128]{2,1,0:T(8,128)(2,1)S(1)}, bf16[32,16,128]{2,1,0:T(8,128)(2,1)S(1)}, u32[]{:S(2)}, u32[]{:S(2)}) collective-permute-start(bf16[32,16,128]{2,1,0:T(8,128)(2,1)S(1)} %get-tuple-element.108), channel_id=1, source_target_pairs={{0,3},{1,2},{2,1},{3,0},{4,7},{5,6},{6,5},{7,4},{8,11},{9,10},{10,... | collective-permute-start | bytes 393224 | tf_op jit(solution)/shard_map/ppermute | solution.py:52
  21.4 0.5 %collective-permute-start.11 = (bf16[32,16,128]{2,1,0:T(8,128)(2,1)S(1)}, bf16[32,16,128]{2,1,0:T(8,128)(2,1)S(1)}, u32[]{:S(2)}, u32[]{:S(2)}) collective-permute-start(bf16[32,16,128]{2,1,0:T(8,128)(2,1)S(1)} %get-tuple-element.109), channel_id=1, source_target_pairs={{0,2},{1,3},{2,0},{3,1},{4,6},{5,7},{6,4},{7,5},{8,10},{9,11},{10,... | collective-permute-start | bytes 393224 | tf_op jit(solution)/shard_map/ppermute | solution.py:40
  21.9 0.0 collective-permute-done.6.side_a
  21.9 0.8 %collective-permute-done.7.side_b = bf16[1,16,256]{2,1,0:T(8,128)(2,1)S(1)} collective-permute-done((bf16[1,16,256]{2,1,0:T(8,128)(2,1)S(1)}, bf16[1,16,256]{2,1,0:T(8,128)(2,1)S(1)}, u32[]{:S(2)}, u32[]{:S(2)}) %collective-permute-start.7) | collective-permute-done | bytes 8224 | tf_op jit(solution)/shard_map/ppermute | solution.py:52
  22.8 2.4 %collective-permute-start.9 = (bf16[10,16,256]{2,1,0:T(8,128)(2,1)S(1)}, bf16[10,16,256]{2,1,0:T(8,128)(2,1)S(1)}, u32[]{:S(2)}, u32[]{:S(2)}) collective-permute-start(bf16[10,16,256]{2,1,0:T(8,128)(2,1)S(1)} %get-tuple-element.112), channel_id=1, source_target_pairs={{0,28},{4,8},{8,4},{12,16},{16,12},{20,24},{24,20},{28,0},{1,29},{... | collective-permute-start | bytes 245768 | tf_op jit(solution)/shard_map/ppermute | solution.py:52
  25.2 0.0 collective-permute-start.8
  25.2 1.6 %post.1 = (f32[8,32,512]{2,1,0:T(8,128)S(1)}, bf16[512,512]{1,0:T(8,128)(2,1)S(1)}) custom-call(s32[1]{0:T(128)} %bitcast.me_ref, f32[14,40,512]{2,1,0:T(8,128)S(1)} %get-tuple-element.102.u1, f32[12,40,512]{2,1,0:T(8,128)S(1)} %get-tuple-element.103.u2_in, f32[14,40,512]{2,1,0:T(8,128)S(1)} %get-tuple-element.104.text_ref), custom_call_target="tpu_custom_call" | custom-call | flops 1073741824 | bytes 4194304 | tf_op jit(solution)/shard_map/post/pallas_call | solution.py:728
  26.8 0.0 collective-permute-done.10.rest_1_
  26.9 2.1 %collective-permute-done.11.rest_2_ = bf16[32,16,128]{2,1,0:T(8,128)(2,1)S(1)} collective-permute-done((bf16[32,16,128]{2,1,0:T(8,128)(2,1)S(1)}, bf16[32,16,128]{2,1,0:T(8,128)(2,1)S(1)}, u32[]{:S(2)}, u32[]{:S(2)}) %collective-permute-start.11) | collective-permute-done | bytes 131104 | tf_op jit(solution)/shard_map/ppermute | solution.py:40
  28.9 1.9 %collective-permute-done.9.slab_b = bf16[10,16,256]{2,1,0:T(8,128)(2,1)S(1)} collective-permute-done((bf16[10,16,256]{2,1,0:T(8,128)(2,1)S(1)}, bf16[10,16,256]{2,1,0:T(8,128)(2,1)S(1)}, u32[]{:S(2)}, u32[]{:S(2)}) %collective-permute-start.9) | collective-permute-done | bytes 81952 | tf_op jit(solution)/shard_map/ppermute | solution.py:52
  30.8 0.6 %collective-permute-done.8.slab_a = bf16[10,16,256]{2,1,0:T(8,128)(2,1)S(1)} collective-permute-done((bf16[10,16,256]{2,1,0:T(8,128)(2,1)S(1)}, bf16[10,16,256]{2,1,0:T(8,128)(2,1)S(1)}, u32[]{:S(2)}, u32[]{:S(2)}) %collective-permute-start.8) | collective-permute-done | bytes 81952 | tf_op jit(solution)/shard_map/ppermute | solution.py:52
  31.5 1.8 %correct.1 = (f32[8,32,512]{2,1,0:T(8,128)}, bf16[144,16,128]{2,1,0:T(8,128)(2,1)}) custom-call(s32[1]{0:T(128)} %bitcast.me_ref, s32[1]{0:T(128)} %bitcast.1.slab_ref, f32[4,16,256]{2,1,0:T(8,128)S(1)} %get-tuple-element.95.ct_ref, bf16[17,16,256]{2,1,0:T(8,128)(2,1)S(1)} %collective-permute-done.6.side_a, ...), custom_call_target="tpu_custom_call" | custom-call | tf_op jit(solution)/shard_map/correct/pallas_call | solution.py:738
  (3 shorter events, 0.0 us)
Async XLA Ops:
  3.3 8.2 %collective-permute-start = (bf16[4,16,512]{2,1,0:T(8,128)(2,1)S(1)}, bf16[4,16,512]{2,1,0:T(8,128)(2,1)S(1)}, u32[]{:S(2)}, u32[]{:S(2)}) collective-permute-start(bf16[4,16,512]{2,1,0:T(8,128)(2,1)S(1)} %get-tuple-element.69), channel_id=1, source_target_pairs={{0,1},{1,0},{2,3},{3,2},{4,5},{5,4},{6,7},{7,6},{8,9},{9,8},{10,11... | collective-permute-start | bytes 196616 | tf_op jit(solution)/shard_map/ppermute | solution.py:52
  3.8 7.7 %collective-permute-start.1 = (bf16[4,16,512]{2,1,0:T(8,128)(2,1)S(1)}, bf16[4,16,512]{2,1,0:T(8,128)(2,1)S(1)}, u32[]{:S(2)}, u32[]{:S(2)}) collective-permute-start(bf16[4,16,512]{2,1,0:T(8,128)(2,1)S(1)} %get-tuple-element.70), channel_id=1, source_target_pairs={{0,3},{1,2},{2,1},{3,0},{4,7},{5,6},{6,5},{7,4},{8,11},{9,10},{10,... | collective-permute-start | bytes 196616 | tf_op jit(solution)/shard_map/ppermute | solution.py:52
  6.5 9.3 %collective-permute-start.2 = (bf16[8,16,512]{2,1,0:T(8,128)(2,1)S(1)}, bf16[8,16,512]{2,1,0:T(8,128)(2,1)S(1)}, u32[]{:S(2)}, u32[]{:S(2)}) collective-permute-start(bf16[8,16,512]{2,1,0:T(8,128)(2,1)S(1)} %get-tuple-element.71), channel_id=1, source_target_pairs={{0,4},{4,0},{8,12},{12,8},{16,20},{20,16},{24,28},{28,24},{1,5},{5... | collective-permute-start | bytes 393224 | tf_op jit(solution)/shard_map/ppermute | solution.py:52
  8.0 8.0 %collective-permute-start.3 = (bf16[8,16,512]{2,1,0:T(8,128)(2,1)S(1)}, bf16[8,16,512]{2,1,0:T(8,128)(2,1)S(1)}, u32[]{:S(2)}, u32[]{:S(2)}) collective-permute-start(bf16[8,16,512]{2,1,0:T(8,128)(2,1)S(1)} %get-tuple-element.72), channel_id=1, source_target_pairs={{0,28},{4,8},{8,4},{12,16},{16,12},{20,24},{24,20},{28,0},{1,29},{... | collective-permute-start | bytes 393224 | tf_op jit(solution)/shard_map/ppermute | solution.py:52
  11.6 5.5 %collective-permute-start.4 = (bf16[2,16,512]{2,1,0:T(8,128)(2,1)S(1)}, bf16[2,16,512]{2,1,0:T(8,128)(2,1)S(1)}, u32[]{:S(2)}, u32[]{:S(2)}) collective-permute-start(bf16[2,16,512]{2,1,0:T(8,128)(2,1)S(1)} %get-tuple-element.78), channel_id=1, source_target_pairs={{0,4},{4,0},{8,12},{12,8},{16,20},{20,16},{24,28},{28,24},{1,5},{5... | collective-permute-start | bytes 98312 | tf_op jit(solution)/shard_map/ppermute | solution.py:52
  11.7 6.7 %collective-permute-start.5 = (bf16[2,16,512]{2,1,0:T(8,128)(2,1)S(1)}, bf16[2,16,512]{2,1,0:T(8,128)(2,1)S(1)}, u32[]{:S(2)}, u32[]{:S(2)}) collective-permute-start(bf16[2,16,512]{2,1,0:T(8,128)(2,1)S(1)} %get-tuple-element.79), channel_id=1, source_target_pairs={{0,28},{4,8},{8,4},{12,16},{16,12},{20,24},{24,20},{28,0},{1,29},{... | collective-permute-start | bytes 98312 | tf_op jit(solution)/shard_map/ppermute | solution.py:52
  19.5 2.4 %collective-permute-start.6 = (bf16[17,16,256]{2,1,0:T(8,128)(2,1)S(1)}, bf16[17,16,256]{2,1,0:T(8,128)(2,1)S(1)}, u32[]{:S(2)}, u32[]{:S(2)}) collective-permute-start(bf16[17,16,256]{2,1,0:T(8,128)(2,1)S(1)} %pad_maximum_fusion), channel_id=1, source_target_pairs={{0,1},{1,0},{2,3},{3,2},{4,5},{5,4},{6,7},{7,6},{8,9},{9,8},{10,11... | collective-permute-start | bytes 417800 | tf_op jit(solution)/shard_map/ppermute | solution.py:52
  19.6 3.1 %collective-permute-start.7 = (bf16[1,16,256]{2,1,0:T(8,128)(2,1)S(1)}, bf16[1,16,256]{2,1,0:T(8,128)(2,1)S(1)}, u32[]{:S(2)}, u32[]{:S(2)}) collective-permute-start(bf16[1,16,256]{2,1,0:T(8,128)(2,1)S(1)} %get-tuple-element.98), channel_id=1, source_target_pairs={{0,3},{1,2},{2,1},{3,0},{4,7},{5,6},{6,5},{7,4},{8,11},{9,10},{10,... | collective-permute-start | bytes 24584 | tf_op jit(solution)/shard_map/ppermute | solution.py:52
  20.2 6.6 %collective-permute-start.10 = (bf16[32,16,128]{2,1,0:T(8,128)(2,1)S(1)}, bf16[32,16,128]{2,1,0:T(8,128)(2,1)S(1)}, u32[]{:S(2)}, u32[]{:S(2)}) collective-permute-start(bf16[32,16,128]{2,1,0:T(8,128)(2,1)S(1)} %get-tuple-element.108), channel_id=1, source_target_pairs={{0,3},{1,2},{2,1},{3,0},{4,7},{5,6},{6,5},{7,4},{8,11},{9,10},{10,... | collective-permute-start | bytes 393224 | tf_op jit(solution)/shard_map/ppermute | solution.py:52
  21.4 7.5 %collective-permute-start.11 = (bf16[32,16,128]{2,1,0:T(8,128)(2,1)S(1)}, bf16[32,16,128]{2,1,0:T(8,128)(2,1)S(1)}, u32[]{:S(2)}, u32[]{:S(2)}) collective-permute-start(bf16[32,16,128]{2,1,0:T(8,128)(2,1)S(1)} %get-tuple-element.109), channel_id=1, source_target_pairs={{0,2},{1,3},{2,0},{3,1},{4,6},{5,7},{6,4},{7,5},{8,10},{9,11},{10,... | collective-permute-start | bytes 393224 | tf_op jit(solution)/shard_map/ppermute | solution.py:40
  22.8 8.0 %collective-permute-start.9 = (bf16[10,16,256]{2,1,0:T(8,128)(2,1)S(1)}, bf16[10,16,256]{2,1,0:T(8,128)(2,1)S(1)}, u32[]{:S(2)}, u32[]{:S(2)}) collective-permute-start(bf16[10,16,256]{2,1,0:T(8,128)(2,1)S(1)} %get-tuple-element.112), channel_id=1, source_target_pairs={{0,28},{4,8},{8,4},{12,16},{16,12},{20,24},{24,20},{28,0},{1,29},{... | collective-permute-start | bytes 245768 | tf_op jit(solution)/shard_map/ppermute | solution.py:52
  25.2 6.3 %collective-permute-start.8 = (bf16[10,16,256]{2,1,0:T(8,128)(2,1)S(1)}, bf16[10,16,256]{2,1,0:T(8,128)(2,1)S(1)}, u32[]{:S(2)}, u32[]{:S(2)}) collective-permute-start(bf16[10,16,256]{2,1,0:T(8,128)(2,1)S(1)} %get-tuple-element.113), channel_id=1, source_target_pairs={{0,4},{4,0},{8,12},{12,8},{16,20},{20,16},{24,28},{28,24},{1,5},{5... | collective-permute-start | bytes 245768 | tf_op jit(solution)/shard_map/ppermute | solution.py:52

commit v10 on v9

--- a/solution.py
+++ b/solution.py
@@ -86,7 +86,7 @@
     copies[0].wait()
     cell_z = cell_ref[...] % nz
     cell_z = (cell_z % tiles) * LANES + cell_z // tiles
-    place_ref[...] = (iota(place_ref.shape, 0) == cell_z).astype(F32).astype(BF16)
+    place_ref[...] = (iota(place_ref.shape, 0) == cell_z).astype(BF16)
     copies[1].wait()
     high, low = halves(raw[...].reshape(rows, nz))
     both = dot(jnp.concatenate([high, low], axis=0), order, 1, 0)
@@ -206,7 +206,7 @@
     start = 0
     for index, out in enumerate(outs):
         size = capacity if index < depths else MIG
-        chosen = (iota((size, agents), 0) == key - start).astype(F32).astype(BF16)
+        chosen = (iota((size, agents), 0) == key - start).astype(BF16)
         placed = dot(chosen, updated, 1, 0).astype(BF16)
         start += size
         blocks = out.shape[0]
@@ -387,7 +387,7 @@
         cell_row = cell_row.astype(jnp.int32) - jnp.where(after, 0, (nx - near) * ny)
         wanted = jnp.logical_and(cell_row >= 0, cell_row < near * ny)
         key = jnp.where(wanted, part.astype(jnp.int32) * (near * ny) + cell_row, -1)
-        one_z = (iota((PART, agents), 0) == place.astype(jnp.int32)).astype(F32).astype(BF16)
+        one_z = (iota((PART, agents), 0) == place.astype(jnp.int32)).astype(BF16)
         key_rows = iota((near * ny * (nz // PART), agents), 0)
         taken = jnp.where(key_rows == key, uptake, 0.0).astype(BF16)
         source = dot(taken, one_z, 1, 1)

time: 33.4 us -> 33.4 us (level)
  no operation moved by 1% of the time
where the time goes in v10:
time: 33.4 us; the launch traced here: 33.3 us
  starting transfers between devices  15.4 us (46%)
  Pallas kernels  10.2 us (31%)
  waiting for transfers between devices  6.86 us (21%)
  between operations  0.74 us (2%)
    ppermute x11, starting transfers between devices, swapped(): return lax.ppermute(x, axis, sorted(pairs))  14.9 us
    ppermute x11, waiting for transfers between devices, swapped(): return lax.ppermute(x, axis, sorted(pairs))  4.79 us
    ppermute x1, waiting for transfers between devices, cyclic(): return lax.ppermute(x, axis, [(i, (i + by) % count) for i in range(count)])  2.07 us
    pallas_call x1, Pallas kernels, local(): pl.pallas_call(functools.partial(correct_kernel, depths), out_shape=(shap...  1.8 us
    pallas_call x1, Pallas kernels, local(): pl.pallas_call(network_kernel, out_shape=tuple((shape((capacity // 32, 16...  1.79 us
    pallas_call x1, Pallas kernels, local(): pl.pallas_call(load_kernel, out_shape=(shape((nx, ny, nz), F32), shape((n...  1.65 us
    pallas_call x1, Pallas kernels, local(): pl.pallas_call(functools.partial(post_kernel, depths), out_shape=(shape((...  1.63 us
    pallas_call x1, Pallas kernels, local(): pl.pallas_call(functools.partial(inner_kernel, depths), out_shape=(shape(...  1.14 us
  transfers between devices with their start and end apart: 12, of which 6 were waited for; matrix products, arithmetic and copies ran while one was open for 0% of the time, Pallas kernels for 14%

profile of v10, /device:TPU:0, one launch (start us, length us, event | category | flops | bytes accessed | tf_op | source)
XLA Modules:
  0.0 33.3 jit_solution(15378341712634002596)
XLA Ops:
  0.6 1.7 %load.1 = (f32[8,32,512]{2,1,0:T(8,128)S(1)}, bf16[512,1024]{1,0:T(8,128)(2,1)S(1)}, bf16[8,16,512]{2,1,0:T(8,128)(2,1)S(1)}, bf16[8,16,512]{2,1,0:T(8,128)(2,1)...) custom-call(s32[1]{0:T(128)} %bitcast.1.slab_ref, ...), custom_call_target="tpu_custom_call" | custom-call | tf_op jit(solution)/shard_map/load/pallas_call | solution.py:618
  2.3 1.0 %uptake.1 = (f32[8,32,512]{2,1,0:T(8,128)S(1)}, f32[8,1024]{1,0:T(8,128)S(1)}, bf16[4,16,512]{2,1,0:T(8,128)(2,1)S(1)}, bf16[4,16,512]{2,1,0:T(8,128)(2,1)S(1)}, f32[8,512]{1,0:T(8,128)S(1)}) custom-call(s32[1]{0:T(128)} %bitcast.me_ref, f32[8,32,512]{2,1,0:T(8,128)S(1)} %get-tuple-element.57.u_ref, bf16[512,1024]{1,0:T(8,128)(2,1)S(1)} %get-tuple-element.58.place_ref, ...), custom_call_target="tpu_custom_call" | custom-call | flops 2147483648 | bytes 1048576 | tf_op jit(solution)/shard_map/uptake/pallas_call | solution.py:636
  3.3 0.5 %collective-permute-start = (bf16[4,16,512]{2,1,0:T(8,128)(2,1)S(1)}, bf16[4,16,512]{2,1,0:T(8,128)(2,1)S(1)}, u32[]{:S(2)}, u32[]{:S(2)}) collective-permute-start(bf16[4,16,512]{2,1,0:T(8,128)(2,1)S(1)} %get-tuple-element.69), channel_id=1, source_target_pairs={{0,1},{1,0},{2,3},{3,2},{4,5},{5,4},{6,7},{7,6},{8,9},{9,8},{10,11... | collective-permute-start | bytes 196616 | tf_op jit(solution)/shard_map/ppermute | solution.py:52
  3.8 2.6 %collective-permute-start.1 = (bf16[4,16,512]{2,1,0:T(8,128)(2,1)S(1)}, bf16[4,16,512]{2,1,0:T(8,128)(2,1)S(1)}, u32[]{:S(2)}, u32[]{:S(2)}) collective-permute-start(bf16[4,16,512]{2,1,0:T(8,128)(2,1)S(1)} %get-tuple-element.70), channel_id=1, source_target_pairs={{0,3},{1,2},{2,1},{3,0},{4,7},{5,6},{6,5},{7,4},{8,11},{9,10},{10,... | collective-permute-start | bytes 196616 | tf_op jit(solution)/shard_map/ppermute | solution.py:52
  6.5 1.5 %collective-permute-start.2 = (bf16[8,16,512]{2,1,0:T(8,128)(2,1)S(1)}, bf16[8,16,512]{2,1,0:T(8,128)(2,1)S(1)}, u32[]{:S(2)}, u32[]{:S(2)}) collective-permute-start(bf16[8,16,512]{2,1,0:T(8,128)(2,1)S(1)} %get-tuple-element.71), channel_id=1, source_target_pairs={{0,4},{4,0},{8,12},{12,8},{16,20},{20,16},{24,28},{28,24},{1,5},{5... | collective-permute-start | bytes 393224 | tf_op jit(solution)/shard_map/ppermute | solution.py:52
  8.0 3.6 %collective-permute-start.3 = (bf16[8,16,512]{2,1,0:T(8,128)(2,1)S(1)}, bf16[8,16,512]{2,1,0:T(8,128)(2,1)S(1)}, u32[]{:S(2)}, u32[]{:S(2)}) collective-permute-start(bf16[8,16,512]{2,1,0:T(8,128)(2,1)S(1)} %get-tuple-element.72), channel_id=1, source_target_pairs={{0,28},{4,8},{8,4},{12,16},{16,12},{20,24},{24,20},{28,0},{1,29},{... | collective-permute-start | bytes 393224 | tf_op jit(solution)/shard_map/ppermute | solution.py:52
  11.5 0.0 collective-permute-done.side_a
  11.5 0.0 collective-permute-done.1.side_b
  11.5 0.1 corner.1
  11.6 0.1 collective-permute-start.4
  11.7 2.3 %collective-permute-start.5 = (bf16[2,16,512]{2,1,0:T(8,128)(2,1)S(1)}, bf16[2,16,512]{2,1,0:T(8,128)(2,1)S(1)}, u32[]{:S(2)}, u32[]{:S(2)}) collective-permute-start(bf16[2,16,512]{2,1,0:T(8,128)(2,1)S(1)} %get-tuple-element.79), channel_id=1, source_target_pairs={{0,28},{4,8},{8,4},{12,16},{16,12},{20,24},{24,20},{28,0},{1,29},{... | collective-permute-start | bytes 98312 | tf_op jit(solution)/shard_map/ppermute | solution.py:52
  14.0 1.8 %network.1 = (bf16[32,16,128]{2,1,0:T(8,128)(2,1)S(1)}, bf16[16,16,256]{2,1,0:T(8,128)(2,1)S(1)}, bf16[32,16,128]{2,1,0:T(8,128)(2,1)S(1)}, bf16[32,16,128]{2,1,...) custom-call(s32[1]{0:T(128)} %bitcast.me_ref, s32[1]{0:T(128)} %bitcast.1.slab_ref, ...), custom_call_target="tpu_custom_call" | custom-call | flops 2147483648 | bytes 1048576 | tf_op jit(solution)/shard_map/network/pallas_call | solution.py:670
  15.8 0.0 collective-permute-done.2.field_a
  15.8 0.2 collective-permute-done.3.field_b
  15.9 1.1 %inner.1 = (f32[16,40,512]{2,1,0:T(8,128)S(1)}, f32[14,40,512]{2,1,0:T(8,128)S(1)}, f32[14,40,512]{2,1,0:T(8,128)S(1)}, f32[12,40,512]{2,1,0:T(8,128)S(1)}, f32[4,32,512]{2,1,0:T(8,128)S(1)}) custom-call(s32[1]{0:T(128)} %bitcast.me_ref, s32[1]{0:T(128)} %bitcast.1.slab_ref, f32[8,32,512]{2,1,0:T(8,128)S(1)} %get-tuple-element.57.u_ref, ...), custom_call_target="tpu_custom_call" | custom-call | flops 1048576 | bytes 1048576 | tf_op jit(solution)/shard_map/inner/pallas_call | solution.py:683
  17.1 0.0 collective-permute-done.4.slab_a
  17.1 1.3 %collective-permute-done.5.slab_b = bf16[2,16,512]{2,1,0:T(8,128)(2,1)S(1)} collective-permute-done((bf16[2,16,512]{2,1,0:T(8,128)(2,1)S(1)}, bf16[2,16,512]{2,1,0:T(8,128)(2,1)S(1)}, u32[]{:S(2)}, u32[]{:S(2)}) %collective-permute-start.5) | collective-permute-done | bytes 32800 | tf_op jit(solution)/shard_map/ppermute | solution.py:52
  18.4 1.1 %smooth.1 = (f32[14,40,512]{2,1,0:T(8,128)S(1)}, f32[14,40,512]{2,1,0:T(8,128)S(1)}, f32[12,40,512]{2,1,0:T(8,128)S(1)}, f32[4,16,256]{2,1,0:T(8,128)S(1)}, bf16...) custom-call(s32[1]{0:T(128)} %bitcast.me_ref, ...), custom_call_target="tpu_custom_call", output_to_operand_aliasing={{0}: (3, {}), {1}: (4, {}), {2}: (5, {})} | custom-call | tf_op jit(solution)/shard_map/smooth/pallas_call | solution.py:699
  19.5 0.1 collective-permute-start.6
  19.6 0.6 %collective-permute-start.7 = (bf16[1,16,256]{2,1,0:T(8,128)(2,1)S(1)}, bf16[1,16,256]{2,1,0:T(8,128)(2,1)S(1)}, u32[]{:S(2)}, u32[]{:S(2)}) collective-permute-start(bf16[1,16,256]{2,1,0:T(8,128)(2,1)S(1)} %get-tuple-element.98), channel_id=1, source_target_pairs={{0,3},{1,2},{2,1},{3,0},{4,7},{5,6},{6,5},{7,4},{8,11},{9,10},{10,... | collective-permute-start | bytes 24584 | tf_op jit(solution)/shard_map/ppermute | solution.py:52
  20.2 1.2 %collective-permute-start.10 = (bf16[32,16,128]{2,1,0:T(8,128)(2,1)S(1)}, bf16[32,16,128]{2,1,0:T(8,128)(2,1)S(1)}, u32[]{:S(2)}, u32[]{:S(2)}) collective-permute-start(bf16[32,16,128]{2,1,0:T(8,128)(2,1)S(1)} %get-tuple-element.108), channel_id=1, source_target_pairs={{0,3},{1,2},{2,1},{3,0},{4,7},{5,6},{6,5},{7,4},{8,11},{9,10},{10,... | collective-permute-start | bytes 393224 | tf_op jit(solution)/shard_map/ppermute | solution.py:52
  21.4 0.5 %collective-permute-start.11 = (bf16[32,16,128]{2,1,0:T(8,128)(2,1)S(1)}, bf16[32,16,128]{2,1,0:T(8,128)(2,1)S(1)}, u32[]{:S(2)}, u32[]{:S(2)}) collective-permute-start(bf16[32,16,128]{2,1,0:T(8,128)(2,1)S(1)} %get-tuple-element.109), channel_id=1, source_target_pairs={{0,2},{1,3},{2,0},{3,1},{4,6},{5,7},{6,4},{7,5},{8,10},{9,11},{10,... | collective-permute-start | bytes 393224 | tf_op jit(solution)/shard_map/ppermute | solution.py:40
  21.9 0.0 collective-permute-done.6.side_a
  21.9 0.8 %collective-permute-done.7.side_b = bf16[1,16,256]{2,1,0:T(8,128)(2,1)S(1)} collective-permute-done((bf16[1,16,256]{2,1,0:T(8,128)(2,1)S(1)}, bf16[1,16,256]{2,1,0:T(8,128)(2,1)S(1)}, u32[]{:S(2)}, u32[]{:S(2)}) %collective-permute-start.7) | collective-permute-done | bytes 8224 | tf_op jit(solution)/shard_map/ppermute | solution.py:52
  22.8 2.4 %collective-permute-start.9 = (bf16[10,16,256]{2,1,0:T(8,128)(2,1)S(1)}, bf16[10,16,256]{2,1,0:T(8,128)(2,1)S(1)}, u32[]{:S(2)}, u32[]{:S(2)}) collective-permute-start(bf16[10,16,256]{2,1,0:T(8,128)(2,1)S(1)} %get-tuple-element.112), channel_id=1, source_target_pairs={{0,28},{4,8},{8,4},{12,16},{16,12},{20,24},{24,20},{28,0},{1,29},{... | collective-permute-start | bytes 245768 | tf_op jit(solution)/shard_map/ppermute | solution.py:52
  25.2 0.0 collective-permute-start.8
  25.2 1.6 %post.1 = (f32[8,32,512]{2,1,0:T(8,128)S(1)}, bf16[512,512]{1,0:T(8,128)(2,1)S(1)}) custom-call(s32[1]{0:T(128)} %bitcast.me_ref, f32[14,40,512]{2,1,0:T(8,128)S(1)} %get-tuple-element.102.u1, f32[12,40,512]{2,1,0:T(8,128)S(1)} %get-tuple-element.103.u2_in, f32[14,40,512]{2,1,0:T(8,128)S(1)} %get-tuple-element.104.text_ref), custom_call_target="tpu_custom_call" | custom-call | flops 1073741824 | bytes 4194304 | tf_op jit(solution)/shard_map/post/pallas_call | solution.py:728
  26.8 0.0 collective-permute-done.10.rest_1_
  26.9 2.1 %collective-permute-done.11.rest_2_ = bf16[32,16,128]{2,1,0:T(8,128)(2,1)S(1)} collective-permute-done((bf16[32,16,128]{2,1,0:T(8,128)(2,1)S(1)}, bf16[32,16,128]{2,1,0:T(8,128)(2,1)S(1)}, u32[]{:S(2)}, u32[]{:S(2)}) %collective-permute-start.11) | collective-permute-done | bytes 131104 | tf_op jit(solution)/shard_map/ppermute | solution.py:40
  28.9 1.9 %collective-permute-done.9.slab_b = bf16[10,16,256]{2,1,0:T(8,128)(2,1)S(1)} collective-permute-done((bf16[10,16,256]{2,1,0:T(8,128)(2,1)S(1)}, bf16[10,16,256]{2,1,0:T(8,128)(2,1)S(1)}, u32[]{:S(2)}, u32[]{:S(2)}) %collective-permute-start.9) | collective-permute-done | bytes 81952 | tf_op jit(solution)/shard_map/ppermute | solution.py:52
  30.8 0.6 %collective-permute-done.8.slab_a = bf16[10,16,256]{2,1,0:T(8,128)(2,1)S(1)} collective-permute-done((bf16[10,16,256]{2,1,0:T(8,128)(2,1)S(1)}, bf16[10,16,256]{2,1,0:T(8,128)(2,1)S(1)}, u32[]{:S(2)}, u32[]{:S(2)}) %collective-permute-start.8) | collective-permute-done | bytes 81952 | tf_op jit(solution)/shard_map/ppermute | solution.py:52
  31.5 1.8 %correct.1 = (f32[8,32,512]{2,1,0:T(8,128)}, bf16[144,16,128]{2,1,0:T(8,128)(2,1)}) custom-call(s32[1]{0:T(128)} %bitcast.me_ref, s32[1]{0:T(128)} %bitcast.1.slab_ref, f32[4,16,256]{2,1,0:T(8,128)S(1)} %get-tuple-element.95.ct_ref, bf16[17,16,256]{2,1,0:T(8,128)(2,1)S(1)} %collective-permute-done.6.side_a, ...), custom_call_target="tpu_custom_call" | custom-call | tf_op jit(solution)/shard_map/correct/pallas_call | solution.py:738
  (3 shorter events, 0.0 us)
Async XLA Ops:
  3.3 8.2 %collective-permute-start = (bf16[4,16,512]{2,1,0:T(8,128)(2,1)S(1)}, bf16[4,16,512]{2,1,0:T(8,128)(2,1)S(1)}, u32[]{:S(2)}, u32[]{:S(2)}) collective-permute-start(bf16[4,16,512]{2,1,0:T(8,128)(2,1)S(1)} %get-tuple-element.69), channel_id=1, source_target_pairs={{0,1},{1,0},{2,3},{3,2},{4,5},{5,4},{6,7},{7,6},{8,9},{9,8},{10,11... | collective-permute-start | bytes 196616 | tf_op jit(solution)/shard_map/ppermute | solution.py:52
  3.8 7.7 %collective-permute-start.1 = (bf16[4,16,512]{2,1,0:T(8,128)(2,1)S(1)}, bf16[4,16,512]{2,1,0:T(8,128)(2,1)S(1)}, u32[]{:S(2)}, u32[]{:S(2)}) collective-permute-start(bf16[4,16,512]{2,1,0:T(8,128)(2,1)S(1)} %get-tuple-element.70), channel_id=1, source_target_pairs={{0,3},{1,2},{2,1},{3,0},{4,7},{5,6},{6,5},{7,4},{8,11},{9,10},{10,... | collective-permute-start | bytes 196616 | tf_op jit(solution)/shard_map/ppermute | solution.py:52
  6.5 9.3 %collective-permute-start.2 = (bf16[8,16,512]{2,1,0:T(8,128)(2,1)S(1)}, bf16[8,16,512]{2,1,0:T(8,128)(2,1)S(1)}, u32[]{:S(2)}, u32[]{:S(2)}) collective-permute-start(bf16[8,16,512]{2,1,0:T(8,128)(2,1)S(1)} %get-tuple-element.71), channel_id=1, source_target_pairs={{0,4},{4,0},{8,12},{12,8},{16,20},{20,16},{24,28},{28,24},{1,5},{5... | collective-permute-start | bytes 393224 | tf_op jit(solution)/shard_map/ppermute | solution.py:52
  8.0 8.0 %collective-permute-start.3 = (bf16[8,16,512]{2,1,0:T(8,128)(2,1)S(1)}, bf16[8,16,512]{2,1,0:T(8,128)(2,1)S(1)}, u32[]{:S(2)}, u32[]{:S(2)}) collective-permute-start(bf16[8,16,512]{2,1,0:T(8,128)(2,1)S(1)} %get-tuple-element.72), channel_id=1, source_target_pairs={{0,28},{4,8},{8,4},{12,16},{16,12},{20,24},{24,20},{28,0},{1,29},{... | collective-permute-start | bytes 393224 | tf_op jit(solution)/shard_map/ppermute | solution.py:52
  11.6 5.5 %collective-permute-start.4 = (bf16[2,16,512]{2,1,0:T(8,128)(2,1)S(1)}, bf16[2,16,512]{2,1,0:T(8,128)(2,1)S(1)}, u32[]{:S(2)}, u32[]{:S(2)}) collective-permute-start(bf16[2,16,512]{2,1,0:T(8,128)(2,1)S(1)} %get-tuple-element.78), channel_id=1, source_target_pairs={{0,4},{4,0},{8,12},{12,8},{16,20},{20,16},{24,28},{28,24},{1,5},{5... | collective-permute-start | bytes 98312 | tf_op jit(solution)/shard_map/ppermute | solution.py:52
  11.7 6.7 %collective-permute-start.5 = (bf16[2,16,512]{2,1,0:T(8,128)(2,1)S(1)}, bf16[2,16,512]{2,1,0:T(8,128)(2,1)S(1)}, u32[]{:S(2)}, u32[]{:S(2)}) collective-permute-start(bf16[2,16,512]{2,1,0:T(8,128)(2,1)S(1)} %get-tuple-element.79), channel_id=1, source_target_pairs={{0,28},{4,8},{8,4},{12,16},{16,12},{20,24},{24,20},{28,0},{1,29},{... | collective-permute-start | bytes 98312 | tf_op jit(solution)/shard_map/ppermute | solution.py:52
  19.5 2.4 %collective-permute-start.6 = (bf16[17,16,256]{2,1,0:T(8,128)(2,1)S(1)}, bf16[17,16,256]{2,1,0:T(8,128)(2,1)S(1)}, u32[]{:S(2)}, u32[]{:S(2)}) collective-permute-start(bf16[17,16,256]{2,1,0:T(8,128)(2,1)S(1)} %pad_maximum_fusion), channel_id=1, source_target_pairs={{0,1},{1,0},{2,3},{3,2},{4,5},{5,4},{6,7},{7,6},{8,9},{9,8},{10,11... | collective-permute-start | bytes 417800 | tf_op jit(solution)/shard_map/ppermute | solution.py:52
  19.6 3.1 %collective-permute-start.7 = (bf16[1,16,256]{2,1,0:T(8,128)(2,1)S(1)}, bf16[1,16,256]{2,1,0:T(8,128)(2,1)S(1)}, u32[]{:S(2)}, u32[]{:S(2)}) collective-permute-start(bf16[1,16,256]{2,1,0:T(8,128)(2,1)S(1)} %get-tuple-element.98), channel_id=1, source_target_pairs={{0,3},{1,2},{2,1},{3,0},{4,7},{5,6},{6,5},{7,4},{8,11},{9,10},{10,... | collective-permute-start | bytes 24584 | tf_op jit(solution)/shard_map/ppermute | solution.py:52
  20.2 6.6 %collective-permute-start.10 = (bf16[32,16,128]{2,1,0:T(8,128)(2,1)S(1)}, bf16[32,16,128]{2,1,0:T(8,128)(2,1)S(1)}, u32[]{:S(2)}, u32[]{:S(2)}) collective-permute-start(bf16[32,16,128]{2,1,0:T(8,128)(2,1)S(1)} %get-tuple-element.108), channel_id=1, source_target_pairs={{0,3},{1,2},{2,1},{3,0},{4,7},{5,6},{6,5},{7,4},{8,11},{9,10},{10,... | collective-permute-start | bytes 393224 | tf_op jit(solution)/shard_map/ppermute | solution.py:52
  21.4 7.5 %collective-permute-start.11 = (bf16[32,16,128]{2,1,0:T(8,128)(2,1)S(1)}, bf16[32,16,128]{2,1,0:T(8,128)(2,1)S(1)}, u32[]{:S(2)}, u32[]{:S(2)}) collective-permute-start(bf16[32,16,128]{2,1,0:T(8,128)(2,1)S(1)} %get-tuple-element.109), channel_id=1, source_target_pairs={{0,2},{1,3},{2,0},{3,1},{4,6},{5,7},{6,4},{7,5},{8,10},{9,11},{10,... | collective-permute-start | bytes 393224 | tf_op jit(solution)/shard_map/ppermute | solution.py:40
  22.8 8.0 %collective-permute-start.9 = (bf16[10,16,256]{2,1,0:T(8,128)(2,1)S(1)}, bf16[10,16,256]{2,1,0:T(8,128)(2,1)S(1)}, u32[]{:S(2)}, u32[]{:S(2)}) collective-permute-start(bf16[10,16,256]{2,1,0:T(8,128)(2,1)S(1)} %get-tuple-element.112), channel_id=1, source_target_pairs={{0,28},{4,8},{8,4},{12,16},{16,12},{20,24},{24,20},{28,0},{1,29},{... | collective-permute-start | bytes 245768 | tf_op jit(solution)/shard_map/ppermute | solution.py:52
  25.2 6.3 %collective-permute-start.8 = (bf16[10,16,256]{2,1,0:T(8,128)(2,1)S(1)}, bf16[10,16,256]{2,1,0:T(8,128)(2,1)S(1)}, u32[]{:S(2)}, u32[]{:S(2)}) collective-permute-start(bf16[10,16,256]{2,1,0:T(8,128)(2,1)S(1)} %get-tuple-element.113), channel_id=1, source_target_pairs={{0,4},{4,0},{8,12},{12,8},{16,20},{20,16},{24,28},{28,24},{1,5},{5... | collective-permute-start | bytes 245768 | tf_op jit(solution)/shard_map/ppermute | solution.py:52
